TPU v7x, 32 devices: a whole 2x2x4 slice. The times are simulated.
32 devices in a mesh: seq: 8 (over z, x), fsdp: 4 (over y, core).
Axes of the slice: x: 2, y: 2, z: 4, core: 2. Of those that a mesh axis runs over, the one named last changes fastest.
Arguments:
- states: bfloat16 [4, 1024, 276], P('fsdp', 'seq'), may hold values from -6 to 6
- targets: bfloat16 [4, 1024, 276], P('fsdp', 'seq'), may hold values from -6 to 6
- lengths: int32 [4], P('fsdp'), may hold values from 1 to 2, as said below
- intervals: int32 [4], replicated, may hold values from 0 to 2
- qkv_copy: bfloat16 [1024, 3072], P(None, 'fsdp'), may hold values from -0.1875 to 0.1875
- qkv_master: float32 [1024, 3072], P('seq', 'fsdp'), may hold values from -0.1875 to 0.1875
- qkv_moment: float32 [1024, 3072], P('seq', 'fsdp')
- out_copy: bfloat16 [1024, 1024], P(None, 'fsdp'), may hold values from -0.1875 to 0.1875
- out_master: float32 [1024, 1024], P('seq', 'fsdp'), may hold values from -0.1875 to 0.1875
- out_moment: float32 [1024, 1024], P('seq', 'fsdp')
- up_copy: bfloat16 [1024, 4096], P(None, 'fsdp'), may hold values from -0.1875 to 0.1875
- up_master: float32 [1024, 4096], P('seq', 'fsdp'), may hold values from -0.1875 to 0.1875
- up_moment: float32 [1024, 4096], P('seq', 'fsdp')
- down_copy: bfloat16 [1024, 4096], P(None, 'fsdp'), may hold values from -0.09375 to 0.09375
- down_master: float32 [1024, 4096], P('seq', 'fsdp'), may hold values from -0.09375 to 0.09375
- down_moment: float32 [1024, 4096], P('seq', 'fsdp')
- ada_copy: bfloat16 [1024, 6144], P(None, 'fsdp'), may hold values from -0.1875 to 0.1875
- ada_master: float32 [1024, 6144], P('seq', 'fsdp'), may hold values from -0.1875 to 0.1875
- ada_first: float32 [1024, 6144], P('seq', 'fsdp'), may hold values from -3.8146973e-06 to 3.8146973e-06
- ada_second: float32 [1024, 6144], P('seq', 'fsdp'), may hold values from 2.5853053e-13 to 1.0243662e-12
- io_proj: float32 [2, 276, 1024], P(None, None, 'fsdp'), may hold values from -0.375 to 0.375
- io_first: float32 [2, 276, 1024], P(None, None, 'fsdp'), may hold values from -3.8146973e-06 to 3.8146973e-06
- io_second: float32 [2, 276, 1024], P(None, None, 'fsdp'), may hold values from 2.5853053e-13 to 1.0243662e-12
- cond_table: float32 [5, 1024], P(None, 'fsdp'), may hold values from -6 to 6
- cond_first: float32 [5, 1024], P(None, 'fsdp'), may hold values from -3.8146973e-06 to 3.8146973e-06
- cond_second: float32 [5, 1024], P(None, 'fsdp'), may hold values from 2.5853053e-13 to 1.0243662e-12
- pos_table: float32 [1024, 1024], P('seq', 'fsdp'), may hold values from -6 to 6
- pos_first: float32 [1024, 1024], P('seq', 'fsdp'), may hold values from -1.1920929e-07 to 1.1920929e-07
- pos_second: float32 [1024, 1024], P('seq', 'fsdp'), may hold values from 2.5247122e-16 to 1.0003577e-15
- biases: float32 [7168], P('fsdp'), may hold values from -1.5 to 1.5
- bias_first: float32 [7168], P('fsdp'), may hold values from -3.8146973e-06 to 3.8146973e-06
- bias_second: float32 [7168], P('fsdp'), may hold values from 2.5853053e-13 to 1.0243662e-12
Outputs:
- loss_total: float32 [], replicated
- grad_norm: float32 [], replicated
- moment_sizes: float32 [4], replicated
- qkv_new: float32 [1024, 3072], P('seq', 'fsdp')
- qkv_moment_new: float32 [1024, 3072], P('seq', 'fsdp')
- qkv_copy_new: bfloat16 [1024, 3072], P(None, 'fsdp')
- out_new: float32 [1024, 1024], P('seq', 'fsdp')
- out_moment_new: float32 [1024, 1024], P('seq', 'fsdp')
- out_copy_new: bfloat16 [1024, 1024], P(None, 'fsdp')
- up_new: float32 [1024, 4096], P('seq', 'fsdp')
- up_moment_new: float32 [1024, 4096], P('seq', 'fsdp')
- up_copy_new: bfloat16 [1024, 4096], P(None, 'fsdp')
- down_new: float32 [1024, 4096], P('seq', 'fsdp')
- down_moment_new: float32 [1024, 4096], P('seq', 'fsdp')
- down_copy_new: bfloat16 [1024, 4096], P(None, 'fsdp')
- ada_new: float32 [1024, 6144], P('seq', 'fsdp')
- ada_first_new: float32 [1024, 6144], P('seq', 'fsdp')
- ada_second_new: float32 [1024, 6144], P('seq', 'fsdp')
- io_new: float32 [2, 276, 1024], P(None, None, 'fsdp')
- io_first_new: float32 [2, 276, 1024], P(None, None, 'fsdp')
- io_second_new: float32 [2, 276, 1024], P(None, None, 'fsdp')
- cond_new: float32 [5, 1024], P(None, 'fsdp')
- cond_first_new: float32 [5, 1024], P(None, 'fsdp')
- cond_second_new: float32 [5, 1024], P(None, 'fsdp')
- pos_new: float32 [1024, 1024], P('seq', 'fsdp')
- pos_first_new: float32 [1024, 1024], P('seq', 'fsdp')
- pos_second_new: float32 [1024, 1024], P('seq', 'fsdp')
- bias_new: float32 [7168], P('fsdp')
- bias_first_new: float32 [7168], P('fsdp')
- bias_second_new: float32 [7168], P('fsdp')
Inputs may be any that keep to these rules, and one draw needn't show every extreme that they name: `lengths`: every value is reached by some sample, 1 and 2 in every draw.
All inputs are finite; a program needn't handle non-finite values.
Results may differ from a plain program's by a relative error of at most 0.03.
Values may be sent and summed in bfloat16 or wider, within the bound.
A program may use at most 448 MiB of HBM per device.

v0:
```python
import math

import jax
import jax.numpy as jnp
from jax import lax
from jax.sharding import PartitionSpec as P

HEADS = 16
HEAD = 64
NI = 3
ROLL = 2
NS_ITERS = 5
STEP_NUM = 10
LON = 32


EPS_NORM = 1e-06
NS_A = 3.4445
NS_B = -4.775
NS_C = 2.0315
MOMENTUM = 0.5
RATE_MUON = 0.15
DECAY_MUON = 0.1
RATE_ADAM = 0.05
RATE_TABLE = 0.5
DECAY_ADAM = 0.1
BETA_FIRST = 0.9
BETA_SECOND = 0.95
CLIP_LIMIT = 0.01
HIGHEST_PRECISION = lax.Precision.HIGHEST


def broadcast(block, axis, owner):
    block = jnp.where(lax.axis_index(axis) == owner, block, jnp.zeros_like(block))
    return lax.psum(block, axis)


def product(left, right):
    return jnp.dot(left, right, preferred_element_type=jnp.float32)


def dot_last(left, right):
    return lax.dot_general(
        left, right, (((left.ndim - 1,), (1,)), ((), ())), preferred_element_type=jnp.float32
    )


def rows_product(left, right):
    flat_left = left.reshape(-1, left.shape[-1])
    flat_right = right.reshape(-1, right.shape[-1])
    return lax.dot_general(
        flat_left, flat_right, (((0,), (0,)), ((), ())), preferred_element_type=jnp.float32
    )


def layer_norm(values):
    centred = values - jnp.mean(values, -1, keepdims=True)
    inverse = lax.rsqrt(jnp.mean(centred * centred, -1, keepdims=True) + EPS_NORM)
    return (centred * inverse, inverse)


def norm_back(grad, normed, inverse):
    return inverse * (
        grad
        - jnp.mean(grad, -1, keepdims=True)
        - normed * jnp.mean(grad * normed, -1, keepdims=True)
    )


def heads_view(values):
    return values.reshape(values.shape[0], values.shape[1], HEADS, HEAD)


def modulation(modul, width):
    return [modul[:, None, column * width : (column + 1) * width] for column in range(6)]


def latitude_weights(local):
    all_patches = local * lax.axis_size("seq")
    band_row = (jnp.arange(all_patches, dtype=jnp.int32) // LON).astype(jnp.float32)
    latitude = (band_row + 0.5) * (math.pi / (all_patches // LON)) - math.pi / 2
    cosine = jnp.cos(latitude)
    weights = cosine / jnp.mean(cosine)
    return lax.dynamic_slice_in_dim(weights, lax.axis_index("seq") * local, local)


def forward_step(weights, state, active, select):
    w_qkv, w_out, w_up, w_down, w_ada, io_all, table, pos, bias = weights
    width = w_out.shape[0]
    cond_vec = jnp.dot(select, table.astype(jnp.float32), precision=HIGHEST_PRECISION)
    silu_low = jax.nn.silu(cond_vec).astype(jnp.bfloat16)
    modul = product(silu_low, w_ada) + bias[: 6 * width].astype(jnp.float32)
    shift1, scale1, gate1, shift2, scale2, gate2 = modulation(modul, width)
    state_low = state.astype(jnp.bfloat16)
    embedded = (
        product(state_low, io_all[0])
        + bias[6 * width :].astype(jnp.float32)
        + pos.astype(jnp.float32)
    )
    normed_one, inverse_one = layer_norm(embedded)
    normed_a = (normed_one * (1.0 + scale1) + shift1).astype(jnp.bfloat16)
    qkv = product(normed_a, w_qkv).astype(jnp.bfloat16)
    queries = qkv[..., :width]
    keys, values = (
        lax.all_gather(qkv[..., width : 2 * width], "seq", axis=1, tiled=True),
        lax.all_gather(qkv[..., 2 * width :], "seq", axis=1, tiled=True),
    )
    scores = jnp.einsum(
        "sphd,snhd->shpn", heads_view(queries), heads_view(keys), preferred_element_type=jnp.float32
    ) * HEAD ** (-0.5)
    top_score = jnp.max(scores, -1, keepdims=True)
    expo = jnp.exp(scores - top_score)
    total_exp = jnp.sum(expo, -1, keepdims=True)
    log_total = top_score + jnp.log(total_exp)
    probs_low = (expo / total_exp).astype(jnp.bfloat16)
    mixed = jnp.einsum(
        "shpn,snhd->sphd", probs_low, heads_view(values), preferred_element_type=jnp.float32
    )
    mixed_low = mixed.reshape(queries.shape).astype(jnp.bfloat16)
    attended = product(mixed_low, w_out)
    after_attn = embedded + gate1 * attended
    normed_two, inverse_two = layer_norm(after_attn)
    normed_b = (normed_two * (1.0 + scale2) + shift2).astype(jnp.bfloat16)
    upward = product(normed_b, w_up)
    hidden = jax.nn.gelu(upward).astype(jnp.bfloat16)
    downward = dot_last(hidden, w_down)
    after_mlp = after_attn + gate2 * downward
    normed_three, inverse_three = layer_norm(after_mlp)
    normed_c = normed_three.astype(jnp.bfloat16)
    delta = dot_last(normed_c, io_all[1])
    kept = (
        cond_vec,
        silu_low,
        modul,
        state_low,
        normed_one,
        inverse_one,
        normed_a,
        queries,
        keys,
        values,
        log_total,
        mixed_low,
        attended,
        normed_two,
        inverse_two,
        normed_b,
        upward,
        hidden,
        downward,
        normed_three,
        inverse_three,
        normed_c,
    )
    return (state + active * delta, kept)


def backward_step(weights, kept, grad_state, active, select):
    w_qkv, w_out, w_up, w_down, w_ada, io_all, table, pos, bias = weights
    (
        cond_vec,
        silu_low,
        modul,
        state_low,
        normed_one,
        inverse_one,
        normed_a,
        queries,
        keys,
        values,
        log_total,
        mixed_low,
        attended,
        normed_two,
        inverse_two,
        normed_b,
        upward,
        hidden,
        downward,
        normed_three,
        inverse_three,
        normed_c,
    ) = kept
    width = w_out.shape[0]
    shift1, scale1, gate1, shift2, scale2, gate2 = modulation(modul, width)
    delta_grad = (active * grad_state).astype(jnp.bfloat16)
    grad_head = rows_product(delta_grad, normed_c)
    grad_mlp = norm_back(product(delta_grad, io_all[1]), normed_three, inverse_three)
    grad_gate2 = jnp.sum(grad_mlp * downward, 1)
    down_grad = (gate2 * grad_mlp).astype(jnp.bfloat16)
    grad_down = rows_product(down_grad, hidden)
    grad_hidden = product(down_grad, w_down)
    up_grad = jax.vjp(jax.nn.gelu, upward)[1](grad_hidden)[0].astype(jnp.bfloat16)
    grad_up = rows_product(normed_b, up_grad)
    grad_normed_b = dot_last(up_grad, w_up)
    grad_scale2 = jnp.sum(grad_normed_b * normed_two, 1)
    grad_shift2 = jnp.sum(grad_normed_b, 1)
    grad_attn = grad_mlp + norm_back(grad_normed_b * (1.0 + scale2), normed_two, inverse_two)
    grad_gate1 = jnp.sum(grad_attn * attended, 1)
    attn_grad = (gate1 * grad_attn).astype(jnp.bfloat16)
    grad_out = rows_product(mixed_low, attn_grad)
    mixed_grad = dot_last(attn_grad, w_out).astype(jnp.bfloat16)
    q_heads = heads_view(queries)
    k_heads = heads_view(keys)
    v_heads = heads_view(values)
    g_heads = heads_view(mixed_grad)
    scores = jnp.einsum(
        "sphd,snhd->shpn", q_heads, k_heads, preferred_element_type=jnp.float32
    ) * HEAD ** (-0.5)
    probs = jnp.exp(scores - log_total)
    probs_low = probs.astype(jnp.bfloat16)
    grad_probs = jnp.einsum("sphd,snhd->shpn", g_heads, v_heads, preferred_element_type=jnp.float32)
    score_grad = (
        HEAD ** (-0.5) * probs * (grad_probs - jnp.sum(grad_probs * probs, -1, keepdims=True))
    ).astype(jnp.bfloat16)
    grad_queries = jnp.einsum(
        "shpn,snhd->sphd", score_grad, k_heads, preferred_element_type=jnp.float32
    ).reshape(queries.shape)
    key_part = jnp.einsum(
        "shpn,sphd->snhd", score_grad, q_heads, preferred_element_type=jnp.float32
    ).reshape(keys.shape)
    value_part = jnp.einsum(
        "shpn,sphd->snhd", probs_low, g_heads, preferred_element_type=jnp.float32
    ).reshape(values.shape)
    grad_keys, grad_values = (
        lax.psum_scatter(key_part, "seq", scatter_dimension=1, tiled=True),
        lax.psum_scatter(value_part, "seq", scatter_dimension=1, tiled=True),
    )
    qkv_grad = jnp.concatenate([grad_queries, grad_keys, grad_values], -1).astype(jnp.bfloat16)
    grad_qkv = rows_product(normed_a, qkv_grad)
    grad_normed_a = dot_last(qkv_grad, w_qkv)
    grad_scale1 = jnp.sum(grad_normed_a * normed_one, 1)
    grad_shift1 = jnp.sum(grad_normed_a, 1)
    grad_embedded = grad_attn + norm_back(grad_normed_a * (1.0 + scale1), normed_one, inverse_one)
    embed_grad = grad_embedded.astype(jnp.bfloat16)
    grad_embed = rows_product(state_low, embed_grad)
    grad_prev = grad_state + dot_last(embed_grad, io_all[0])
    grad_modul = jnp.concatenate(
        [grad_shift1, grad_scale1, grad_gate1, grad_shift2, grad_scale2, grad_gate2], -1
    )
    grad_ada = lax.dot_general(
        silu_low.astype(jnp.float32),
        grad_modul,
        (((0,), (0,)), ((), ())),
        precision=HIGHEST_PRECISION,
    )
    grad_silu = lax.dot_general(
        grad_modul, w_ada.astype(jnp.float32), (((1,), (1,)), ((), ())), precision=HIGHEST_PRECISION
    )
    grad_cond = jax.vjp(jax.nn.silu, cond_vec)[1](grad_silu)[0]
    grad_table = lax.dot_general(
        select, grad_cond, (((0,), (0,)), ((), ())), precision=HIGHEST_PRECISION
    )
    grad_bias = jnp.concatenate([jnp.sum(grad_modul, 0), jnp.sum(grad_embedded, (0, 1))])
    grad_pos = jnp.sum(grad_embedded, 0)
    grads = (
        grad_qkv,
        grad_out,
        grad_up,
        grad_down,
        grad_ada,
        jnp.stack([grad_embed, grad_head]),
        grad_table,
        grad_pos,
        grad_bias,
    )
    return (grad_prev, grads)


def gram_part(block_cols):
    return lax.dot_general(
        block_cols, block_cols, (((1,), (1,)), ((), ())), preferred_element_type=jnp.float32
    )


def zero_gram(block_cols):
    return jnp.zeros((block_cols.shape[0], block_cols.shape[0]), jnp.float32)


def newton_step(block_cols, gram):
    gram_low = gram.astype(jnp.bfloat16)
    poly = (NS_B * gram_low.astype(jnp.float32) + NS_C * product(gram_low, gram_low)).astype(
        jnp.bfloat16
    )
    return (NS_A * block_cols.astype(jnp.float32) + product(poly, block_cols)).astype(jnp.bfloat16)


def keep_block(block_cols, gram):
    return block_cols


def adam_update(weight, first, second, grad, rate):
    first_new = BETA_FIRST * first + (1.0 - BETA_FIRST) * grad
    second_new = BETA_SECOND * second + (1.0 - BETA_SECOND) * grad * grad
    unbiased = first_new / (1.0 - BETA_FIRST**STEP_NUM)
    spread = jnp.sqrt(second_new / (1.0 - BETA_SECOND**STEP_NUM)) + 1e-08
    return (weight * (1.0 - rate * DECAY_ADAM) - rate * unbiased / spread, first_new, second_new)


def body(
    states,
    targets,
    lengths,
    intervals,
    qkv_copy,
    qkv_master,
    qkv_moment,
    out_copy,
    out_master,
    out_moment,
    up_copy,
    up_master,
    up_moment,
    down_copy,
    down_master,
    down_moment,
    ada_copy,
    ada_master,
    ada_first,
    ada_second,
    io_proj,
    io_first,
    io_second,
    cond_table,
    cond_first,
    cond_second,
    pos_table,
    pos_first,
    pos_second,
    biases,
    bias_first,
    bias_second,
):
    weights = (
        lax.all_gather(qkv_copy, "fsdp", axis=1, tiled=True),
        lax.all_gather(out_copy, "fsdp", axis=1, tiled=True),
        lax.all_gather(up_copy, "fsdp", axis=1, tiled=True),
        lax.all_gather(down_copy, "fsdp", axis=1, tiled=True),
        lax.all_gather(ada_copy, "fsdp", axis=1, tiled=True),
        lax.all_gather(io_proj.astype(jnp.bfloat16), "fsdp", axis=2, tiled=True),
        lax.all_gather(cond_table.astype(jnp.bfloat16), "fsdp", axis=1, tiled=True),
        lax.all_gather(pos_table.astype(jnp.bfloat16), "fsdp", axis=1, tiled=True),
        lax.all_gather(biases.astype(jnp.bfloat16), "fsdp", axis=0, tiled=True),
    )
    samples, local, values_count = states.shape
    table_rows = cond_table.shape[0]
    my_ids = lax.dynamic_slice_in_dim(intervals, lax.axis_index("fsdp") * samples, samples)
    counts = jnp.sum(
        (intervals[:, None] == jnp.arange(NI, dtype=jnp.int32)[None]).astype(jnp.float32), 0
    )
    id_counts = jnp.sum(
        (my_ids[:, None] == jnp.arange(NI, dtype=jnp.int32)[None]).astype(jnp.float32)
        * counts[None],
        1,
    )
    weight = 1.0 / (NI * local * lax.axis_size("seq") * values_count * id_counts)
    rows_iota = jnp.arange(table_rows, dtype=jnp.int32)
    id_select = (my_ids[:, None] == rows_iota[None]).astype(jnp.float32)
    state = states.astype(jnp.float32)
    seen_states = []
    kept_all = []
    for step in range(ROLL):
        select = id_select + (rows_iota == NI + step).astype(jnp.float32)[None]
        active = (step < lengths).astype(jnp.float32)[:, None, None]
        seen_states.append(state)
        state, kept = forward_step(weights, state, active, select)
        kept_all.append(kept)
    lat = latitude_weights(local)
    diff = state - targets.astype(jnp.float32)
    err = jnp.sum(jnp.sum(diff * diff, -1) * lat[None], -1)
    loss_local = jnp.sum(weight * err)
    grad_state = 2.0 * weight[:, None, None] * lat[None, :, None] * diff
    totals = None
    for step in reversed(range(ROLL)):
        select = id_select + (rows_iota == NI + step).astype(jnp.float32)[None]
        active = (step < lengths).astype(jnp.float32)[:, None, None]
        kept = kept_all[step]
        grad_state, grads = backward_step(weights, kept, grad_state, active, select)
        totals = grads if totals is None else jax.tree.map(jnp.add, totals, grads)
    reduced = (
        lax.psum_scatter(totals[0], "fsdp", scatter_dimension=1, tiled=True),
        lax.psum_scatter(totals[1], "fsdp", scatter_dimension=1, tiled=True),
        lax.psum_scatter(totals[2], "fsdp", scatter_dimension=1, tiled=True),
        lax.psum_scatter(totals[3], "fsdp", scatter_dimension=1, tiled=True),
        lax.psum_scatter(totals[4], "fsdp", scatter_dimension=1, tiled=True),
        lax.psum_scatter(totals[5], "fsdp", scatter_dimension=2, tiled=True),
        lax.psum_scatter(totals[6], "fsdp", scatter_dimension=1, tiled=True),
        lax.psum_scatter(totals[7], "fsdp", scatter_dimension=1, tiled=True),
        lax.psum_scatter(totals[8], "fsdp", scatter_dimension=0, tiled=True),
    )
    large = (
        lax.psum_scatter(reduced[0], "seq", scatter_dimension=0, tiled=True),
        lax.psum_scatter(reduced[1], "seq", scatter_dimension=0, tiled=True),
        lax.psum_scatter(reduced[2], "seq", scatter_dimension=0, tiled=True),
        lax.psum_scatter(reduced[3], "seq", scatter_dimension=0, tiled=True),
        lax.psum_scatter(reduced[4], "seq", scatter_dimension=0, tiled=True),
    )
    small = lax.psum((reduced[5], reduced[6], reduced[8]), "seq")
    grad_pos = reduced[7]
    first_copy = (lax.axis_index("seq") == 0).astype(jnp.float32)
    squares = jnp.sum(grad_pos * grad_pos)
    for item in large:
        squares = squares + jnp.sum(item * item)
    small_squares = jnp.float32(0.0)
    for item in small:
        small_squares = small_squares + jnp.sum(item * item)
    squares, loss_total = lax.psum(
        (squares + first_copy * small_squares, loss_local), ("seq", "fsdp")
    )
    grad_norm = jnp.sqrt(squares)
    clip = jnp.minimum(1.0, CLIP_LIMIT / (grad_norm + 1e-06))
    masters = (qkv_master, out_master, up_master, down_master)
    moments = [
        MOMENTUM * old + clip * grad
        for old, grad in zip((qkv_moment, out_moment, up_moment, down_moment), large[:4])
    ]
    norms = lax.psum(
        (
            jnp.sum(moments[0] * moments[0]),
            jnp.sum(moments[1] * moments[1]),
            jnp.sum(moments[2] * moments[2]),
            jnp.sum(moments[3] * moments[3]),
        ),
        ("seq", "fsdp"),
    )
    sizes = [jnp.sqrt(norms[which]) for which in range(4)]
    moment_sizes = jnp.stack(sizes) / CLIP_LIMIT
    scaled = [(moments[which] / (sizes[which] + 1e-07)).astype(jnp.bfloat16) for which in range(4)]
    columns = (
        lax.all_gather(scaled[0], "seq", axis=0, tiled=True),
        lax.all_gather(scaled[1], "seq", axis=0, tiled=True),
        lax.all_gather(scaled[2], "seq", axis=0, tiled=True),
        lax.all_gather(scaled[3], "seq", axis=0, tiled=True),
    )
    seq_index = lax.axis_index("seq")
    seq_count = lax.axis_size("seq")
    owners = [seq_index == which % seq_count for which in range(4)]
    blocks = list(columns)
    for turn in range(NS_ITERS):
        partial_value = [
            lax.cond(owners[which], gram_part, zero_gram, blocks[which]) for which in range(4)
        ]
        grams = lax.psum(
            (partial_value[0], partial_value[1], partial_value[2], partial_value[3]), "fsdp"
        )
        blocks = [
            lax.cond(owners[which], newton_step, keep_block, blocks[which], grams[which])
            for which in range(4)
        ]
    blocks = [broadcast(blocks[which], "seq", which % seq_count) for which in range(4)]
    row_count = qkv_master.shape[0]
    fresh = []
    for which in range(4):
        my_rows = lax.dynamic_slice_in_dim(
            blocks[which], seq_index * row_count, row_count, 0
        ).astype(jnp.float32)
        all_cols = masters[which].shape[1] * lax.axis_size("fsdp")
        fresh.append(
            masters[which] * (1.0 - RATE_MUON * DECAY_MUON)
            - RATE_MUON * 0.2 * math.sqrt(all_cols) * my_rows
        )
    copies = (
        lax.all_gather(fresh[0].astype(jnp.bfloat16), "seq", axis=0, tiled=True),
        lax.all_gather(fresh[1].astype(jnp.bfloat16), "seq", axis=0, tiled=True),
        lax.all_gather(fresh[2].astype(jnp.bfloat16), "seq", axis=0, tiled=True),
        lax.all_gather(fresh[3].astype(jnp.bfloat16), "seq", axis=0, tiled=True),
    )
    ada_res = adam_update(ada_master, ada_first, ada_second, clip * large[4], RATE_ADAM)
    io_res = adam_update(io_proj, io_first, io_second, clip * small[0], RATE_ADAM)
    cond_res = adam_update(cond_table, cond_first, cond_second, clip * small[1], RATE_TABLE)
    pos_res = adam_update(pos_table, pos_first, pos_second, clip * grad_pos, RATE_TABLE)
    bias_res = adam_update(biases, bias_first, bias_second, clip * small[2], RATE_ADAM)
    return (
        loss_total,
        grad_norm,
        moment_sizes,
        fresh[0],
        moments[0],
        copies[0],
        fresh[1],
        moments[1],
        copies[1],
        fresh[2],
        moments[2],
        copies[2],
        fresh[3],
        moments[3],
        copies[3],
        ada_res[0],
        ada_res[1],
        ada_res[2],
        io_res[0],
        io_res[1],
        io_res[2],
        cond_res[0],
        cond_res[1],
        cond_res[2],
        pos_res[0],
        pos_res[1],
        pos_res[2],
        bias_res[0],
        bias_res[1],
        bias_res[2],
    )


def solution(mesh):
    return jax.shard_map(
        body,
        mesh=mesh,
        in_specs=(
            P("fsdp", "seq", None),
            P("fsdp", "seq", None),
            P("fsdp"),
            P(),
            P(None, "fsdp"),
            P("seq", "fsdp"),
            P("seq", "fsdp"),
            P(None, "fsdp"),
            P("seq", "fsdp"),
            P("seq", "fsdp"),
            P(None, "fsdp"),
            P("seq", "fsdp"),
            P("seq", "fsdp"),
            P(None, "fsdp"),
            P("seq", "fsdp"),
            P("seq", "fsdp"),
            P(None, "fsdp"),
            P("seq", "fsdp"),
            P("seq", "fsdp"),
            P("seq", "fsdp"),
            P(None, None, "fsdp"),
            P(None, None, "fsdp"),
            P(None, None, "fsdp"),
            P(None, "fsdp"),
            P(None, "fsdp"),
            P(None, "fsdp"),
            P("seq", "fsdp"),
            P("seq", "fsdp"),
            P("seq", "fsdp"),
            P("fsdp"),
            P("fsdp"),
            P("fsdp"),
        ),
        out_specs=(
            P(),
            P(),
            P(),
            P("seq", "fsdp"),
            P("seq", "fsdp"),
            P(None, "fsdp"),
            P("seq", "fsdp"),
            P("seq", "fsdp"),
            P(None, "fsdp"),
            P("seq", "fsdp"),
            P("seq", "fsdp"),
            P(None, "fsdp"),
            P("seq", "fsdp"),
            P("seq", "fsdp"),
            P(None, "fsdp"),
            P("seq", "fsdp"),
            P("seq", "fsdp"),
            P("seq", "fsdp"),
            P(None, None, "fsdp"),
            P(None, None, "fsdp"),
            P(None, None, "fsdp"),
            P(None, "fsdp"),
            P(None, "fsdp"),
            P(None, "fsdp"),
            P("seq", "fsdp"),
            P("seq", "fsdp"),
            P("seq", "fsdp"),
            P("fsdp"),
            P("fsdp"),
            P("fsdp"),
        ),
        check_vma=False,
    )
```

profile of v0, /device:TPU:0, one launch (start us, length us, event | category | flops | bytes accessed | tf_op | source)
XLA Modules:
  0.0 4348.7 jit_solution(2908969322451352261)
XLA Ops:
  37.5 76.7 %all-gather.20.cloned.1.call-done = bf16[1024,6144]{1,0:T(8,128)(2,1)} async-done(((bf16[1024,1536]{1,0:T(8,128)(2,1)}), bf16[1024,6144]{1,0:T(8,128)(2,1)}) %all-gather.20.cloned.1.call-update) | async-done | bytes 12582928 | tf_op jit(solution)/shard_map/all_gather | solution.py:339
  124.4 37.8 all-gather.22.cloned.1.call-done
  172.3 44.0 %all-gather.26.cloned.1.call-done = bf16[1,1024,1024]{2,1,0:T(8,128)(2,1)} async-done(((bf16[1,128,1024]{2,1,0:T(8,128)(2,1)}), bf16[1,1024,1024]{2,1,0:T(8,128)(2,1)}) %all-gather.26.cloned.1.call-update) | async-done | bytes 2097168 | tf_op jit(solution)/shard_map/all_gather | solution.py:105
  219.2 47.5 %all-gather.24.cloned.1.call-done = bf16[1,1024,1024]{2,1,0:T(8,128)(2,1)} async-done(((bf16[1,128,1024]{2,1,0:T(8,128)(2,1)}), bf16[1,1024,1024]{2,1,0:T(8,128)(2,1)}) %all-gather.24.cloned.1.call-update) | async-done | bytes 2097168 | tf_op jit(solution)/shard_map/all_gather | solution.py:106
  278.1 11.4 all-gather.28.cloned.1.call-done
  292.6 56.8 %all-gather.30.cloned.1.call-done = bf16[1024,4096]{1,0:T(8,128)(2,1)} async-done(((bf16[1024,1024]{1,0:T(8,128)(2,1)}), bf16[1024,4096]{1,0:T(8,128)(2,1)}) %all-gather.30.cloned.1.call-update) | async-done | bytes 8388624 | tf_op jit(solution)/shard_map/all_gather | solution.py:337
  354.2 55.1 %all-gather.32.cloned.1.call-done = bf16[1024,4096]{1,0:T(8,128)(2,1)} async-done(((bf16[1024,1024]{1,0:T(8,128)(2,1)}), bf16[1024,4096]{1,0:T(8,128)(2,1)}) %all-gather.32.cloned.1.call-update) | async-done | bytes 8388624 | tf_op jit(solution)/shard_map/all_gather | solution.py:338
  425.6 44.6 %all-gather.36.cloned.1.call-done = bf16[1,1024,1024]{2,1,0:T(8,128)(2,1)} async-done(((bf16[1,128,1024]{2,1,0:T(8,128)(2,1)}), bf16[1,1024,1024]{2,1,0:T(8,128)(2,1)}) %all-gather.36.cloned.1.call-update) | async-done | bytes 2097168 | tf_op jit(solution)/shard_map/all_gather | solution.py:105
  478.5 42.1 all-gather.34.cloned.1.call-done
  578.5 74.2 %reduce-scatter.18.cloned.1.call-done = f32[1,128,1024]{1,2,0:T(8,128)} async-done(((f32[1,1024,1024]{1,2,0:T(8,128)}), f32[1,128,1024]{1,2,0:T(8,128)}) %reduce-scatter.18.cloned.1.call-update) | async-done | bytes 524304 | tf_op jit(solution)/shard_map/reduce_scatter | solution.py:226
  654.5 90.4 %reduce-scatter.20.cloned.1.call-done = f32[1,128,1024]{1,2,0:T(8,128)} async-done(((f32[1,1024,1024]{1,2,0:T(8,128)}), f32[1,128,1024]{1,2,0:T(8,128)}) %reduce-scatter.20.cloned.1.call-update) | async-done | bytes 524304 | tf_op jit(solution)/shard_map/reduce_scatter | solution.py:227
  804.4 67.0 %reduce-scatter.22.cloned.1.call-done = f32[1,128,1024]{1,2,0:T(8,128)} async-done(((f32[1,1024,1024]{1,2,0:T(8,128)}), f32[1,128,1024]{1,2,0:T(8,128)}) %reduce-scatter.22.cloned.1.call-update) | async-done | bytes 524304 | tf_op jit(solution)/shard_map/reduce_scatter | solution.py:226
  872.5 90.9 %reduce-scatter.24.cloned.1.call-done = f32[1,128,1024]{1,2,0:T(8,128)} async-done(((f32[1,1024,1024]{1,2,0:T(8,128)}), f32[1,128,1024]{1,2,0:T(8,128)}) %reduce-scatter.24.cloned.1.call-update) | async-done | bytes 524304 | tf_op jit(solution)/shard_map/reduce_scatter | solution.py:227
  1012.2 13.4 multiply_add_fusion
  1026.8 12.7 fusion.183
  1039.6 12.8 fusion.181
  1055.4 91.5 %reduce-scatter.28.cloned.1.call-done = f32[1024,768]{1,0:T(8,128)} async-done(((f32[1024,3072]{1,0:T(8,128)}), f32[1024,768]{1,0:T(8,128)}) %reduce-scatter.28.cloned.1.call-update) | async-done | bytes 3145744 | tf_op jit(solution)/shard_map/reduce_scatter | solution.py:381
  1147.0 128.5 %reduce-scatter.36.cloned.1.call-done = f32[1024,1024]{1,0:T(8,128)} async-done(((f32[1024,4096]{1,0:T(8,128)}), f32[1024,1024]{1,0:T(8,128)}) %reduce-scatter.36.cloned.1.call-update) | async-done | bytes 4194320 | tf_op jit(solution)/shard_map/reduce_scatter | solution.py:383
  1275.6 128.8 %reduce-scatter.40.cloned.1.call-done = f32[1024,1024]{1,0:T(8,128)} async-done(((f32[1024,4096]{1,0:T(8,128)}), f32[1024,1024]{1,0:T(8,128)}) %reduce-scatter.40.cloned.1.call-update) | async-done | bytes 4194320 | tf_op jit(solution)/shard_map/reduce_scatter | solution.py:384
  1404.5 182.9 %reduce-scatter.44.cloned.1.call-done = f32[1024,1536]{1,0:T(8,128)} async-done(((f32[1024,6144]{1,0:T(8,128)}), f32[1024,1536]{1,0:T(8,128)}) %reduce-scatter.44.cloned.1.call-update) | async-done | bytes 6291472 | tf_op jit(solution)/shard_map/reduce_scatter | solution.py:385
  1589.3 10.3 all-reduce
  1599.6 10.2 reduce-scatter.50.cloned.1.call-done
  1609.8 37.1 all-reduce.2
  1649.7 52.2 %reduce-scatter.34.cloned.1.call-done = f32[128,256]{1,0:T(8,128)} async-done(((f32[1024,256]{1,0:T(8,128)}), f32[128,256]{1,0:T(8,128)}) %reduce-scatter.34.cloned.1.call-update) | async-done | bytes 131088 | tf_op jit(solution)/shard_map/reduce_scatter | solution.py:393
  1703.5 73.3 %all-reduce.17.cloned.1.call-done = f32[2,276,256]{2,1,0:T(8,128)} async-done(((f32[2,276,256]{2,1,0:T(8,128)}), f32[2,276,256]{2,1,0:T(8,128)}) %all-reduce.17.cloned.1.call-update) | async-done | bytes 565264 | tf_op jit(solution)/shard_map/psum | solution.py:398
  1780.6 74.1 %reduce-scatter.30.cloned.1.call-done = f32[128,768]{1,0:T(8,128)} async-done(((f32[1024,768]{1,0:T(8,128)}), f32[128,768]{1,0:T(8,128)}) %reduce-scatter.30.cloned.1.call-update) | async-done | bytes 393232 | tf_op jit(solution)/shard_map/reduce_scatter | solution.py:392
  1858.4 87.2 %reduce-scatter.38.cloned.1.call-done = f32[128,1024]{1,0:T(8,128)} async-done(((f32[1024,1024]{1,0:T(8,128)}), f32[128,1024]{1,0:T(8,128)}) %reduce-scatter.38.cloned.1.call-update) | async-done | bytes 524304 | tf_op jit(solution)/shard_map/reduce_scatter | solution.py:394
  1948.2 88.7 %reduce-scatter.42.cloned.1.call-done = f32[128,1024]{1,0:T(8,128)} async-done(((f32[1024,1024]{1,0:T(8,128)}), f32[128,1024]{1,0:T(8,128)}) %reduce-scatter.42.cloned.1.call-update) | async-done | bytes 524304 | tf_op jit(solution)/shard_map/reduce_scatter | solution.py:395
  2039.3 119.2 %reduce-scatter.46.cloned.1.call-done = f32[128,1536]{1,0:T(8,128)} async-done(((f32[1024,1536]{1,0:T(8,128)}), f32[128,1536]{1,0:T(8,128)}) %reduce-scatter.46.cloned.1.call-update) | async-done | bytes 786448 | tf_op jit(solution)/shard_map/reduce_scatter | solution.py:396
  2161.8 39.4 psum.235
  2205.8 40.4 all-reduce.1
  2251.5 32.5 all_gather.102
  2300.2 45.2 %all-gather.46.cloned.1.call-done = bf16[1024,1024]{1,0:T(8,128)(2,1)} async-done(((bf16[128,1024]{1,0:T(8,128)(2,1)}), bf16[1024,1024]{1,0:T(8,128)(2,1)}) %all-gather.46.cloned.1.call-update) | async-done | bytes 2097168 | tf_op jit(solution)/shard_map/all_gather | solution.py:433
  2347.9 48.2 %all-gather.42.cloned.1.call-done = bf16[1024,1024]{1,0:T(8,128)(2,1)} async-done(((bf16[128,1024]{1,0:T(8,128)(2,1)}), bf16[1024,1024]{1,0:T(8,128)(2,1)}) %all-gather.42.cloned.1.call-update) | async-done | bytes 2097168 | tf_op jit(solution)/shard_map/all_gather | solution.py:432
  2398.7 286.3 %all-reduce.20 = (bf16[1024,1024]{1,0:T(8,128)(2,1)}, bf16[1024,1024]{1,0:T(8,128)(2,1)}, bf16[1024,1024]{1,0:T(8,128)(2,1)}, bf16[1024,1024]{1,0:T(8,128)(2,1)}) all-reduce(f32[1024,1024]{1,0:T(8,128)} %get-tuple-element.682, f32[1024,1024]{1,0:T(8,128)} %get-tuple-element.692, ...), channel_id=1, replica_groups=mesh['seq'=8,'fsdp'=4] {'fsdp'}, use_global_device_ids=true, to_apply=%region_91.92 | all-reduce | flops 4194304 | bytes 25165824 | tf_op jit(solution)/shard_map/psum | solution.py:443
  2694.2 11.8 conditional.41
  2712.2 288.0 %all-reduce.21 = (bf16[1024,1024]{1,0:T(8,128)(2,1)}, bf16[1024,1024]{1,0:T(8,128)(2,1)}, bf16[1024,1024]{1,0:T(8,128)(2,1)}, bf16[1024,1024]{1,0:T(8,128)(2,1)}) all-reduce(f32[1024,1024]{1,0:T(8,128)} %get-tuple-element.684, f32[1024,1024]{1,0:T(8,128)} %get-tuple-element.694, ...), channel_id=1, replica_groups=mesh['seq'=8,'fsdp'=4] {'fsdp'}, use_global_device_ids=true, to_apply=%region_96.97 | all-reduce | flops 4194304 | bytes 25165824 | tf_op jit(solution)/shard_map/psum | solution.py:443
  3008.0 11.8 conditional.43
  3025.6 286.2 %all-reduce.22 = (bf16[1024,1024]{1,0:T(8,128)(2,1)}, bf16[1024,1024]{1,0:T(8,128)(2,1)}, bf16[1024,1024]{1,0:T(8,128)(2,1)}, bf16[1024,1024]{1,0:T(8,128)(2,1)}) all-reduce(f32[1024,1024]{1,0:T(8,128)} %get-tuple-element.686, f32[1024,1024]{1,0:T(8,128)} %get-tuple-element.696, ...), channel_id=1, replica_groups=mesh['seq'=8,'fsdp'=4] {'fsdp'}, use_global_device_ids=true, to_apply=%region_101.102 | all-reduce | flops 4194304 | bytes 25165824 | tf_op jit(solution)/shard_map/psum | solution.py:443
  3321.3 11.8 conditional.45
  3338.8 287.7 %all-reduce.23 = (bf16[1024,1024]{1,0:T(8,128)(2,1)}, bf16[1024,1024]{1,0:T(8,128)(2,1)}, bf16[1024,1024]{1,0:T(8,128)(2,1)}, bf16[1024,1024]{1,0:T(8,128)(2,1)}) all-reduce(f32[1024,1024]{1,0:T(8,128)} %get-tuple-element.688, f32[1024,1024]{1,0:T(8,128)} %get-tuple-element.698, ...), channel_id=1, replica_groups=mesh['seq'=8,'fsdp'=4] {'fsdp'}, use_global_device_ids=true, to_apply=%region_106.107 | all-reduce | flops 4194304 | bytes 25165824 | tf_op jit(solution)/shard_map/psum | solution.py:443
  3635.7 11.8 conditional.47
  3653.3 286.2 %all-reduce.24 = (bf16[1024,1024]{1,0:T(8,128)(2,1)}, bf16[1024,1024]{1,0:T(8,128)(2,1)}, bf16[1024,1024]{1,0:T(8,128)(2,1)}, bf16[1024,1024]{1,0:T(8,128)(2,1)}) all-reduce(f32[1024,1024]{1,0:T(8,128)} %get-tuple-element.690, f32[1024,1024]{1,0:T(8,128)} %get-tuple-element.700, ...), channel_id=1, replica_groups=mesh['seq'=8,'fsdp'=4] {'fsdp'}, use_global_device_ids=true, to_apply=%region_111.112 | all-reduce | flops 4194304 | bytes 25165824 | tf_op jit(solution)/shard_map/psum | solution.py:443
  3944.3 9.8 conditional.49
  3955.4 225.5 %all-reduce.19.cloned.1.call-done = (bf16[1024,768]{1,0:T(8,128)(2,1)}, bf16[1024,256]{1,0:T(8,128)(2,1)}, bf16[1024,1024]{1,0:T(8,128)(2,1)}, bf16[1024,1024]{1,0:T(8,128)(2,1)}) async-done(((bf16[1024,768]{1,0:T(8,128)(2,1)}, bf16[1024,256]{1,0:T(8,128)(2,1)}, bf16[1024,1024]{1,0:T(8,128)(2,1)}, bf16[1024,1024]{1,0:T(8,128)(2,1)}), (bf16[1024,768]{1,0:T(8,128)(2,1)}, bf16[1024,256]{1,0:T(8,128)(2,1)}, ...) | async-done | bytes 6291472 | tf_op jit(solution)/shard_map/psum | solution.py:35
  4196.8 32.4 all_gather.103
  4231.3 51.5 %all-gather.44.cloned.1.call-done = bf16[1024,1024]{1,0:T(8,128)(2,1)} async-done(((bf16[128,1024]{1,0:T(8,128)(2,1)}), bf16[1024,1024]{1,0:T(8,128)(2,1)}) %all-gather.44.cloned.1.call-update) | async-done | bytes 2097168 | tf_op jit(solution)/shard_map/all_gather | solution.py:465
  4282.7 50.5 %all-gather.48.cloned.1.call-done = bf16[1024,1024]{1,0:T(8,128)(2,1)} async-done(((bf16[128,1024]{1,0:T(8,128)(2,1)}), bf16[1024,1024]{1,0:T(8,128)(2,1)}) %all-gather.48.cloned.1.call-update) | async-done | bytes 2097168 | tf_op jit(solution)/shard_map/all_gather | solution.py:466
  (768 shorter events, 522.5 us)
Async XLA Ops:
  7.2 24.9 all-gather.18.cloned.1.call-start
  9.3 104.8 %all-gather.20.cloned.1.call-start = ((), (), s32[]{:S(2)}) async-start(), calls=%async_computation.18 | async-start | bytes 15728640 | tf_op jit(solution)/shard_map/all_gather | solution.py:339
  10.0 152.1 %all-gather.22.cloned.1.call-start = ((), (), s32[]{:S(2)}) async-start(), calls=%async_computation.19 | async-start | bytes 7864320 | tf_op jit(solution)/shard_map/all_gather | solution.py:335
  10.8 205.6 %all-gather.26.cloned.1.call-start = ((), (), s32[]{:S(2)}) async-start(), calls=%async_computation.21 | async-start | bytes 2359296 | tf_op jit(solution)/shard_map/all_gather | solution.py:105
  124.3 225.1 %copy-start.98 = (f32[1,1024]{1,0:T(1,128)}, f32[1,1024]{1,0:T(1,128)S(1)}, u32[]{:S(2)}) copy-start(f32[1,1024]{1,0:T(1,128)S(1)} %get-tuple-element.582) | copy-start | bytes 12292
  124.4 225.0 %copy-start.105 = (f32[1,1024]{1,0:T(1,128)}, f32[1,1024]{1,0:T(1,128)S(1)}, u32[]{:S(2)}) copy-start(f32[1,1024]{1,0:T(1,128)S(1)} %get-tuple-element.581) | copy-start | bytes 12292
  124.4 284.9 %copy-start.123 = (f32[1,1024]{1,0:T(1,128)}, f32[1,1024]{1,0:T(1,128)S(1)}, u32[]{:S(2)}) copy-start(f32[1,1024]{1,0:T(1,128)S(1)} %get-tuple-element.580) | copy-start | bytes 12292
  166.9 99.8 %all-gather.24.cloned.1.call-start = ((), (), s32[]{:S(2)}) async-start(), calls=%async_computation.20 | async-start | bytes 2359296 | tf_op jit(solution)/shard_map/all_gather | solution.py:106
  167.5 122.0 %all-gather.28.cloned.1.call-start = ((), (), s32[]{:S(2)}) async-start(), calls=%async_computation.22 | async-start | bytes 2621440 | tf_op jit(solution)/shard_map/all_gather | solution.py:336
  168.1 181.3 %all-gather.30.cloned.1.call-start = ((), (), s32[]{:S(2)}) async-start(), calls=%async_computation.23 | async-start | bytes 10485760 | tf_op jit(solution)/shard_map/all_gather | solution.py:337
  168.8 240.5 %all-gather.32.cloned.1.call-start = ((), (), s32[]{:S(2)}) async-start(), calls=%async_computation.24 | async-start | bytes 10485760 | tf_op jit(solution)/shard_map/all_gather | solution.py:338
  169.6 300.7 %all-gather.36.cloned.1.call-start = ((), (), s32[]{:S(2)}) async-start(), calls=%async_computation.26 | async-start | bytes 2359296 | tf_op jit(solution)/shard_map/all_gather | solution.py:105
  420.8 99.8 %all-gather.34.cloned.1.call-start = ((), (), s32[]{:S(2)}) async-start(), calls=%async_computation.25 | async-start | bytes 2359296 | tf_op jit(solution)/shard_map/all_gather | solution.py:106
  421.4 231.4 %reduce-scatter.18.cloned.1.call-start = ((), (), s32[]{:S(2)}) async-start(), calls=%async_computation.27 | async-start | bytes 4718592 | tf_op jit(solution)/shard_map/reduce_scatter | solution.py:226
  565.6 179.3 %reduce-scatter.20.cloned.1.call-start = ((), (), s32[]{:S(2)}) async-start(), calls=%async_computation.28 | async-start | bytes 4718592 | tf_op jit(solution)/shard_map/reduce_scatter | solution.py:227
  572.9 298.5 %reduce-scatter.22.cloned.1.call-start = ((), (), s32[]{:S(2)}) async-start(), calls=%async_computation.29 | async-start | bytes 4718592 | tf_op jit(solution)/shard_map/reduce_scatter | solution.py:226
  578.5 167.5 %copy-start.75 = (bf16[16,64,128]{2,1,0:T(8,128)(2,1)}, bf16[16,64,128]{2,1,0:T(8,128)(2,1)S(1)}, u32[]{:S(2)}) copy-start(bf16[16,64,128]{2,1,0:T(8,128)(2,1)S(1)} %convolution_convert_fusion.4) | copy-start | bytes 786436
  783.0 180.4 %reduce-scatter.24.cloned.1.call-start = ((), (), s32[]{:S(2)}) async-start(), calls=%async_computation.30 | async-start | bytes 4718592 | tf_op jit(solution)/shard_map/reduce_scatter | solution.py:227
  790.3 263.8 %reduce-scatter.32.cloned.1.call-start = ((), (), s32[]{:S(2)}) async-start(), calls=%async_computation.34 | async-start | bytes 5242880 | tf_op jit(solution)/shard_map/reduce_scatter | solution.py:382
  794.9 260.0 %reduce-scatter.48.cloned.1.call-start = ((), (), s32[]{:S(2)}) async-start(), calls=%async_computation.42 | async-start | bytes 2867200 | tf_op jit(solution)/shard_map/reduce_scatter | solution.py:386
  974.8 172.2 %reduce-scatter.28.cloned.1.call-start = ((), (), s32[]{:S(2)}) async-start(), calls=%async_computation.32 | async-start | bytes 15728640 | tf_op jit(solution)/shard_map/reduce_scatter | solution.py:381
  984.9 290.6 %reduce-scatter.36.cloned.1.call-start = ((), (), s32[]{:S(2)}) async-start(), calls=%async_computation.36 | async-start | bytes 20971520 | tf_op jit(solution)/shard_map/reduce_scatter | solution.py:383
  998.0 406.4 %reduce-scatter.40.cloned.1.call-start = ((), (), s32[]{:S(2)}) async-start(), calls=%async_computation.38 | async-start | bytes 20971520 | tf_op jit(solution)/shard_map/reduce_scatter | solution.py:384
  1011.5 575.9 %reduce-scatter.44.cloned.1.call-start = ((), (), s32[]{:S(2)}) async-start(), calls=%async_computation.40 | async-start | bytes 31457280 | tf_op jit(solution)/shard_map/reduce_scatter | solution.py:385
  1025.6 584.2 %reduce-scatter.50.cloned.1.call-start = ((), (), s32[]{:S(2)}) async-start(), calls=%async_computation.44 | async-start | bytes 40960 | tf_op jit(solution)/shard_map/reduce_scatter | solution.py:387
  1053.1 595.0 %reduce-scatter.26.cloned.1.call-start = ((), (), s32[]{:S(2)}) async-start(), calls=%async_computation.31 | async-start | bytes 655360 | tf_op jit(solution)/shard_map/reduce_scatter | solution.py:388
  1054.1 647.8 %reduce-scatter.34.cloned.1.call-start = ((), (), s32[]{:S(2)}) async-start(), calls=%async_computation.35 | async-start | bytes 1179648 | tf_op jit(solution)/shard_map/reduce_scatter | solution.py:393
  1054.8 722.0 %all-reduce.17.cloned.1.call-start = ((), (), s32[]{:S(2)}) async-start(), calls=%async_computation.43 | async-start | bytes 1146880 | tf_op jit(solution)/shard_map/psum | solution.py:398
  1055.4 799.3 %reduce-scatter.30.cloned.1.call-start = ((), (), s32[]{:S(2)}) async-start(), calls=%async_computation.33 | async-start | bytes 3538944 | tf_op jit(solution)/shard_map/reduce_scatter | solution.py:392
  1147.0 798.7 %reduce-scatter.38.cloned.1.call-start = ((), (), s32[]{:S(2)}) async-start(), calls=%async_computation.37 | async-start | bytes 4718592 | tf_op jit(solution)/shard_map/reduce_scatter | solution.py:394
  1275.5 761.3 %reduce-scatter.42.cloned.1.call-start = ((), (), s32[]{:S(2)}) async-start(), calls=%async_computation.39 | async-start | bytes 4718592 | tf_op jit(solution)/shard_map/reduce_scatter | solution.py:395
  1404.4 754.1 %reduce-scatter.46.cloned.1.call-start = ((), (), s32[]{:S(2)}) async-start(), calls=%async_computation.41 | async-start | bytes 7077888 | tf_op jit(solution)/shard_map/reduce_scatter | solution.py:396
  1587.4 614.5 %copy-start.101 = (f32[128,768]{1,0:T(8,128)S(1)}, f32[128,768]{1,0:T(8,128)}, u32[]{:S(2)}) copy-start(f32[128,768]{1,0:T(8,128)} %param.118) | copy-start | bytes 1179652
  1587.4 706.9 %all-gather.38.cloned.1.call-start = ((), (), s32[]{:S(2)}) async-start(), calls=%async_computation.45 | async-start | bytes 1769472 | tf_op jit(solution)/shard_map/all_gather | solution.py:430
  1701.9 500.7 %copy-start.93 = (f32[128,256]{1,0:T(8,128)S(1)}, f32[128,256]{1,0:T(8,128)}, u32[]{:S(2)}) copy-start(f32[128,256]{1,0:T(8,128)} %reduce-scatter.34.cloned.1.call-done) | copy-start | bytes 393220
  1703.5 500.8 %copy-start.96 = (f32[128,1024]{1,0:T(8,128)S(1)}, f32[128,1024]{1,0:T(8,128)}, u32[]{:S(2)}) copy-start(f32[128,1024]{1,0:T(8,128)} %param.124) | copy-start | bytes 1572868
  1854.7 347.2 %copy-start.69 = (f32[128,768]{1,0:T(8,128)S(1)}, f32[128,768]{1,0:T(8,128)}, u32[]{:S(2)}) copy-start(f32[128,768]{1,0:T(8,128)} %reduce-scatter.30.cloned.1.call-done) | copy-start | bytes 1179652
  1945.6 258.6 %copy-start.67 = (f32[128,1024]{1,0:T(8,128)S(1)}, f32[128,1024]{1,0:T(8,128)}, u32[]{:S(2)}) copy-start(f32[128,1024]{1,0:T(8,128)} %reduce-scatter.38.cloned.1.call-done) | copy-start | bytes 1572868
  2247.6 97.7 %all-gather.46.cloned.1.call-start = ((), (), s32[]{:S(2)}) async-start(), calls=%async_computation.49 | async-start | bytes 2359296 | tf_op jit(solution)/shard_map/all_gather | solution.py:433
  2249.2 147.0 %all-gather.42.cloned.1.call-start = ((), (), s32[]{:S(2)}) async-start(), calls=%async_computation.47 | async-start | bytes 2359296 | tf_op jit(solution)/shard_map/all_gather | solution.py:432
  2250.7 1930.1 %all-reduce.19.cloned.1.call-start = ((), (), s32[]{:S(2)}) async-start(), calls=%async_computation.51 | async-start | bytes 12582912 | tf_op jit(solution)/shard_map/psum | solution.py:35
  2398.7 286.3 %copy-start.4 = (bf16[1024,1024]{1,0:T(8,128)(2,1)S(1)}, bf16[1024,1024]{1,0:T(8,128)(2,1)}, u32[]{:S(2)}) copy-start(bf16[1024,1024]{1,0:T(8,128)(2,1)} %all-gather.46.cloned.1.call-done) | copy-start | bytes 6291460
  3955.3 225.5 %copy-start.102 = (f32[128,768]{1,0:T(8,128)S(1)}, f32[128,768]{1,0:T(8,128)}, u32[]{:S(2)}) copy-start(f32[128,768]{1,0:T(8,128)} %param.117) | copy-start | bytes 1179652
  3955.3 227.4 %copy-start.94 = (f32[128,1024]{1,0:T(8,128)S(1)}, f32[128,1024]{1,0:T(8,128)}, u32[]{:S(2)}) copy-start(f32[128,1024]{1,0:T(8,128)} %param.123) | copy-start | bytes 1572868
  3955.3 229.6 %copy-start.95 = (f32[128,1024]{1,0:T(8,128)S(1)}, f32[128,1024]{1,0:T(8,128)}, u32[]{:S(2)}) copy-start(f32[128,1024]{1,0:T(8,128)} %param.126) | copy-start | bytes 1572868
  3955.3 275.9 %all-gather.40.cloned.1.call-start = ((), (), s32[]{:S(2)}) async-start(), calls=%async_computation.46 | async-start | bytes 1769472 | tf_op jit(solution)/shard_map/all_gather | solution.py:463
  4182.7 100.1 %all-gather.44.cloned.1.call-start = ((), (), s32[]{:S(2)}) async-start(), calls=%async_computation.48 | async-start | bytes 2359296 | tf_op jit(solution)/shard_map/all_gather | solution.py:465
  4184.8 148.4 %all-gather.48.cloned.1.call-start = ((), (), s32[]{:S(2)}) async-start(), calls=%async_computation.50 | async-start | bytes 2359296 | tf_op jit(solution)/shard_map/all_gather | solution.py:466
  (202 other events, 2952.1 us)
Sparse Core Ops, SparseCore 0:
  10.2 20.2 all-gather.17
  32.0 82.0 all-gather.19
  115.7 46.4 all-gather.21
  167.0 49.2 all-gather.25
  218.9 47.7 all-gather.23
  268.1 21.3 all-gather.27
  291.0 58.3 all-gather.29
  351.0 58.2 all-gather.31
  420.9 49.2 all-gather.35
  472.8 47.7 all-gather.33
  565.7 86.9 reduce-scatter.17
  656.7 88.2 reduce-scatter.19
  783.1 88.2 reduce-scatter.21
  875.3 88.0 reduce-scatter.23
  965.8 44.2 reduce-scatter.31
  1012.7 32.6 reduce-scatter.47
  1047.8 99.0 reduce-scatter.27
  1149.4 126.0 reduce-scatter.35
  1278.3 126.1 reduce-scatter.39
  1406.8 180.4 reduce-scatter.43
  1590.5 19.3 reduce-scatter.49
  1612.9 21.6 reduce-scatter.25
  1638.4 63.4 reduce-scatter.33
  1705.2 71.6 all-reduce.16
  1780.9 73.8 reduce-scatter.29
  1858.6 86.9 reduce-scatter.37
  1949.1 87.6 reduce-scatter.41
  2040.8 117.6 reduce-scatter.45
  2247.7 46.4 all-gather.37
  2297.0 48.3 all-gather.45
  2348.3 47.7 all-gather.41
  3955.4 225.3 all-reduce.18
  4183.4 47.7 all-gather.39
  4234.0 48.7 all-gather.43
  4285.4 47.7 all-gather.47
where the time goes:
time: 4360 us; the launch traced here: 4350 us
  waiting for transfers between devices  2210 us (51%)
  blocking collectives  1640 us (38%)
  matrix products  264 us (6%)
  local copies, waits for them, and re-layouts  108 us (2%)
  other arithmetic  82.4 us (2%)
    psum x5, blocking collectives, body(): lax.psum((partial_value[0], partial_value[1], partial_value[2], partial_v...  1430 us
    psum x1, waiting for transfers between devices, broadcast(): return lax.psum(block, axis)  225 us
    reduce_scatter x1, waiting for transfers between devices, body(): lax.psum_scatter(totals[4], 'fsdp', scatter_dimension=1, tiled=True)  183 us
    reduce_scatter x2, waiting for transfers between devices, backward_step(): lax.psum_scatter(value_part, 'seq', scatter_dimension=1, tiled=True)  181 us
    reduce_scatter x2, waiting for transfers between devices, backward_step(): lax.psum_scatter(key_part, 'seq', scatter_dimension=1, tiled=True)  141 us
    reduce_scatter x1, waiting for transfers between devices, body(): lax.psum_scatter(totals[3], 'fsdp', scatter_dimension=1, tiled=True)  129 us
    reduce_scatter x1, waiting for transfers between devices, body(): lax.psum_scatter(totals[2], 'fsdp', scatter_dimension=1, tiled=True)  128 us
    reduce_scatter x1, waiting for transfers between devices, body(): lax.psum_scatter(reduced[4], 'seq', scatter_dimension=0, tiled=True)  119 us
  transfers between devices with their start and end apart: 35, of which 31 were waited for; matrix products, arithmetic and copies ran while one was open for 5% of the time, Pallas kernels for 0%

commit v1 on v0

--- a/solution.py
+++ b/solution.py
@@ -1,8 +1,11 @@
+import functools
 import math
 
 import jax
 import jax.numpy as jnp
 from jax import lax
+from jax.experimental import pallas as pl
+from jax.experimental.pallas import tpu as pltpu
 from jax.sharding import PartitionSpec as P
 
 HEADS = 16
@@ -297,7 +300,7 @@
     return (weight * (1.0 - rate * DECAY_ADAM) - rate * unbiased / spread, first_new, second_new)
 
 
-def body(
+def general_body(
     states,
     targets,
     lengths,
@@ -504,7 +507,864 @@
     )
 
 
+LANES = 128
+MATRICES = 4
+LOW = jnp.bfloat16
+MESH = pl.DeviceIdType.MESH
+
+
+def round_up(value, unit):
+    return -(-value // unit) * unit
+
+
+class Moves:
+    def __init__(self, name, ids):
+        self.name = name
+        self.ids = ids
+        self.operands = []
+        self.outputs = []
+        self.moves = []
+        self.locals = []
+        self.peers = {}
+
+    def operand(self, array):
+        self.operands.append(array)
+        return (0, len(self.operands) - 1)
+
+    def output(self, shape, dtype):
+        self.outputs.append(jax.ShapeDtypeStruct(shape, dtype))
+        return (1, len(self.outputs) - 1)
+
+    def keep(self, source, source_at, target, target_at):
+        self.locals.append((source, source_at, target, target_at))
+
+    def move(self, peer_key, peer, source, source_at, target, target_at, after=()):
+        self.peers.setdefault(peer_key, peer)
+        self.moves.append((peer_key, source, source_at, target, target_at, after))
+        return len(self.moves) - 1
+
+    def kernel(self, *refs):
+        ins = refs[: len(self.operands)]
+        outs = refs[len(self.operands) : len(self.operands) + len(self.outputs)]
+        local_sem, send_sem, recv_sem = refs[len(self.operands) + len(self.outputs) :]
+
+        def view(which, index):
+            ref = (ins, outs)[which[0]][which[1]]
+            return ref.at[index()] if index is not None else ref
+
+        devices = {key: peer() for key, peer in self.peers.items()}
+        barrier = pltpu.get_barrier_semaphore()
+        for device in devices.values():
+            pl.semaphore_signal(barrier, inc=1, device_id=device, device_id_type=MESH)
+        pl.semaphore_wait(barrier, len(devices))
+        remote = []
+        for number, (key, source, source_at, target, target_at, after) in enumerate(self.moves):
+            remote.append(
+                pltpu.make_async_remote_copy(
+                    src_ref=view(source, source_at),
+                    dst_ref=view(target, target_at),
+                    send_sem=send_sem.at[number],
+                    recv_sem=recv_sem.at[number],
+                    device_id=devices[key],
+                    device_id_type=MESH,
+                )
+            )
+            if not after:
+                remote[number].start()
+        local = [
+            pltpu.make_async_copy(view(source, source_at), view(target, target_at), local_sem.at[number])
+            for number, (source, source_at, target, target_at) in enumerate(self.locals)
+        ]
+        for copy in local:
+            copy.start()
+        arrived = set()
+        for number, entry in enumerate(self.moves):
+            if entry[-1]:
+                for earlier in entry[-1]:
+                    if earlier not in arrived:
+                        remote[earlier].wait_recv()
+                        arrived.add(earlier)
+                remote[number].start()
+        for copy in local:
+            copy.wait()
+        for number, copy in enumerate(remote):
+            if number not in arrived:
+                copy.wait_recv()
+            copy.wait_send()
+
+    def run(self):
+        in_any = pl.BlockSpec(memory_space=pl.ANY)
+        return pl.pallas_call(
+            self.kernel,
+            out_shape=self.outputs,
+            in_specs=[in_any] * len(self.operands),
+            out_specs=[in_any] * len(self.outputs),
+            scratch_shapes=[
+                pltpu.SemaphoreType.DMA((max(1, len(self.locals)),)),
+                pltpu.SemaphoreType.DMA((len(self.moves),)),
+                pltpu.SemaphoreType.DMA((len(self.moves),)),
+            ],
+            compiler_params=pltpu.CompilerParams(
+                collective_id=self.ids.setdefault(self.name, len(self.ids)), has_side_effects=True
+            ),
+            name=self.name,
+        )(*self.operands)
+
+    def along(self, axis, source, target, pairs):
+        count = lax.axis_size(axis)
+
+        def other(shift):
+            return lax.rem(lax.axis_index(axis) + shift, count)
+
+        for shift in range(1, count):
+            for source_at, target_at in pairs:
+                self.move(
+                    (axis, shift),
+                    lambda shift=shift: {axis: other(shift)},
+                    source,
+                    None if source_at is None else (lambda at=source_at, shift=shift: at(other(shift))),
+                    target,
+                    lambda at=target_at: at(lax.axis_index(axis)),
+                )
+        for source_at, target_at in pairs:
+            self.keep(
+                source,
+                None if source_at is None else (lambda at=source_at: at(lax.axis_index(axis))),
+                target,
+                lambda at=target_at: at(lax.axis_index(axis)),
+            )
+
+    def gather(self, axis, array):
+        target = self.output((lax.axis_size(axis),) + array.shape, array.dtype)
+        self.along(axis, self.operand(array), target, [(None, lambda sender: (sender,))])
+
+    def gather_columns(self, axis, array):
+        width = array.shape[-1]
+        target = self.output(array.shape[:-1] + (lax.axis_size(axis) * width,), array.dtype)
+        lead = (slice(None),) * (array.ndim - 1)
+        self.along(
+            axis,
+            self.operand(array),
+            target,
+            [(None, lambda sender: lead + (pl.ds(pl.multiple_of(sender * width, LANES), width),))],
+        )
+
+    def exchange(self, axis, array):
+        target = self.output(array.shape, array.dtype)
+        self.along(axis, self.operand(array), target, [(lambda receiver: (receiver,), lambda sender: (sender,))])
+
+    def exchange_columns(self, axis, array):
+        width = array.shape[-1] // lax.axis_size(axis)
+        target = self.output((lax.axis_size(axis), array.shape[0], width), array.dtype)
+        self.along(
+            axis,
+            self.operand(array),
+            target,
+            [
+                (
+                    lambda receiver: (slice(None), pl.ds(pl.multiple_of(receiver * width, LANES), width)),
+                    lambda sender: (sender,),
+                )
+            ],
+        )
+
+    def rows_to_heads(self, axis, array, planes):
+        count, rows = lax.axis_size(axis), array.shape[0]
+        columns = array.shape[1] // planes
+        width = columns // count
+        target = self.output((planes, rows * count, width), array.dtype)
+        self.along(
+            axis,
+            self.operand(array),
+            target,
+            [
+                (
+                    lambda receiver, plane=plane: (
+                        slice(None),
+                        pl.ds(pl.multiple_of(plane * columns + receiver * width, LANES), width),
+                    ),
+                    lambda sender, plane=plane: (plane, pl.ds(pl.multiple_of(sender * rows, rows), rows)),
+                )
+                for plane in range(planes)
+            ],
+        )
+
+    def heads_to_rows(self, axis, array):
+        count = lax.axis_size(axis)
+        planes, all_rows, width = array.shape
+        rows, columns = all_rows // count, width * count
+        target = self.output((rows, planes * columns), array.dtype)
+        self.along(
+            axis,
+            self.operand(array),
+            target,
+            [
+                (
+                    lambda receiver, plane=plane: (plane, pl.ds(pl.multiple_of(receiver * rows, rows), rows)),
+                    lambda sender, plane=plane: (
+                        slice(None),
+                        pl.ds(pl.multiple_of(plane * columns + sender * width, LANES), width),
+                    ),
+                )
+                for plane in range(planes)
+            ],
+        )
+
+
+def total_kernel(x_ref, o_ref, near, far, near_send, near_recv, far_send, far_recv):
+    near_count, far_count = near.shape[0], far.shape[0]
+    near_me, far_me = lax.axis_index("fsdp"), lax.axis_index("seq")
+    barrier = pltpu.get_barrier_semaphore()
+    for shift in range(1, near_count):
+        pl.semaphore_signal(
+            barrier, inc=1, device_id={"fsdp": lax.rem(near_me + shift, near_count)}, device_id_type=MESH
+        )
+    for shift in range(1, far_count):
+        pl.semaphore_signal(
+            barrier, inc=1, device_id={"seq": lax.rem(far_me + shift, far_count)}, device_id_type=MESH
+        )
+    pl.semaphore_wait(barrier, near_count + far_count - 2)
+
+    def spread(axis, me, count, buffer, send, recv):
+        copies = []
+        for shift in range(1, count):
+            copy = pltpu.make_async_remote_copy(
+                src_ref=buffer.at[me],
+                dst_ref=buffer.at[me],
+                send_sem=send.at[shift - 1],
+                recv_sem=recv.at[shift - 1],
+                device_id={axis: lax.rem(me + shift, count)},
+                device_id_type=MESH,
+            )
+            copy.start()
+            copies.append(copy)
+        for copy in copies:
+            copy.wait()
+        return jnp.sum(buffer[...], 0)
+
+    near[near_me] = x_ref[...]
+    far[far_me] = spread("fsdp", near_me, near_count, near, near_send, near_recv)
+    o_ref[...] = spread("seq", far_me, far_count, far, far_send, far_recv)
+
+
+def total_of(ids, values):
+    near_count, far_count = lax.axis_size("fsdp"), lax.axis_size("seq")
+    in_vmem = pl.BlockSpec(memory_space=pltpu.VMEM)
+    return pl.pallas_call(
+        total_kernel,
+        out_shape=jax.ShapeDtypeStruct(values.shape, values.dtype),
+        in_specs=[in_vmem],
+        out_specs=in_vmem,
+        scratch_shapes=[
+            pltpu.VMEM((near_count,) + values.shape, values.dtype),
+            pltpu.VMEM((far_count,) + values.shape, values.dtype),
+            pltpu.SemaphoreType.DMA((near_count - 1,)),
+            pltpu.SemaphoreType.DMA((near_count - 1,)),
+            pltpu.SemaphoreType.DMA((far_count - 1,)),
+            pltpu.SemaphoreType.DMA((far_count - 1,)),
+        ],
+        compiler_params=pltpu.CompilerParams(
+            collective_id=ids.setdefault("total", len(ids)), has_side_effects=True
+        ),
+        name="total",
+    )(values)
+
+
+def contract(left, right, left_dim, right_dim):
+    return lax.dot_general(
+        left, right, (((left_dim,), (right_dim,)), ((), ())), preferred_element_type=jnp.float32
+    )
+
+
+QUERY_BLOCK = 256
+
+
+def attention_kernel(heads, qkv_ref, mixed_ref):
+    rows = pl.ds(pl.multiple_of(pl.program_id(0) * QUERY_BLOCK, QUERY_BLOCK), QUERY_BLOCK)
+    mixed = []
+    for head in range(heads):
+        lanes = pl.ds(head * HEAD, HEAD)
+        queries, keys, values = qkv_ref[0, rows, lanes], qkv_ref[1, :, lanes], qkv_ref[2, :, lanes]
+        scores = contract(queries, keys, 1, 1) * HEAD ** (-0.5)
+        expo = jnp.exp(scores - jnp.max(scores, -1, keepdims=True))
+        probs = (expo / jnp.sum(expo, -1, keepdims=True)).astype(LOW)
+        mixed.append(contract(probs, values, 1, 0))
+    mixed_ref[...] = jnp.concatenate(mixed, -1).astype(LOW)
+
+
+def attention(qkv):
+    _, patches, width = qkv.shape
+    return pl.pallas_call(
+        functools.partial(attention_kernel, width // HEAD),
+        out_shape=jax.ShapeDtypeStruct((patches, width), LOW),
+        grid=(patches // QUERY_BLOCK,),
+        in_specs=[pl.BlockSpec(qkv.shape, lambda block: (0, 0, 0))],
+        out_specs=pl.BlockSpec((QUERY_BLOCK, width), lambda block: (block, 0)),
+        compiler_params=pltpu.CompilerParams(vmem_limit_bytes=48 * 2**20),
+        name="attention",
+    )(qkv)
+
+
+def attention_back_kernel(heads, qkv_ref, grad_ref, out_ref, key_total, value_total):
+    block = pl.program_id(0)
+    rows = pl.ds(pl.multiple_of(block * QUERY_BLOCK, QUERY_BLOCK), QUERY_BLOCK)
+
+    @pl.when(block == 0)
+    def _():
+        key_total[...] = jnp.zeros_like(key_total)
+        value_total[...] = jnp.zeros_like(value_total)
+
+    query_parts = []
+    for head in range(heads):
+        lanes = pl.ds(head * HEAD, HEAD)
+        queries, keys, values = qkv_ref[0, rows, lanes], qkv_ref[1, :, lanes], qkv_ref[2, :, lanes]
+        grads = grad_ref[rows, lanes]
+        scores = contract(keys, queries, 1, 1) * HEAD ** (-0.5)
+        expo = jnp.exp(scores - jnp.max(scores, 0, keepdims=True))
+        probs = expo / jnp.sum(expo, 0, keepdims=True)
+        grad_probs = contract(values, grads, 1, 1)
+        shared = jnp.sum(grad_probs * probs, 0, keepdims=True)
+        score_grad = (HEAD ** (-0.5) * probs * (grad_probs - shared)).astype(LOW)
+        query_parts.append(contract(score_grad, keys, 0, 0))
+        key_total[head] += contract(score_grad, queries, 1, 0)
+        value_total[head] += contract(probs.astype(LOW), grads, 1, 0)
+    out_ref[0, rows, :] = jnp.concatenate(query_parts, -1).astype(LOW)
+
+    @pl.when(block == pl.num_programs(0) - 1)
+    def _():
+        out_ref[1] = jnp.concatenate([key_total[head] for head in range(heads)], -1).astype(LOW)
+        out_ref[2] = jnp.concatenate([value_total[head] for head in range(heads)], -1).astype(LOW)
+
+
+def attention_back(qkv, grads):
+    _, patches, width = qkv.shape
+    heads = width // HEAD
+    return pl.pallas_call(
+        functools.partial(attention_back_kernel, heads),
+        out_shape=jax.ShapeDtypeStruct(qkv.shape, LOW),
+        grid=(patches // QUERY_BLOCK,),
+        in_specs=[
+            pl.BlockSpec(qkv.shape, lambda block: (0, 0, 0)),
+            pl.BlockSpec(grads.shape, lambda block: (0, 0)),
+        ],
+        out_specs=pl.BlockSpec(qkv.shape, lambda block: (0, 0, 0)),
+        scratch_shapes=[
+            pltpu.VMEM((heads, patches, HEAD), jnp.float32),
+            pltpu.VMEM((heads, patches, HEAD), jnp.float32),
+        ],
+        compiler_params=pltpu.CompilerParams(vmem_limit_bytes=48 * 2**20),
+        name="attention_back",
+    )(qkv, grads)
+
+
+def product_high(left, right):
+    left_high, right_high = left.astype(LOW), right.astype(LOW)
+    left_rest = (left - left_high.astype(jnp.float32)).astype(LOW)
+    right_rest = (right - right_high.astype(jnp.float32)).astype(LOW)
+    return product(left_high, right_high) + (product(left_high, right_rest) + product(left_rest, right_high))
+
+
+def product_low(left, right):
+    return product(left.astype(LOW), right.astype(LOW))
+
+
+def newton_schulz(block, gram):
+    for turn in range(NS_ITERS):
+        times = product_high if 2 <= turn < NS_ITERS - 1 else product_low
+        poly = NS_B * gram + NS_C * times(gram, gram)
+        if turn < NS_ITERS - 1:
+            once = times(poly, gram)
+            gram = NS_A * NS_A * gram + 2.0 * NS_A * once + times(poly, once)
+        block = (NS_A * block.astype(jnp.float32) + product(poly.astype(LOW), block)).astype(LOW)
+    return block
+
+
+def fast_body(
+    states,
+    targets,
+    lengths,
+    intervals,
+    qkv_copy,
+    qkv_master,
+    qkv_moment,
+    out_copy,
+    out_master,
+    out_moment,
+    up_copy,
+    up_master,
+    up_moment,
+    down_copy,
+    down_master,
+    down_moment,
+    ada_copy,
+    ada_master,
+    ada_first,
+    ada_second,
+    io_proj,
+    io_first,
+    io_second,
+    cond_table,
+    cond_first,
+    cond_second,
+    pos_table,
+    pos_first,
+    pos_second,
+    biases,
+    bias_first,
+    bias_second,
+):
+    ids = {}
+    f32 = jnp.float32
+    seq_count, shards = lax.axis_size("seq"), lax.axis_size("fsdp")
+    seq_index, shard = lax.axis_index("seq"), lax.axis_index("fsdp")
+    members = seq_count // MATRICES
+    group, member = seq_index // members, lax.rem(seq_index, members)
+    samples, local, values_count = states.shape
+    table_rows, table_cols = cond_table.shape
+    width = table_cols * shards
+    ada_cols = ada_copy.shape[1]
+    padded = round_up(values_count, LANES)
+
+    moves = Moves("embeddings", ids)
+    moves.gather("fsdp", jnp.pad(io_proj.astype(LOW), ((0, 0), (0, padded - values_count), (0, 0))))
+    moves.gather("fsdp", cond_table)
+    moves.gather("fsdp", pos_table.astype(LOW))
+    moves.gather("fsdp", biases[None])
+    io_parts, table_parts, pos_parts, bias_parts = moves.run()
+    io_all = jnp.moveaxis(io_parts, 0, 2).reshape(2, padded, width)
+    table = jnp.moveaxis(table_parts, 0, 1).reshape(table_rows, width).astype(LOW).astype(f32)
+    pos = jnp.moveaxis(pos_parts, 0, 1).reshape(local, width).astype(f32)
+    bias = bias_parts.reshape(-1).astype(LOW).astype(f32)
+    w_qkv = lax.all_gather(qkv_copy, "fsdp", axis=1, tiled=True)
+    w_out = lax.all_gather(out_copy, "fsdp", axis=1, tiled=True)
+
+    rows_iota = jnp.arange(table_rows, dtype=jnp.int32)
+    id_rows = (intervals[:, None] == rows_iota[None]).astype(f32)
+    step_rows = (rows_iota[None] == NI + jnp.arange(ROLL, dtype=jnp.int32)[:, None]).astype(f32)
+    select = (id_rows[:, None] + step_rows[None]).reshape(-1, table_rows)
+    cond_vec = jnp.sum(select[:, :, None] * table[None], 1)
+    silu_low = jax.nn.silu(cond_vec).astype(LOW)
+    modul_shard = product(silu_low, ada_copy) + lax.dynamic_slice_in_dim(bias, shard * ada_cols, ada_cols)[None]
+    moves = Moves("modulation", ids)
+    moves.exchange("fsdp", modul_shard.reshape(shards, ROLL, ada_cols))
+    modul = jnp.moveaxis(moves.run()[0], 0, 1).reshape(ROLL, 6 * width)
+
+    momenta = (qkv_moment, out_moment, up_moment, down_moment)
+    group_cols = [item.shape[1] // members for item in momenta]
+    most_cols = max(group_cols)
+
+    def widen(item):
+        return jnp.pad(item, ((0, 0), (0, most_cols - item.shape[1])))
+
+    moment_parts = jnp.stack(
+        [
+            widen(item[:, part * cols : (part + 1) * cols].astype(LOW))
+            for item, cols in zip(momenta, group_cols)
+            for part in range(members)
+        ]
+    )
+
+    counts = jnp.sum((intervals[:, None] == jnp.arange(NI, dtype=jnp.int32)[None]).astype(f32), 0)
+    my_id = lax.dynamic_slice_in_dim(intervals, shard, 1)
+    id_count = jnp.sum((my_id == jnp.arange(NI, dtype=jnp.int32)).astype(f32) * counts)
+    weight = 1.0 / (NI * local * seq_count * values_count * id_count)
+    length = lengths[0]
+    value_pad = ((0, 0), (0, padded - values_count))
+    state = jnp.pad(states[0].astype(f32), value_pad)
+    embed_bias = bias[6 * width :]
+    kept = []
+    moment_group = None
+    for step in range(ROLL):
+        shift1, scale1, gate1, shift2, scale2, gate2 = jnp.split(modul[step][None], 6, -1)
+        state_low = state.astype(LOW)
+        embedded = product(state_low, io_all[0]) + embed_bias + pos
+        normed_one, inverse_one = layer_norm(embedded)
+        normed_a = (normed_one * (1.0 + scale1) + shift1).astype(LOW)
+        qkv_rows = product(normed_a, w_qkv).astype(LOW)
+        moves = Moves("qkv_heads", ids)
+        moves.rows_to_heads("seq", qkv_rows, 3)
+        qkv = moves.run()[0]
+        mixed_heads = attention(qkv)
+        moves = Moves("mixed_rows", ids)
+        moves.heads_to_rows("seq", mixed_heads[None])
+        mixed = moves.run()[0]
+        attended = product(mixed, w_out)
+        after_attn = embedded + gate1 * attended
+        normed_two, inverse_two = layer_norm(after_attn)
+        normed_b = (normed_two * (1.0 + scale2) + shift2).astype(LOW)
+        moves = Moves("tokens" if step else "tokens_momenta", ids)
+        moves.gather("fsdp", normed_b)
+        if step == 0:
+            moves.exchange("seq", moment_parts)
+            tokens_b, moment_group = moves.run()
+        else:
+            tokens_b = moves.run()[0]
+        tokens_b = tokens_b.reshape(shards * local, width)
+        upward = product(tokens_b, up_copy)
+        hidden = jax.nn.gelu(upward).astype(LOW)
+        down_part = contract(hidden, down_copy, 1, 1).astype(LOW).reshape(shards, local, width)
+        moves = Moves("token_sums", ids)
+        moves.exchange("fsdp", down_part)
+        downward = jnp.sum(moves.run()[0].astype(f32), 0)
+        after_mlp = after_attn + gate2 * downward
+        normed_three, inverse_three = layer_norm(after_mlp)
+        normed_c = normed_three.astype(LOW)
+        delta = contract(normed_c, io_all[1], 1, 1)
+        kept.append(
+            (
+                state_low,
+                normed_one,
+                inverse_one,
+                normed_a,
+                qkv,
+                mixed,
+                attended,
+                normed_two,
+                inverse_two,
+                tokens_b,
+                upward,
+                hidden,
+                downward,
+                normed_three,
+                inverse_three,
+                normed_c,
+            )
+        )
+        state = state + (step < length).astype(f32) * delta
+
+    lat = latitude_weights(local)
+    diff = state - jnp.pad(targets[0].astype(f32), value_pad)
+    loss_local = weight * jnp.sum(jnp.sum(diff * diff, -1) * lat)
+    grad_state = 2.0 * weight * lat[:, None] * diff
+
+    back = [None] * ROLL
+    for step in reversed(range(ROLL)):
+        (
+            state_low,
+            normed_one,
+            inverse_one,
+            normed_a,
+            qkv,
+            mixed,
+            attended,
+            normed_two,
+            inverse_two,
+            tokens_b,
+            upward,
+            hidden,
+            downward,
+            normed_three,
+            inverse_three,
+            normed_c,
+        ) = kept[step]
+        shift1, scale1, gate1, shift2, scale2, gate2 = jnp.split(modul[step][None], 6, -1)
+        delta_grad = ((step < length).astype(f32) * grad_state).astype(LOW)
+        grad_mlp = norm_back(product(delta_grad, io_all[1]), normed_three, inverse_three)
+        grad_gate2 = jnp.sum(grad_mlp * downward, 0)
+        moves = Moves("tokens", ids)
+        moves.gather("fsdp", (gate2 * grad_mlp).astype(LOW))
+        tokens_down = moves.run()[0].reshape(shards * local, width)
+        grad_hidden = product(tokens_down, down_copy)
+        up_grad = jax.vjp(jax.nn.gelu, upward)[1](grad_hidden)[0].astype(LOW)
+        up_part = contract(up_grad, up_copy, 1, 1).astype(LOW).reshape(shards, local, width)
+        moves = Moves("token_sums", ids)
+        moves.exchange("fsdp", up_part)
+        grad_normed_b = jnp.sum(moves.run()[0].astype(f32), 0)
+        grad_scale2 = jnp.sum(grad_normed_b * normed_two, 0)
+        grad_shift2 = jnp.sum(grad_normed_b, 0)
+        grad_attn = grad_mlp + norm_back(grad_normed_b * (1.0 + scale2), normed_two, inverse_two)
+        grad_gate1 = jnp.sum(grad_attn * attended, 0)
+        attn_grad = (gate1 * grad_attn).astype(LOW)
+        mixed_grad = contract(attn_grad, w_out, 1, 1).astype(LOW)
+        moves = Moves("mixed_heads", ids)
+        moves.rows_to_heads("seq", mixed_grad, 1)
+        qkv_grad_heads = attention_back(qkv, moves.run()[0][0])
+        moves = Moves("qkv_rows", ids)
+        moves.heads_to_rows("seq", qkv_grad_heads)
+        qkv_grad = moves.run()[0]
+        grad_normed_a = contract(qkv_grad, w_qkv, 1, 1)
+        grad_scale1 = jnp.sum(grad_normed_a * normed_one, 0)
+        grad_shift1 = jnp.sum(grad_normed_a, 0)
+        grad_embedded = grad_attn + norm_back(grad_normed_a * (1.0 + scale1), normed_one, inverse_one)
+        embed_grad = grad_embedded.astype(LOW)
+        grad_state = grad_state + contract(embed_grad, io_all[0], 1, 1)
+        grad_modul = jnp.concatenate([grad_shift1, grad_scale1, grad_gate1, grad_shift2, grad_scale2, grad_gate2])
+        back[step] = (
+            normed_a,
+            mixed,
+            state_low,
+            delta_grad,
+            qkv_grad,
+            attn_grad,
+            embed_grad,
+            normed_c,
+            grad_modul,
+            jnp.sum(grad_embedded, 0),
+            tokens_b,
+            up_grad,
+            tokens_down,
+            hidden,
+        )
+
+    (
+        all_a,
+        all_mixed,
+        all_state,
+        all_delta,
+        all_qkv,
+        all_attn,
+        all_embed,
+        all_c,
+        grad_modul,
+        grad_bias_embed,
+        all_b,
+        all_up,
+        all_down,
+        all_hidden,
+    ) = [jnp.concatenate([item if item.ndim == 2 else item[None] for item in items], 0) for items in zip(*back)]
+    modul_parts = jnp.moveaxis(grad_modul.reshape(ROLL, shards, ada_cols), 1, 0)
+    embed_parts = jnp.sum(grad_bias_embed, 0).reshape(shards, 1, -1)
+    vectors = jnp.concatenate(
+        [modul_parts, jnp.pad(embed_parts, ((0, 0), (0, 0), (0, ada_cols - embed_parts.shape[-1])))], 1
+    )
+    moves = Moves("samples", ids)
+    for array in (all_a, all_mixed, all_state, all_delta):
+        moves.gather("fsdp", array)
+    for array in (all_qkv, all_attn, all_embed, all_c):
+        moves.exchange_columns("fsdp", array)
+    moves.exchange("fsdp", vectors)
+    all_a, all_mixed, all_state, all_delta, all_qkv, all_attn, all_embed, all_c, vectors = moves.run()
+    grad_pos = jnp.sum(all_embed.reshape(shards * ROLL, local, -1).astype(f32), 0)
+    grads_here = (
+        rows_product(all_a, all_qkv),
+        rows_product(all_mixed, all_attn),
+        rows_product(all_b, all_up),
+        rows_product(all_down, all_hidden),
+    )
+    io_here = jnp.stack([rows_product(all_state, all_embed), rows_product(all_delta, all_c)])
+    io_cols = io_here.shape[-1]
+
+    def member_peer(shift):
+        seq_me = lax.axis_index("seq")
+        return {"seq": seq_me // members * members + lax.rem(lax.rem(seq_me, members) + shift, members)}
+
+    moves = Moves("member_sums", ids)
+    halves = []
+    for item, cols in zip(grads_here, group_cols):
+        source = moves.operand(item.astype(LOW))
+        target = moves.output((members - 1, item.shape[0], cols), LOW)
+        for shift in range(1, members):
+            moves.move(
+                ("member", shift),
+                functools.partial(member_peer, shift),
+                source,
+                lambda shift=shift, cols=cols: (
+                    slice(None),
+                    pl.ds(
+                        pl.multiple_of(
+                            lax.rem(lax.rem(lax.axis_index("seq"), members) + shift, members) * cols, LANES
+                        ),
+                        cols,
+                    ),
+                ),
+                target,
+                lambda shift=shift: (shift - 1,),
+            )
+    moves.gather("seq", vectors.reshape(-1, ada_cols))
+    moves.exchange("seq", io_here.reshape(seq_count, -1, io_cols).astype(LOW))
+    *halves, vectors, io_parts = moves.run()
+    vectors = jnp.sum(vectors, 0).reshape(shards, ROLL + 1, ada_cols)
+    io_slice = jnp.sum(io_parts.astype(f32), 0)
+    member_sums = [
+        lax.dynamic_slice_in_dim(item, member * cols, cols, 1) + jnp.sum(half.astype(f32), 0)
+        for item, half, cols in zip(grads_here, halves, group_cols)
+    ]
+    modul_all = vectors[:, :ROLL].reshape(-1, ada_cols)
+    bias_part = jnp.concatenate([jnp.sum(modul_all, 0), jnp.sum(vectors[:, ROLL, : width // shards], 0)])
+    silu_part = lax.dot_general(
+        modul_all, ada_copy.astype(f32), (((1,), (1,)), ((), ())), precision=HIGHEST_PRECISION
+    )
+
+    moves = Moves("group_sums", ids)
+    source = moves.operand(jnp.stack([widen(item.astype(LOW)) for item in member_sums]))
+    target = moves.output((MATRICES,) + (member_sums[0].shape[0], most_cols), LOW)
+    for shift in range(1, MATRICES):
+        moves.move(
+            ("group", shift),
+            lambda shift=shift: {"seq": lax.rem(lax.axis_index("seq") + shift * members, seq_count)},
+            source,
+            lambda shift=shift: (lax.rem(lax.axis_index("seq") // members + shift, MATRICES),),
+            target,
+            lambda: (lax.axis_index("seq") // members,),
+        )
+    moves.keep(source, lambda: (lax.axis_index("seq") // members,), target, lambda: (lax.axis_index("seq") // members,))
+    moves.gather("fsdp", silu_part)
+    moves.gather("fsdp", bias_part[None])
+    grad_parts, silu_parts, bias_parts = moves.run()
+    grad_group = jnp.sum(grad_parts.astype(f32), 0)
+    grad_silu = jnp.sum(silu_parts, 0)
+    grad_cond = jax.vjp(jax.nn.silu, cond_vec)[1](grad_silu)[0]
+    grad_table_all = lax.dot_general(select, grad_cond, (((0,), (0,)), ((), ())), precision=HIGHEST_PRECISION)
+    grad_table = lax.dynamic_slice_in_dim(grad_table_all, shard * table_cols, table_cols, 1)
+    bias_parts = bias_parts[:, 0]
+    grad_bias_all = jnp.concatenate([bias_parts[:, :ada_cols].reshape(-1), bias_parts[:, ada_cols:].reshape(-1)])
+    grad_bias = lax.dynamic_slice_in_dim(grad_bias_all, shard * biases.shape[0], biases.shape[0])
+    silu_rows = lax.dynamic_slice_in_dim(silu_low, seq_index * ada_master.shape[0], ada_master.shape[0], 1)
+    grad_ada = lax.dot_general(
+        silu_rows.astype(f32), modul_all, (((0,), (0,)), ((), ())), precision=HIGHEST_PRECISION
+    )
+
+    moment_group = moment_group.reshape(-1, most_cols).astype(f32)
+    grad_squares = jnp.sum(grad_group * grad_group)
+    squares = (
+        grad_squares
+        + jnp.sum(grad_ada * grad_ada)
+        + jnp.sum(io_slice * io_slice)
+        + jnp.sum(grad_pos * grad_pos)
+        + (seq_index == 0).astype(f32) * (jnp.sum(grad_table * grad_table) + jnp.sum(grad_bias * grad_bias))
+    )
+    lane = jnp.arange(LANES, dtype=jnp.int32)
+    place = 2 + 3 * group
+    entries = jnp.where(lane == 0, squares, 0.0) + jnp.where(lane == 1, loss_local, 0.0)
+    entries = entries + jnp.where(lane == place, jnp.sum(moment_group * moment_group), 0.0)
+    entries = entries + jnp.where(lane == place + 1, jnp.sum(moment_group * grad_group), 0.0)
+    entries = entries + jnp.where(lane == place + 2, grad_squares, 0.0)
+    sums = total_of(ids, jnp.broadcast_to(entries[None], (8, LANES)))[0]
+    grad_norm = jnp.sqrt(sums[0])
+    loss_total = sums[1]
+    clip = jnp.minimum(1.0, CLIP_LIMIT / (grad_norm + 1e-06))
+    terms = sums[2 : 2 + 3 * MATRICES].reshape(MATRICES, 3)
+    size_squares = MOMENTUM * MOMENTUM * terms[:, 0] + 2.0 * MOMENTUM * clip * terms[:, 1] + clip * clip * terms[:, 2]
+    sizes = jnp.sqrt(jnp.maximum(size_squares, 0.0))
+    moment_sizes = sizes / CLIP_LIMIT
+    my_size = lax.dynamic_slice_in_dim(sizes, group, 1)[0]
+    block = ((MOMENTUM * moment_group + clip * grad_group) / (my_size + 1e-07)).astype(LOW)
+
+    moves = Moves("columns", ids)
+    source = moves.operand(block)
+    block_rows = block.shape[0]
+    peers = members * shards
+    target = moves.output((block_rows, peers * most_cols), LOW)
+
+    def slot(back_member, back_pair):
+        who_member = lax.rem(lax.rem(lax.axis_index("seq"), members) + members - back_member, members)
+        who_shard = lax.rem(lax.axis_index("fsdp") + shards - 2 * back_pair, shards)
+        start = (who_member * shards + who_shard) * most_cols
+        return (slice(None), pl.ds(pl.multiple_of(start, LANES), most_cols))
+
+    def sibling():
+        index = lax.axis_index("fsdp")
+        return {"fsdp": index + 1 - 2 * lax.rem(index, 2)}
+
+    moves.move(("sibling",), sibling, source, None, target, lambda: slot(0, 0))
+    moves.keep(source, None, target, lambda: slot(0, 0))
+    for far_member in range(members):
+        for far_pair in range(shards // 2):
+            if far_member or far_pair:
+
+                def peer(far_member=far_member, far_pair=far_pair):
+                    seq_me = lax.axis_index("seq")
+                    return {
+                        "seq": seq_me // members * members + lax.rem(lax.rem(seq_me, members) + far_member, members),
+                        "fsdp": lax.rem(lax.axis_index("fsdp") + 2 * far_pair, shards),
+                    }
+
+                number = moves.move(("plane", far_member, far_pair), peer, source, None, target, lambda: slot(0, 0))
+                arrived = functools.partial(slot, far_member, far_pair)
+                moves.move(("sibling",), sibling, target, arrived, target, arrived, (number,))
+    moves.exchange("seq", grad_group.astype(LOW).reshape(seq_count, -1, most_cols))
+    moves.gather("seq", io_slice)
+    columns, grad_rows, io_slices = moves.run()
+
+    def row_blocks(parts):
+        return [
+            jnp.concatenate(
+                [parts[which * members + part][:, : group_cols[which]] for part in range(members)], -1
+            ).astype(f32)
+            for which in range(MATRICES)
+        ]
+
+    moments = [MOMENTUM * old + clip * grad for old, grad in zip(momenta, row_blocks(grad_rows))]
+    block = newton_schulz(block, contract(columns, columns, 1, 1))
+    moves = Moves("update_rows", ids)
+    moves.exchange("seq", block.reshape(seq_count, -1, most_cols))
+    masters = (qkv_master, out_master, up_master, down_master)
+    fresh = [
+        master * (1.0 - RATE_MUON * DECAY_MUON) - RATE_MUON * 0.2 * math.sqrt(master.shape[1] * shards) * rows
+        for master, rows in zip(masters, row_blocks(moves.run()[0]))
+    ]
+
+    moves = Moves("copies", ids)
+    rows = qkv_master.shape[0]
+
+    def row_place(back_group, back_member):
+        seq_me = lax.axis_index("seq")
+        who = lax.rem(seq_me // members + MATRICES - back_group, MATRICES) * members
+        who = who + lax.rem(lax.rem(seq_me, members) + members - back_member, members)
+        return (pl.ds(pl.multiple_of(who * rows, rows), rows),)
+
+    places = []
+    for item in fresh:
+        source = moves.operand(item.astype(LOW))
+        target = moves.output((rows * seq_count, item.shape[1]), LOW)
+        moves.keep(source, None, target, lambda: row_place(0, 0))
+        places.append((source, target, []))
+    for shift in range(1, MATRICES):
+        for source, target, numbers in places:
+            numbers.append(
+                moves.move(
+                    ("group", shift),
+                    lambda shift=shift: {"seq": lax.rem(lax.axis_index("seq") + shift * members, seq_count)},
+                    source,
+                    None,
+                    target,
+                    lambda: row_place(0, 0),
+                )
+            )
+    for shift in range(1, members):
+        for source, target, numbers in places:
+            moves.move(
+                ("member", shift),
+                functools.partial(member_peer, shift),
+                source,
+                None,
+                target,
+                lambda: row_place(0, 0),
+            )
+    for far in range(1, MATRICES):
+        for source, target, numbers in places:
+            for shift in range(1, members):
+                place = functools.partial(row_place, far, 0)
+                moves.move(
+                    ("member", shift),
+                    functools.partial(member_peer, shift),
+                    target,
+                    place,
+                    target,
+                    place,
+                    (numbers[far - 1],),
+                )
+    copies = moves.run()
+
+    io_grad = io_slices.reshape(2, padded, io_cols)[:, :values_count]
+    ada_res = adam_update(ada_master, ada_first, ada_second, clip * grad_ada, RATE_ADAM)
+    io_res = adam_update(io_proj, io_first, io_second, clip * io_grad, RATE_ADAM)
+    cond_res = adam_update(cond_table, cond_first, cond_second, clip * grad_table, RATE_TABLE)
+    pos_res = adam_update(pos_table, pos_first, pos_second, clip * grad_pos, RATE_TABLE)
+    bias_res = adam_update(biases, bias_first, bias_second, clip * grad_bias, RATE_ADAM)
+    matrices = []
+    for which in range(MATRICES):
+        matrices += [fresh[which], moments[which], copies[which]]
+    return (loss_total, grad_norm, moment_sizes, *matrices, *ada_res, *io_res, *cond_res, *pos_res, *bias_res)
+
+
+def fits_fast(mesh):
+    seq, shards = mesh.shape["seq"], mesh.shape["fsdp"]
+    return HEADS % seq == 0 and (HEADS // seq * HEAD) % LANES == 0 and seq % MATRICES == 0 and shards % 2 == 0
+
+
 def solution(mesh):
+    body = fast_body if fits_fast(mesh) else general_body
     return jax.shard_map(
         body,
         mesh=mesh,

time: 4360 us -> 1200 us (0.28)
  waiting for transfers between devices: 2210 us -> 1.42 us
  blocking collectives: 1640 us -> 0 us
  Pallas kernels: 0 us -> 805 us
  matrix products: 264 us -> 195 us
  local copies, waits for them, and re-layouts: 108 us -> 62.6 us
    psum x8 -> x0, blocking collectives: 1550 us -> none  [the longest x5 1430 us: body(): lax.psum((partial_value[0], partial_value[1], partial_value[2], partial_v...]
    reduce_scatter x17 -> x0, waiting for transfers between devices: 1290 us -> none  [the longest x1 183 us: body(): lax.psum_scatter(totals[4], 'fsdp', scatter_dimension=1, tiled=True)]
    pallas_call x0 -> x29, Pallas kernels: none -> 805 us  [the longest x24 736 us: run(): pl.pallas_call(self.kernel, out_shape=self.outputs, in_specs=[in_any] * l...]
    all_gather x16 -> x2, waiting for transfers between devices: 621 us -> 0.04 us  [the longest x1 0.02 us: fast_body(): w_qkv = lax.all_gather(qkv_copy, 'fsdp', axis=1, tiled=True)]
    psum x2 -> x0, waiting for transfers between devices: 299 us -> none  [the longest x1 225 us: broadcast(): return lax.psum(block, axis)]
    dot_general x32 -> x15, matrix products: 141 us -> 44.7 us  [the longest x12 38.6 us: contract(): lax.dot_general(left, right, (((left_dim,), (right_dim,)), ((), ())), pre...]
    all_gather x5 -> x0, blocking collectives: 82.6 us -> none  [the longest x1 32.5 us: body(): lax.all_gather(scaled[1], 'seq', axis=0, tiled=True)]
    dot_general x19 -> x42, matrix products: 78.1 us -> 130 us  [product(): return jnp.dot(left, right, preferred_element_type=jnp.float32)]
  transfers between devices with their start and end apart: 35 -> 2, of which waited for: 31 -> 0; matrix products, arithmetic and copies ran while one was open for 5% -> 4% of each run, Pallas kernels for 0% -> 8%
where the time goes in v1:
time: 1200 us; the launch traced here: 1170 us
  Pallas kernels  805 us (67%)
  matrix products  195 us (16%)
  other arithmetic  86.6 us (7%)
  local copies, waits for them, and re-layouts  62.6 us (5%)
  between operations  25.1 us (2%)
    pallas_call x24, Pallas kernels, run(): pl.pallas_call(self.kernel, out_shape=self.outputs, in_specs=[in_any] * l...  736 us
    dot_general x42, matrix products, product(): return jnp.dot(left, right, preferred_element_type=jnp.float32)  130 us
    unnamed x345, local copies, waits for them, and re-layouts  38.7 us
    dot_general x12, matrix products, contract(): lax.dot_general(left, right, (((left_dim,), (right_dim,)), ((), ())), pre...  38.6 us
    pallas_call x1, Pallas kernels, total_of(): pl.pallas_call(total_kernel, out_shape=jax.ShapeDtypeStruct(values.shape,...  31.7 us
  transfers between devices with their start and end apart: 2, of which 0 were waited for; matrix products, arithmetic and copies ran while one was open for 4% of the time, Pallas kernels for 8%

profile of v1, /device:TPU:0, one launch (start us, length us, event | category | flops | bytes accessed | tf_op | source)
XLA Modules:
  0.0 1174.9 jit_solution(18161254876596016529)
XLA Ops:
  28.1 45.3 %embeddings.1 = (bf16[4,2,384,256]{3,2,1,0:T(8,128)(2,1)}, f32[4,5,256]{2,1,0:T(8,128)}, bf16[4,128,256]{2,1,0:T(8,128)(2,1)}, f32[4,1,1792]{2,1,0:T(1,128)}) custom-call(bf16[2,384,256]{2,1,0:T(8,128)(2,1)} %pad.44.refs_0_, f32[5,256]{1,0:T(8,128)} %refs_1_.1, bf16[128,256]{1,0:T(8,128)(2,1)} %convert_element_type.448.refs_2_, ...), custom_call_target="tpu_custom_call" | custom-call | tf_op jit(solution)/shard_map/embeddings/pallas_call | solution.py:597
  81.7 4.2 modulation.1
  103.5 4.7 convolution_convert_fusion.1.refs_0_
  108.2 18.4 %qkv_heads.2.qkv_ref = bf16[3,1024,128]{2,1,0:T(8,128)(2,1)} custom-call(bf16[128,3072]{1,0:T(8,128)(2,1)} %convolution_convert_fusion.1.refs_0_), custom_call_target="tpu_custom_call" | custom-call | tf_op jit(solution)/shard_map/qkv_heads/pallas_call | solution.py:597
  127.7 6.4 attention.2
  134.8 13.8 %mixed_rows.2 = bf16[128,1024]{1,0:T(8,128)(2,1)} custom-call(bf16[1,1024,128]{2,1,0:T(8,128)(2,1)} %bitcast.243), custom_call_target="tpu_custom_call" | custom-call | tf_op jit(solution)/shard_map/mixed_rows/pallas_call | solution.py:597
  153.3 21.4 %tokens_momenta.1 = (bf16[4,128,1024]{2,1,0:T(8,128)(2,1)}, bf16[8,128,512]{2,1,0:T(8,128)(2,1)}) custom-call(bf16[128,1024]{1,0:T(8,128)(2,1)} %add_convert_fusion.10.refs_0_, bf16[8,128,512]{2,1,0:T(8,128)(2,1)} %fusion.73.refs_1_), custom_call_target="tpu_custom_call" | custom-call | tf_op jit(solution)/shard_map/tokens_momenta/pallas_call | solution.py:597
  174.8 4.9 multiply_convert_fusion.1
  182.0 13.1 %token_sums.4 = bf16[4,128,1024]{2,1,0:T(8,128)(2,1)} custom-call(bf16[4,128,1024]{2,1,0:T(8,128)(2,1)} %bitcast.268), custom_call_target="tpu_custom_call" | custom-call | tf_op jit(solution)/shard_map/token_sums/pallas_call | solution.py:597
  201.6 4.7 convolution_convert_fusion.refs_0_
  206.3 22.2 %qkv_heads.3.qkv_ref = bf16[3,1024,128]{2,1,0:T(8,128)(2,1)} custom-call(bf16[128,3072]{1,0:T(8,128)(2,1)} %convolution_convert_fusion.refs_0_), custom_call_target="tpu_custom_call" | custom-call | tf_op jit(solution)/shard_map/qkv_heads/pallas_call | solution.py:597
  229.6 6.7 attention.3
  237.0 14.5 %mixed_rows.3 = bf16[128,1024]{1,0:T(8,128)(2,1)} custom-call(bf16[1,1024,128]{2,1,0:T(8,128)(2,1)} %bitcast.244), custom_call_target="tpu_custom_call" | custom-call | tf_op jit(solution)/shard_map/mixed_rows/pallas_call | solution.py:597
  257.9 13.5 %tokens.3 = bf16[4,128,1024]{2,1,0:T(8,128)(2,1)} custom-call(bf16[128,1024]{1,0:T(8,128)(2,1)} %add_convert_fusion.8.refs_0_), custom_call_target="tpu_custom_call" | custom-call | tf_op jit(solution)/shard_map/tokens/pallas_call | solution.py:597
  271.4 4.9 multiply_convert_fusion
  278.6 14.1 %token_sums.5 = bf16[4,128,1024]{2,1,0:T(8,128)(2,1)} custom-call(bf16[4,128,1024]{2,1,0:T(8,128)(2,1)} %bitcast.269), custom_call_target="tpu_custom_call" | custom-call | tf_op jit(solution)/shard_map/token_sums/pallas_call | solution.py:597
  300.5 14.1 %tokens.4 = bf16[4,128,1024]{2,1,0:T(8,128)(2,1)} custom-call(bf16[128,1024]{1,0:T(8,128)(2,1)} %multiply_convert_fusion.5.refs_0_), custom_call_target="tpu_custom_call" | custom-call | tf_op jit(solution)/shard_map/tokens/pallas_call | solution.py:597
  314.6 5.0 fusion.13
  321.8 14.1 %token_sums.6 = bf16[4,128,1024]{2,1,0:T(8,128)(2,1)} custom-call(bf16[4,128,1024]{2,1,0:T(8,128)(2,1)} %bitcast.270), custom_call_target="tpu_custom_call" | custom-call | tf_op jit(solution)/shard_map/token_sums/pallas_call | solution.py:597
  341.9 11.3 mixed_heads.2
  355.3 11.9 %attention_back.2.refs_0_ = bf16[3,1024,128]{2,1,0:T(8,128)(2,1)S(1)} custom-call(bf16[3,1024,128]{2,1,0:T(8,128)(2,1)S(1)} %copy-done.5, bf16[1024,128]{1,0:T(8,128)(2,1)S(1)} %bitcast.241), custom_call_target="tpu_custom_call" | custom-call | tf_op jit(solution)/shard_map/attention_back/pallas_call | solution.py:842
  368.0 19.0 %qkv_rows.2 = bf16[128,3072]{1,0:T(8,128)(2,1)} custom-call(bf16[3,1024,128]{2,1,0:T(8,128)(2,1)} %copy-done.6), custom_call_target="tpu_custom_call" | custom-call | tf_op jit(solution)/shard_map/qkv_rows/pallas_call | solution.py:597
  387.1 5.6 multiply_reduce_fusion.5
  397.0 12.6 %tokens.5 = bf16[4,128,1024]{2,1,0:T(8,128)(2,1)} custom-call(bf16[128,1024]{1,0:T(8,128)(2,1)} %multiply_convert_fusion.3.refs_0_), custom_call_target="tpu_custom_call" | custom-call | tf_op jit(solution)/shard_map/tokens/pallas_call | solution.py:597
  409.6 5.0 fusion.6
  417.0 5.1 fusion.187
  422.1 5.1 fusion.188
  427.9 14.1 %token_sums.7 = bf16[4,128,1024]{2,1,0:T(8,128)(2,1)} custom-call(bf16[4,128,1024]{2,1,0:T(8,128)(2,1)} %bitcast.266), custom_call_target="tpu_custom_call" | custom-call | tf_op jit(solution)/shard_map/token_sums/pallas_call | solution.py:597
  448.8 14.0 %mixed_heads.3 = bf16[1,1024,128]{2,1,0:T(8,128)(2,1)} custom-call(bf16[128,1024]{1,0:T(8,128)(2,1)} %convolution_convert_fusion.6.refs_0_), custom_call_target="tpu_custom_call" | custom-call | tf_op jit(solution)/shard_map/mixed_heads/pallas_call | solution.py:597
  465.0 11.7 attention_back.3.refs_0_
  477.5 18.7 %qkv_rows.3 = bf16[128,3072]{1,0:T(8,128)(2,1)} custom-call(bf16[3,1024,128]{2,1,0:T(8,128)(2,1)} %copy-done.7), custom_call_target="tpu_custom_call" | custom-call | tf_op jit(solution)/shard_map/qkv_rows/pallas_call | solution.py:597
  499.1 5.3 multiply_reduce_fusion.9
  506.3 100.4 %samples.1 = (bf16[4,256,1024]{2,1,0:T(8,128)(2,1)}, bf16[4,256,1024]{2,1,0:T(8,128)(2,1)}, bf16[4,256,384]{2,1,0:T(8,128)(2,1)}, bf16[4,256,384]{2,1,0:T(8,128)...) custom-call(bf16[256,1024]{1,0:T(8,128)(2,1)} %get-tuple-element.235, ...), custom_call_target="tpu_custom_call" | custom-call | tf_op jit(solution)/shard_map/samples/pallas_call | solution.py:597
  618.5 90.4 %member_sums.1 = (bf16[1,1024,384]{2,1,0:T(8,128)(2,1)}, bf16[1,1024,128]{2,1,0:T(8,128)(2,1)}, bf16[1,1024,512]{2,1,0:T(8,128)(2,1)}, bf16[1,1024,512]{2,1,0:T(...) custom-call(bf16[1024,768]{1,0:T(8,128)(2,1)} %get-tuple-element.223.refs_0_, ...), custom_call_target="tpu_custom_call" | custom-call | tf_op jit(solution)/shard_map/member_sums/pallas_call | solution.py:597
  726.9 72.4 %group_sums.1 = (bf16[4,1024,512]{2,1,0:T(8,128)(2,1)}, f32[4,8,1024]{2,1,0:T(8,128)}, f32[4,1,1792]{2,1,0:T(1,128)}) custom-call(bf16[4,1024,512]{2,1,0:T(8,128)(2,1)} %pad_maximum_fusion.refs_0_, f32[8,1024]{1,0:T(8,128)} %fusion.191.refs_1_, f32[1,1792]{1,0:T(1,128)} %broadcast_in_dim.35.refs_2_), custom_call_target="tpu_custom_call" | custom-call | tf_op jit(solution)/shard_map/group_sums/pallas_call | solution.py:597
  818.9 31.7 %total.1 = f32[8,128]{1,0:T(8,128)} custom-call(f32[8,128]{1,0:T(8,128)} %broadcast_in_dim.42.x_ref), custom_call_target="tpu_custom_call" | custom-call | tf_op jit(solution)/shard_map/total/pallas_call | solution.py:753
  854.7 4.1 bitcast_convert_fusion
  858.9 69.1 %columns.1 = (bf16[1024,4096]{1,0:T(8,128)(2,1)}, bf16[8,128,512]{2,1,0:T(8,128)(2,1)}, f32[8,96,256]{2,1,0:T(8,128)}) custom-call(bf16[1024,512]{1,0:T(8,128)(2,1)} %get-tuple-element.164.refs_0_, bf16[8,128,512]{2,1,0:T(8,128)(2,1)} %get-tuple-element.163.refs_1_, f32[96,256]{1,0:T(8,128)} %copy-done.75), custom_call_target="tpu_custom_call" | custom-call | tf_op jit(solution)/shard_map/columns/pallas_call | solution.py:597
  927.9 12.8 %fusion.192 = f32[1024,1024]{1,0:T(8,128)S(1)} fusion(bf16[1024,4096]{1,0:T(8,128)(2,1)} %get-tuple-element.85), kind=kOutput, calls=%fused_computation.438 | convolution fusion | flops 8589934592 | bytes 12582912 | tf_op jit(solution)/shard_map/dot_general | solution.py:774
  973.2 4.8 fusion.115
  978.0 4.3 fusion.118
  982.3 6.6 add_add_fusion.2
  1003.7 4.4 fusion.110
  1008.1 4.3 fusion.113
  1019.2 7.3 add_add_fusion
  1026.5 9.6 add_convert_fusion.3
  1036.0 20.0 %update_rows.1 = bf16[8,128,512]{2,1,0:T(8,128)(2,1)} custom-call(bf16[8,128,512]{2,1,0:T(8,128)(2,1)} %bitcast.267), custom_call_target="tpu_custom_call" | custom-call | tf_op jit(solution)/shard_map/update_rows/pallas_call | solution.py:597
  1061.2 85.7 %copies.1 = (bf16[1024,768]{1,0:T(8,128)(2,1)}, bf16[1024,256]{1,0:T(8,128)(2,1)}, bf16[1024,1024]{1,0:T(8,128)(2,1)}, bf16[1024,1024]{1,0:T(8,128)(2,1)}) custom-call(bf16[128,768]{1,0:T(8,128)(2,1)} %get-tuple-element.137.refs_0_, bf16[128,256]{1,0:T(8,128)(2,1)} %get-tuple-element.135.refs_1_, bf16[128,1024]{1,0:T(8,128)(2,1)} %get-tuple-element.133.refs_2_, ...), custom_call_target="tpu_custom_call" | custom-call | tf_op jit(solution)/shard_map/copies/pallas_call | solution.py:597
  (561 shorter events, 237.0 us)
Async XLA Ops:
  7.2 73.3 %copy-start = (bf16[1024,1536]{1,0:T(8,128)(2,1)S(1)}, bf16[1024,1536]{1,0:T(8,128)(2,1)}, u32[]{:S(2)}) copy-start(bf16[1024,1536]{1,0:T(8,128)(2,1)} %param.48) | copy-start | bytes 9437188
  7.2 7.9 copy-start.108
  7.2 14.9 %copy-start.59 = (f32[128,768]{1,0:T(8,128)S(1)}, f32[128,768]{1,0:T(8,128)}, u32[]{:S(2)}) copy-start(f32[128,768]{1,0:T(8,128)} %param.38) | copy-start | bytes 1179652
  7.3 96.3 %all-gather.3.cloned.1.call-start = ((), (), s32[]{:S(2)}) async-start(), calls=%async_computation | async-start | bytes 7864320 | tf_op jit(solution)/shard_map/all_gather | solution.py:938
  8.0 140.7 %all-gather.5.cloned.1.call-start = ((), (), s32[]{:S(2)}) async-start(), calls=%async_computation.1 | async-start | bytes 2621440 | tf_op jit(solution)/shard_map/all_gather | solution.py:939
  15.1 10.9 copy-start.114
  73.5 5.7 copy-start.110
  81.0 16.3 %copy-start.62 = (bf16[1,128,276]{2,1,0:T(8,128)(2,1)S(1)}, bf16[1,128,276]{2,1,0:T(8,128)(2,1)}, u32[]{:S(2)}) copy-start(bf16[1,128,276]{2,1,0:T(8,128)(2,1)} %copy.94) | copy-start | bytes 211972
  87.8 12.8 %copy-start.100 = (f32[4,2,1536]{2,1,0:T(2,128)S(1)}, f32[4,2,1536]{2,1,0:T(2,128)}, u32[]{:S(2)}) copy-start(f32[4,2,1536]{2,1,0:T(2,128)} %modulation.1) | copy-start | bytes 147460
  92.8 7.9 copy-start.70
  200.0 6.3 copy-start.127
  341.9 45.1 %copy-start.128 = (f32[128]{0:T(128)S(1)}, f32[128]{0:T(128)}, u32[]{:S(2)}) copy-start(f32[128]{0:T(128)} %copy-done.127) | copy-start | bytes 1540
  387.0 5.7 copy-start.25
  387.1 5.7 copy-start.41
  387.1 5.7 copy-start.129
  387.1 5.7 copy-start.137
  387.1 6.0 copy-start.29
  387.1 6.0 copy-start.79
  387.1 6.0 copy-start.139
  427.2 16.6 %copy-start.124 = (f32[128]{0:T(128)S(1)}, f32[128]{0:T(128)}, u32[]{:S(2)}) copy-start(f32[128]{0:T(128)} %copy-done.123) | copy-start | bytes 1540
  427.2 16.6 %copy-start.133 = (f32[128]{0:T(128)S(1)}, f32[128]{0:T(128)}, u32[]{:S(2)}) copy-start(f32[128]{0:T(128)} %copy-done.132) | copy-start | bytes 1540
  477.5 21.5 %copy-start.122 = (f32[128]{0:T(128)S(1)}, f32[128]{0:T(128)}, u32[]{:S(2)}) copy-start(f32[128]{0:T(128)} %copy-done.121) | copy-start | bytes 1540
  477.5 21.5 %copy-start.131 = (f32[128]{0:T(128)S(1)}, f32[128]{0:T(128)}, u32[]{:S(2)}) copy-start(f32[128]{0:T(128)} %copy-done.130) | copy-start | bytes 1540
  499.0 5.3 copy-start.39
  499.0 5.6 copy-start.49
  710.8 8.9 copy-start.99
  712.0 6.7 copy-start.111
  712.0 6.7 copy-start.140
  712.9 6.5 copy-start.78
  712.9 6.5 copy-start.83
  726.9 73.3 %copy-start.141 = (f32[128]{0:T(128)S(1)}, f32[128]{0:T(128)}, u32[]{:S(2)}) copy-start(f32[128]{0:T(128)} %get-tuple-element.184) | copy-start | bytes 1540
  726.9 75.3 %copy-start.89 = (bf16[4,256,256]{2,1,0:T(8,128)(2,1)S(1)}, bf16[4,256,256]{2,1,0:T(8,128)(2,1)}, u32[]{:S(2)}) copy-start(bf16[4,256,256]{2,1,0:T(8,128)(2,1)} %get-tuple-element.72) | copy-start | bytes 1572868
  726.9 76.0 %copy-start.96 = (bf16[8,96,256]{2,1,0:T(8,128)(2,1)S(1)}, bf16[8,96,256]{2,1,0:T(8,128)(2,1)}, u32[]{:S(2)}) copy-start(bf16[8,96,256]{2,1,0:T(8,128)(2,1)} %get-tuple-element.81) | copy-start | bytes 1179652
  806.7 7.3 copy-start.74
  808.1 8.2 copy-start.120
  1036.0 21.6 %copy-start.101 = (f32[128,256]{1,0:T(8,128)S(1)}, f32[128,256]{1,0:T(8,128)}, u32[]{:S(2)}) copy-start(f32[128,256]{1,0:T(8,128)} %param.40) | copy-start | bytes 393220
  1059.2 87.7 %copy-start.112 = (f32[5,256]{1,0:T(8,128)S(1)}, f32[5,256]{1,0:T(8,128)}, u32[]{:S(2)}) copy-start(f32[5,256]{1,0:T(8,128)} %refs_1_.1) | copy-start | bytes 15364
  1059.2 87.7 %copy-start.116 = (f32[5,256]{1,0:T(8,128)S(1)}, f32[5,256]{1,0:T(8,128)}, u32[]{:S(2)}) copy-start(f32[5,256]{1,0:T(8,128)} %param.56) | copy-start | bytes 15364
  1059.2 87.7 %copy-start.117 = (f32[5,256]{1,0:T(8,128)S(1)}, f32[5,256]{1,0:T(8,128)}, u32[]{:S(2)}) copy-start(f32[5,256]{1,0:T(8,128)} %param.57) | copy-start | bytes 15364
  1059.2 89.0 %copy-start.64 = (f32[128,256]{1,0:T(8,128)S(1)}, f32[128,256]{1,0:T(8,128)}, u32[]{:S(2)}) copy-start(f32[128,256]{1,0:T(8,128)} %copy-done.63) | copy-start | bytes 393220
  1059.2 89.0 %copy-start.90 = (f32[128,256]{1,0:T(8,128)S(1)}, f32[128,256]{1,0:T(8,128)}, u32[]{:S(2)}) copy-start(f32[128,256]{1,0:T(8,128)} %param.58) | copy-start | bytes 393220
  1059.2 90.8 %copy-start.91 = (f32[128,256]{1,0:T(8,128)S(1)}, f32[128,256]{1,0:T(8,128)}, u32[]{:S(2)}) copy-start(f32[128,256]{1,0:T(8,128)} %param.41) | copy-start | bytes 393220
  1060.2 91.4 %copy-start.60 = (f32[128,768]{1,0:T(8,128)S(1)}, f32[128,768]{1,0:T(8,128)}, u32[]{:S(2)}) copy-start(f32[128,768]{1,0:T(8,128)} %param.38) | copy-start | bytes 1179652
  1060.2 93.2 %copy-start.52 = (f32[128,1024]{1,0:T(8,128)S(1)}, f32[128,1024]{1,0:T(8,128)}, u32[]{:S(2)}) copy-start(f32[128,1024]{1,0:T(8,128)} %param.47) | copy-start | bytes 1572868
  1061.2 93.1 %copy-start.53 = (f32[128,1024]{1,0:T(8,128)S(1)}, f32[128,1024]{1,0:T(8,128)}, u32[]{:S(2)}) copy-start(f32[128,1024]{1,0:T(8,128)} %param.44) | copy-start | bytes 1572868
  1150.0 5.8 copy-start.51
  1150.0 5.8 copy-start.85
  1150.1 5.8 copy-start.86
  (114 other events, 297.9 us)
Sparse Core Ops, SparseCore 0:
  9.7 69.3 all-gather.2
  80.6 22.8 all-gather.4

commit v2 on v1

--- a/solution.py
+++ b/solution.py
@@ -8,6 +8,8 @@
 from jax.experimental.pallas import tpu as pltpu
 from jax.sharding import PartitionSpec as P
 
+PATCHES = "seq"
+SHARDS = "fsdp"
 HEADS = 16
 HEAD = 64
 NI = 3
@@ -79,12 +81,12 @@
 
 
 def latitude_weights(local):
-    all_patches = local * lax.axis_size("seq")
+    all_patches = local * lax.axis_size(PATCHES)
     band_row = (jnp.arange(all_patches, dtype=jnp.int32) // LON).astype(jnp.float32)
     latitude = (band_row + 0.5) * (math.pi / (all_patches // LON)) - math.pi / 2
     cosine = jnp.cos(latitude)
     weights = cosine / jnp.mean(cosine)
-    return lax.dynamic_slice_in_dim(weights, lax.axis_index("seq") * local, local)
+    return lax.dynamic_slice_in_dim(weights, lax.axis_index(PATCHES) * local, local)
 
 
 def forward_step(weights, state, active, select):
@@ -105,8 +107,8 @@
     qkv = product(normed_a, w_qkv).astype(jnp.bfloat16)
     queries = qkv[..., :width]
     keys, values = (
-        lax.all_gather(qkv[..., width : 2 * width], "seq", axis=1, tiled=True),
-        lax.all_gather(qkv[..., 2 * width :], "seq", axis=1, tiled=True),
+        lax.all_gather(qkv[..., width : 2 * width], PATCHES, axis=1, tiled=True),
+        lax.all_gather(qkv[..., 2 * width :], PATCHES, axis=1, tiled=True),
     )
     scores = jnp.einsum(
         "sphd,snhd->shpn", heads_view(queries), heads_view(keys), preferred_element_type=jnp.float32
@@ -226,8 +228,8 @@
         "shpn,sphd->snhd", probs_low, g_heads, preferred_element_type=jnp.float32
     ).reshape(values.shape)
     grad_keys, grad_values = (
-        lax.psum_scatter(key_part, "seq", scatter_dimension=1, tiled=True),
-        lax.psum_scatter(value_part, "seq", scatter_dimension=1, tiled=True),
+        lax.psum_scatter(key_part, PATCHES, scatter_dimension=1, tiled=True),
+        lax.psum_scatter(value_part, PATCHES, scatter_dimension=1, tiled=True),
     )
     qkv_grad = jnp.concatenate([grad_queries, grad_keys, grad_values], -1).astype(jnp.bfloat16)
     grad_qkv = rows_product(normed_a, qkv_grad)
@@ -335,19 +337,19 @@
     bias_second,
 ):
     weights = (
-        lax.all_gather(qkv_copy, "fsdp", axis=1, tiled=True),
-        lax.all_gather(out_copy, "fsdp", axis=1, tiled=True),
-        lax.all_gather(up_copy, "fsdp", axis=1, tiled=True),
-        lax.all_gather(down_copy, "fsdp", axis=1, tiled=True),
-        lax.all_gather(ada_copy, "fsdp", axis=1, tiled=True),
-        lax.all_gather(io_proj.astype(jnp.bfloat16), "fsdp", axis=2, tiled=True),
-        lax.all_gather(cond_table.astype(jnp.bfloat16), "fsdp", axis=1, tiled=True),
-        lax.all_gather(pos_table.astype(jnp.bfloat16), "fsdp", axis=1, tiled=True),
-        lax.all_gather(biases.astype(jnp.bfloat16), "fsdp", axis=0, tiled=True),
+        lax.all_gather(qkv_copy, SHARDS, axis=1, tiled=True),
+        lax.all_gather(out_copy, SHARDS, axis=1, tiled=True),
+        lax.all_gather(up_copy, SHARDS, axis=1, tiled=True),
+        lax.all_gather(down_copy, SHARDS, axis=1, tiled=True),
+        lax.all_gather(ada_copy, SHARDS, axis=1, tiled=True),
+        lax.all_gather(io_proj.astype(jnp.bfloat16), SHARDS, axis=2, tiled=True),
+        lax.all_gather(cond_table.astype(jnp.bfloat16), SHARDS, axis=1, tiled=True),
+        lax.all_gather(pos_table.astype(jnp.bfloat16), SHARDS, axis=1, tiled=True),
+        lax.all_gather(biases.astype(jnp.bfloat16), SHARDS, axis=0, tiled=True),
     )
     samples, local, values_count = states.shape
     table_rows = cond_table.shape[0]
-    my_ids = lax.dynamic_slice_in_dim(intervals, lax.axis_index("fsdp") * samples, samples)
+    my_ids = lax.dynamic_slice_in_dim(intervals, lax.axis_index(SHARDS) * samples, samples)
     counts = jnp.sum(
         (intervals[:, None] == jnp.arange(NI, dtype=jnp.int32)[None]).astype(jnp.float32), 0
     )
@@ -356,7 +358,7 @@
         * counts[None],
         1,
     )
-    weight = 1.0 / (NI * local * lax.axis_size("seq") * values_count * id_counts)
+    weight = 1.0 / (NI * local * lax.axis_size(PATCHES) * values_count * id_counts)
     rows_iota = jnp.arange(table_rows, dtype=jnp.int32)
     id_select = (my_ids[:, None] == rows_iota[None]).astype(jnp.float32)
     state = states.astype(jnp.float32)
@@ -381,26 +383,26 @@
         grad_state, grads = backward_step(weights, kept, grad_state, active, select)
         totals = grads if totals is None else jax.tree.map(jnp.add, totals, grads)
     reduced = (
-        lax.psum_scatter(totals[0], "fsdp", scatter_dimension=1, tiled=True),
-        lax.psum_scatter(totals[1], "fsdp", scatter_dimension=1, tiled=True),
-        lax.psum_scatter(totals[2], "fsdp", scatter_dimension=1, tiled=True),
-        lax.psum_scatter(totals[3], "fsdp", scatter_dimension=1, tiled=True),
-        lax.psum_scatter(totals[4], "fsdp", scatter_dimension=1, tiled=True),
-        lax.psum_scatter(totals[5], "fsdp", scatter_dimension=2, tiled=True),
-        lax.psum_scatter(totals[6], "fsdp", scatter_dimension=1, tiled=True),
-        lax.psum_scatter(totals[7], "fsdp", scatter_dimension=1, tiled=True),
-        lax.psum_scatter(totals[8], "fsdp", scatter_dimension=0, tiled=True),
+        lax.psum_scatter(totals[0], SHARDS, scatter_dimension=1, tiled=True),
+        lax.psum_scatter(totals[1], SHARDS, scatter_dimension=1, tiled=True),
+        lax.psum_scatter(totals[2], SHARDS, scatter_dimension=1, tiled=True),
+        lax.psum_scatter(totals[3], SHARDS, scatter_dimension=1, tiled=True),
+        lax.psum_scatter(totals[4], SHARDS, scatter_dimension=1, tiled=True),
+        lax.psum_scatter(totals[5], SHARDS, scatter_dimension=2, tiled=True),
+        lax.psum_scatter(totals[6], SHARDS, scatter_dimension=1, tiled=True),
+        lax.psum_scatter(totals[7], SHARDS, scatter_dimension=1, tiled=True),
+        lax.psum_scatter(totals[8], SHARDS, scatter_dimension=0, tiled=True),
     )
     large = (
-        lax.psum_scatter(reduced[0], "seq", scatter_dimension=0, tiled=True),
-        lax.psum_scatter(reduced[1], "seq", scatter_dimension=0, tiled=True),
-        lax.psum_scatter(reduced[2], "seq", scatter_dimension=0, tiled=True),
-        lax.psum_scatter(reduced[3], "seq", scatter_dimension=0, tiled=True),
-        lax.psum_scatter(reduced[4], "seq", scatter_dimension=0, tiled=True),
-    )
-    small = lax.psum((reduced[5], reduced[6], reduced[8]), "seq")
+        lax.psum_scatter(reduced[0], PATCHES, scatter_dimension=0, tiled=True),
+        lax.psum_scatter(reduced[1], PATCHES, scatter_dimension=0, tiled=True),
+        lax.psum_scatter(reduced[2], PATCHES, scatter_dimension=0, tiled=True),
+        lax.psum_scatter(reduced[3], PATCHES, scatter_dimension=0, tiled=True),
+        lax.psum_scatter(reduced[4], PATCHES, scatter_dimension=0, tiled=True),
+    )
+    small = lax.psum((reduced[5], reduced[6], reduced[8]), PATCHES)
     grad_pos = reduced[7]
-    first_copy = (lax.axis_index("seq") == 0).astype(jnp.float32)
+    first_copy = (lax.axis_index(PATCHES) == 0).astype(jnp.float32)
     squares = jnp.sum(grad_pos * grad_pos)
     for item in large:
         squares = squares + jnp.sum(item * item)
@@ -408,7 +410,7 @@
     for item in small:
         small_squares = small_squares + jnp.sum(item * item)
     squares, loss_total = lax.psum(
-        (squares + first_copy * small_squares, loss_local), ("seq", "fsdp")
+        (squares + first_copy * small_squares, loss_local), (PATCHES, SHARDS)
     )
     grad_norm = jnp.sqrt(squares)
     clip = jnp.minimum(1.0, CLIP_LIMIT / (grad_norm + 1e-06))
@@ -424,19 +426,19 @@
             jnp.sum(moments[2] * moments[2]),
             jnp.sum(moments[3] * moments[3]),
         ),
-        ("seq", "fsdp"),
+        (PATCHES, SHARDS),
     )
     sizes = [jnp.sqrt(norms[which]) for which in range(4)]
     moment_sizes = jnp.stack(sizes) / CLIP_LIMIT
     scaled = [(moments[which] / (sizes[which] + 1e-07)).astype(jnp.bfloat16) for which in range(4)]
     columns = (
-        lax.all_gather(scaled[0], "seq", axis=0, tiled=True),
-        lax.all_gather(scaled[1], "seq", axis=0, tiled=True),
-        lax.all_gather(scaled[2], "seq", axis=0, tiled=True),
-        lax.all_gather(scaled[3], "seq", axis=0, tiled=True),
-    )
-    seq_index = lax.axis_index("seq")
-    seq_count = lax.axis_size("seq")
+        lax.all_gather(scaled[0], PATCHES, axis=0, tiled=True),
+        lax.all_gather(scaled[1], PATCHES, axis=0, tiled=True),
+        lax.all_gather(scaled[2], PATCHES, axis=0, tiled=True),
+        lax.all_gather(scaled[3], PATCHES, axis=0, tiled=True),
+    )
+    seq_index = lax.axis_index(PATCHES)
+    seq_count = lax.axis_size(PATCHES)
     owners = [seq_index == which % seq_count for which in range(4)]
     blocks = list(columns)
     for turn in range(NS_ITERS):
@@ -444,29 +446,29 @@
             lax.cond(owners[which], gram_part, zero_gram, blocks[which]) for which in range(4)
         ]
         grams = lax.psum(
-            (partial_value[0], partial_value[1], partial_value[2], partial_value[3]), "fsdp"
+            (partial_value[0], partial_value[1], partial_value[2], partial_value[3]), SHARDS
         )
         blocks = [
             lax.cond(owners[which], newton_step, keep_block, blocks[which], grams[which])
             for which in range(4)
         ]
-    blocks = [broadcast(blocks[which], "seq", which % seq_count) for which in range(4)]
+    blocks = [broadcast(blocks[which], PATCHES, which % seq_count) for which in range(4)]
     row_count = qkv_master.shape[0]
     fresh = []
     for which in range(4):
         my_rows = lax.dynamic_slice_in_dim(
             blocks[which], seq_index * row_count, row_count, 0
         ).astype(jnp.float32)
-        all_cols = masters[which].shape[1] * lax.axis_size("fsdp")
+        all_cols = masters[which].shape[1] * lax.axis_size(SHARDS)
         fresh.append(
             masters[which] * (1.0 - RATE_MUON * DECAY_MUON)
             - RATE_MUON * 0.2 * math.sqrt(all_cols) * my_rows
         )
     copies = (
-        lax.all_gather(fresh[0].astype(jnp.bfloat16), "seq", axis=0, tiled=True),
-        lax.all_gather(fresh[1].astype(jnp.bfloat16), "seq", axis=0, tiled=True),
-        lax.all_gather(fresh[2].astype(jnp.bfloat16), "seq", axis=0, tiled=True),
-        lax.all_gather(fresh[3].astype(jnp.bfloat16), "seq", axis=0, tiled=True),
+        lax.all_gather(fresh[0].astype(jnp.bfloat16), PATCHES, axis=0, tiled=True),
+        lax.all_gather(fresh[1].astype(jnp.bfloat16), PATCHES, axis=0, tiled=True),
+        lax.all_gather(fresh[2].astype(jnp.bfloat16), PATCHES, axis=0, tiled=True),
+        lax.all_gather(fresh[3].astype(jnp.bfloat16), PATCHES, axis=0, tiled=True),
     )
     ada_res = adam_update(ada_master, ada_first, ada_second, clip * large[4], RATE_ADAM)
     io_res = adam_update(io_proj, io_first, io_second, clip * small[0], RATE_ADAM)
@@ -517,95 +519,161 @@
     return -(-value // unit) * unit
 
 
+def member_peer(members, shift):
+    index = lax.axis_index(PATCHES)
+    return {PATCHES: index // members * members + lax.rem(lax.rem(index, members) + shift, members)}
+
+
+def group_peer(members, shift):
+    return {PATCHES: lax.rem(lax.axis_index(PATCHES) + shift * members, lax.axis_size(PATCHES))}
+
+
+def sibling_peer():
+    index = lax.axis_index(SHARDS)
+    return {SHARDS: index + 1 - 2 * lax.rem(index, 2)}
+
+
+def where(condition, action):
+    if condition is None:
+        action()
+    else:
+        pl.when(condition())(action)
+
+
 class Moves:
-    def __init__(self, name, ids):
+    def __init__(self, name, ids, vmem=None):
         self.name = name
         self.ids = ids
+        self.vmem = vmem
         self.operands = []
+        self.operand_specs = []
         self.outputs = []
+        self.output_specs = []
+        self.scratches = []
         self.moves = []
         self.locals = []
+        self.steps = []
         self.peers = {}
 
-    def operand(self, array):
+    def operand(self, array, space=pl.ANY):
         self.operands.append(array)
+        self.operand_specs.append(pl.BlockSpec(memory_space=space))
         return (0, len(self.operands) - 1)
 
-    def output(self, shape, dtype):
+    def output(self, shape, dtype, space=pl.ANY):
         self.outputs.append(jax.ShapeDtypeStruct(shape, dtype))
+        self.output_specs.append(pl.BlockSpec(memory_space=space))
         return (1, len(self.outputs) - 1)
+
+    def scratch(self, shape, dtype):
+        self.scratches.append(pltpu.VMEM(shape, dtype))
+        return (2, len(self.scratches) - 1)
 
     def keep(self, source, source_at, target, target_at):
         self.locals.append((source, source_at, target, target_at))
-
-    def move(self, peer_key, peer, source, source_at, target, target_at, after=()):
+        return len(self.locals) - 1
+
+    def move(
+        self, peer_key, peer, source, source_at, target, target_at, after=(), sends=None, takes=None, later=False
+    ):
+        number = len(self.moves)
         self.peers.setdefault(peer_key, peer)
-        self.moves.append((peer_key, source, source_at, target, target_at, after))
-        return len(self.moves) - 1
+        self.moves.append((peer_key, source, source_at, target, target_at, sends, takes, later or bool(after)))
+        for earlier in after:
+            self.steps.append((self.await_move, earlier))
+        if after:
+            self.steps.append((self.start_move, number))
+        return number
+
+    def wait_for(self, number):
+        self.steps.append((self.await_move, number))
+
+    def start(self, number):
+        self.steps.append((self.start_move, number))
+
+    def wait_local(self, number):
+        self.steps.append((self.await_local, number))
+
+    def task(self, action):
+        self.steps.append((self.do_task, action))
+
+    def await_move(self, number):
+        if number not in self.arrived:
+            self.arrived.add(number)
+            where(self.moves[number][6], self.remote[number].wait_recv)
+
+    def start_move(self, number):
+        where(self.moves[number][5], self.remote[number].start)
+
+    def await_local(self, number):
+        if number not in self.kept:
+            self.kept.add(number)
+            self.local[number].wait()
+
+    def do_task(self, action):
+        action(self.ref)
+
+    def ref(self, which):
+        return self.refs[which[0]][which[1]]
+
+    def view(self, which, index):
+        ref = self.ref(which)
+        return ref.at[index()] if index is not None else ref
 
     def kernel(self, *refs):
-        ins = refs[: len(self.operands)]
-        outs = refs[len(self.operands) : len(self.operands) + len(self.outputs)]
-        local_sem, send_sem, recv_sem = refs[len(self.operands) + len(self.outputs) :]
-
-        def view(which, index):
-            ref = (ins, outs)[which[0]][which[1]]
-            return ref.at[index()] if index is not None else ref
-
+        sizes = (len(self.operands), len(self.outputs), len(self.scratches))
+        self.refs = (refs[: sizes[0]], refs[sizes[0] : sizes[0] + sizes[1]], refs[sizes[0] + sizes[1] : sum(sizes)])
+        local_sem, send_sem, recv_sem = refs[sum(sizes) :]
+        self.arrived, self.kept = set(), set()
         devices = {key: peer() for key, peer in self.peers.items()}
         barrier = pltpu.get_barrier_semaphore()
         for device in devices.values():
             pl.semaphore_signal(barrier, inc=1, device_id=device, device_id_type=MESH)
         pl.semaphore_wait(barrier, len(devices))
-        remote = []
-        for number, (key, source, source_at, target, target_at, after) in enumerate(self.moves):
-            remote.append(
+        self.remote = []
+        for number, (key, source, source_at, target, target_at, _, _, later) in enumerate(self.moves):
+            self.remote.append(
                 pltpu.make_async_remote_copy(
-                    src_ref=view(source, source_at),
-                    dst_ref=view(target, target_at),
+                    src_ref=self.view(source, source_at),
+                    dst_ref=self.view(target, target_at),
                     send_sem=send_sem.at[number],
                     recv_sem=recv_sem.at[number],
                     device_id=devices[key],
                     device_id_type=MESH,
                 )
             )
-            if not after:
-                remote[number].start()
-        local = [
-            pltpu.make_async_copy(view(source, source_at), view(target, target_at), local_sem.at[number])
+            if not later:
+                self.start_move(number)
+        self.local = [
+            pltpu.make_async_copy(self.view(source, source_at), self.view(target, target_at), local_sem.at[number])
             for number, (source, source_at, target, target_at) in enumerate(self.locals)
         ]
-        for copy in local:
+        for copy in self.local:
             copy.start()
-        arrived = set()
-        for number, entry in enumerate(self.moves):
-            if entry[-1]:
-                for earlier in entry[-1]:
-                    if earlier not in arrived:
-                        remote[earlier].wait_recv()
-                        arrived.add(earlier)
-                remote[number].start()
-        for copy in local:
-            copy.wait()
-        for number, copy in enumerate(remote):
-            if number not in arrived:
-                copy.wait_recv()
-            copy.wait_send()
+        for action, number in self.steps:
+            action(number)
+        for number in range(len(self.locals)):
+            self.await_local(number)
+        for number, copy in enumerate(self.remote):
+            self.await_move(number)
+            where(self.moves[number][5], copy.wait_send)
 
     def run(self):
-        in_any = pl.BlockSpec(memory_space=pl.ANY)
         return pl.pallas_call(
             self.kernel,
             out_shape=self.outputs,
-            in_specs=[in_any] * len(self.operands),
-            out_specs=[in_any] * len(self.outputs),
+            in_specs=self.operand_specs,
+            out_specs=self.output_specs,
             scratch_shapes=[
+                *self.scratches,
                 pltpu.SemaphoreType.DMA((max(1, len(self.locals)),)),
                 pltpu.SemaphoreType.DMA((len(self.moves),)),
                 pltpu.SemaphoreType.DMA((len(self.moves),)),
             ],
             compiler_params=pltpu.CompilerParams(
-                collective_id=self.ids.setdefault(self.name, len(self.ids)), has_side_effects=True
+                collective_id=self.ids.setdefault(self.name, len(self.ids)),
+                has_side_effects=True,
+                vmem_limit_bytes=self.vmem,
             ),
             name=self.name,
         )(*self.operands)
@@ -648,6 +716,61 @@
             target,
             [(None, lambda sender: lead + (pl.ds(pl.multiple_of(sender * width, LANES), width),))],
         )
+
+    def gather_twice(self, arrays, members):
+        shards = lax.axis_size(SHARDS)
+        entries = []
+        for array in arrays:
+            source = self.operand(array)
+            target = self.output((shards,) + array.shape, array.dtype)
+            rows = array.shape[0] // members
+
+            def place(back_member, back_pair, rows=rows):
+                index = lax.rem(lax.rem(lax.axis_index(PATCHES), members) + members - back_member, members)
+                who = lax.rem(lax.axis_index(SHARDS) + shards - 2 * back_pair, shards)
+                return (who, pl.ds(pl.multiple_of(index * rows, rows), rows))
+
+            def mine(rows=rows):
+                index = lax.rem(lax.axis_index(PATCHES), members)
+                return (pl.ds(pl.multiple_of(index * rows, rows), rows),)
+
+            firsts = [
+                self.move(
+                    (SHARDS, 2 * pair),
+                    lambda pair=pair: {SHARDS: lax.rem(lax.axis_index(SHARDS) + 2 * pair, shards)},
+                    source,
+                    mine,
+                    target,
+                    functools.partial(place, 0, 0),
+                )
+                for pair in range(1, shards // 2)
+            ]
+            entries.append((source, target, place, firsts))
+        for source, target, _, _ in entries:
+            own = lambda: (lax.axis_index(SHARDS),)
+            self.move((SHARDS,), sibling_peer, source, None, target, own)
+            self.keep(source, None, target, own)
+        last = []
+        for _, target, place, firsts in entries:
+            for pair, first in enumerate(firsts, 1):
+                near = functools.partial(place, 0, pair)
+                for shift in range(1, members):
+                    number = self.move(
+                        (PATCHES, members, shift),
+                        functools.partial(member_peer, members, shift),
+                        target,
+                        near,
+                        target,
+                        near,
+                        (first,),
+                    )
+                    last.append((target, functools.partial(place, shift, pair), number))
+                self.move((SHARDS,), sibling_peer, target, near, target, near, (first,))
+        self.to_sibling(last)
+
+    def to_sibling(self, waiting):
+        for target, place, number in waiting:
+            self.move((SHARDS,), sibling_peer, target, place, target, place, (number,))
 
     def exchange(self, axis, array):
         target = self.output(array.shape, array.dtype)
@@ -713,15 +836,15 @@
 
 def total_kernel(x_ref, o_ref, near, far, near_send, near_recv, far_send, far_recv):
     near_count, far_count = near.shape[0], far.shape[0]
-    near_me, far_me = lax.axis_index("fsdp"), lax.axis_index("seq")
+    near_me, far_me = lax.axis_index(SHARDS), lax.axis_index(PATCHES)
     barrier = pltpu.get_barrier_semaphore()
     for shift in range(1, near_count):
         pl.semaphore_signal(
-            barrier, inc=1, device_id={"fsdp": lax.rem(near_me + shift, near_count)}, device_id_type=MESH
+            barrier, inc=1, device_id={SHARDS: lax.rem(near_me + shift, near_count)}, device_id_type=MESH
         )
     for shift in range(1, far_count):
         pl.semaphore_signal(
-            barrier, inc=1, device_id={"seq": lax.rem(far_me + shift, far_count)}, device_id_type=MESH
+            barrier, inc=1, device_id={PATCHES: lax.rem(far_me + shift, far_count)}, device_id_type=MESH
         )
     pl.semaphore_wait(barrier, near_count + far_count - 2)
 
@@ -743,12 +866,12 @@
         return jnp.sum(buffer[...], 0)
 
     near[near_me] = x_ref[...]
-    far[far_me] = spread("fsdp", near_me, near_count, near, near_send, near_recv)
-    o_ref[...] = spread("seq", far_me, far_count, far, far_send, far_recv)
+    far[far_me] = spread(SHARDS, near_me, near_count, near, near_send, near_recv)
+    o_ref[...] = spread(PATCHES, far_me, far_count, far, far_send, far_recv)
 
 
 def total_of(ids, values):
-    near_count, far_count = lax.axis_size("fsdp"), lax.axis_size("seq")
+    near_count, far_count = lax.axis_size(SHARDS), lax.axis_size(PATCHES)
     in_vmem = pl.BlockSpec(memory_space=pltpu.VMEM)
     return pl.pallas_call(
         total_kernel,
@@ -777,6 +900,8 @@
 
 
 QUERY_BLOCK = 256
+CHAIN_CHUNKS = 4
+GRAM_ROWS = 256
 
 
 def attention_kernel(heads, qkv_ref, mixed_ref):
@@ -857,26 +982,106 @@
     )(qkv, grads)
 
 
-def product_high(left, right):
-    left_high, right_high = left.astype(LOW), right.astype(LOW)
-    left_rest = (left - left_high.astype(jnp.float32)).astype(LOW)
-    right_rest = (right - right_high.astype(jnp.float32)).astype(LOW)
-    return product(left_high, right_high) + (product(left_high, right_rest) + product(left_rest, right_high))
-
-
-def product_low(left, right):
-    return product(left.astype(LOW), right.astype(LOW))
-
-
-def newton_schulz(block, gram):
-    for turn in range(NS_ITERS):
-        times = product_high if 2 <= turn < NS_ITERS - 1 else product_low
-        poly = NS_B * gram + NS_C * times(gram, gram)
-        if turn < NS_ITERS - 1:
-            once = times(poly, gram)
-            gram = NS_A * NS_A * gram + 2.0 * NS_A * once + times(poly, once)
-        block = (NS_A * block.astype(jnp.float32) + product(poly.astype(LOW), block)).astype(LOW)
-    return block
+def newton_kernel(gram_ref, block_ref, out_ref, gram, poly, once, gram_low, poly_low, once_low, block):
+    size = gram_ref.shape[0]
+    tiles = size // GRAM_ROWS
+    eye = jnp.equal(
+        lax.broadcasted_iota(jnp.int32, (GRAM_ROWS, GRAM_ROWS), 0),
+        lax.broadcasted_iota(jnp.int32, (GRAM_ROWS, GRAM_ROWS), 1),
+    ).astype(jnp.float32)
+
+    def rows_at(tile):
+        return pl.ds(pl.multiple_of(tile * GRAM_ROWS, GRAM_ROWS), GRAM_ROWS)
+
+    def split(full, low):
+        def add(tile, total):
+            return total + jnp.sum(full[rows_at(tile), rows_at(tile)] * eye)
+
+        mean = lax.fori_loop(0, tiles, add, jnp.float32(0.0)) / size
+
+        @pl.loop(0, tiles)
+        def _(tile):
+            rows = rows_at(tile)
+            low[rows, :] = full[rows, :].astype(LOW)
+            low[rows, rows] = (full[rows, rows] - mean * eye).astype(LOW)
+
+        return mean
+
+    def multiply(target, left, left_mean, left_low, right, right_mean, right_low, finish):
+        @pl.loop(0, tiles)
+        def _(tile):
+            rows = rows_at(tile)
+            value = contract(left_low[rows, :], right_low[...], 1, 0)
+            value = value + left_mean * right[rows, :] + right_mean * left[rows, :]
+            target[rows, :] = finish(value, rows)
+
+    def mend(target, amount):
+        @pl.loop(0, tiles)
+        def _(tile):
+            rows = rows_at(tile)
+            target[rows, rows] -= amount * eye
+
+    def advance(last):
+        gram_mean = split(gram, gram_low)
+        multiply(
+            poly,
+            gram,
+            gram_mean,
+            gram_low,
+            gram,
+            gram_mean,
+            gram_low,
+            lambda value, rows: NS_B * gram[rows, :] + NS_C * value,
+        )
+        mend(poly, NS_C * gram_mean * gram_mean)
+        poly_mean = split(poly, poly_low)
+        out_ref[...] = block[...]
+
+        @pl.loop(0, tiles)
+        def _(tile):
+            rows = rows_at(tile)
+            value = contract(poly_low[rows, :], out_ref[...], 1, 0)
+            block[rows, :] = (value + (NS_A + poly_mean) * out_ref[rows, :].astype(jnp.float32)).astype(LOW)
+
+        if not last:
+            multiply(once, poly, poly_mean, poly_low, gram, gram_mean, gram_low, lambda value, rows: value)
+            mend(once, poly_mean * gram_mean)
+            once_mean = split(once, once_low)
+            multiply(
+                gram,
+                poly,
+                poly_mean,
+                poly_low,
+                once,
+                once_mean,
+                once_low,
+                lambda value, rows: NS_A * NS_A * gram[rows, :] + 2.0 * NS_A * once[rows, :] + value,
+            )
+            mend(gram, poly_mean * once_mean)
+
+    gram[...] = gram_ref[...]
+    block[...] = block_ref[...]
+
+    @pl.loop(0, NS_ITERS - 1)
+    def _(turn):
+        advance(False)
+
+    advance(True)
+    out_ref[...] = block[...]
+
+
+def newton_schulz(gram, block):
+    in_vmem = pl.BlockSpec(memory_space=pltpu.VMEM)
+    full, low = pltpu.VMEM(gram.shape, jnp.float32), pltpu.VMEM(gram.shape, LOW)
+    return pl.pallas_call(
+        newton_kernel,
+        out_shape=jax.ShapeDtypeStruct(block.shape, block.dtype),
+        in_specs=[in_vmem, in_vmem],
+        out_specs=in_vmem,
+        scratch_shapes=[full, full, full, low, low, low, pltpu.VMEM(block.shape, LOW)],
+        compiler_params=pltpu.CompilerParams(vmem_limit_bytes=48 * 2**20),
+        name="newton",
+    )(gram, block)
 
 
 def fast_body(
@@ -915,8 +1120,8 @@
 ):
     ids = {}
     f32 = jnp.float32
-    seq_count, shards = lax.axis_size("seq"), lax.axis_size("fsdp")
-    seq_index, shard = lax.axis_index("seq"), lax.axis_index("fsdp")
+    seq_count, shards = lax.axis_size(PATCHES), lax.axis_size(SHARDS)
+    seq_index, shard = lax.axis_index(PATCHES), lax.axis_index(SHARDS)
     members = seq_count // MATRICES
     group, member = seq_index // members, lax.rem(seq_index, members)
     samples, local, values_count = states.shape
@@ -925,19 +1130,12 @@
     ada_cols = ada_copy.shape[1]
     padded = round_up(values_count, LANES)
 
-    moves = Moves("embeddings", ids)
-    moves.gather("fsdp", jnp.pad(io_proj.astype(LOW), ((0, 0), (0, padded - values_count), (0, 0))))
-    moves.gather("fsdp", cond_table)
-    moves.gather("fsdp", pos_table.astype(LOW))
-    moves.gather("fsdp", biases[None])
-    io_parts, table_parts, pos_parts, bias_parts = moves.run()
-    io_all = jnp.moveaxis(io_parts, 0, 2).reshape(2, padded, width)
+    moves = Moves("tables", ids)
+    moves.gather(SHARDS, cond_table)
+    moves.gather(SHARDS, biases[None])
+    table_parts, bias_parts = moves.run()
     table = jnp.moveaxis(table_parts, 0, 1).reshape(table_rows, width).astype(LOW).astype(f32)
-    pos = jnp.moveaxis(pos_parts, 0, 1).reshape(local, width).astype(f32)
     bias = bias_parts.reshape(-1).astype(LOW).astype(f32)
-    w_qkv = lax.all_gather(qkv_copy, "fsdp", axis=1, tiled=True)
-    w_out = lax.all_gather(out_copy, "fsdp", axis=1, tiled=True)
-
     rows_iota = jnp.arange(table_rows, dtype=jnp.int32)
     id_rows = (intervals[:, None] == rows_iota[None]).astype(f32)
     step_rows = (rows_iota[None] == NI + jnp.arange(ROLL, dtype=jnp.int32)[:, None]).astype(f32)
@@ -945,11 +1143,20 @@
     cond_vec = jnp.sum(select[:, :, None] * table[None], 1)
     silu_low = jax.nn.silu(cond_vec).astype(LOW)
     modul_shard = product(silu_low, ada_copy) + lax.dynamic_slice_in_dim(bias, shard * ada_cols, ada_cols)[None]
-    moves = Moves("modulation", ids)
-    moves.exchange("fsdp", modul_shard.reshape(shards, ROLL, ada_cols))
-    modul = jnp.moveaxis(moves.run()[0], 0, 1).reshape(ROLL, 6 * width)
-
-    momenta = (qkv_moment, out_moment, up_moment, down_moment)
+
+    moves = Moves("weights", ids)
+    moves.exchange(SHARDS, modul_shard.reshape(shards, ROLL, ada_cols))
+    moves.gather_columns(SHARDS, pos_table.astype(LOW))
+    io_low = jnp.pad(io_proj.astype(LOW), ((0, 0), (0, padded - values_count), (0, 0)))
+    moves.gather_twice((io_low.reshape(2 * padded, -1), out_copy, qkv_copy), members)
+    modul, pos, *parts = moves.run()
+    io_all, w_out, w_qkv = [jnp.moveaxis(item, 0, 1).reshape(item.shape[1], -1) for item in parts]
+    io_all = io_all.reshape(2, padded, width)
+    modul = jnp.moveaxis(modul, 0, 1).reshape(ROLL, 6 * width)
+    pos = pos.astype(f32)
+
+    masters = (qkv_master, up_master, down_master, out_master)
+    momenta = (qkv_moment, up_moment, down_moment, out_moment)
     group_cols = [item.shape[1] // members for item in momenta]
     most_cols = max(group_cols)
 
@@ -963,6 +1170,7 @@
             for part in range(members)
         ]
     )
+    half_rows = moment_parts.shape[1] // 2
 
     counts = jnp.sum((intervals[:, None] == jnp.arange(NI, dtype=jnp.int32)[None]).astype(f32), 0)
     my_id = lax.dynamic_slice_in_dim(intervals, shard, 1)
@@ -973,7 +1181,16 @@
     state = jnp.pad(states[0].astype(f32), value_pad)
     embed_bias = bias[6 * width :]
     kept = []
-    moment_group = None
+    gathered = {}
+    moment_halves = []
+
+    def run_with(moves, names):
+        results = moves.run()
+        first = len(results) - len(names)
+        for name, result in zip(names, results[first:]):
+            gathered.setdefault(name, {})[step] = result
+        return results[:first]
+
     for step in range(ROLL):
         shift1, scale1, gate1, shift2, scale2, gate2 = jnp.split(modul[step][None], 6, -1)
         state_low = state.astype(LOW)
@@ -981,30 +1198,36 @@
         normed_one, inverse_one = layer_norm(embedded)
         normed_a = (normed_one * (1.0 + scale1) + shift1).astype(LOW)
         qkv_rows = product(normed_a, w_qkv).astype(LOW)
-        moves = Moves("qkv_heads", ids)
-        moves.rows_to_heads("seq", qkv_rows, 3)
-        qkv = moves.run()[0]
+        moves = Moves(f"heads{step}", ids)
+        moves.rows_to_heads(PATCHES, qkv_rows, 3)
+        moves.gather(SHARDS, normed_a)
+        if step:
+            moves.gather(SHARDS, kept[-1][5])
+            qkv, gathered_a, gathered_mixed = moves.run()
+            gathered["mixed"] = {step - 1: gathered_mixed}
+        else:
+            qkv, gathered_a = moves.run()
+        gathered.setdefault("a", {})[step] = gathered_a
         mixed_heads = attention(qkv)
         moves = Moves("mixed_rows", ids)
-        moves.heads_to_rows("seq", mixed_heads[None])
-        mixed = moves.run()[0]
+        moves.heads_to_rows(PATCHES, mixed_heads[None])
+        moves.gather(SHARDS, state_low)
+        (mixed,) = run_with(moves, ["state"])
         attended = product(mixed, w_out)
         after_attn = embedded + gate1 * attended
         normed_two, inverse_two = layer_norm(after_attn)
         normed_b = (normed_two * (1.0 + scale2) + shift2).astype(LOW)
-        moves = Moves("tokens" if step else "tokens_momenta", ids)
-        moves.gather("fsdp", normed_b)
-        if step == 0:
-            moves.exchange("seq", moment_parts)
-            tokens_b, moment_group = moves.run()
-        else:
-            tokens_b = moves.run()[0]
+        moves = Moves("tokens_moment", ids)
+        moves.gather(SHARDS, normed_b)
+        moves.exchange(PATCHES, moment_parts[:, step * half_rows : (step + 1) * half_rows])
+        tokens_b, moment_half = moves.run()
+        moment_halves.append(moment_half)
         tokens_b = tokens_b.reshape(shards * local, width)
         upward = product(tokens_b, up_copy)
         hidden = jax.nn.gelu(upward).astype(LOW)
         down_part = contract(hidden, down_copy, 1, 1).astype(LOW).reshape(shards, local, width)
         moves = Moves("token_sums", ids)
-        moves.exchange("fsdp", down_part)
+        moves.exchange(SHARDS, down_part)
         downward = jnp.sum(moves.run()[0].astype(f32), 0)
         after_mlp = after_attn + gate2 * downward
         normed_three, inverse_three = layer_norm(after_mlp)
@@ -1038,6 +1261,20 @@
     grad_state = 2.0 * weight * lat[:, None] * diff
 
     back = [None] * ROLL
+    mlp_back = []
+
+    def patch_sum(item, cols):
+        mine = lax.dynamic_slice_in_dim(item, member * cols, cols, 1)
+        low = item.astype(LOW)
+        for shift in range(1, members):
+            pairs = [
+                (index, index // members * members + (index + shift) % members) for index in range(seq_count)
+            ]
+            to_member = lax.rem(member + shift, members)
+            outgoing = lax.dynamic_slice_in_dim(low, to_member * cols, cols, 1)
+            mine = mine + lax.ppermute(outgoing, PATCHES, pairs).astype(f32)
+        return mine
+
     for step in reversed(range(ROLL)):
         (
             state_low,
@@ -1062,13 +1299,20 @@
         grad_mlp = norm_back(product(delta_grad, io_all[1]), normed_three, inverse_three)
         grad_gate2 = jnp.sum(grad_mlp * downward, 0)
         moves = Moves("tokens", ids)
-        moves.gather("fsdp", (gate2 * grad_mlp).astype(LOW))
+        moves.gather(SHARDS, (gate2 * grad_mlp).astype(LOW))
         tokens_down = moves.run()[0].reshape(shards * local, width)
         grad_hidden = product(tokens_down, down_copy)
         up_grad = jax.vjp(jax.nn.gelu, upward)[1](grad_hidden)[0].astype(LOW)
+        mlp_back.append((tokens_b, up_grad, tokens_down, hidden))
+        if step == 0:
+            all_b, all_up, all_down, all_hidden = [jnp.concatenate(items, 0) for items in zip(*mlp_back)]
+            mlp_sums = [
+                patch_sum(rows_product(left, right), cols)
+                for left, right, cols in ((all_b, all_up, group_cols[1]), (all_down, all_hidden, group_cols[2]))
+            ]
         up_part = contract(up_grad, up_copy, 1, 1).astype(LOW).reshape(shards, local, width)
         moves = Moves("token_sums", ids)
-        moves.exchange("fsdp", up_part)
+        moves.exchange(SHARDS, up_part)
         grad_normed_b = jnp.sum(moves.run()[0].astype(f32), 0)
         grad_scale2 = jnp.sum(grad_normed_b * normed_two, 0)
         grad_shift2 = jnp.sum(grad_normed_b, 0)
@@ -1076,12 +1320,27 @@
         grad_gate1 = jnp.sum(grad_attn * attended, 0)
         attn_grad = (gate1 * grad_attn).astype(LOW)
         mixed_grad = contract(attn_grad, w_out, 1, 1).astype(LOW)
-        moves = Moves("mixed_heads", ids)
-        moves.rows_to_heads("seq", mixed_grad, 1)
-        qkv_grad_heads = attention_back(qkv, moves.run()[0][0])
-        moves = Moves("qkv_rows", ids)
-        moves.heads_to_rows("seq", qkv_grad_heads)
-        qkv_grad = moves.run()[0]
+        moves = Moves(f"mixed_heads{step}", ids)
+        moves.rows_to_heads(PATCHES, mixed_grad, 1)
+        if step < ROLL - 1:
+            moves.exchange_columns(SHARDS, back[step + 1][0])
+            moves.exchange_columns(SHARDS, back[step + 1][1])
+            mixed_grad_heads, gathered_qkv, gathered_embed = moves.run()
+            gathered.setdefault("qkv", {})[step + 1] = gathered_qkv
+            gathered.setdefault("embed", {})[step + 1] = gathered_embed
+        else:
+            (mixed_grad_heads,) = moves.run()
+        qkv_grad_heads = attention_back(qkv, mixed_grad_heads[0])
+        moves = Moves(f"rows{step}", ids)
+        moves.heads_to_rows(PATCHES, qkv_grad_heads)
+        moves.exchange_columns(SHARDS, attn_grad)
+        moves.exchange_columns(SHARDS, normed_c)
+        moves.gather(SHARDS, delta_grad)
+        names = ["attn", "c", "delta"]
+        if step == ROLL - 1:
+            moves.gather(SHARDS, mixed)
+            names.append("mixed")
+        (qkv_grad,) = run_with(moves, names)
         grad_normed_a = contract(qkv_grad, w_qkv, 1, 1)
         grad_scale1 = jnp.sum(grad_normed_a * normed_one, 0)
         grad_shift1 = jnp.sum(grad_normed_a, 0)
@@ -1089,119 +1348,154 @@
         embed_grad = grad_embedded.astype(LOW)
         grad_state = grad_state + contract(embed_grad, io_all[0], 1, 1)
         grad_modul = jnp.concatenate([grad_shift1, grad_scale1, grad_gate1, grad_shift2, grad_scale2, grad_gate2])
-        back[step] = (
-            normed_a,
-            mixed,
-            state_low,
-            delta_grad,
-            qkv_grad,
-            attn_grad,
-            embed_grad,
-            normed_c,
-            grad_modul,
-            jnp.sum(grad_embedded, 0),
-            tokens_b,
-            up_grad,
-            tokens_down,
-            hidden,
-        )
-
-    (
-        all_a,
-        all_mixed,
-        all_state,
-        all_delta,
-        all_qkv,
-        all_attn,
-        all_embed,
-        all_c,
-        grad_modul,
-        grad_bias_embed,
-        all_b,
-        all_up,
-        all_down,
-        all_hidden,
-    ) = [jnp.concatenate([item if item.ndim == 2 else item[None] for item in items], 0) for items in zip(*back)]
-    modul_parts = jnp.moveaxis(grad_modul.reshape(ROLL, shards, ada_cols), 1, 0)
-    embed_parts = jnp.sum(grad_bias_embed, 0).reshape(shards, 1, -1)
+        back[step] = (qkv_grad, embed_grad, grad_modul, jnp.sum(grad_embedded, 0))
+
+    qkv_grad, embed_grad, _, _ = back[0]
+    mlp_low = [item.astype(LOW) for item in mlp_sums]
+    modul_parts = jnp.stack([item[2].reshape(shards, ada_cols) for item in back], 1)
+    embed_parts = sum(item[3] for item in back).reshape(shards, 1, -1)
     vectors = jnp.concatenate(
         [modul_parts, jnp.pad(embed_parts, ((0, 0), (0, 0), (0, ada_cols - embed_parts.shape[-1])))], 1
     )
+
+    def to_group(moves, item, which, start, size):
+        source = moves.operand(item)
+        target = moves.output((MATRICES - 1, size, item.shape[1]), LOW)
+        for shift in range(1, MATRICES):
+            moves.move(
+                (PATCHES, seq_count, shift),
+                functools.partial(group_peer, members, shift),
+                source,
+                lambda: (pl.ds(start, size),),
+                target,
+                lambda shift=shift: (shift - 1,),
+                sends=lambda shift=shift: lax.axis_index(PATCHES) // members == (which - shift) % MATRICES,
+                takes=lambda: lax.axis_index(PATCHES) // members == which,
+            )
+
+    block_rows = qkv_copy.shape[0]
+    early = (1, 2)
+    first_rows = block_rows * 7 // 16
     moves = Moves("samples", ids)
-    for array in (all_a, all_mixed, all_state, all_delta):
-        moves.gather("fsdp", array)
-    for array in (all_qkv, all_attn, all_embed, all_c):
-        moves.exchange_columns("fsdp", array)
-    moves.exchange("fsdp", vectors)
-    all_a, all_mixed, all_state, all_delta, all_qkv, all_attn, all_embed, all_c, vectors = moves.run()
-    grad_pos = jnp.sum(all_embed.reshape(shards * ROLL, local, -1).astype(f32), 0)
-    grads_here = (
-        rows_product(all_a, all_qkv),
-        rows_product(all_mixed, all_attn),
-        rows_product(all_b, all_up),
-        rows_product(all_down, all_hidden),
-    )
-    io_here = jnp.stack([rows_product(all_state, all_embed), rows_product(all_delta, all_c)])
+    moves.exchange_columns(SHARDS, qkv_grad)
+    moves.exchange_columns(SHARDS, embed_grad)
+    moves.exchange(SHARDS, vectors)
+    for item, which in zip(mlp_low, early):
+        to_group(moves, item, which, 0, first_rows)
+    gathered["qkv"][0], gathered["embed"][0], vectors, *mlp_first = moves.run()
+    grad_pos = sum(jnp.sum(item.astype(f32), 0) for item in gathered["embed"].values())
+
+    def from_all(left, right):
+        both = [
+            jnp.concatenate([gathered[name][step].reshape(shards * local, -1) for step in range(ROLL)], 0)
+            for name in (left, right)
+        ]
+        return rows_product(*both)
+
+    io_here = jnp.stack([from_all("state", "embed"), from_all("delta", "c")])
     io_cols = io_here.shape[-1]
-
-    def member_peer(shift):
-        seq_me = lax.axis_index("seq")
-        return {"seq": seq_me // members * members + lax.rem(lax.rem(seq_me, members) + shift, members)}
+    grads_here = [from_all("a", "qkv"), from_all("mixed", "attn")]
+    late = (0, MATRICES - 1)
 
     moves = Moves("member_sums", ids)
-    halves = []
-    for item, cols in zip(grads_here, group_cols):
+    for item, which in zip(grads_here, late):
+        cols = group_cols[which]
         source = moves.operand(item.astype(LOW))
         target = moves.output((members - 1, item.shape[0], cols), LOW)
         for shift in range(1, members):
+
+            def source_at(shift=shift, cols=cols):
+                to_member = lax.rem(lax.rem(lax.axis_index(PATCHES), members) + shift, members)
+                return (slice(None), pl.ds(pl.multiple_of(to_member * cols, LANES), cols))
+
             moves.move(
-                ("member", shift),
-                functools.partial(member_peer, shift),
+                (PATCHES, members, shift),
+                functools.partial(member_peer, members, shift),
                 source,
-                lambda shift=shift, cols=cols: (
-                    slice(None),
-                    pl.ds(
-                        pl.multiple_of(
-                            lax.rem(lax.rem(lax.axis_index("seq"), members) + shift, members) * cols, LANES
-                        ),
-                        cols,
-                    ),
-                ),
+                source_at,
                 target,
                 lambda shift=shift: (shift - 1,),
             )
-    moves.gather("seq", vectors.reshape(-1, ada_cols))
-    moves.exchange("seq", io_here.reshape(seq_count, -1, io_cols).astype(LOW))
-    *halves, vectors, io_parts = moves.run()
-    vectors = jnp.sum(vectors, 0).reshape(shards, ROLL + 1, ada_cols)
+    modul_here, embed_here = vectors[:, :ROLL].reshape(-1), jnp.sum(vectors[:, ROLL, : width // shards], 0)
+    flat = jnp.concatenate([modul_here, embed_here]).astype(LOW)
+    flat_rows = round_up(flat.size, 16 * LANES) // LANES
+    moves.gather(PATCHES, jnp.pad(flat, (0, flat_rows * LANES - flat.size)).reshape(flat_rows, LANES))
+    moves.exchange(PATCHES, io_here.reshape(seq_count, -1, io_cols).astype(LOW))
+    for item, which in zip(mlp_low, early):
+        to_group(moves, item, which, first_rows, block_rows - first_rows)
+    *halves, vectors, io_parts, up_rest, down_rest = moves.run()
+    mlp_sums = [
+        mine + jnp.concatenate([jnp.sum(part.astype(f32), 0) for part in parts], 0)
+        for mine, *parts in zip(mlp_sums, mlp_first, (up_rest, down_rest))
+    ]
+    vectors = jnp.sum(vectors.astype(f32), 0).reshape(-1)
     io_slice = jnp.sum(io_parts.astype(f32), 0)
-    member_sums = [
-        lax.dynamic_slice_in_dim(item, member * cols, cols, 1) + jnp.sum(half.astype(f32), 0)
-        for item, half, cols in zip(grads_here, halves, group_cols)
+    late_sums = [
+        lax.dynamic_slice_in_dim(item, member * group_cols[which], group_cols[which], 1)
+        + jnp.sum(half.astype(f32), 0)
+        for item, half, which in zip(grads_here, halves, late)
     ]
-    modul_all = vectors[:, :ROLL].reshape(-1, ada_cols)
-    bias_part = jnp.concatenate([jnp.sum(modul_all, 0), jnp.sum(vectors[:, ROLL, : width // shards], 0)])
+    modul_all = vectors[: modul_here.size].reshape(-1, ada_cols)
+    bias_part = jnp.concatenate([jnp.sum(modul_all, 0), vectors[modul_here.size : flat.size]])
     silu_part = lax.dot_general(
         modul_all, ada_copy.astype(f32), (((1,), (1,)), ((), ())), precision=HIGHEST_PRECISION
     )
 
     moves = Moves("group_sums", ids)
-    source = moves.operand(jnp.stack([widen(item.astype(LOW)) for item in member_sums]))
-    target = moves.output((MATRICES,) + (member_sums[0].shape[0], most_cols), LOW)
-    for shift in range(1, MATRICES):
-        moves.move(
-            ("group", shift),
-            lambda shift=shift: {"seq": lax.rem(lax.axis_index("seq") + shift * members, seq_count)},
-            source,
-            lambda shift=shift: (lax.rem(lax.axis_index("seq") // members + shift, MATRICES),),
-            target,
-            lambda: (lax.axis_index("seq") // members,),
-        )
-    moves.keep(source, lambda: (lax.axis_index("seq") // members,), target, lambda: (lax.axis_index("seq") // members,))
-    moves.gather("fsdp", silu_part)
-    moves.gather("fsdp", bias_part[None])
-    grad_parts, silu_parts, bias_parts = moves.run()
-    grad_group = jnp.sum(grad_parts.astype(f32), 0)
+    moves.vmem = 32 * 2**20
+    chains = []
+    for item, which in zip(late_sums, late):
+        away = -1 if which else 1
+
+        def has_source(which=which):
+            return lax.axis_index(PATCHES) // members != (0 if which else MATRICES - 1)
+
+        def is_source(which=which):
+            return lax.axis_index(PATCHES) // members != which
+
+        mine = moves.operand(item, pltpu.VMEM)
+        total = moves.output(item.shape, f32, pltpu.VMEM)
+        arriving, leaving = moves.scratch(item.shape, LOW), moves.scratch(item.shape, LOW)
+        chains.append((mine, total, arriving, leaving, away, has_source, is_source))
+    chunk = block_rows // CHAIN_CHUNKS
+    for part in range(CHAIN_CHUNKS):
+        for mine, total, arriving, leaving, away, has_source, is_source in chains:
+            place = (pl.ds(part * chunk, chunk),)
+            number = moves.move(
+                (PATCHES, seq_count, away),
+                functools.partial(group_peer, members, MATRICES - away),
+                leaving,
+                lambda place=place: place,
+                arriving,
+                lambda place=place: place,
+                sends=is_source,
+                takes=has_source,
+                later=True,
+            )
+
+            def add(ref, mine=mine, total=total, arriving=arriving, leaving=leaving, has_source=has_source, place=place):
+                def with_arriving():
+                    ref(total)[place] = ref(mine)[place] + ref(arriving)[place].astype(f32)
+
+                def alone():
+                    ref(total)[place] = ref(mine)[place]
+
+                pl.when(has_source())(with_arriving)
+                pl.when(jnp.logical_not(has_source()))(alone)
+                ref(leaving)[place] = ref(total)[place].astype(LOW)
+
+            moves.wait_for(number)
+            moves.task(add)
+            moves.start(number)
+    moves.gather(SHARDS, silu_part)
+    moves.gather(SHARDS, bias_part[None])
+    *late_sums, silu_parts, bias_parts = moves.run()
+    late_sums = [widen(item) for item in late_sums]
+    grad_group = jnp.where(
+        group == late[0],
+        late_sums[0],
+        jnp.where(group == late[1], late_sums[1], widen(jnp.where(group == early[0], *mlp_sums))),
+    )
     grad_silu = jnp.sum(silu_parts, 0)
     grad_cond = jax.vjp(jax.nn.silu, cond_vec)[1](grad_silu)[0]
     grad_table_all = lax.dot_general(select, grad_cond, (((0,), (0,)), ((), ())), precision=HIGHEST_PRECISION)
@@ -1214,7 +1508,21 @@
         silu_rows.astype(f32), modul_all, (((0,), (0,)), ((), ())), precision=HIGHEST_PRECISION
     )
 
-    moment_group = moment_group.reshape(-1, most_cols).astype(f32)
+    io_rows = io_slice.size // most_cols
+    outgoing = jnp.concatenate(
+        [
+            grad_group.astype(LOW).reshape(MATRICES, members, -1, most_cols),
+            jnp.broadcast_to(io_slice.astype(LOW).reshape(1, 1, -1, most_cols), (MATRICES, members, io_rows, most_cols)),
+        ],
+        2,
+    )
+    by_member = [lax.dynamic_index_in_dim(outgoing, member, 1, False)]
+    for shift in range(1, members):
+        part = lax.dynamic_index_in_dim(outgoing, lax.rem(member + shift, members), 1, False)
+        routes = [(index, index // members * members + (index + shift) % members) for index in range(seq_count)]
+        by_member.append(lax.ppermute(part, PATCHES, routes))
+
+    moment_group = jnp.concatenate(moment_halves, 1).reshape(-1, most_cols).astype(f32)
     grad_squares = jnp.sum(grad_group * grad_group)
     squares = (
         grad_squares
@@ -1229,6 +1537,15 @@
     entries = entries + jnp.where(lane == place, jnp.sum(moment_group * moment_group), 0.0)
     entries = entries + jnp.where(lane == place + 1, jnp.sum(moment_group * grad_group), 0.0)
     entries = entries + jnp.where(lane == place + 2, grad_squares, 0.0)
+    entries, by_member = lax.optimization_barrier((entries, by_member))
+    order = lax.rem(member + members - jnp.arange(members, dtype=jnp.int32), members)
+    by_member = jnp.take(jnp.stack(by_member), order, axis=0)
+    by_group = [lax.dynamic_index_in_dim(by_member, group, 1, False)]
+    for shift in range(1, MATRICES):
+        part = lax.dynamic_index_in_dim(by_member, lax.rem(group + shift, MATRICES), 1, False)
+        routes = [(index, (index + shift * members) % seq_count) for index in range(seq_count)]
+        by_group.append(lax.ppermute(part, PATCHES, routes))
+
     sums = total_of(ids, jnp.broadcast_to(entries[None], (8, LANES)))[0]
     grad_norm = jnp.sqrt(sums[0])
     loss_total = sums[1]
@@ -1236,45 +1553,122 @@
     terms = sums[2 : 2 + 3 * MATRICES].reshape(MATRICES, 3)
     size_squares = MOMENTUM * MOMENTUM * terms[:, 0] + 2.0 * MOMENTUM * clip * terms[:, 1] + clip * clip * terms[:, 2]
     sizes = jnp.sqrt(jnp.maximum(size_squares, 0.0))
-    moment_sizes = sizes / CLIP_LIMIT
+    moment_sizes = sizes[jnp.array([0, 3, 1, 2])] / CLIP_LIMIT
     my_size = lax.dynamic_slice_in_dim(sizes, group, 1)[0]
     block = ((MOMENTUM * moment_group + clip * grad_group) / (my_size + 1e-07)).astype(LOW)
 
-    moves = Moves("columns", ids)
+    moves = Moves("columns", ids, 40 * 2**20)
     source = moves.operand(block)
-    block_rows = block.shape[0]
-    peers = members * shards
-    target = moves.output((block_rows, peers * most_cols), LOW)
-
-    def slot(back_member, back_pair):
-        who_member = lax.rem(lax.rem(lax.axis_index("seq"), members) + members - back_member, members)
-        who_shard = lax.rem(lax.axis_index("fsdp") + shards - 2 * back_pair, shards)
-        start = (who_member * shards + who_shard) * most_cols
-        return (slice(None), pl.ds(pl.multiple_of(start, LANES), most_cols))
-
-    def sibling():
-        index = lax.axis_index("fsdp")
-        return {"fsdp": index + 1 - 2 * lax.rem(index, 2)}
-
-    moves.move(("sibling",), sibling, source, None, target, lambda: slot(0, 0))
-    moves.keep(source, None, target, lambda: slot(0, 0))
-    for far_member in range(members):
-        for far_pair in range(shards // 2):
-            if far_member or far_pair:
-
-                def peer(far_member=far_member, far_pair=far_pair):
-                    seq_me = lax.axis_index("seq")
-                    return {
-                        "seq": seq_me // members * members + lax.rem(lax.rem(seq_me, members) + far_member, members),
-                        "fsdp": lax.rem(lax.axis_index("fsdp") + 2 * far_pair, shards),
-                    }
-
-                number = moves.move(("plane", far_member, far_pair), peer, source, None, target, lambda: slot(0, 0))
-                arrived = functools.partial(slot, far_member, far_pair)
-                moves.move(("sibling",), sibling, target, arrived, target, arrived, (number,))
-    moves.exchange("seq", grad_group.astype(LOW).reshape(seq_count, -1, most_cols))
-    moves.gather("seq", io_slice)
-    columns, grad_rows, io_slices = moves.run()
+    target = moves.scratch((members * shards, block_rows, most_cols), LOW)
+    gram = moves.output((block_rows, block_rows), f32, pltpu.VMEM)
+    pairs = shards // 2
+
+    def slot(back_member, back_pair, part=None):
+        who_member = lax.rem(lax.rem(lax.axis_index(PATCHES), members) + members - back_member, members)
+        who_shard = lax.rem(lax.axis_index(SHARDS) + shards - 2 * back_pair, shards)
+        index = who_member * shards + who_shard
+        return (index,) if part is None else (index, pl.ds(part * block_rows // 2, block_rows // 2))
+
+    def add_gram(place):
+        def action(ref):
+            (index,) = place()
+
+            @pl.loop(0, block_rows // GRAM_ROWS)
+            def _(tile):
+                rows = pl.ds(pl.multiple_of(tile * GRAM_ROWS, GRAM_ROWS), GRAM_ROWS)
+                ref(gram)[rows, :] += contract(ref(target)[index, rows, :], ref(target)[index], 1, 1)
+
+        return action
+
+    def start_gram(ref):
+        ref(gram)[...] = jnp.zeros((block_rows, block_rows), f32)
+
+    def pair_peer(shift):
+        return {SHARDS: lax.rem(lax.axis_index(SHARDS) + 2 * shift, shards)}
+
+    slot_own = functools.partial(slot, 0, 0)
+    own_copy = moves.keep(source, None, target, slot_own)
+    by_member = {
+        shift: moves.move(
+            (PATCHES, members, shift), functools.partial(member_peer, members, shift), source, None, target, slot_own
+        )
+        for shift in range(1, members)
+    }
+    by_pair = {
+        shift: moves.move((SHARDS, 2 * shift), functools.partial(pair_peer, shift), source, None, target, slot_own)
+        for shift in range(1, pairs)
+    }
+    from_sibling = [(moves.move((SHARDS,), sibling_peer, source, None, target, slot_own), slot_own)]
+    moves.task(start_gram)
+    moves.wait_local(own_copy)
+    moves.task(add_gram(slot_own))
+
+    def sibling_place(place):
+        def at():
+            (index,) = place()
+            return (index + 1 - 2 * lax.rem(index, 2),)
+
+        return at
+
+    def hand_on(place, arrivals):
+        if len(arrivals) == 1:
+            parts = [(place, arrivals[0])]
+        else:
+            parts = [(functools.partial(place, part), number) for part, number in enumerate(arrivals)]
+        numbers = [
+            moves.move((SHARDS,), sibling_peer, target, at, target, at, (number,)) for at, number in parts
+        ]
+        from_sibling.append((numbers, place))
+        moves.task(add_gram(place))
+
+    across = []
+    for shift_member, first in by_member.items():
+        for shift_pair, second in by_pair.items():
+            top = functools.partial(slot, shift_member, 0, 0)
+            bottom = functools.partial(slot, 0, shift_pair, 1)
+            halves = [
+                moves.move(
+                    (SHARDS, 2 * shift_pair),
+                    functools.partial(pair_peer, shift_pair),
+                    target,
+                    top,
+                    target,
+                    top,
+                    (first,),
+                ),
+                moves.move(
+                    (PATCHES, members, shift_member),
+                    functools.partial(member_peer, members, shift_member),
+                    target,
+                    bottom,
+                    target,
+                    bottom,
+                    (second,),
+                ),
+            ]
+            across.append((functools.partial(slot, shift_member, shift_pair), halves))
+    for shift, number in by_member.items():
+        hand_on(functools.partial(slot, shift, 0), [number])
+    for shift, number in by_pair.items():
+        hand_on(functools.partial(slot, 0, shift), [number])
+    moves.wait_for(from_sibling[0][0])
+    moves.task(add_gram(sibling_place(slot_own)))
+    for place, halves in across:
+        hand_on(place, halves)
+    for numbers, place in from_sibling[1:]:
+        for number in numbers:
+            moves.wait_for(number)
+        moves.task(add_gram(sibling_place(place)))
+    (gram,) = moves.run()
+    gram, by_group = lax.optimization_barrier((gram, by_group))
+    order = lax.rem(group + MATRICES - jnp.arange(MATRICES, dtype=jnp.int32), MATRICES)
+    arrived = jnp.take(jnp.stack(by_group), order, axis=0).reshape(seq_count, -1, most_cols)
+    grad_rows = arrived[:, : block_rows // seq_count]
+    io_slices = arrived[:, block_rows // seq_count :].astype(f32)
+    block = newton_schulz(gram, block)
+    block, grad_ada, grad_table, grad_pos, grad_bias, grad_rows, io_slices = lax.optimization_barrier(
+        (block, grad_ada, grad_table, grad_pos, grad_bias, grad_rows, io_slices)
+    )
 
     def row_blocks(parts):
         return [
@@ -1285,10 +1679,8 @@
         ]
 
     moments = [MOMENTUM * old + clip * grad for old, grad in zip(momenta, row_blocks(grad_rows))]
-    block = newton_schulz(block, contract(columns, columns, 1, 1))
     moves = Moves("update_rows", ids)
-    moves.exchange("seq", block.reshape(seq_count, -1, most_cols))
-    masters = (qkv_master, out_master, up_master, down_master)
+    moves.exchange(PATCHES, block.reshape(seq_count, -1, most_cols))
     fresh = [
         master * (1.0 - RATE_MUON * DECAY_MUON) - RATE_MUON * 0.2 * math.sqrt(master.shape[1] * shards) * rows
         for master, rows in zip(masters, row_blocks(moves.run()[0]))
@@ -1297,52 +1689,65 @@
     moves = Moves("copies", ids)
     rows = qkv_master.shape[0]
 
-    def row_place(back_group, back_member):
-        seq_me = lax.axis_index("seq")
-        who = lax.rem(seq_me // members + MATRICES - back_group, MATRICES) * members
-        who = who + lax.rem(lax.rem(seq_me, members) + members - back_member, members)
+    def row_place(back_group):
+        who = lax.axis_index(PATCHES) - back_group * members
         return (pl.ds(pl.multiple_of(who * rows, rows), rows),)
+
+    def has_group(offset):
+        place = lax.axis_index(PATCHES) // members + offset
+        return jnp.logical_and(place >= 0, place < MATRICES)
+
+    def member_copies(source, source_at, target, target_at, after, there):
+        for shift in range(1, members):
+            moves.move(
+                (PATCHES, members, shift),
+                functools.partial(member_peer, members, shift),
+                source,
+                source_at,
+                target,
+                target_at,
+                after,
+                there,
+                there,
+            )
 
     places = []
     for item in fresh:
         source = moves.operand(item.astype(LOW))
         target = moves.output((rows * seq_count, item.shape[1]), LOW)
-        moves.keep(source, None, target, lambda: row_place(0, 0))
-        places.append((source, target, []))
-    for shift in range(1, MATRICES):
+        own = functools.partial(row_place, 0)
+        moves.keep(source, None, target, own)
+        places.append((source, target, {}))
+
+    def along_line(distance, way, source, target, numbers):
+        both = lambda: jnp.logical_and(has_group(way), has_group(-distance * way))
+        place = functools.partial(row_place, distance * way)
+        numbers[way] = moves.move(
+            (PATCHES, seq_count, way),
+            functools.partial(group_peer, members, (MATRICES + way) % MATRICES),
+            target if distance else source,
+            place if distance else None,
+            target,
+            place,
+            (numbers[way],) if distance else (),
+            both,
+            functools.partial(has_group, -(distance + 1) * way),
+        )
+
+    for source, target, numbers in places:
+        for way in (1, -1):
+            along_line(0, way, source, target, numbers)
+    for source, target, numbers in places:
+        member_copies(source, None, target, own, (), None)
+    for distance in range(1, MATRICES):
         for source, target, numbers in places:
-            numbers.append(
-                moves.move(
-                    ("group", shift),
-                    lambda shift=shift: {"seq": lax.rem(lax.axis_index("seq") + shift * members, seq_count)},
-                    source,
-                    None,
-                    target,
-                    lambda: row_place(0, 0),
-                )
-            )
-    for shift in range(1, members):
-        for source, target, numbers in places:
-            moves.move(
-                ("member", shift),
-                functools.partial(member_peer, shift),
-                source,
-                None,
-                target,
-                lambda: row_place(0, 0),
-            )
-    for far in range(1, MATRICES):
-        for source, target, numbers in places:
-            for shift in range(1, members):
-                place = functools.partial(row_place, far, 0)
-                moves.move(
-                    ("member", shift),
-                    functools.partial(member_peer, shift),
-                    target,
-                    place,
-                    target,
-                    place,
-                    (numbers[far - 1],),
+            for way in (1, -1):
+                number = numbers[way]
+                if distance < MATRICES - 1:
+                    along_line(distance, way, source, target, numbers)
+                place = functools.partial(row_place, distance * way)
+                member_copies(
+                    target, place, target, place, (number,), functools.partial(has_group, -distance * way)
                 )
     copies = moves.run()
 
@@ -1353,13 +1758,13 @@
     pos_res = adam_update(pos_table, pos_first, pos_second, clip * grad_pos, RATE_TABLE)
     bias_res = adam_update(biases, bias_first, bias_second, clip * grad_bias, RATE_ADAM)
     matrices = []
-    for which in range(MATRICES):
+    for which in (0, 3, 1, 2):
         matrices += [fresh[which], moments[which], copies[which]]
     return (loss_total, grad_norm, moment_sizes, *matrices, *ada_res, *io_res, *cond_res, *pos_res, *bias_res)
 
 
 def fits_fast(mesh):
-    seq, shards = mesh.shape["seq"], mesh.shape["fsdp"]
+    seq, shards = mesh.shape[PATCHES], mesh.shape[SHARDS]
     return HEADS % seq == 0 and (HEADS // seq * HEAD) % LANES == 0 and seq % MATRICES == 0 and shards % 2 == 0
 
 
@@ -1369,70 +1774,70 @@
         body,
         mesh=mesh,
         in_specs=(
-            P("fsdp", "seq", None),
-            P("fsdp", "seq", None),
-            P("fsdp"),
+            P(SHARDS, PATCHES, None),
+            P(SHARDS, PATCHES, None),
+            P(SHARDS),
             P(),
-            P(None, "fsdp"),
-            P("seq", "fsdp"),
-            P("seq", "fsdp"),
-            P(None, "fsdp"),
-            P("seq", "fsdp"),
-            P("seq", "fsdp"),
-            P(None, "fsdp"),
-            P("seq", "fsdp"),
-            P("seq", "fsdp"),
-            P(None, "fsdp"),
-            P("seq", "fsdp"),
-            P("seq", "fsdp"),
-            P(None, "fsdp"),
-            P("seq", "fsdp"),
-            P("seq", "fsdp"),
-            P("seq", "fsdp"),
-            P(None, None, "fsdp"),
-            P(None, None, "fsdp"),
-            P(None, None, "fsdp"),
-            P(None, "fsdp"),
-            P(None, "fsdp"),
-            P(None, "fsdp"),
-            P("seq", "fsdp"),
-            P("seq", "fsdp"),
-            P("seq", "fsdp"),
-            P("fsdp"),
-            P("fsdp"),
-            P("fsdp"),
+            P(None, SHARDS),
+            P(PATCHES, SHARDS),
+            P(PATCHES, SHARDS),
+            P(None, SHARDS),
+            P(PATCHES, SHARDS),
+            P(PATCHES, SHARDS),
+            P(None, SHARDS),
+            P(PATCHES, SHARDS),
+            P(PATCHES, SHARDS),
+            P(None, SHARDS),
+            P(PATCHES, SHARDS),
+            P(PATCHES, SHARDS),
+            P(None, SHARDS),
+            P(PATCHES, SHARDS),
+            P(PATCHES, SHARDS),
+            P(PATCHES, SHARDS),
+            P(None, None, SHARDS),
+            P(None, None, SHARDS),
+            P(None, None, SHARDS),
+            P(None, SHARDS),
+            P(None, SHARDS),
+            P(None, SHARDS),
+            P(PATCHES, SHARDS),
+            P(PATCHES, SHARDS),
+            P(PATCHES, SHARDS),
+            P(SHARDS),
+            P(SHARDS),
+            P(SHARDS),
         ),
         out_specs=(
             P(),
             P(),
             P(),
-            P("seq", "fsdp"),
-            P("seq", "fsdp"),
-            P(None, "fsdp"),
-            P("seq", "fsdp"),
-            P("seq", "fsdp"),
-            P(None, "fsdp"),
-            P("seq", "fsdp"),
-            P("seq", "fsdp"),
-            P(None, "fsdp"),
-            P("seq", "fsdp"),
-            P("seq", "fsdp"),
-            P(None, "fsdp"),
-            P("seq", "fsdp"),
-            P("seq", "fsdp"),
-            P("seq", "fsdp"),
-            P(None, None, "fsdp"),
-            P(None, None, "fsdp"),
-            P(None, None, "fsdp"),
-            P(None, "fsdp"),
-            P(None, "fsdp"),
-            P(None, "fsdp"),
-            P("seq", "fsdp"),
-            P("seq", "fsdp"),
-            P("seq", "fsdp"),
-            P("fsdp"),
-            P("fsdp"),
-            P("fsdp"),
+            P(PATCHES, SHARDS),
+            P(PATCHES, SHARDS),
+            P(None, SHARDS),
+            P(PATCHES, SHARDS),
+            P(PATCHES, SHARDS),
+            P(None, SHARDS),
+            P(PATCHES, SHARDS),
+            P(PATCHES, SHARDS),
+            P(None, SHARDS),
+            P(PATCHES, SHARDS),
+            P(PATCHES, SHARDS),
+            P(None, SHARDS),
+            P(PATCHES, SHARDS),
+            P(PATCHES, SHARDS),
+            P(PATCHES, SHARDS),
+            P(None, None, SHARDS),
+            P(None, None, SHARDS),
+            P(None, None, SHARDS),
+            P(None, SHARDS),
+            P(None, SHARDS),
+            P(None, SHARDS),
+            P(PATCHES, SHARDS),
+            P(PATCHES, SHARDS),
+            P(PATCHES, SHARDS),
+            P(SHARDS),
+            P(SHARDS),
+            P(SHARDS),
         ),
         check_vma=False,
     )

time: 1200 us -> 1080 us (0.900); the launches traced: 1170 us -> 1070 us
  matrix products: 195 us -> 94.6 us
  Pallas kernels: 805 us -> 766 us
  local copies, waits for them, and re-layouts: 62.6 us -> 90.5 us
  between operations: 25.1 us -> 12.5 us
    dot_general x42 -> x13, matrix products: 130 us -> 44.5 us  [product(): return jnp.dot(left, right, preferred_element_type=jnp.float32)]
    pallas_call x24 -> x25, Pallas kernels: 736 us -> 713 us  [the longest x24 645 us: run(): pl.pallas_call(self.kernel, out_shape=self.outputs, in_specs=self.operand...]
    pallas_call x1, Pallas kernels: 31.7 us -> 17 us  [total_of(): pl.pallas_call(total_kernel, out_shape=jax.ShapeDtypeStruct(values.shape,...]
    transpose x0 -> x2, local copies, waits for them, and re-layouts: none -> 12.9 us  [fast_body(): jnp.moveaxis(item, 0, 1).reshape(item.shape[1], -1)]
    dot_general x12 -> x11, matrix products: 38.6 us -> 26 us  [contract(): lax.dot_general(left, right, (((left_dim,), (right_dim,)), ((), ())), pre...]
    unnamed x345 -> x446, local copies, waits for them, and re-layouts: 38.7 us -> 37.1 us
  transfers between devices with their start and end apart: 2 -> 6, of which waited for: 0 -> 1; matrix products, arithmetic and copies ran while one was open for 4% -> 4% of each run, Pallas kernels for 8% -> 10%
where the time goes in v2:
time: 1080 us; the launch traced here: 1070 us
  Pallas kernels  766 us (71%)
  other arithmetic  96.5 us (9%)
  matrix products  94.6 us (9%)
  local copies, waits for them, and re-layouts  90.5 us (8%)
  between operations  12.5 us (1%)
    pallas_call x24, Pallas kernels, run(): pl.pallas_call(self.kernel, out_shape=self.outputs, in_specs=self.operand...  645 us
    pallas_call x1, Pallas kernels, newton_schulz(): pl.pallas_call(newton_kernel, out_shape=jax.ShapeDtypeStruct(block.shape,...  68.4 us
    dot_general x13, matrix products, product(): return jnp.dot(left, right, preferred_element_type=jnp.float32)  44.5 us
    unnamed x446, local copies, waits for them, and re-layouts  37.1 us
    dot_general x11, matrix products, contract(): lax.dot_general(left, right, (((left_dim,), (right_dim,)), ((), ())), pre...  26 us
    pallas_call x2, Pallas kernels, attention_back(): pl.pallas_call(functools.partial(attention_back_kernel, heads), out_shape...  23.5 us
  transfers between devices with their start and end apart: 6, of which 1 were waited for; matrix products, arithmetic and copies ran while one was open for 4% of the time, Pallas kernels for 10%

profile of v2, /device:TPU:0, one launch (start us, length us, event | category | flops | bytes accessed | tf_op | source)
XLA Modules:
  0.0 1069.8 jit_solution(4824739985825384206)
XLA Ops:
  5.0 5.3 tables.1
  16.7 81.3 %weights.1 = (f32[4,2,1536]{2,1,0:T(2,128)}, bf16[128,1024]{1,0:T(8,128)(2,1)}, bf16[4,768,256]{2,1,0:T(8,128)(2,1)}, bf16[4,1024,256]{2,1,0:T(8,128)(2,1)}, bf16[4,1024,768]{2,1,0:T(8,128)(2,1)}) custom-call(f32[4,2,1536]{2,1,0:T(2,128)} %reshape.529.refs_0_, bf16[128,256]{1,0:T(8,128)(2,1)} %convert_element_type.342.refs_1_, bf16[768,256]{1,0:T(8,128)(2,1)} %bitcast.259, ...), custom_call_target="tpu_custom_call" | custom-call | tf_op jit(solution)/shard_map/weights/pallas_call | solution.py:662
  109.8 8.7 copy.79
  119.8 6.0 convolution_convert_fusion.1.refs_0_
  125.8 18.3 %heads0.1 = (bf16[3,1024,128]{2,1,0:T(8,128)(2,1)}, bf16[4,128,1024]{2,1,0:T(8,128)(2,1)}) custom-call(bf16[128,3072]{1,0:T(8,128)(2,1)} %convolution_convert_fusion.1.refs_0_, bf16[128,1024]{1,0:T(8,128)(2,1)} %copy-done.63), custom_call_target="tpu_custom_call" | custom-call | tf_op jit(solution)/shard_map/heads0/pallas_call | solution.py:662
  145.2 6.2 attention.2
  152.1 4.1 copy.80
  156.2 14.1 %mixed_rows.2 = (bf16[128,1024]{1,0:T(8,128)(2,1)}, bf16[4,128,384]{2,1,0:T(8,128)(2,1)}) custom-call(bf16[1,1024,128]{2,1,0:T(8,128)(2,1)} %bitcast.236, bf16[128,384]{1,0:T(8,128)(2,1)} %pad.47.refs_1_), custom_call_target="tpu_custom_call" | custom-call | tf_op jit(solution)/shard_map/mixed_rows/pallas_call | solution.py:662
  170.4 3.5 fusion.153
  177.2 15.7 %tokens_moment.2 = (bf16[4,128,1024]{2,1,0:T(8,128)(2,1)}, bf16[8,64,512]{2,1,0:T(8,128)(2,1)}) custom-call(bf16[128,1024]{1,0:T(8,128)(2,1)} %add_convert_fusion.2.refs_0_, bf16[8,64,512]{2,1,0:T(8,128)(2,1)} %get-tuple-element.264.refs_1_), custom_call_target="tpu_custom_call" | custom-call | tf_op jit(solution)/shard_map/tokens_moment/pallas_call | solution.py:662
  192.9 4.9 multiply_convert_fusion.1
  200.1 12.6 %token_sums.4 = bf16[4,128,1024]{2,1,0:T(8,128)(2,1)} custom-call(bf16[4,128,1024]{2,1,0:T(8,128)(2,1)} %bitcast.270), custom_call_target="tpu_custom_call" | custom-call | tf_op jit(solution)/shard_map/token_sums/pallas_call | solution.py:662
  224.8 6.0 convolution_convert_fusion.refs_0_
  230.7 27.7 %heads1.1 = (bf16[3,1024,128]{2,1,0:T(8,128)(2,1)}, bf16[4,128,1024]{2,1,0:T(8,128)(2,1)}, bf16[4,128,1024]{2,1,0:T(8,128)(2,1)}) custom-call(bf16[128,3072]{1,0:T(8,128)(2,1)} %convolution_convert_fusion.refs_0_, bf16[128,1024]{1,0:T(8,128)(2,1)} %copy-done.60, bf16[128,1024]{1,0:T(8,128)(2,1)} %get-tuple-element.104.refs_2_), custom_call_target="tpu_custom_call" | custom-call | tf_op jit(solution)/shard_map/heads1/pallas_call | solution.py:662
  259.6 6.5 attention.3
  266.8 8.1 mixed_rows.3
  274.9 3.4 fusion.151
  280.0 17.6 %tokens_moment.3 = (bf16[4,128,1024]{2,1,0:T(8,128)(2,1)}, bf16[8,64,512]{2,1,0:T(8,128)(2,1)}) custom-call(bf16[128,1024]{1,0:T(8,128)(2,1)} %add_convert_fusion.refs_0_, bf16[8,64,512]{2,1,0:T(8,128)(2,1)} %get-tuple-element.263.refs_1_), custom_call_target="tpu_custom_call" | custom-call | tf_op jit(solution)/shard_map/tokens_moment/pallas_call | solution.py:662
  297.6 5.0 multiply_convert_fusion
  304.9 14.1 %token_sums.5 = bf16[4,128,1024]{2,1,0:T(8,128)(2,1)} custom-call(bf16[4,128,1024]{2,1,0:T(8,128)(2,1)} %bitcast.271), custom_call_target="tpu_custom_call" | custom-call | tf_op jit(solution)/shard_map/token_sums/pallas_call | solution.py:662
  335.2 14.1 %tokens.2 = bf16[4,128,1024]{2,1,0:T(8,128)(2,1)} custom-call(bf16[128,1024]{1,0:T(8,128)(2,1)} %multiply_convert_fusion.5.refs_0_), custom_call_target="tpu_custom_call" | custom-call | tf_op jit(solution)/shard_map/tokens/pallas_call | solution.py:662
  349.3 5.0 fusion.13
  356.6 14.1 %token_sums.6 = bf16[4,128,1024]{2,1,0:T(8,128)(2,1)} custom-call(bf16[4,128,1024]{2,1,0:T(8,128)(2,1)} %bitcast.272), custom_call_target="tpu_custom_call" | custom-call | tf_op jit(solution)/shard_map/token_sums/pallas_call | solution.py:662
  378.0 9.1 mixed_heads1.1
  389.2 11.9 %attention_back.2.refs_0_ = bf16[3,1024,128]{2,1,0:T(8,128)(2,1)S(1)} custom-call(bf16[3,1024,128]{2,1,0:T(8,128)(2,1)S(1)} %copy-done.9, bf16[1024,128]{1,0:T(8,128)(2,1)S(1)} %bitcast.235), custom_call_target="tpu_custom_call" | custom-call | tf_op jit(solution)/shard_map/attention_back/pallas_call | solution.py:967
  401.9 27.5 %rows1.1 = (bf16[128,3072]{1,0:T(8,128)(2,1)}, bf16[4,128,256]{2,1,0:T(8,128)(2,1)}, bf16[4,128,256]{2,1,0:T(8,128)(2,1)}, bf16[4,128,384]{2,1,0:T(8,128)(2,1)}, bf16[4,128,1024]{2,1,0:T(8,128)(2,1)}) custom-call(bf16[3,1024,128]{2,1,0:T(8,128)(2,1)} %copy-done.5, bf16[128,1024]{1,0:T(8,128)(2,1)} %copy-done.59, bf16[128,1024]{1,0:T(8,128)(2,1)} %copy-done.62, ...), custom_call_target="tpu_custom_call" | custom-call | tf_op jit(solution)/shard_map/rows1/pallas_call | solution.py:662
  429.6 5.0 multiply_reduce_fusion.5
  439.1 14.1 %tokens.3 = bf16[4,128,1024]{2,1,0:T(8,128)(2,1)} custom-call(bf16[128,1024]{1,0:T(8,128)(2,1)} %multiply_convert_fusion.3.refs_0_), custom_call_target="tpu_custom_call" | custom-call | tf_op jit(solution)/shard_map/tokens/pallas_call | solution.py:662
  453.2 5.0 fusion.6
  459.1 4.4 fusion.18
  466.9 4.1 fusion.25
  480.0 13.5 %token_sums.7 = bf16[4,128,1024]{2,1,0:T(8,128)(2,1)} custom-call(bf16[4,128,1024]{2,1,0:T(8,128)(2,1)} %bitcast.269), custom_call_target="tpu_custom_call" | custom-call | tf_op jit(solution)/shard_map/token_sums/pallas_call | solution.py:662
  499.6 18.0 %mixed_heads0.1 = (bf16[1,1024,128]{2,1,0:T(8,128)(2,1)}, bf16[4,128,768]{2,1,0:T(8,128)(2,1)}, bf16[4,128,256]{2,1,0:T(8,128)(2,1)}) custom-call(bf16[128,1024]{1,0:T(8,128)(2,1)} %convolution_convert_fusion.6.refs_0_, bf16[128,3072]{1,0:T(8,128)(2,1)} %get-tuple-element.111.refs_1_, bf16[128,1024]{1,0:T(8,128)(2,1)} %copy-done.64), custom_call_target="tpu_custom_call" | custom-call | tf_op jit(solution)/shard_map/mixed_heads0/pallas_call | solution.py:662
  519.7 11.7 %attention_back.3.refs_0_ = bf16[3,1024,128]{2,1,0:T(8,128)(2,1)S(1)} custom-call(bf16[3,1024,128]{2,1,0:T(8,128)(2,1)S(1)} %copy-done.7, bf16[1024,128]{1,0:T(8,128)(2,1)S(1)} %bitcast.238), custom_call_target="tpu_custom_call" | custom-call | tf_op jit(solution)/shard_map/attention_back/pallas_call | solution.py:967
  532.3 16.9 %rows0.1 = (bf16[128,3072]{1,0:T(8,128)(2,1)}, bf16[4,128,256]{2,1,0:T(8,128)(2,1)}, bf16[4,128,256]{2,1,0:T(8,128)(2,1)}, bf16[4,128,384]{2,1,0:T(8,128)(2,1)}) custom-call(bf16[3,1024,128]{2,1,0:T(8,128)(2,1)} %copy-done.10, bf16[128,1024]{1,0:T(8,128)(2,1)} %copy-done.61, bf16[128,1024]{1,0:T(8,128)(2,1)} %copy-done.65, bf16[128,384]{1,0:T(8,128)(2,1)} %copy-done.85), custom_call_target="tpu_custom_call" | custom-call | tf_op jit(solution)/shard_map/rows0/pallas_call | solution.py:662
  549.4 4.4 multiply_reduce_fusion.9
  562.3 3.7 fusion.166
  572.0 25.3 %samples.1 = (bf16[4,128,768]{2,1,0:T(8,128)(2,1)}, bf16[4,128,256]{2,1,0:T(8,128)(2,1)}, f32[4,3,1536]{2,1,0:T(4,128)}, bf16[3,448,512]{2,1,0:T(8,128)(2,1)}, bf16[3,448,512]{2,1,0:T(8,128)(2,1)}) custom-call(bf16[128,3072]{1,0:T(8,128)(2,1)} %get-tuple-element.113.refs_0_, bf16[128,1024]{1,0:T(8,128)(2,1)} %get-tuple-element.230.refs_1_, ...), custom_call_target="tpu_custom_call" | custom-call | tf_op jit(solution)/shard_map/samples/pallas_call | solution.py:662
  603.4 4.1 fusion.165
  607.5 41.4 %member_sums.1 = (bf16[1,1024,384]{2,1,0:T(8,128)(2,1)}, bf16[1,1024,128]{2,1,0:T(8,128)(2,1)}, bf16[8,112,128]{2,1,0:T(8,128)(2,1)}, bf16[8,96,256]{2,1,0:T(8,1...) custom-call(bf16[1024,768]{1,0:T(8,128)(2,1)} %get-tuple-element.304.refs_0_, ...), custom_call_target="tpu_custom_call" | custom-call | tf_op jit(solution)/shard_map/member_sums/pallas_call | solution.py:662
  657.2 94.2 %group_sums.1 = (f32[1024,384]{1,0:T(8,128)S(1)}, f32[1024,128]{1,0:T(8,128)S(1)}, f32[4,8,1024]{2,1,0:T(8,128)S(1)}, f32[4,1,1792]{2,1,0:T(1,128)S(1)}) custom-call(f32[1024,384]{1,0:T(8,128)S(1)} %convert_add_fusion.2.refs_0_, f32[1024,128]{1,0:T(8,128)S(1)} %convert_add_fusion.3.refs_1_, f32[8,1024]{1,0:T(8,128)S(1)} %fusion.169.refs_2_, ...), custom_call_target="tpu_custom_call" | custom-call | tf_op jit(solution)/shard_map/group_sums/pallas_call | solution.py:662
  756.6 4.1 fusion.145
  779.3 17.0 %total.1 = f32[8,128]{1,0:T(8,128)} custom-call(f32[8,128]{1,0:T(8,128)} %broadcast_in_dim.122.x_ref), custom_call_target="tpu_custom_call" | custom-call | tf_op jit(solution)/shard_map/total/pallas_call | solution.py:876
  814.5 44.6 %columns.1.gram_ref = f32[1024,1024]{1,0:T(8,128)S(1)} custom-call(bf16[1024,512]{1,0:T(8,128)(2,1)S(1)} %fusion.43.refs_0_.block_ref), custom_call_target="tpu_custom_call" | custom-call | tf_op jit(solution)/shard_map/columns/pallas_call | solution.py:662
  864.9 3.2 gather_fusion.2
  871.8 68.4 %newton.1 = bf16[1024,512]{1,0:T(8,128)(2,1)S(1)} custom-call(f32[1024,1024]{1,0:T(8,128)} %copy-done.1, bf16[1024,512]{1,0:T(8,128)(2,1)S(1)} %copy-done.3), custom_call_target="tpu_custom_call" | custom-call | tf_op jit(solution)/shard_map/newton/pallas_call | solution.py:1076
  941.2 19.6 %update_rows.1 = bf16[8,128,512]{2,1,0:T(8,128)(2,1)} custom-call(bf16[8,128,512]{2,1,0:T(8,128)(2,1)} %bitcast.234), custom_call_target="tpu_custom_call" | custom-call | tf_op jit(solution)/shard_map/update_rows/pallas_call | solution.py:662
  968.1 77.7 %copies.1 = (bf16[1024,768]{1,0:T(8,128)(2,1)}, bf16[1024,1024]{1,0:T(8,128)(2,1)}, bf16[1024,1024]{1,0:T(8,128)(2,1)}, bf16[1024,256]{1,0:T(8,128)(2,1)}) custom-call(bf16[128,768]{1,0:T(8,128)(2,1)} %get-tuple-element.207.refs_0_, bf16[128,1024]{1,0:T(8,128)(2,1)} %get-tuple-element.205.refs_1_, bf16[128,1024]{1,0:T(8,128)(2,1)} %get-tuple-element.203.refs_2_, ...), custom_call_target="tpu_custom_call" | custom-call | tf_op jit(solution)/shard_map/copies/pallas_call | solution.py:662
  (663 shorter events, 206.3 us)
Async XLA Ops:
  0.7 12.1 %copy-start = (bf16[1024,1536]{1,0:T(8,128)(2,1)S(1)}, bf16[1024,1536]{1,0:T(8,128)(2,1)}, u32[]{:S(2)}) copy-start(bf16[1024,1536]{1,0:T(8,128)(2,1)} %param.49) | copy-start | bytes 9437188
  0.7 13.3 %copy-start.102 = (f32[128,256]{1,0:T(8,128)S(1)}, f32[128,256]{1,0:T(8,128)}, u32[]{:S(2)}) copy-start(f32[128,256]{1,0:T(8,128)} %param.59) | copy-start | bytes 393220
  97.9 8.8 copy-start.84
  152.1 18.3 %copy-start.126 = (f32[1,1024]{1,0:T(1,128)S(1)}, f32[1,1024]{1,0:T(1,128)}, u32[]{:S(2)}) copy-start(f32[1,1024]{1,0:T(1,128)} %get-tuple-element.282) | copy-start | bytes 12292
  200.1 14.1 %copy-start.128 = (f32[1,1024]{1,0:T(1,128)S(1)}, f32[1,1024]{1,0:T(1,128)}, u32[]{:S(2)}) copy-start(f32[1,1024]{1,0:T(1,128)} %get-tuple-element.279) | copy-start | bytes 12292
  216.9 6.9 copy-start.65
  223.8 6.9 copy-start.120
  223.8 51.1 %copy-start.130 = (f32[1,1024]{1,0:T(1,128)}, f32[1,1024]{1,0:T(1,128)S(1)}, u32[]{:S(2)}) copy-start(f32[1,1024]{1,0:T(1,128)S(1)} %get-tuple-element.276) | copy-start | bytes 12292
  223.9 54.7 %copy-start.124 = (f32[1,1024]{1,0:T(1,128)}, f32[1,1024]{1,0:T(1,128)S(1)}, u32[]{:S(2)}) copy-start(f32[1,1024]{1,0:T(1,128)S(1)} %get-tuple-element.275) | copy-start | bytes 12292
  223.9 96.6 %copy-start.132 = (f32[1,1024]{1,0:T(1,128)}, f32[1,1024]{1,0:T(1,128)S(1)}, u32[]{:S(2)}) copy-start(f32[1,1024]{1,0:T(1,128)S(1)} %get-tuple-element.273) | copy-start | bytes 12292
  223.9 6.8 copy-start.159
  278.3 24.3 %copy-start.161 = (f32[128]{0:T(128)}, f32[128]{0:T(128)S(1)}, u32[]{:S(2)}) copy-start(f32[128]{0:T(128)S(1)} %broadcast_multiply_fusion.15) | copy-start | bytes 1540
  278.5 24.1 %copy-start.174 = (f32[128]{0:T(128)}, f32[128]{0:T(128)S(1)}, u32[]{:S(2)}) copy-start(f32[128]{0:T(128)S(1)} %add_rsqrt_fusion.1) | copy-start | bytes 1540
  319.0 7.2 copy-start.202
  326.2 7.4 copy-start.62
  356.5 16.5 %copy-start.125 = (f32[1,1024]{1,0:T(1,128)S(1)}, f32[1,1024]{1,0:T(1,128)}, u32[]{:S(2)}) copy-start(f32[1,1024]{1,0:T(1,128)} %copy-done.124) | copy-start | bytes 12292
  356.6 16.5 %copy-start.162 = (f32[128]{0:T(128)S(1)}, f32[128]{0:T(128)}, u32[]{:S(2)}) copy-start(f32[128]{0:T(128)} %copy-done.161) | copy-start | bytes 1540
  356.6 16.5 %copy-start.175 = (f32[128]{0:T(128)S(1)}, f32[128]{0:T(128)}, u32[]{:S(2)}) copy-start(f32[128]{0:T(128)} %copy-done.174) | copy-start | bytes 1540
  376.9 24.2 %copy-start.59 = (bf16[128,1024]{1,0:T(8,128)(2,1)}, bf16[128,1024]{1,0:T(8,128)(2,1)S(1)}, u32[]{:S(2)}) copy-start(bf16[128,1024]{1,0:T(8,128)(2,1)S(1)} %multiply_convert_fusion.4.refs_1_) | copy-start | bytes 786436
  378.0 51.5 %copy-start.121 = (f32[1,1024]{1,0:T(1,128)S(1)}, f32[1,1024]{1,0:T(1,128)}, u32[]{:S(2)}) copy-start(f32[1,1024]{1,0:T(1,128)} %copy-done.120) | copy-start | bytes 12292
  378.0 51.5 %copy-start.160 = (f32[128]{0:T(128)S(1)}, f32[128]{0:T(128)}, u32[]{:S(2)}) copy-start(f32[128]{0:T(128)} %copy-done.159) | copy-start | bytes 1540
  378.0 51.5 %copy-start.173 = (f32[128]{0:T(128)S(1)}, f32[128]{0:T(128)}, u32[]{:S(2)}) copy-start(f32[128]{0:T(128)} %copy-done.172) | copy-start | bytes 1540
  466.4 100.3 %collective-permute-start = (bf16[1024,512]{1,0:T(8,128)(2,1)}, bf16[1024,512]{1,0:T(8,128)(2,1)}, u32[]{:S(2)}, u32[]{:S(2)}) collective-permute-start(bf16[1024,512]{1,0:T(8,128)(2,1)} %dynamic-slice_convert_fusion.1), channel_id=1, source_target_pairs={{0,4},{4,0},{8,12},{12,8},{16,20},{20,16},{24,28},{28,24},{1,5},{5... | collective-permute-start | bytes 3145736 | tf_op jit(solution)/shard_map/ppermute | solution.py:1275
  466.9 8.7 copy-start.209
  474.1 95.3 %collective-permute-start.1 = (bf16[1024,512]{1,0:T(8,128)(2,1)}, bf16[1024,512]{1,0:T(8,128)(2,1)}, u32[]{:S(2)}, u32[]{:S(2)}) collective-permute-start(bf16[1024,512]{1,0:T(8,128)(2,1)} %dynamic-slice_convert_fusion), channel_id=1, source_target_pairs={{0,4},{4,0},{8,12},{12,8},{16,20},{20,16},{24,28},{28,24},{1,5},{5... | collective-permute-start | bytes 3145736 | tf_op jit(solution)/shard_map/ppermute | solution.py:1275
  477.9 17.5 %copy-start.123 = (f32[1,1024]{1,0:T(1,128)S(1)}, f32[1,1024]{1,0:T(1,128)}, u32[]{:S(2)}) copy-start(f32[1,1024]{1,0:T(1,128)} %get-tuple-element.281) | copy-start | bytes 12292
  477.9 17.5 %copy-start.156 = (f32[128]{0:T(128)S(1)}, f32[128]{0:T(128)}, u32[]{:S(2)}) copy-start(f32[128]{0:T(128)} %copy-done.155) | copy-start | bytes 1540
  477.9 17.6 %copy-start.169 = (f32[128]{0:T(128)S(1)}, f32[128]{0:T(128)}, u32[]{:S(2)}) copy-start(f32[128]{0:T(128)} %copy-done.168) | copy-start | bytes 1540
  498.4 33.0 %copy-start.61 = (bf16[128,1024]{1,0:T(8,128)(2,1)}, bf16[128,1024]{1,0:T(8,128)(2,1)S(1)}, u32[]{:S(2)}) copy-start(bf16[128,1024]{1,0:T(8,128)(2,1)S(1)} %multiply_convert_fusion.2.refs_1_) | copy-start | bytes 786436
  499.6 49.6 %copy-start.119 = (f32[1,1024]{1,0:T(1,128)S(1)}, f32[1,1024]{1,0:T(1,128)}, u32[]{:S(2)}) copy-start(f32[1,1024]{1,0:T(1,128)} %get-tuple-element.284) | copy-start | bytes 12292
  499.6 49.6 %copy-start.153 = (f32[128]{0:T(128)S(1)}, f32[128]{0:T(128)}, u32[]{:S(2)}) copy-start(f32[128]{0:T(128)} %copy-done.152) | copy-start | bytes 1540
  499.6 49.6 %copy-start.166 = (f32[128]{0:T(128)S(1)}, f32[128]{0:T(128)}, u32[]{:S(2)}) copy-start(f32[128]{0:T(128)} %add_rsqrt_fusion.5) | copy-start | bytes 1540
  549.3 6.7 copy-start.198
  549.3 6.7 copy-start.199
  549.3 6.7 copy-start.200
  549.3 6.7 copy-start.201
  655.1 97.2 %copy-start.81 = (bf16[3,448,512]{2,1,0:T(8,128)(2,1)S(1)}, bf16[3,448,512]{2,1,0:T(8,128)(2,1)}, u32[]{:S(2)}) copy-start(bf16[3,448,512]{2,1,0:T(8,128)(2,1)} %get-tuple-element.136) | copy-start | bytes 4128772
  657.1 95.0 %copy-start.76 = (bf16[3,576,512]{2,1,0:T(8,128)(2,1)S(1)}, bf16[3,576,512]{2,1,0:T(8,128)(2,1)}, u32[]{:S(2)}) copy-start(bf16[3,576,512]{2,1,0:T(8,128)(2,1)} %get-tuple-element.137) | copy-start | bytes 5308420
  657.1 96.7 %copy-start.80 = (bf16[3,448,512]{2,1,0:T(8,128)(2,1)S(1)}, bf16[3,448,512]{2,1,0:T(8,128)(2,1)}, u32[]{:S(2)}) copy-start(bf16[3,448,512]{2,1,0:T(8,128)(2,1)} %get-tuple-element.134) | copy-start | bytes 4128772
  763.4 9.1 copy-start.147
  764.6 7.9 copy-start.134
  767.1 11.6 %collective-permute-start.2 = (bf16[4,176,512]{2,1,0:T(8,128)(2,1)}, bf16[4,176,512]{2,1,0:T(8,128)(2,1)}, u32[]{:S(2)}, u32[]{:S(2)}) collective-permute-start(bf16[4,176,512]{2,1,0:T(8,128)(2,1)} %get-tuple-element.245), channel_id=1, source_target_pairs={{0,4},{4,0},{8,12},{12,8},{16,20},{20,16},{24,28},{28,24},{1,5},{5... | collective-permute-start | bytes 2162696 | tf_op jit(solution)/shard_map/ppermute | solution.py:1523
  805.7 7.7 copy-start.53
  808.4 54.1 %collective-permute-start.3 = (bf16[2,176,512]{2,1,0:T(8,128)(2,1)}, bf16[2,176,512]{2,1,0:T(8,128)(2,1)}, u32[]{:S(2)}, u32[]{:S(2)}) collective-permute-start(bf16[2,176,512]{2,1,0:T(8,128)(2,1)} %get-tuple-element.243), channel_id=1, source_target_pairs={{0,8},{4,12},{8,16},{12,20},{16,24},{20,28},{24,0},{28,4},{1,9},{5... | collective-permute-start | bytes 1081352 | tf_op jit(solution)/shard_map/ppermute | solution.py:1547
  809.5 52.9 %collective-permute-start.4 = (bf16[2,176,512]{2,1,0:T(8,128)(2,1)}, bf16[2,176,512]{2,1,0:T(8,128)(2,1)}, u32[]{:S(2)}, u32[]{:S(2)}) collective-permute-start(bf16[2,176,512]{2,1,0:T(8,128)(2,1)} %get-tuple-element.242), channel_id=1, source_target_pairs={{0,16},{4,20},{8,24},{12,28},{16,0},{20,4},{24,8},{28,12},{1,17},{... | collective-permute-start | bytes 1081352 | tf_op jit(solution)/shard_map/ppermute | solution.py:1547
  812.0 50.4 %collective-permute-start.5 = (bf16[2,176,512]{2,1,0:T(8,128)(2,1)}, bf16[2,176,512]{2,1,0:T(8,128)(2,1)}, u32[]{:S(2)}, u32[]{:S(2)}) collective-permute-start(bf16[2,176,512]{2,1,0:T(8,128)(2,1)} %get-tuple-element.241), channel_id=1, source_target_pairs={{0,24},{4,28},{8,0},{12,4},{16,8},{20,12},{24,16},{28,20},{1,25},{... | collective-permute-start | bytes 1081352 | tf_op jit(solution)/shard_map/ppermute | solution.py:1547
  814.5 44.6 %copy-start.2 = (bf16[1024,512]{1,0:T(8,128)(2,1)}, bf16[1024,512]{1,0:T(8,128)(2,1)S(1)}, u32[]{:S(2)}) copy-start(bf16[1024,512]{1,0:T(8,128)(2,1)S(1)} %fusion.43.refs_0_.block_ref) | copy-start | bytes 3145732
  967.5 83.3 %copy-start.79 = (f32[128,768]{1,0:T(8,128)S(1)}, f32[128,768]{1,0:T(8,128)}, u32[]{:S(2)}) copy-start(f32[128,768]{1,0:T(8,128)} %param.39) | copy-start | bytes 1179652
  (170 other events, 553.8 us)

commit v3 on v2

--- a/solution.py
+++ b/solution.py
@@ -706,6 +706,32 @@
         target = self.output((lax.axis_size(axis),) + array.shape, array.dtype)
         self.along(axis, self.operand(array), target, [(None, lambda sender: (sender,))])
 
+    def gather_pairs(self, array, parts=1):
+        shards = lax.axis_size(SHARDS)
+        source = self.operand(array)
+        target = self.output((shards,) + array.shape, array.dtype)
+        rows = array.shape[0] // parts
+
+        def place(back_pair, part):
+            return (lax.rem(lax.axis_index(SHARDS) + shards - 2 * back_pair, shards), pl.ds(part * rows, rows))
+
+        firsts = []
+        for part in range(parts):
+            for pair in range(1, shards // 2):
+                number = self.move(
+                    (SHARDS, 2 * pair),
+                    lambda pair=pair: {SHARDS: lax.rem(lax.axis_index(SHARDS) + 2 * pair, shards)},
+                    source,
+                    lambda part=part: (pl.ds(part * rows, rows),),
+                    target,
+                    functools.partial(place, 0, part),
+                )
+                firsts.append((functools.partial(place, pair, part), number))
+        own = lambda: (lax.axis_index(SHARDS),)
+        self.move((SHARDS,), sibling_peer, source, None, target, own)
+        self.keep(source, None, target, own)
+        self.to_sibling([(target, at, number) for at, number in firsts])
+
     def gather_columns(self, axis, array):
         width = array.shape[-1]
         target = self.output(array.shape[:-1] + (lax.axis_size(axis) * width,), array.dtype)
@@ -722,13 +748,17 @@
         entries = []
         for array in arrays:
             source = self.operand(array)
-            target = self.output((shards,) + array.shape, array.dtype)
+            width = array.shape[1]
+            target = self.output((array.shape[0], shards * width), array.dtype)
             rows = array.shape[0] // members
 
-            def place(back_member, back_pair, rows=rows):
+            def columns(back_pair, width=width):
+                who = lax.rem(lax.axis_index(SHARDS) + shards - 2 * back_pair, shards)
+                return pl.ds(pl.multiple_of(who * width, LANES), width)
+
+            def place(back_member, back_pair, rows=rows, columns=columns):
                 index = lax.rem(lax.rem(lax.axis_index(PATCHES), members) + members - back_member, members)
-                who = lax.rem(lax.axis_index(SHARDS) + shards - 2 * back_pair, shards)
-                return (who, pl.ds(pl.multiple_of(index * rows, rows), rows))
+                return (pl.ds(pl.multiple_of(index * rows, rows), rows), columns(back_pair))
 
             def mine(rows=rows):
                 index = lax.rem(lax.axis_index(PATCHES), members)
@@ -746,10 +776,7 @@
                 for pair in range(1, shards // 2)
             ]
             entries.append((source, target, place, firsts))
-        for source, target, _, _ in entries:
-            own = lambda: (lax.axis_index(SHARDS),)
-            self.move((SHARDS,), sibling_peer, source, None, target, own)
-            self.keep(source, None, target, own)
+            self.move((SHARDS,), sibling_peer, source, None, target, lambda columns=columns: (slice(None), columns(0)))
         last = []
         for _, target, place, firsts in entries:
             for pair, first in enumerate(firsts, 1):
@@ -900,7 +927,7 @@
 
 
 QUERY_BLOCK = 256
-CHAIN_CHUNKS = 4
+CHAIN_CHUNKS = 8
 GRAM_ROWS = 256
 
 
@@ -993,80 +1020,67 @@
     def rows_at(tile):
         return pl.ds(pl.multiple_of(tile * GRAM_ROWS, GRAM_ROWS), GRAM_ROWS)
 
-    def split(full, low):
-        def add(tile, total):
-            return total + jnp.sum(full[rows_at(tile), rows_at(tile)] * eye)
-
-        mean = lax.fori_loop(0, tiles, add, jnp.float32(0.0)) / size
-
-        @pl.loop(0, tiles)
-        def _(tile):
-            rows = rows_at(tile)
-            low[rows, :] = full[rows, :].astype(LOW)
-            low[rows, rows] = (full[rows, rows] - mean * eye).astype(LOW)
-
-        return mean
-
-    def multiply(target, left, left_mean, left_low, right, right_mean, right_low, finish):
-        @pl.loop(0, tiles)
-        def _(tile):
-            rows = rows_at(tile)
-            value = contract(left_low[rows, :], right_low[...], 1, 0)
-            value = value + left_mean * right[rows, :] + right_mean * left[rows, :]
-            target[rows, :] = finish(value, rows)
-
-    def mend(target, amount):
-        @pl.loop(0, tiles)
-        def _(tile):
-            rows = rows_at(tile)
-            target[rows, rows] -= amount * eye
-
-    def advance(last):
-        gram_mean = split(gram, gram_low)
-        multiply(
-            poly,
-            gram,
-            gram_mean,
-            gram_low,
-            gram,
-            gram_mean,
-            gram_low,
-            lambda value, rows: NS_B * gram[rows, :] + NS_C * value,
-        )
-        mend(poly, NS_C * gram_mean * gram_mean)
-        poly_mean = split(poly, poly_low)
+    def over_tiles(action):
+        return lax.fori_loop(0, tiles, lambda tile, total: total + action(rows_at(tile)), jnp.float32(0.0))
+
+    def store(full, low, rows, value, mean, excess):
+        full[rows, :] = value
+        low[rows, :] = value.astype(LOW)
+        corner = full[rows, rows] - excess * eye
+        full[rows, rows] = corner
+        low[rows, rows] = (corner - mean * eye).astype(LOW)
+
+    def advance(gram_mean, gram_squares, last):
+        poly_mean = NS_B * gram_mean + NS_C * gram_squares / size
+
+        def poly_rows(rows):
+            own = gram[rows, :]
+            value = contract(gram_low[rows, :], gram_low[...], 1, 0)
+            value = NS_C * value + (NS_B + 2.0 * NS_C * gram_mean) * own
+            store(poly, poly_low, rows, value, poly_mean, NS_C * gram_mean * gram_mean)
+            return jnp.sum(value * own)
+
+        poly_gram = over_tiles(poly_rows) - NS_C * gram_mean * gram_mean * gram_mean * size
+        once_mean = poly_gram / size
         out_ref[...] = block[...]
 
-        @pl.loop(0, tiles)
-        def _(tile):
-            rows = rows_at(tile)
-            value = contract(poly_low[rows, :], out_ref[...], 1, 0)
+        def block_rows(rows):
+            left = poly_low[rows, :]
+            value = contract(left, out_ref[...], 1, 0)
             block[rows, :] = (value + (NS_A + poly_mean) * out_ref[rows, :].astype(jnp.float32)).astype(LOW)
-
-        if not last:
-            multiply(once, poly, poly_mean, poly_low, gram, gram_mean, gram_low, lambda value, rows: value)
-            mend(once, poly_mean * gram_mean)
-            once_mean = split(once, once_low)
-            multiply(
-                gram,
-                poly,
-                poly_mean,
-                poly_low,
-                once,
-                once_mean,
-                once_low,
-                lambda value, rows: NS_A * NS_A * gram[rows, :] + 2.0 * NS_A * once[rows, :] + value,
-            )
-            mend(gram, poly_mean * once_mean)
-
-    gram[...] = gram_ref[...]
+            if last:
+                return jnp.float32(0.0)
+            value = contract(left, gram_low[...], 1, 0)
+            own = poly[rows, :]
+            value = value + poly_mean * gram[rows, :] + gram_mean * own
+            store(once, once_low, rows, value, once_mean, poly_mean * gram_mean)
+            return jnp.sum(value * own)
+
+        poly_once = over_tiles(block_rows) - poly_mean * gram_mean * poly_mean * size
+        if last:
+            return None
+        mean_next = NS_A * NS_A * gram_mean + 2.0 * NS_A * once_mean + poly_once / size
+
+        def gram_rows(rows):
+            value = contract(poly_low[rows, :], once_low[...], 1, 0)
+            value = value + (2.0 * NS_A + poly_mean) * once[rows, :] + once_mean * poly[rows, :]
+            value = value + NS_A * NS_A * gram[rows, :]
+            store(gram, gram_low, rows, value, mean_next, poly_mean * once_mean)
+            return jnp.sum(value * value)
+
+        excess = poly_mean * once_mean
+        return mean_next, over_tiles(gram_rows) - excess * (2.0 * mean_next + excess) * size
+
     block[...] = block_ref[...]
-
-    @pl.loop(0, NS_ITERS - 1)
-    def _(turn):
-        advance(False)
-
-    advance(True)
+    mean = over_tiles(lambda rows: jnp.sum(gram_ref[rows, rows] * eye)) / size
+
+    def start(rows):
+        value = gram_ref[rows, :]
+        store(gram, gram_low, rows, value, mean, 0.0)
+        return jnp.sum(value * value)
+
+    state = lax.fori_loop(0, NS_ITERS - 1, lambda turn, state: advance(*state, False), (mean, over_tiles(start)))
+    advance(*state, True)
     out_ref[...] = block[...]
 
 
@@ -1148,9 +1162,12 @@
     moves.exchange(SHARDS, modul_shard.reshape(shards, ROLL, ada_cols))
     moves.gather_columns(SHARDS, pos_table.astype(LOW))
     io_low = jnp.pad(io_proj.astype(LOW), ((0, 0), (0, padded - values_count), (0, 0)))
-    moves.gather_twice((io_low.reshape(2 * padded, -1), out_copy, qkv_copy), members)
+    own_parts = (io_low.reshape(2 * padded, -1), out_copy, qkv_copy)
+    moves.gather_twice(own_parts, members)
     modul, pos, *parts = moves.run()
-    io_all, w_out, w_qkv = [jnp.moveaxis(item, 0, 1).reshape(item.shape[1], -1) for item in parts]
+    io_all, w_out, w_qkv = [
+        lax.dynamic_update_slice_in_dim(part, own, shard * own.shape[1], 1) for part, own in zip(parts, own_parts)
+    ]
     io_all = io_all.reshape(2, padded, width)
     modul = jnp.moveaxis(modul, 0, 1).reshape(ROLL, 6 * width)
     pos = pos.astype(f32)
@@ -1200,9 +1217,9 @@
         qkv_rows = product(normed_a, w_qkv).astype(LOW)
         moves = Moves(f"heads{step}", ids)
         moves.rows_to_heads(PATCHES, qkv_rows, 3)
-        moves.gather(SHARDS, normed_a)
+        moves.gather_pairs(normed_a)
         if step:
-            moves.gather(SHARDS, kept[-1][5])
+            moves.gather_pairs(kept[-1][5])
             qkv, gathered_a, gathered_mixed = moves.run()
             gathered["mixed"] = {step - 1: gathered_mixed}
         else:
@@ -1211,14 +1228,14 @@
         mixed_heads = attention(qkv)
         moves = Moves("mixed_rows", ids)
         moves.heads_to_rows(PATCHES, mixed_heads[None])
-        moves.gather(SHARDS, state_low)
+        moves.gather_pairs(state_low)
         (mixed,) = run_with(moves, ["state"])
         attended = product(mixed, w_out)
         after_attn = embedded + gate1 * attended
         normed_two, inverse_two = layer_norm(after_attn)
         normed_b = (normed_two * (1.0 + scale2) + shift2).astype(LOW)
         moves = Moves("tokens_moment", ids)
-        moves.gather(SHARDS, normed_b)
+        moves.gather_pairs(normed_b, 2)
         moves.exchange(PATCHES, moment_parts[:, step * half_rows : (step + 1) * half_rows])
         tokens_b, moment_half = moves.run()
         moment_halves.append(moment_half)
@@ -1299,7 +1316,7 @@
         grad_mlp = norm_back(product(delta_grad, io_all[1]), normed_three, inverse_three)
         grad_gate2 = jnp.sum(grad_mlp * downward, 0)
         moves = Moves("tokens", ids)
-        moves.gather(SHARDS, (gate2 * grad_mlp).astype(LOW))
+        moves.gather_pairs((gate2 * grad_mlp).astype(LOW), 2)
         tokens_down = moves.run()[0].reshape(shards * local, width)
         grad_hidden = product(tokens_down, down_copy)
         up_grad = jax.vjp(jax.nn.gelu, upward)[1](grad_hidden)[0].astype(LOW)
@@ -1335,10 +1352,10 @@
         moves.heads_to_rows(PATCHES, qkv_grad_heads)
         moves.exchange_columns(SHARDS, attn_grad)
         moves.exchange_columns(SHARDS, normed_c)
-        moves.gather(SHARDS, delta_grad)
+        moves.gather_pairs(delta_grad)
         names = ["attn", "c", "delta"]
         if step == ROLL - 1:
-            moves.gather(SHARDS, mixed)
+            moves.gather_pairs(mixed)
             names.append("mixed")
         (qkv_grad,) = run_with(moves, names)
         grad_normed_a = contract(qkv_grad, w_qkv, 1, 1)
@@ -1443,54 +1460,51 @@
 
     moves = Moves("group_sums", ids)
     moves.vmem = 32 * 2**20
-    chains = []
-    for item, which in zip(late_sums, late):
-        away = -1 if which else 1
-
-        def has_source(which=which):
-            return lax.axis_index(PATCHES) // members != (0 if which else MATRICES - 1)
-
-        def is_source(which=which):
-            return lax.axis_index(PATCHES) // members != which
-
-        mine = moves.operand(item, pltpu.VMEM)
-        total = moves.output(item.shape, f32, pltpu.VMEM)
-        arriving, leaving = moves.scratch(item.shape, LOW), moves.scratch(item.shape, LOW)
-        chains.append((mine, total, arriving, leaving, away, has_source, is_source))
+    to_group(moves, late_sums[1].astype(LOW), late[1], 0, block_rows)
+
+    def has_source():
+        return lax.axis_index(PATCHES) // members < MATRICES - 1
+
+    def is_source():
+        return lax.axis_index(PATCHES) // members > 0
+
+    chain = late_sums[0]
+    mine = moves.operand(chain, pltpu.VMEM)
+    chain_total = moves.output(chain.shape, f32, pltpu.VMEM)
+    arriving, leaving = moves.scratch(chain.shape, LOW), moves.scratch(chain.shape, LOW)
     chunk = block_rows // CHAIN_CHUNKS
     for part in range(CHAIN_CHUNKS):
-        for mine, total, arriving, leaving, away, has_source, is_source in chains:
-            place = (pl.ds(part * chunk, chunk),)
-            number = moves.move(
-                (PATCHES, seq_count, away),
-                functools.partial(group_peer, members, MATRICES - away),
-                leaving,
-                lambda place=place: place,
-                arriving,
-                lambda place=place: place,
-                sends=is_source,
-                takes=has_source,
-                later=True,
-            )
-
-            def add(ref, mine=mine, total=total, arriving=arriving, leaving=leaving, has_source=has_source, place=place):
-                def with_arriving():
-                    ref(total)[place] = ref(mine)[place] + ref(arriving)[place].astype(f32)
-
-                def alone():
-                    ref(total)[place] = ref(mine)[place]
-
-                pl.when(has_source())(with_arriving)
-                pl.when(jnp.logical_not(has_source()))(alone)
-                ref(leaving)[place] = ref(total)[place].astype(LOW)
-
-            moves.wait_for(number)
-            moves.task(add)
-            moves.start(number)
+        place = (pl.ds(part * chunk, chunk),)
+        number = moves.move(
+            (PATCHES, seq_count, MATRICES - 1),
+            functools.partial(group_peer, members, MATRICES - 1),
+            leaving,
+            lambda place=place: place,
+            arriving,
+            lambda place=place: place,
+            sends=is_source,
+            takes=has_source,
+            later=True,
+        )
+
+        def add(ref, place=place):
+            def with_arriving():
+                ref(chain_total)[place] = ref(mine)[place] + ref(arriving)[place].astype(f32)
+
+            def alone():
+                ref(chain_total)[place] = ref(mine)[place]
+
+            pl.when(has_source())(with_arriving)
+            pl.when(jnp.logical_not(has_source()))(alone)
+            ref(leaving)[place] = ref(chain_total)[place].astype(LOW)
+
+        moves.wait_for(number)
+        moves.task(add)
+        moves.start(number)
     moves.gather(SHARDS, silu_part)
     moves.gather(SHARDS, bias_part[None])
-    *late_sums, silu_parts, bias_parts = moves.run()
-    late_sums = [widen(item) for item in late_sums]
+    out_parts, chain, silu_parts, bias_parts = moves.run()
+    late_sums = [widen(chain), widen(late_sums[1] + jnp.sum(out_parts.astype(f32), 0))]
     grad_group = jnp.where(
         group == late[0],
         late_sums[0],
@@ -1538,14 +1552,12 @@
     entries = entries + jnp.where(lane == place + 1, jnp.sum(moment_group * grad_group), 0.0)
     entries = entries + jnp.where(lane == place + 2, grad_squares, 0.0)
     entries, by_member = lax.optimization_barrier((entries, by_member))
-    order = lax.rem(member + members - jnp.arange(members, dtype=jnp.int32), members)
-    by_member = jnp.take(jnp.stack(by_member), order, axis=0)
+    by_member = jnp.stack(by_member)
     by_group = [lax.dynamic_index_in_dim(by_member, group, 1, False)]
     for shift in range(1, MATRICES):
         part = lax.dynamic_index_in_dim(by_member, lax.rem(group + shift, MATRICES), 1, False)
         routes = [(index, (index + shift * members) % seq_count) for index in range(seq_count)]
         by_group.append(lax.ppermute(part, PATCHES, routes))
-
     sums = total_of(ids, jnp.broadcast_to(entries[None], (8, LANES)))[0]
     grad_norm = jnp.sqrt(sums[0])
     loss_total = sums[1]
@@ -1661,29 +1673,45 @@
         moves.task(add_gram(sibling_place(place)))
     (gram,) = moves.run()
     gram, by_group = lax.optimization_barrier((gram, by_group))
-    order = lax.rem(group + MATRICES - jnp.arange(MATRICES, dtype=jnp.int32), MATRICES)
-    arrived = jnp.take(jnp.stack(by_group), order, axis=0).reshape(seq_count, -1, most_cols)
-    grad_rows = arrived[:, : block_rows // seq_count]
-    io_slices = arrived[:, block_rows // seq_count :].astype(f32)
     block = newton_schulz(gram, block)
-    block, grad_ada, grad_table, grad_pos, grad_bias, grad_rows, io_slices = lax.optimization_barrier(
-        (block, grad_ada, grad_table, grad_pos, grad_bias, grad_rows, io_slices)
-    )
-
-    def row_blocks(parts):
-        return [
-            jnp.concatenate(
-                [parts[which * members + part][:, : group_cols[which]] for part in range(members)], -1
-            ).astype(f32)
+    block, grad_ada, grad_table, grad_pos, grad_bias, by_group = lax.optimization_barrier(
+        (block, grad_ada, grad_table, grad_pos, grad_bias, by_group)
+    )
+
+    def pick(parts, index):
+        value = parts[0]
+        for number, part in enumerate(parts[1:], 1):
+            value = jnp.where(index == number, part, value)
+        return value
+
+    def came_from(which, part):
+        back_group = lax.rem(group + MATRICES - which, MATRICES)
+        back_member = lax.rem(member + members - part, members)
+        return pick([pick([item[back] for back in range(members)], back_member) for item in by_group], back_group)
+
+    def rows_of(which, of_part):
+        return jnp.concatenate(
+            [of_part(which, part)[: block_rows // seq_count, : group_cols[which]] for part in range(members)], -1
+        ).astype(f32)
+
+    moments = [MOMENTUM * old + clip * rows_of(which, came_from) for which, old in enumerate(momenta)]
+    io_slices = jnp.stack(
+        [
+            came_from(which, part)[block_rows // seq_count :].astype(f32)
             for which in range(MATRICES)
+            for part in range(members)
         ]
-
-    moments = [MOMENTUM * old + clip * grad for old, grad in zip(momenta, row_blocks(grad_rows))]
+    )
     moves = Moves("update_rows", ids)
     moves.exchange(PATCHES, block.reshape(seq_count, -1, most_cols))
+    (update,) = moves.run()
     fresh = [
-        master * (1.0 - RATE_MUON * DECAY_MUON) - RATE_MUON * 0.2 * math.sqrt(master.shape[1] * shards) * rows
-        for master, rows in zip(masters, row_blocks(moves.run()[0]))
+        master * (1.0 - RATE_MUON * DECAY_MUON)
+        - RATE_MUON
+        * 0.2
+        * math.sqrt(master.shape[1] * shards)
+        * rows_of(which, lambda which, part: update[which * members + part])
+        for which, master in enumerate(masters)
     ]
 
     moves = Moves("copies", ids)

time: 1080 us -> 962 us (0.89)
  Pallas kernels: 766 us -> 659 us
    pallas_call x24, Pallas kernels: 645 us -> 543 us  [run(): pl.pallas_call(self.kernel, out_shape=self.outputs, in_specs=self.operand...]
    transpose x2 -> x0, local copies, waits for them, and re-layouts: 12.9 us -> none  [fast_body(): jnp.moveaxis(item, 0, 1).reshape(item.shape[1], -1)]
    unnamed x446 -> x415, local copies, waits for them, and re-layouts: 37.1 us -> 45.8 us
  transfers between devices with their start and end apart: 6 -> 6, of which waited for: 1 -> 1; matrix products, arithmetic and copies ran while one was open for 4% -> 4% of each run, Pallas kernels for 10% -> 11%
where the time goes in v3:
time: 962 us; the launch traced here: 954 us
  Pallas kernels  659 us (69%)
  other arithmetic  95.6 us (10%)
  matrix products  91.7 us (10%)
  local copies, waits for them, and re-layouts  83.1 us (9%)
  between operations  12.1 us (1%)
    pallas_call x24, Pallas kernels, run(): pl.pallas_call(self.kernel, out_shape=self.outputs, in_specs=self.operand...  543 us
    pallas_call x1, Pallas kernels, newton_schulz(): pl.pallas_call(newton_kernel, out_shape=jax.ShapeDtypeStruct(block.shape,...  69.5 us
    unnamed x415, local copies, waits for them, and re-layouts  45.8 us
    dot_general x13, matrix products, product(): return jnp.dot(left, right, preferred_element_type=jnp.float32)  40 us
    dot_general x11, matrix products, contract(): lax.dot_general(left, right, (((left_dim,), (right_dim,)), ((), ())), pre...  27.6 us
    pallas_call x2, Pallas kernels, attention_back(): pl.pallas_call(functools.partial(attention_back_kernel, heads), out_shape...  23.5 us
    dot_general x6, matrix products, rows_product(): lax.dot_general(flat_left, flat_right, (((0,), (0,)), ((), ())), preferre...  19.3 us
  transfers between devices with their start and end apart: 6, of which 1 were waited for; matrix products, arithmetic and copies ran while one was open for 4% of the time, Pallas kernels for 11%

profile of v3, /device:TPU:0, one launch (start us, length us, event | category | flops | bytes accessed | tf_op | source)
XLA Modules:
  0.0 954.4 jit_solution(1271673354773436560)
XLA Ops:
  4.9 5.3 tables.1
  18.0 55.5 %weights.1 = (f32[4,2,1536]{2,1,0:T(2,128)}, bf16[128,1024]{1,0:T(8,128)(2,1)}, bf16[768,1024]{1,0:T(8,128)(2,1)}, bf16[1024,1024]{1,0:T(8,128)(2,1)}, bf16[1024,3072]{1,0:T(8,128)(2,1)}) custom-call(f32[4,2,1536]{2,1,0:T(2,128)} %reshape.528.refs_0_, bf16[128,256]{1,0:T(8,128)(2,1)} %convert_element_type.355.refs_1_, bf16[768,256]{1,0:T(8,128)(2,1)} %bitcast.213, ...), custom_call_target="tpu_custom_call" | custom-call | tf_op jit(solution)/shard_map/weights/pallas_call | solution.py:662
  83.6 4.8 convolution_convert_fusion.1.refs_0_
  88.4 18.0 %heads0.1 = (bf16[3,1024,128]{2,1,0:T(8,128)(2,1)}, bf16[4,128,1024]{2,1,0:T(8,128)(2,1)}) custom-call(bf16[128,3072]{1,0:T(8,128)(2,1)} %convolution_convert_fusion.1.refs_0_, bf16[128,1024]{1,0:T(8,128)(2,1)} %copy-done.57), custom_call_target="tpu_custom_call" | custom-call | tf_op jit(solution)/shard_map/heads0/pallas_call | solution.py:662
  107.5 6.4 attention.2
  116.5 14.3 %mixed_rows.2 = (bf16[128,1024]{1,0:T(8,128)(2,1)}, bf16[4,128,384]{2,1,0:T(8,128)(2,1)}) custom-call(bf16[1,1024,128]{2,1,0:T(8,128)(2,1)} %bitcast.209, bf16[128,384]{1,0:T(8,128)(2,1)} %pad.47.refs_1_), custom_call_target="tpu_custom_call" | custom-call | tf_op jit(solution)/shard_map/mixed_rows/pallas_call | solution.py:662
  130.8 3.1 fusion.166
  137.2 15.7 %tokens_moment.2 = (bf16[4,128,1024]{2,1,0:T(8,128)(2,1)}, bf16[8,64,512]{2,1,0:T(8,128)(2,1)}) custom-call(bf16[128,1024]{1,0:T(8,128)(2,1)} %add_convert_fusion.2.refs_0_, bf16[8,64,512]{2,1,0:T(8,128)(2,1)} %get-tuple-element.268.refs_1_), custom_call_target="tpu_custom_call" | custom-call | tf_op jit(solution)/shard_map/tokens_moment/pallas_call | solution.py:662
  152.9 4.9 multiply_convert_fusion.1
  160.1 13.8 %token_sums.4 = bf16[4,128,1024]{2,1,0:T(8,128)(2,1)} custom-call(bf16[4,128,1024]{2,1,0:T(8,128)(2,1)} %bitcast.225), custom_call_target="tpu_custom_call" | custom-call | tf_op jit(solution)/shard_map/token_sums/pallas_call | solution.py:662
  181.1 4.8 convolution_convert_fusion.refs_0_
  185.8 23.7 %heads1.1 = (bf16[3,1024,128]{2,1,0:T(8,128)(2,1)}, bf16[4,128,1024]{2,1,0:T(8,128)(2,1)}, bf16[4,128,1024]{2,1,0:T(8,128)(2,1)}) custom-call(bf16[128,3072]{1,0:T(8,128)(2,1)} %convolution_convert_fusion.refs_0_, bf16[128,1024]{1,0:T(8,128)(2,1)} %copy-done.56, bf16[128,1024]{1,0:T(8,128)(2,1)} %get-tuple-element.105.refs_2_), custom_call_target="tpu_custom_call" | custom-call | tf_op jit(solution)/shard_map/heads1/pallas_call | solution.py:662
  210.6 6.5 attention.3
  217.9 9.1 mixed_rows.3
  227.0 3.0 fusion.164
  231.7 14.9 %tokens_moment.3 = (bf16[4,128,1024]{2,1,0:T(8,128)(2,1)}, bf16[8,64,512]{2,1,0:T(8,128)(2,1)}) custom-call(bf16[128,1024]{1,0:T(8,128)(2,1)} %add_convert_fusion.refs_0_, bf16[8,64,512]{2,1,0:T(8,128)(2,1)} %get-tuple-element.267.refs_1_), custom_call_target="tpu_custom_call" | custom-call | tf_op jit(solution)/shard_map/tokens_moment/pallas_call | solution.py:662
  246.6 4.9 multiply_convert_fusion
  253.8 13.0 %token_sums.5 = bf16[4,128,1024]{2,1,0:T(8,128)(2,1)} custom-call(bf16[4,128,1024]{2,1,0:T(8,128)(2,1)} %bitcast.226), custom_call_target="tpu_custom_call" | custom-call | tf_op jit(solution)/shard_map/token_sums/pallas_call | solution.py:662
  276.1 2.9 multiply_reduce_fusion.26
  283.1 11.0 %tokens.2 = bf16[4,128,1024]{2,1,0:T(8,128)(2,1)} custom-call(bf16[128,1024]{1,0:T(8,128)(2,1)} %multiply_convert_fusion.5.refs_0_), custom_call_target="tpu_custom_call" | custom-call | tf_op jit(solution)/shard_map/tokens/pallas_call | solution.py:662
  294.1 5.0 fusion.13
  301.4 13.5 %token_sums.6 = bf16[4,128,1024]{2,1,0:T(8,128)(2,1)} custom-call(bf16[4,128,1024]{2,1,0:T(8,128)(2,1)} %bitcast.227), custom_call_target="tpu_custom_call" | custom-call | tf_op jit(solution)/shard_map/token_sums/pallas_call | solution.py:662
  322.6 10.0 %mixed_heads1.1 = bf16[1,1024,128]{2,1,0:T(8,128)(2,1)} custom-call(bf16[128,1024]{1,0:T(8,128)(2,1)} %convolution_convert_fusion.7.refs_0_), custom_call_target="tpu_custom_call" | custom-call | tf_op jit(solution)/shard_map/mixed_heads1/pallas_call | solution.py:662
  334.7 11.9 %attention_back.2.refs_0_ = bf16[3,1024,128]{2,1,0:T(8,128)(2,1)S(1)} custom-call(bf16[3,1024,128]{2,1,0:T(8,128)(2,1)S(1)} %copy-done.9, bf16[1024,128]{1,0:T(8,128)(2,1)S(1)} %bitcast.208), custom_call_target="tpu_custom_call" | custom-call | tf_op jit(solution)/shard_map/attention_back/pallas_call | solution.py:994
  347.5 24.5 %rows1.1 = (bf16[128,3072]{1,0:T(8,128)(2,1)}, bf16[4,128,256]{2,1,0:T(8,128)(2,1)}, bf16[4,128,256]{2,1,0:T(8,128)(2,1)}, bf16[4,128,384]{2,1,0:T(8,128)(2,1)}, bf16[4,128,1024]{2,1,0:T(8,128)(2,1)}) custom-call(bf16[3,1024,128]{2,1,0:T(8,128)(2,1)} %copy-done.5, bf16[128,1024]{1,0:T(8,128)(2,1)} %copy-done.60, bf16[128,1024]{1,0:T(8,128)(2,1)} %copy-done.82, ...), custom_call_target="tpu_custom_call" | custom-call | tf_op jit(solution)/shard_map/rows1/pallas_call | solution.py:662
  372.0 5.6 multiply_reduce_fusion.5
  382.1 11.5 %tokens.3 = bf16[4,128,1024]{2,1,0:T(8,128)(2,1)} custom-call(bf16[128,1024]{1,0:T(8,128)(2,1)} %multiply_convert_fusion.3.refs_0_), custom_call_target="tpu_custom_call" | custom-call | tf_op jit(solution)/shard_map/tokens/pallas_call | solution.py:662
  393.6 5.0 fusion.6
  399.6 4.4 fusion.22
  407.4 4.1 fusion.29
  416.9 12.7 %token_sums.7 = bf16[4,128,1024]{2,1,0:T(8,128)(2,1)} custom-call(bf16[4,128,1024]{2,1,0:T(8,128)(2,1)} %bitcast.224), custom_call_target="tpu_custom_call" | custom-call | tf_op jit(solution)/shard_map/token_sums/pallas_call | solution.py:662
  436.1 21.6 %mixed_heads0.1 = (bf16[1,1024,128]{2,1,0:T(8,128)(2,1)}, bf16[4,128,768]{2,1,0:T(8,128)(2,1)}, bf16[4,128,256]{2,1,0:T(8,128)(2,1)}) custom-call(bf16[128,1024]{1,0:T(8,128)(2,1)} %convolution_convert_fusion.6.refs_0_, bf16[128,3072]{1,0:T(8,128)(2,1)} %get-tuple-element.113.refs_1_, bf16[128,1024]{1,0:T(8,128)(2,1)} %copy-done.83), custom_call_target="tpu_custom_call" | custom-call | tf_op jit(solution)/shard_map/mixed_heads0/pallas_call | solution.py:662
  459.8 11.7 %attention_back.3.refs_0_ = bf16[3,1024,128]{2,1,0:T(8,128)(2,1)S(1)} custom-call(bf16[3,1024,128]{2,1,0:T(8,128)(2,1)S(1)} %copy-done.7, bf16[1024,128]{1,0:T(8,128)(2,1)S(1)} %bitcast.211), custom_call_target="tpu_custom_call" | custom-call | tf_op jit(solution)/shard_map/attention_back/pallas_call | solution.py:994
  472.4 16.1 %rows0.1 = (bf16[128,3072]{1,0:T(8,128)(2,1)}, bf16[4,128,256]{2,1,0:T(8,128)(2,1)}, bf16[4,128,256]{2,1,0:T(8,128)(2,1)}, bf16[4,128,384]{2,1,0:T(8,128)(2,1)}) custom-call(bf16[3,1024,128]{2,1,0:T(8,128)(2,1)} %copy-done.10, bf16[128,1024]{1,0:T(8,128)(2,1)} %copy-done.61, bf16[128,1024]{1,0:T(8,128)(2,1)} %copy-done.62, bf16[128,384]{1,0:T(8,128)(2,1)} %copy-done.104), custom_call_target="tpu_custom_call" | custom-call | tf_op jit(solution)/shard_map/rows0/pallas_call | solution.py:662
  488.6 5.5 multiply_reduce_fusion.9
  501.4 3.7 fusion.178
  511.1 23.6 %samples.1 = (bf16[4,128,768]{2,1,0:T(8,128)(2,1)}, bf16[4,128,256]{2,1,0:T(8,128)(2,1)}, f32[4,3,1536]{2,1,0:T(4,128)}, bf16[3,448,512]{2,1,0:T(8,128)(2,1)}, bf16[3,448,512]{2,1,0:T(8,128)(2,1)}) custom-call(bf16[128,3072]{1,0:T(8,128)(2,1)} %get-tuple-element.119.refs_0_, bf16[128,1024]{1,0:T(8,128)(2,1)} %get-tuple-element.244.refs_1_, ...), custom_call_target="tpu_custom_call" | custom-call | tf_op jit(solution)/shard_map/samples/pallas_call | solution.py:662
  540.8 4.1 fusion.177
  544.9 42.7 %member_sums.1 = (bf16[1,1024,384]{2,1,0:T(8,128)(2,1)}, bf16[1,1024,128]{2,1,0:T(8,128)(2,1)}, bf16[8,112,128]{2,1,0:T(8,128)(2,1)}, bf16[8,96,256]{2,1,0:T(8,1...) custom-call(bf16[1024,768]{1,0:T(8,128)(2,1)} %get-tuple-element.314.refs_0_, ...), custom_call_target="tpu_custom_call" | custom-call | tf_op jit(solution)/shard_map/member_sums/pallas_call | solution.py:662
  596.9 32.5 %group_sums.1 = (bf16[3,1024,128]{2,1,0:T(8,128)(2,1)S(1)}, f32[1024,384]{1,0:T(8,128)S(1)}, f32[4,8,1024]{2,1,0:T(8,128)S(1)}, f32[4,1,1792]{2,1,0:T(1,128)S(1)}) custom-call(bf16[1024,128]{1,0:T(8,128)(2,1)S(1)} %fusion.99.refs_0_, f32[1024,384]{1,0:T(8,128)S(1)} %convert_add_fusion.2.refs_1_, f32[8,1024]{1,0:T(8,128)S(1)} %fusion.181.refs_2_, ...), custom_call_target="tpu_custom_call" | custom-call | tf_op jit(solution)/shard_map/group_sums/pallas_call | solution.py:662
  635.1 4.0 fusion.158
  654.5 6.6 collective-permute-done.2
  661.7 10.5 %total.1 = f32[8,128]{1,0:T(8,128)} custom-call(f32[8,128]{1,0:T(8,128)} %broadcast_in_dim.49.x_ref), custom_call_target="tpu_custom_call" | custom-call | tf_op jit(solution)/shard_map/total/pallas_call | solution.py:903
  684.3 44.8 %columns.1.gram_ref = f32[1024,1024]{1,0:T(8,128)S(1)} custom-call(bf16[1024,512]{1,0:T(8,128)(2,1)S(1)} %fusion.43.refs_0_.block_ref), custom_call_target="tpu_custom_call" | custom-call | tf_op jit(solution)/shard_map/columns/pallas_call | solution.py:662
  733.6 69.5 %newton.1 = bf16[1024,512]{1,0:T(8,128)(2,1)S(1)} custom-call(f32[1024,1024]{1,0:T(8,128)} %copy-done.1, bf16[1024,512]{1,0:T(8,128)(2,1)S(1)} %copy-done.3), custom_call_target="tpu_custom_call" | custom-call | tf_op jit(solution)/shard_map/newton/pallas_call | solution.py:1090
  804.1 18.5 %update_rows.1 = bf16[8,128,512]{2,1,0:T(8,128)(2,1)} custom-call(bf16[8,128,512]{2,1,0:T(8,128)(2,1)} %bitcast.207), custom_call_target="tpu_custom_call" | custom-call | tf_op jit(solution)/shard_map/update_rows/pallas_call | solution.py:662
  836.0 76.8 %copies.1 = (bf16[1024,768]{1,0:T(8,128)(2,1)}, bf16[1024,1024]{1,0:T(8,128)(2,1)}, bf16[1024,1024]{1,0:T(8,128)(2,1)}, bf16[1024,256]{1,0:T(8,128)(2,1)}) custom-call(bf16[128,768]{1,0:T(8,128)(2,1)} %get-tuple-element.221.refs_0_, bf16[128,1024]{1,0:T(8,128)(2,1)} %get-tuple-element.219.refs_1_, bf16[128,1024]{1,0:T(8,128)(2,1)} %get-tuple-element.217.refs_2_, ...), custom_call_target="tpu_custom_call" | custom-call | tf_op jit(solution)/shard_map/copies/pallas_call | solution.py:662
  940.1 2.9 divide_subtract_fusion.1
  (624 shorter events, 203.8 us)
Async XLA Ops:
  0.7 12.6 %copy-start = (bf16[1024,1536]{1,0:T(8,128)(2,1)S(1)}, bf16[1024,1536]{1,0:T(8,128)(2,1)}, u32[]{:S(2)}) copy-start(bf16[1024,1536]{1,0:T(8,128)(2,1)} %param.49) | copy-start | bytes 9437188
  0.7 13.8 %copy-start.97 = (f32[128,256]{1,0:T(8,128)S(1)}, f32[128,256]{1,0:T(8,128)}, u32[]{:S(2)}) copy-start(f32[128,256]{1,0:T(8,128)} %param.59) | copy-start | bytes 393220
  18.0 59.2 %copy-start.58 = (bf16[2,384,256]{2,1,0:T(8,128)(2,1)S(1)}, bf16[2,384,256]{2,1,0:T(8,128)(2,1)}, u32[]{:S(2)}) copy-start(bf16[2,384,256]{2,1,0:T(8,128)(2,1)} %pad.49.clone) | copy-start | bytes 1179652
  80.6 7.8 copy-start.151
  88.4 42.4 %copy-start.118 = (f32[1,1024]{1,0:T(1,128)S(1)}, f32[1,1024]{1,0:T(1,128)}, u32[]{:S(2)}) copy-start(f32[1,1024]{1,0:T(1,128)} %get-tuple-element.294) | copy-start | bytes 12292
  160.1 15.4 %copy-start.119 = (f32[1,1024]{1,0:T(1,128)S(1)}, f32[1,1024]{1,0:T(1,128)}, u32[]{:S(2)}) copy-start(f32[1,1024]{1,0:T(1,128)} %get-tuple-element.289) | copy-start | bytes 12292
  179.1 6.7 copy-start.87
  266.8 7.2 copy-start.183
  269.7 6.4 copy-start.148
  273.9 7.6 copy-start.82
  301.3 15.9 %copy-start.147 = (f32[128]{0:T(128)S(1)}, f32[128]{0:T(128)}, u32[]{:S(2)}) copy-start(f32[128]{0:T(128)} %copy-done.146) | copy-start | bytes 1540
  301.4 15.9 %copy-start.160 = (f32[128]{0:T(128)S(1)}, f32[128]{0:T(128)}, u32[]{:S(2)}) copy-start(f32[128]{0:T(128)} %copy-done.159) | copy-start | bytes 1540
  321.0 25.6 %copy-start.60 = (bf16[128,1024]{1,0:T(8,128)(2,1)}, bf16[128,1024]{1,0:T(8,128)(2,1)S(1)}, u32[]{:S(2)}) copy-start(bf16[128,1024]{1,0:T(8,128)(2,1)S(1)} %multiply_convert_fusion.4.refs_1_) | copy-start | bytes 786436
  322.6 49.4 %copy-start.145 = (f32[128]{0:T(128)S(1)}, f32[128]{0:T(128)}, u32[]{:S(2)}) copy-start(f32[128]{0:T(128)} %copy-done.144) | copy-start | bytes 1540
  322.6 49.4 %copy-start.158 = (f32[128]{0:T(128)S(1)}, f32[128]{0:T(128)}, u32[]{:S(2)}) copy-start(f32[128]{0:T(128)} %copy-done.157) | copy-start | bytes 1540
  372.0 6.6 copy-start.33
  372.0 6.5 copy-start.168
  372.0 6.5 copy-start.184
  406.8 99.0 %collective-permute-start = (bf16[1024,512]{1,0:T(8,128)(2,1)}, bf16[1024,512]{1,0:T(8,128)(2,1)}, u32[]{:S(2)}, u32[]{:S(2)}) collective-permute-start(bf16[1024,512]{1,0:T(8,128)(2,1)} %dynamic-slice_convert_fusion.1), channel_id=1, source_target_pairs={{0,4},{4,0},{8,12},{12,8},{16,20},{20,16},{24,28},{28,24},{1,5},{5... | collective-permute-start | bytes 3145736 | tf_op jit(solution)/shard_map/ppermute | solution.py:1292
  407.4 6.7 copy-start.190
  412.7 95.9 %collective-permute-start.1 = (bf16[1024,512]{1,0:T(8,128)(2,1)}, bf16[1024,512]{1,0:T(8,128)(2,1)}, u32[]{:S(2)}, u32[]{:S(2)}) collective-permute-start(bf16[1024,512]{1,0:T(8,128)(2,1)} %dynamic-slice_convert_fusion), channel_id=1, source_target_pairs={{0,4},{4,0},{8,12},{12,8},{16,20},{20,16},{24,28},{28,24},{1,5},{5... | collective-permute-start | bytes 3145736 | tf_op jit(solution)/shard_map/ppermute | solution.py:1292
  416.9 15.0 %copy-start.141 = (f32[128]{0:T(128)S(1)}, f32[128]{0:T(128)}, u32[]{:S(2)}) copy-start(f32[128]{0:T(128)} %copy-done.140) | copy-start | bytes 1540
  416.9 15.0 %copy-start.154 = (f32[128]{0:T(128)S(1)}, f32[128]{0:T(128)}, u32[]{:S(2)}) copy-start(f32[128]{0:T(128)} %copy-done.153) | copy-start | bytes 1540
  434.5 36.9 %copy-start.61 = (bf16[128,1024]{1,0:T(8,128)(2,1)}, bf16[128,1024]{1,0:T(8,128)(2,1)S(1)}, u32[]{:S(2)}) copy-start(bf16[128,1024]{1,0:T(8,128)(2,1)S(1)} %multiply_convert_fusion.2.refs_1_) | copy-start | bytes 786436
  436.1 52.4 %copy-start.139 = (f32[128]{0:T(128)S(1)}, f32[128]{0:T(128)}, u32[]{:S(2)}) copy-start(f32[128]{0:T(128)} %copy-done.138) | copy-start | bytes 1540
  436.1 52.4 %copy-start.152 = (f32[128]{0:T(128)S(1)}, f32[128]{0:T(128)}, u32[]{:S(2)}) copy-start(f32[128]{0:T(128)} %copy-done.151) | copy-start | bytes 1540
  488.5 7.2 copy-start.165
  488.5 7.8 copy-start.131
  488.5 7.8 copy-start.129
  488.6 7.8 copy-start.130
  488.6 7.8 copy-start.128
  488.6 7.8 copy-start.179
  488.6 7.8 copy-start.180
  488.6 7.8 copy-start.181
  488.6 7.8 copy-start.182
  595.0 34.5 %copy-start.73 = (bf16[3,576,512]{2,1,0:T(8,128)(2,1)S(1)}, bf16[3,576,512]{2,1,0:T(8,128)(2,1)}, u32[]{:S(2)}) copy-start(bf16[3,576,512]{2,1,0:T(8,128)(2,1)} %get-tuple-element.139) | copy-start | bytes 5308420
  596.9 32.9 %copy-start.79 = (bf16[3,448,512]{2,1,0:T(8,128)(2,1)S(1)}, bf16[3,448,512]{2,1,0:T(8,128)(2,1)}, u32[]{:S(2)}) copy-start(bf16[3,448,512]{2,1,0:T(8,128)(2,1)} %get-tuple-element.138) | copy-start | bytes 4128772
  641.7 8.0 copy-start.112
  641.7 8.0 copy-start.133
  644.9 16.2 %collective-permute-start.2 = (bf16[4,176,512]{2,1,0:T(8,128)(2,1)}, bf16[4,176,512]{2,1,0:T(8,128)(2,1)}, u32[]{:S(2)}, u32[]{:S(2)}) collective-permute-start(bf16[4,176,512]{2,1,0:T(8,128)(2,1)} %get-tuple-element.257), channel_id=1, source_target_pairs={{0,4},{4,0},{8,12},{12,8},{16,20},{20,16},{24,28},{28,24},{1,5},{5... | collective-permute-start | bytes 2162696 | tf_op jit(solution)/shard_map/ppermute | solution.py:1537
  675.1 7.0 copy-start.18
  675.2 7.0 copy-start.49
  678.3 54.0 %collective-permute-start.3 = (bf16[2,176,512]{2,1,0:T(8,128)(2,1)}, bf16[2,176,512]{2,1,0:T(8,128)(2,1)}, u32[]{:S(2)}, u32[]{:S(2)}) collective-permute-start(bf16[2,176,512]{2,1,0:T(8,128)(2,1)} %get-tuple-element.255), channel_id=1, source_target_pairs={{0,8},{4,12},{8,16},{12,20},{16,24},{20,28},{24,0},{28,4},{1,9},{5... | collective-permute-start | bytes 1081352 | tf_op jit(solution)/shard_map/ppermute | solution.py:1560
  679.0 53.4 %collective-permute-start.4 = (bf16[2,176,512]{2,1,0:T(8,128)(2,1)}, bf16[2,176,512]{2,1,0:T(8,128)(2,1)}, u32[]{:S(2)}, u32[]{:S(2)}) collective-permute-start(bf16[2,176,512]{2,1,0:T(8,128)(2,1)} %get-tuple-element.256), channel_id=1, source_target_pairs={{0,16},{4,20},{8,24},{12,28},{16,0},{20,4},{24,8},{28,12},{1,17},{... | collective-permute-start | bytes 1081352 | tf_op jit(solution)/shard_map/ppermute | solution.py:1560
  679.7 52.7 %collective-permute-start.5 = (bf16[2,176,512]{2,1,0:T(8,128)(2,1)}, bf16[2,176,512]{2,1,0:T(8,128)(2,1)}, u32[]{:S(2)}, u32[]{:S(2)}) collective-permute-start(bf16[2,176,512]{2,1,0:T(8,128)(2,1)} %get-tuple-element.253), channel_id=1, source_target_pairs={{0,24},{4,28},{8,0},{12,4},{16,8},{20,12},{24,16},{28,20},{1,25},{... | collective-permute-start | bytes 1081352 | tf_op jit(solution)/shard_map/ppermute | solution.py:1560
  684.3 44.8 %copy-start.2 = (bf16[1024,512]{1,0:T(8,128)(2,1)}, bf16[1024,512]{1,0:T(8,128)(2,1)S(1)}, u32[]{:S(2)}) copy-start(bf16[1024,512]{1,0:T(8,128)(2,1)S(1)} %fusion.43.refs_0_.block_ref) | copy-start | bytes 3145732
  836.0 97.7 %copy-start.76 = (f32[128,768]{1,0:T(8,128)S(1)}, f32[128,768]{1,0:T(8,128)}, u32[]{:S(2)}) copy-start(f32[128,768]{1,0:T(8,128)} %param.39) | copy-start | bytes 1179652
  933.7 6.3 copy-start.63
  (150 other events, 470.0 us)

commit v4 on v3

--- a/solution.py
+++ b/solution.py
@@ -678,7 +678,8 @@
             name=self.name,
         )(*self.operands)
 
-    def along(self, axis, source, target, pairs):
+    def along(self, axis, source, target, pairs, later=False):
+        numbers = []
         count = lax.axis_size(axis)
 
         def other(shift):
@@ -686,13 +687,16 @@
 
         for shift in range(1, count):
             for source_at, target_at in pairs:
-                self.move(
-                    (axis, shift),
-                    lambda shift=shift: {axis: other(shift)},
-                    source,
-                    None if source_at is None else (lambda at=source_at, shift=shift: at(other(shift))),
-                    target,
-                    lambda at=target_at: at(lax.axis_index(axis)),
+                numbers.append(
+                    self.move(
+                        (axis, shift),
+                        lambda shift=shift: {axis: other(shift)},
+                        source,
+                        None if source_at is None else (lambda at=source_at, shift=shift: at(other(shift))),
+                        target,
+                        lambda at=target_at: at(lax.axis_index(axis)),
+                        later=later,
+                    )
                 )
         for source_at, target_at in pairs:
             self.keep(
@@ -701,12 +705,13 @@
                 target,
                 lambda at=target_at: at(lax.axis_index(axis)),
             )
+        return numbers
 
     def gather(self, axis, array):
         target = self.output((lax.axis_size(axis),) + array.shape, array.dtype)
         self.along(axis, self.operand(array), target, [(None, lambda sender: (sender,))])
 
-    def gather_pairs(self, array, parts=1):
+    def gather_pairs(self, array, parts=1, hold=False):
         shards = lax.axis_size(SHARDS)
         source = self.operand(array)
         target = self.output((shards,) + array.shape, array.dtype)
@@ -730,7 +735,10 @@
         own = lambda: (lax.axis_index(SHARDS),)
         self.move((SHARDS,), sibling_peer, source, None, target, own)
         self.keep(source, None, target, own)
-        self.to_sibling([(target, at, number) for at, number in firsts])
+        waiting = [(target, at, number) for at, number in firsts]
+        if hold:
+            return waiting
+        self.to_sibling(waiting)
 
     def gather_columns(self, axis, array):
         width = array.shape[-1]
@@ -799,9 +807,11 @@
         for target, place, number in waiting:
             self.move((SHARDS,), sibling_peer, target, place, target, place, (number,))
 
-    def exchange(self, axis, array):
+    def exchange(self, axis, array, later=False):
         target = self.output(array.shape, array.dtype)
-        self.along(axis, self.operand(array), target, [(lambda receiver: (receiver,), lambda sender: (sender,))])
+        return self.along(
+            axis, self.operand(array), target, [(lambda receiver: (receiver,), lambda sender: (sender,))], later
+        )
 
     def exchange_columns(self, axis, array):
         width = array.shape[-1] // lax.axis_size(axis)
@@ -818,12 +828,11 @@
             ],
         )
 
-    def rows_to_heads(self, axis, array, planes):
+    def rows_to_heads(self, axis, array, planes, target):
         count, rows = lax.axis_size(axis), array.shape[0]
         columns = array.shape[1] // planes
         width = columns // count
-        target = self.output((planes, rows * count, width), array.dtype)
-        self.along(
+        return self.along(
             axis,
             self.operand(array),
             target,
@@ -839,85 +848,82 @@
             ],
         )
 
-    def heads_to_rows(self, axis, array):
+    def head_rows(self, source, target, planes, rows, columns, members, back_group):
+        count = lax.axis_size(PATCHES)
+        width = columns // count
+        for shift_member in range(members):
+            for plane in planes:
+
+                def peer(shift_member=shift_member):
+                    index = lax.axis_index(PATCHES)
+                    there = lax.rem(index // members + back_group, MATRICES) * members
+                    return there + lax.rem(lax.rem(index, members) + shift_member, members)
+
+                def source_at(peer=peer, plane=plane):
+                    return (plane, pl.ds(pl.multiple_of(peer() * rows, rows), rows))
+
+                def target_at(plane=plane):
+                    start = plane * columns + lax.axis_index(PATCHES) * width
+                    return (slice(None), pl.ds(pl.multiple_of(start, LANES), width))
+
+                if shift_member or back_group:
+                    self.start(
+                        self.move(
+                            (PATCHES, count, back_group, shift_member),
+                            lambda peer=peer: {PATCHES: peer()},
+                            source,
+                            source_at,
+                            target,
+                            target_at,
+                            later=True,
+                        )
+                    )
+                else:
+
+                    def own(ref, source_at=source_at, target_at=target_at):
+                        ref(target)[target_at()] = ref(source)[source_at()]
+
+                    self.task(own)
+
+
+def total_of(ids, values, shared):
+    moves = Moves("total", ids)
+    source, result = moves.operand(values, pltpu.VMEM), moves.output(values.shape, values.dtype, pltpu.VMEM)
+    moves.gather(PATCHES, shared)
+    for axis in (SHARDS, PATCHES):
         count = lax.axis_size(axis)
-        planes, all_rows, width = array.shape
-        rows, columns = all_rows // count, width * count
-        target = self.output((rows, planes * columns), array.dtype)
-        self.along(
-            axis,
-            self.operand(array),
-            target,
-            [
-                (
-                    lambda receiver, plane=plane: (plane, pl.ds(pl.multiple_of(receiver * rows, rows), rows)),
-                    lambda sender, plane=plane: (
-                        slice(None),
-                        pl.ds(pl.multiple_of(plane * columns + sender * width, LANES), width),
-                    ),
+        buffer = moves.scratch((count,) + values.shape, values.dtype)
+
+        def own(axis=axis):
+            return (lax.axis_index(axis),)
+
+        def put(ref, source=source, buffer=buffer, own=own):
+            ref(buffer)[own()] = ref(source)[...]
+
+        moves.task(put)
+        numbers = []
+        for shift in range(1, count):
+            numbers.append(
+                moves.move(
+                    (axis, shift),
+                    lambda axis=axis, shift=shift, count=count: {axis: lax.rem(lax.axis_index(axis) + shift, count)},
+                    buffer,
+                    own,
+                    buffer,
+                    own,
+                    later=True,
                 )
-                for plane in range(planes)
-            ],
-        )
-
-
-def total_kernel(x_ref, o_ref, near, far, near_send, near_recv, far_send, far_recv):
-    near_count, far_count = near.shape[0], far.shape[0]
-    near_me, far_me = lax.axis_index(SHARDS), lax.axis_index(PATCHES)
-    barrier = pltpu.get_barrier_semaphore()
-    for shift in range(1, near_count):
-        pl.semaphore_signal(
-            barrier, inc=1, device_id={SHARDS: lax.rem(near_me + shift, near_count)}, device_id_type=MESH
-        )
-    for shift in range(1, far_count):
-        pl.semaphore_signal(
-            barrier, inc=1, device_id={PATCHES: lax.rem(far_me + shift, far_count)}, device_id_type=MESH
-        )
-    pl.semaphore_wait(barrier, near_count + far_count - 2)
-
-    def spread(axis, me, count, buffer, send, recv):
-        copies = []
-        for shift in range(1, count):
-            copy = pltpu.make_async_remote_copy(
-                src_ref=buffer.at[me],
-                dst_ref=buffer.at[me],
-                send_sem=send.at[shift - 1],
-                recv_sem=recv.at[shift - 1],
-                device_id={axis: lax.rem(me + shift, count)},
-                device_id_type=MESH,
             )
-            copy.start()
-            copies.append(copy)
-        for copy in copies:
-            copy.wait()
-        return jnp.sum(buffer[...], 0)
-
-    near[near_me] = x_ref[...]
-    far[far_me] = spread(SHARDS, near_me, near_count, near, near_send, near_recv)
-    o_ref[...] = spread(PATCHES, far_me, far_count, far, far_send, far_recv)
-
-
-def total_of(ids, values):
-    near_count, far_count = lax.axis_size(SHARDS), lax.axis_size(PATCHES)
-    in_vmem = pl.BlockSpec(memory_space=pltpu.VMEM)
-    return pl.pallas_call(
-        total_kernel,
-        out_shape=jax.ShapeDtypeStruct(values.shape, values.dtype),
-        in_specs=[in_vmem],
-        out_specs=in_vmem,
-        scratch_shapes=[
-            pltpu.VMEM((near_count,) + values.shape, values.dtype),
-            pltpu.VMEM((far_count,) + values.shape, values.dtype),
-            pltpu.SemaphoreType.DMA((near_count - 1,)),
-            pltpu.SemaphoreType.DMA((near_count - 1,)),
-            pltpu.SemaphoreType.DMA((far_count - 1,)),
-            pltpu.SemaphoreType.DMA((far_count - 1,)),
-        ],
-        compiler_params=pltpu.CompilerParams(
-            collective_id=ids.setdefault("total", len(ids)), has_side_effects=True
-        ),
-        name="total",
-    )(values)
+            moves.start(numbers[-1])
+        for number in numbers:
+            moves.wait_for(number)
+
+        def add(ref, buffer=buffer):
+            ref(result)[...] = jnp.sum(ref(buffer)[...], 0)
+
+        moves.task(add)
+        source = result
+    return moves.run()
 
 
 def contract(left, right, left_dim, right_dim):
@@ -926,176 +932,168 @@
     )
 
 
-QUERY_BLOCK = 256
 CHAIN_CHUNKS = 8
-GRAM_ROWS = 256
-
-
-def attention_kernel(heads, qkv_ref, mixed_ref):
-    rows = pl.ds(pl.multiple_of(pl.program_id(0) * QUERY_BLOCK, QUERY_BLOCK), QUERY_BLOCK)
-    mixed = []
-    for head in range(heads):
-        lanes = pl.ds(head * HEAD, HEAD)
-        queries, keys, values = qkv_ref[0, rows, lanes], qkv_ref[1, :, lanes], qkv_ref[2, :, lanes]
-        scores = contract(queries, keys, 1, 1) * HEAD ** (-0.5)
-        expo = jnp.exp(scores - jnp.max(scores, -1, keepdims=True))
-        probs = (expo / jnp.sum(expo, -1, keepdims=True)).astype(LOW)
-        mixed.append(contract(probs, values, 1, 0))
-    mixed_ref[...] = jnp.concatenate(mixed, -1).astype(LOW)
-
-
-def attention(qkv):
-    _, patches, width = qkv.shape
-    return pl.pallas_call(
-        functools.partial(attention_kernel, width // HEAD),
-        out_shape=jax.ShapeDtypeStruct((patches, width), LOW),
-        grid=(patches // QUERY_BLOCK,),
-        in_specs=[pl.BlockSpec(qkv.shape, lambda block: (0, 0, 0))],
-        out_specs=pl.BlockSpec((QUERY_BLOCK, width), lambda block: (block, 0)),
-        compiler_params=pltpu.CompilerParams(vmem_limit_bytes=48 * 2**20),
-        name="attention",
-    )(qkv)
-
-
-def attention_back_kernel(heads, qkv_ref, grad_ref, out_ref, key_total, value_total):
-    block = pl.program_id(0)
-    rows = pl.ds(pl.multiple_of(block * QUERY_BLOCK, QUERY_BLOCK), QUERY_BLOCK)
-
-    @pl.when(block == 0)
-    def _():
-        key_total[...] = jnp.zeros_like(key_total)
-        value_total[...] = jnp.zeros_like(value_total)
-
-    query_parts = []
-    for head in range(heads):
-        lanes = pl.ds(head * HEAD, HEAD)
-        queries, keys, values = qkv_ref[0, rows, lanes], qkv_ref[1, :, lanes], qkv_ref[2, :, lanes]
-        grads = grad_ref[rows, lanes]
-        scores = contract(keys, queries, 1, 1) * HEAD ** (-0.5)
-        expo = jnp.exp(scores - jnp.max(scores, 0, keepdims=True))
-        probs = expo / jnp.sum(expo, 0, keepdims=True)
-        grad_probs = contract(values, grads, 1, 1)
-        shared = jnp.sum(grad_probs * probs, 0, keepdims=True)
-        score_grad = (HEAD ** (-0.5) * probs * (grad_probs - shared)).astype(LOW)
-        query_parts.append(contract(score_grad, keys, 0, 0))
-        key_total[head] += contract(score_grad, queries, 1, 0)
-        value_total[head] += contract(probs.astype(LOW), grads, 1, 0)
-    out_ref[0, rows, :] = jnp.concatenate(query_parts, -1).astype(LOW)
-
-    @pl.when(block == pl.num_programs(0) - 1)
-    def _():
-        out_ref[1] = jnp.concatenate([key_total[head] for head in range(heads)], -1).astype(LOW)
-        out_ref[2] = jnp.concatenate([value_total[head] for head in range(heads)], -1).astype(LOW)
-
-
-def attention_back(qkv, grads):
-    _, patches, width = qkv.shape
+GRAM_COLS = 256
+
+
+def attend(queries, keys, values):
+    scores = contract(queries, keys, 1, 1) * HEAD ** (-0.5)
+    expo = jnp.exp(scores - jnp.max(scores, -1, keepdims=True))
+    probs = (expo / jnp.sum(expo, -1, keepdims=True)).astype(LOW)
+    return contract(probs, values, 1, 0)
+
+
+def group_rows(rows, members, shift):
+    size = rows * members
+    there = lax.rem(lax.axis_index(PATCHES) // members + shift, MATRICES)
+    return pl.ds(pl.multiple_of(there * size, size), size)
+
+
+def add_attention(moves, qkv, mixed, arrivals, rows, members, waiting):
+    for number in arrivals:
+        moves.wait_for(number)
+    for number in range(3):
+        moves.wait_local(number)
+    moves.to_sibling(waiting)
+    count = lax.axis_size(PATCHES)
+    width = HEADS // count * HEAD
+    buffer = moves.scratch((1, rows * count, width), LOW)
+    for shift in (*range(1, MATRICES), 0):
+
+        def work(ref, shift=shift):
+            at = group_rows(rows, members, shift)
+            parts = []
+            for head in range(width // HEAD):
+                lanes = pl.ds(head * HEAD, HEAD)
+                parts.append(attend(ref(qkv)[0, at, lanes], ref(qkv)[1, :, lanes], ref(qkv)[2, :, lanes]))
+            ref(buffer)[0, at, :] = jnp.concatenate(parts, -1).astype(LOW)
+
+        moves.task(work)
+        moves.head_rows(buffer, mixed, (0,), rows, width * count, members, shift)
+
+
+def add_attention_back(moves, qkv, grads, result, arrivals, rows, members, waiting):
+    for number in arrivals:
+        moves.wait_for(number)
+    moves.wait_local(0)
+    moves.to_sibling(waiting)
+    count = lax.axis_size(PATCHES)
+    width = HEADS // count * HEAD
     heads = width // HEAD
-    return pl.pallas_call(
-        functools.partial(attention_back_kernel, heads),
-        out_shape=jax.ShapeDtypeStruct(qkv.shape, LOW),
-        grid=(patches // QUERY_BLOCK,),
-        in_specs=[
-            pl.BlockSpec(qkv.shape, lambda block: (0, 0, 0)),
-            pl.BlockSpec(grads.shape, lambda block: (0, 0)),
-        ],
-        out_specs=pl.BlockSpec(qkv.shape, lambda block: (0, 0, 0)),
-        scratch_shapes=[
-            pltpu.VMEM((heads, patches, HEAD), jnp.float32),
-            pltpu.VMEM((heads, patches, HEAD), jnp.float32),
-        ],
-        compiler_params=pltpu.CompilerParams(vmem_limit_bytes=48 * 2**20),
-        name="attention_back",
-    )(qkv, grads)
-
-
-def newton_kernel(gram_ref, block_ref, out_ref, gram, poly, once, gram_low, poly_low, once_low, block):
-    size = gram_ref.shape[0]
-    tiles = size // GRAM_ROWS
+    buffer = moves.scratch((3, rows * count, width), LOW)
+    key_total = moves.scratch((heads, rows * count, HEAD), jnp.float32)
+    value_total = moves.scratch((heads, rows * count, HEAD), jnp.float32)
+    for shift in (*range(1, MATRICES), 0):
+
+        def work(ref, shift=shift):
+            at = group_rows(rows, members, shift)
+            parts = []
+            for head in range(heads):
+                lanes = pl.ds(head * HEAD, HEAD)
+                queries, keys, values = ref(qkv)[0, at, lanes], ref(qkv)[1, :, lanes], ref(qkv)[2, :, lanes]
+                grad = ref(grads)[0, at, lanes]
+                scores = contract(keys, queries, 1, 1) * HEAD ** (-0.5)
+                expo = jnp.exp(scores - jnp.max(scores, 0, keepdims=True))
+                probs = expo / jnp.sum(expo, 0, keepdims=True)
+                grad_probs = contract(values, grad, 1, 1)
+                shared = jnp.sum(grad_probs * probs, 0, keepdims=True)
+                score_grad = (HEAD ** (-0.5) * probs * (grad_probs - shared)).astype(LOW)
+                parts.append(contract(score_grad, keys, 0, 0))
+                key_part = contract(score_grad, queries, 1, 0)
+                value_part = contract(probs.astype(LOW), grad, 1, 0)
+                if shift == 1:
+                    ref(key_total)[head] = key_part
+                    ref(value_total)[head] = value_part
+                else:
+                    ref(key_total)[head] += key_part
+                    ref(value_total)[head] += value_part
+            ref(buffer)[0, at, :] = jnp.concatenate(parts, -1).astype(LOW)
+
+        moves.task(work)
+        moves.head_rows(buffer, result, (0,), rows, width * count, members, shift)
+
+    def finish(ref):
+        for plane, total in ((1, key_total), (2, value_total)):
+            ref(buffer)[plane] = jnp.concatenate([ref(total)[head] for head in range(heads)], -1).astype(LOW)
+
+    moves.task(finish)
+    for shift in (*range(1, MATRICES), 0):
+        moves.head_rows(buffer, result, (1, 2), rows, width * count, members, shift)
+
+
+def newton_schulz(source, gram, poly, once, gram_low, poly_low, once_low, block, block_next):
+    size = gram.shape[0]
     eye = jnp.equal(
-        lax.broadcasted_iota(jnp.int32, (GRAM_ROWS, GRAM_ROWS), 0),
-        lax.broadcasted_iota(jnp.int32, (GRAM_ROWS, GRAM_ROWS), 1),
+        lax.broadcasted_iota(jnp.int32, (GRAM_COLS, GRAM_COLS), 0),
+        lax.broadcasted_iota(jnp.int32, (GRAM_COLS, GRAM_COLS), 1),
     ).astype(jnp.float32)
 
-    def rows_at(tile):
-        return pl.ds(pl.multiple_of(tile * GRAM_ROWS, GRAM_ROWS), GRAM_ROWS)
-
-    def over_tiles(action):
-        return lax.fori_loop(0, tiles, lambda tile, total: total + action(rows_at(tile)), jnp.float32(0.0))
-
-    def store(full, low, rows, value, mean, excess):
-        full[rows, :] = value
-        low[rows, :] = value.astype(LOW)
-        corner = full[rows, rows] - excess * eye
-        full[rows, rows] = corner
-        low[rows, rows] = (corner - mean * eye).astype(LOW)
+    def over_tiles(action, width=size):
+        def step(tile, total):
+            return total + action(pl.ds(pl.multiple_of(tile * GRAM_COLS, GRAM_COLS), GRAM_COLS))
+
+        return lax.fori_loop(0, width // GRAM_COLS, step, jnp.float32(0.0))
+
+    def store(full, low, cols, value, mean, excess):
+        full[:, cols] = value
+        low[:, cols] = value.astype(LOW)
+        corner = full[cols, cols] - excess * eye
+        full[cols, cols] = corner
+        low[cols, cols] = (corner - mean * eye).astype(LOW)
 
     def advance(gram_mean, gram_squares, last):
         poly_mean = NS_B * gram_mean + NS_C * gram_squares / size
 
-        def poly_rows(rows):
-            own = gram[rows, :]
-            value = contract(gram_low[rows, :], gram_low[...], 1, 0)
+        def poly_cols(cols):
+            own = gram[:, cols]
+            value = contract(gram_low[...], gram_low[:, cols], 1, 0)
             value = NS_C * value + (NS_B + 2.0 * NS_C * gram_mean) * own
-            store(poly, poly_low, rows, value, poly_mean, NS_C * gram_mean * gram_mean)
+            store(poly, poly_low, cols, value, poly_mean, NS_C * gram_mean * gram_mean)
             return jnp.sum(value * own)
 
-        poly_gram = over_tiles(poly_rows) - NS_C * gram_mean * gram_mean * gram_mean * size
-        once_mean = poly_gram / size
-        out_ref[...] = block[...]
-
-        def block_rows(rows):
-            left = poly_low[rows, :]
-            value = contract(left, out_ref[...], 1, 0)
-            block[rows, :] = (value + (NS_A + poly_mean) * out_ref[rows, :].astype(jnp.float32)).astype(LOW)
-            if last:
-                return jnp.float32(0.0)
-            value = contract(left, gram_low[...], 1, 0)
-            own = poly[rows, :]
-            value = value + poly_mean * gram[rows, :] + gram_mean * own
-            store(once, once_low, rows, value, once_mean, poly_mean * gram_mean)
-            return jnp.sum(value * own)
-
-        poly_once = over_tiles(block_rows) - poly_mean * gram_mean * poly_mean * size
+        once_mean = over_tiles(poly_cols) / size - NS_C * gram_mean * gram_mean * gram_mean
+
+        def block_cols(cols):
+            value = contract(poly_low[...], block[:, cols], 1, 0)
+            block_next[:, cols] = (value + (NS_A + poly_mean) * block[:, cols].astype(jnp.float32)).astype(LOW)
+            return jnp.float32(0.0)
+
+        over_tiles(block_cols, block.shape[1])
+        block[...] = block_next[...]
         if last:
             return None
-        mean_next = NS_A * NS_A * gram_mean + 2.0 * NS_A * once_mean + poly_once / size
-
-        def gram_rows(rows):
-            value = contract(poly_low[rows, :], once_low[...], 1, 0)
-            value = value + (2.0 * NS_A + poly_mean) * once[rows, :] + once_mean * poly[rows, :]
-            value = value + NS_A * NS_A * gram[rows, :]
-            store(gram, gram_low, rows, value, mean_next, poly_mean * once_mean)
+
+        def once_cols(cols):
+            own = poly[:, cols]
+            value = contract(poly_low[...], gram_low[:, cols], 1, 0)
+            value = value + poly_mean * gram[:, cols] + gram_mean * own
+            store(once, once_low, cols, value, once_mean, poly_mean * gram_mean)
+            return jnp.sum(value * own)
+
+        poly_once = over_tiles(once_cols) / size - poly_mean * gram_mean * poly_mean
+        mean_next = NS_A * NS_A * gram_mean + 2.0 * NS_A * once_mean + poly_once
+        excess = poly_mean * once_mean
+
+        def gram_cols(cols):
+            value = contract(poly_low[...], once_low[:, cols], 1, 0)
+            value = value + (2.0 * NS_A + poly_mean) * once[:, cols] + once_mean * poly[:, cols]
+            value = value + NS_A * NS_A * gram[:, cols]
+            store(gram, gram_low, cols, value, mean_next, excess)
             return jnp.sum(value * value)
 
-        excess = poly_mean * once_mean
-        return mean_next, over_tiles(gram_rows) - excess * (2.0 * mean_next + excess) * size
-
-    block[...] = block_ref[...]
-    mean = over_tiles(lambda rows: jnp.sum(gram_ref[rows, rows] * eye)) / size
-
-    def start(rows):
-        value = gram_ref[rows, :]
-        store(gram, gram_low, rows, value, mean, 0.0)
+        return mean_next, over_tiles(gram_cols) - excess * (2.0 * mean_next + excess) * size
+
+    block[...] = source[...]
+    mean = over_tiles(lambda cols: jnp.sum(gram[cols, cols] * eye)) / size
+
+    def start(cols):
+        value = gram[:, cols]
+        gram_low[:, cols] = value.astype(LOW)
+        gram_low[cols, cols] = (gram[cols, cols] - mean * eye).astype(LOW)
         return jnp.sum(value * value)
 
     state = lax.fori_loop(0, NS_ITERS - 1, lambda turn, state: advance(*state, False), (mean, over_tiles(start)))
     advance(*state, True)
-    out_ref[...] = block[...]
-
-
-def newton_schulz(gram, block):
-    in_vmem = pl.BlockSpec(memory_space=pltpu.VMEM)
-    full, low = pltpu.VMEM(gram.shape, jnp.float32), pltpu.VMEM(gram.shape, LOW)
-    return pl.pallas_call(
-        newton_kernel,
-        out_shape=jax.ShapeDtypeStruct(block.shape, block.dtype),
-        in_specs=[in_vmem, in_vmem],
-        out_specs=in_vmem,
-        scratch_shapes=[full, full, full, low, low, low, pltpu.VMEM(block.shape, LOW)],
-        compiler_params=pltpu.CompilerParams(vmem_limit_bytes=48 * 2**20),
-        name="newton",
-    )(gram, block)
 
 
 def fast_body(
@@ -1201,13 +1199,6 @@
     gathered = {}
     moment_halves = []
 
-    def run_with(moves, names):
-        results = moves.run()
-        first = len(results) - len(names)
-        for name, result in zip(names, results[first:]):
-            gathered.setdefault(name, {})[step] = result
-        return results[:first]
-
     for step in range(ROLL):
         shift1, scale1, gate1, shift2, scale2, gate2 = jnp.split(modul[step][None], 6, -1)
         state_low = state.astype(LOW)
@@ -1215,21 +1206,20 @@
         normed_one, inverse_one = layer_norm(embedded)
         normed_a = (normed_one * (1.0 + scale1) + shift1).astype(LOW)
         qkv_rows = product(normed_a, w_qkv).astype(LOW)
-        moves = Moves(f"heads{step}", ids)
-        moves.rows_to_heads(PATCHES, qkv_rows, 3)
-        moves.gather_pairs(normed_a)
+        moves = Moves(f"attend{step}", ids, 48 * 2**20)
+        qkv_out = moves.output((3, local * seq_count, width // seq_count), LOW, pltpu.VMEM)
+        mixed_out = moves.output((local, width), LOW, pltpu.VMEM)
+        arrivals = moves.rows_to_heads(PATCHES, qkv_rows, 3, qkv_out)
+        waiting = moves.gather_pairs(normed_a, hold=True)
+        waiting += moves.gather_pairs(state_low, hold=True)
         if step:
-            moves.gather_pairs(kept[-1][5])
-            qkv, gathered_a, gathered_mixed = moves.run()
-            gathered["mixed"] = {step - 1: gathered_mixed}
-        else:
-            qkv, gathered_a = moves.run()
+            waiting += moves.gather_pairs(kept[-1][5], hold=True)
+        add_attention(moves, qkv_out, mixed_out, arrivals, local, members, waiting)
+        qkv, mixed, gathered_a, gathered_state, *gathered_mixed = moves.run()
         gathered.setdefault("a", {})[step] = gathered_a
-        mixed_heads = attention(qkv)
-        moves = Moves("mixed_rows", ids)
-        moves.heads_to_rows(PATCHES, mixed_heads[None])
-        moves.gather_pairs(state_low)
-        (mixed,) = run_with(moves, ["state"])
+        gathered.setdefault("state", {})[step] = gathered_state
+        if step:
+            gathered["mixed"] = {step - 1: gathered_mixed[0]}
         attended = product(mixed, w_out)
         after_attn = embedded + gate1 * attended
         normed_two, inverse_two = layer_norm(after_attn)
@@ -1337,27 +1327,27 @@
         grad_gate1 = jnp.sum(grad_attn * attended, 0)
         attn_grad = (gate1 * grad_attn).astype(LOW)
         mixed_grad = contract(attn_grad, w_out, 1, 1).astype(LOW)
-        moves = Moves(f"mixed_heads{step}", ids)
-        moves.rows_to_heads(PATCHES, mixed_grad, 1)
-        if step < ROLL - 1:
+        moves = Moves(f"attend_back{step}", ids, 48 * 2**20)
+        grads_in = moves.scratch((1, local * seq_count, width // seq_count), LOW)
+        result = moves.output((local, 3 * width), LOW, pltpu.VMEM)
+        arrivals = moves.rows_to_heads(PATCHES, mixed_grad, 1, grads_in)
+        names = ["attn", "c", "delta"]
+        moves.exchange_columns(SHARDS, attn_grad)
+        moves.exchange_columns(SHARDS, normed_c)
+        waiting = moves.gather_pairs(delta_grad, hold=True)
+        if step == ROLL - 1:
+            waiting += moves.gather_pairs(mixed, hold=True)
+            names.append("mixed")
+        else:
             moves.exchange_columns(SHARDS, back[step + 1][0])
             moves.exchange_columns(SHARDS, back[step + 1][1])
-            mixed_grad_heads, gathered_qkv, gathered_embed = moves.run()
-            gathered.setdefault("qkv", {})[step + 1] = gathered_qkv
-            gathered.setdefault("embed", {})[step + 1] = gathered_embed
-        else:
-            (mixed_grad_heads,) = moves.run()
-        qkv_grad_heads = attention_back(qkv, mixed_grad_heads[0])
-        moves = Moves(f"rows{step}", ids)
-        moves.heads_to_rows(PATCHES, qkv_grad_heads)
-        moves.exchange_columns(SHARDS, attn_grad)
-        moves.exchange_columns(SHARDS, normed_c)
-        moves.gather_pairs(delta_grad)
-        names = ["attn", "c", "delta"]
-        if step == ROLL - 1:
-            moves.gather_pairs(mixed)
-            names.append("mixed")
-        (qkv_grad,) = run_with(moves, names)
+            names += ["qkv", "embed"]
+        add_attention_back(
+            moves, moves.operand(qkv, pltpu.VMEM), grads_in, result, arrivals, local, members, waiting
+        )
+        qkv_grad, *others = moves.run()
+        for name, item in zip(names, others):
+            gathered.setdefault(name, {})[step + (name in ("qkv", "embed"))] = item
         grad_normed_a = contract(qkv_grad, w_qkv, 1, 1)
         grad_scale1 = jnp.sum(grad_normed_a * normed_one, 0)
         grad_shift1 = jnp.sum(grad_normed_a, 0)
@@ -1522,20 +1512,6 @@
         silu_rows.astype(f32), modul_all, (((0,), (0,)), ((), ())), precision=HIGHEST_PRECISION
     )
 
-    io_rows = io_slice.size // most_cols
-    outgoing = jnp.concatenate(
-        [
-            grad_group.astype(LOW).reshape(MATRICES, members, -1, most_cols),
-            jnp.broadcast_to(io_slice.astype(LOW).reshape(1, 1, -1, most_cols), (MATRICES, members, io_rows, most_cols)),
-        ],
-        2,
-    )
-    by_member = [lax.dynamic_index_in_dim(outgoing, member, 1, False)]
-    for shift in range(1, members):
-        part = lax.dynamic_index_in_dim(outgoing, lax.rem(member + shift, members), 1, False)
-        routes = [(index, index // members * members + (index + shift) % members) for index in range(seq_count)]
-        by_member.append(lax.ppermute(part, PATCHES, routes))
-
     moment_group = jnp.concatenate(moment_halves, 1).reshape(-1, most_cols).astype(f32)
     grad_squares = jnp.sum(grad_group * grad_group)
     squares = (
@@ -1551,14 +1527,8 @@
     entries = entries + jnp.where(lane == place, jnp.sum(moment_group * moment_group), 0.0)
     entries = entries + jnp.where(lane == place + 1, jnp.sum(moment_group * grad_group), 0.0)
     entries = entries + jnp.where(lane == place + 2, grad_squares, 0.0)
-    entries, by_member = lax.optimization_barrier((entries, by_member))
-    by_member = jnp.stack(by_member)
-    by_group = [lax.dynamic_index_in_dim(by_member, group, 1, False)]
-    for shift in range(1, MATRICES):
-        part = lax.dynamic_index_in_dim(by_member, lax.rem(group + shift, MATRICES), 1, False)
-        routes = [(index, (index + shift * members) % seq_count) for index in range(seq_count)]
-        by_group.append(lax.ppermute(part, PATCHES, routes))
-    sums = total_of(ids, jnp.broadcast_to(entries[None], (8, LANES)))[0]
+    sums, io_slices = total_of(ids, jnp.broadcast_to(entries[None], (8, LANES)), io_slice.astype(LOW))
+    sums = sums[0]
     grad_norm = jnp.sqrt(sums[0])
     loss_total = sums[1]
     clip = jnp.minimum(1.0, CLIP_LIMIT / (grad_norm + 1e-06))
@@ -1569,10 +1539,14 @@
     my_size = lax.dynamic_slice_in_dim(sizes, group, 1)[0]
     block = ((MOMENTUM * moment_group + clip * grad_group) / (my_size + 1e-07)).astype(LOW)
 
-    moves = Moves("columns", ids, 40 * 2**20)
-    source = moves.operand(block)
-    target = moves.scratch((members * shards, block_rows, most_cols), LOW)
-    gram = moves.output((block_rows, block_rows), f32, pltpu.VMEM)
+    moves = Moves("muon", ids, 56 * 2**20)
+    source = moves.operand(block, pltpu.VMEM)
+    full, low = (block_rows, block_rows), (block_rows, most_cols)
+    update = moves.output((seq_count, block_rows // seq_count, most_cols), LOW, pltpu.VMEM)
+    target = moves.scratch((members * shards,) + low, LOW)
+    gram, poly, once = [moves.scratch(full, f32) for _ in range(3)]
+    gram_low, poly_low, once_low = [moves.scratch(full, LOW) for _ in range(3)]
+    state, state_next = [moves.scratch(low, LOW) for _ in range(2)]
     pairs = shards // 2
 
     def slot(back_member, back_pair, part=None):
@@ -1585,21 +1559,23 @@
         def action(ref):
             (index,) = place()
 
-            @pl.loop(0, block_rows // GRAM_ROWS)
+            @pl.loop(0, block_rows // GRAM_COLS)
             def _(tile):
-                rows = pl.ds(pl.multiple_of(tile * GRAM_ROWS, GRAM_ROWS), GRAM_ROWS)
-                ref(gram)[rows, :] += contract(ref(target)[index, rows, :], ref(target)[index], 1, 1)
+                cols = pl.ds(pl.multiple_of(tile * GRAM_COLS, GRAM_COLS), GRAM_COLS)
+                ref(gram)[:, cols] += contract(ref(target)[index], ref(target)[index, cols, :], 1, 1)
 
         return action
 
     def start_gram(ref):
-        ref(gram)[...] = jnp.zeros((block_rows, block_rows), f32)
+        @pl.loop(0, block_rows // GRAM_COLS)
+        def _(tile):
+            cols = pl.ds(pl.multiple_of(tile * GRAM_COLS, GRAM_COLS), GRAM_COLS)
+            ref(gram)[:, cols] = contract(ref(source)[...], ref(source)[cols, :], 1, 1)
 
     def pair_peer(shift):
         return {SHARDS: lax.rem(lax.axis_index(SHARDS) + 2 * shift, shards)}
 
     slot_own = functools.partial(slot, 0, 0)
-    own_copy = moves.keep(source, None, target, slot_own)
     by_member = {
         shift: moves.move(
             (PATCHES, members, shift), functools.partial(member_peer, members, shift), source, None, target, slot_own
@@ -1612,8 +1588,6 @@
     }
     from_sibling = [(moves.move((SHARDS,), sibling_peer, source, None, target, slot_own), slot_own)]
     moves.task(start_gram)
-    moves.wait_local(own_copy)
-    moves.task(add_gram(slot_own))
 
     def sibling_place(place):
         def at():
@@ -1671,46 +1645,48 @@
         for number in numbers:
             moves.wait_for(number)
         moves.task(add_gram(sibling_place(place)))
-    (gram,) = moves.run()
-    gram, by_group = lax.optimization_barrier((gram, by_group))
-    block = newton_schulz(gram, block)
-    block, grad_ada, grad_table, grad_pos, grad_bias, by_group = lax.optimization_barrier(
-        (block, grad_ada, grad_table, grad_pos, grad_bias, by_group)
-    )
-
-    def pick(parts, index):
-        value = parts[0]
-        for number, part in enumerate(parts[1:], 1):
-            value = jnp.where(index == number, part, value)
-        return value
-
-    def came_from(which, part):
-        back_group = lax.rem(group + MATRICES - which, MATRICES)
-        back_member = lax.rem(member + members - part, members)
-        return pick([pick([item[back] for back in range(members)], back_member) for item in by_group], back_group)
-
-    def rows_of(which, of_part):
+
+    for number in moves.exchange(PATCHES, grad_group.astype(LOW).reshape(seq_count, -1, most_cols), later=True):
+        moves.start(number)
+    moves.task(
+        lambda ref: newton_schulz(
+            *[ref(item) for item in (source, gram, poly, once, gram_low, poly_low, once_low, state, state_next)]
+        )
+    )
+
+    def row_part(shift):
+        there = lax.rem(lax.axis_index(PATCHES) + shift, seq_count)
+        size = block_rows // seq_count
+        return (pl.ds(pl.multiple_of(there * size, size), size),)
+
+    for shift in range(1, seq_count):
+        moves.start(
+            moves.move(
+                (PATCHES, shift),
+                lambda shift=shift: {PATCHES: lax.rem(lax.axis_index(PATCHES) + shift, seq_count)},
+                state,
+                functools.partial(row_part, shift),
+                update,
+                lambda: (lax.axis_index(PATCHES),),
+                later=True,
+            )
+        )
+
+    def keep_rows(ref):
+        ref(update)[lax.axis_index(PATCHES)] = ref(state)[row_part(0)]
+
+    moves.task(keep_rows)
+    update, grad_rows = moves.run()
+
+    def rows_of(which, parts):
         return jnp.concatenate(
-            [of_part(which, part)[: block_rows // seq_count, : group_cols[which]] for part in range(members)], -1
+            [parts[which * members + part][:, : group_cols[which]] for part in range(members)], -1
         ).astype(f32)
 
-    moments = [MOMENTUM * old + clip * rows_of(which, came_from) for which, old in enumerate(momenta)]
-    io_slices = jnp.stack(
-        [
-            came_from(which, part)[block_rows // seq_count :].astype(f32)
-            for which in range(MATRICES)
-            for part in range(members)
-        ]
-    )
-    moves = Moves("update_rows", ids)
-    moves.exchange(PATCHES, block.reshape(seq_count, -1, most_cols))
-    (update,) = moves.run()
+    moments = [MOMENTUM * old + clip * rows_of(which, grad_rows) for which, old in enumerate(momenta)]
     fresh = [
         master * (1.0 - RATE_MUON * DECAY_MUON)
-        - RATE_MUON
-        * 0.2
-        * math.sqrt(master.shape[1] * shards)
-        * rows_of(which, lambda which, part: update[which * members + part])
+        - RATE_MUON * 0.2 * math.sqrt(master.shape[1] * shards) * rows_of(which, update)
         for which, master in enumerate(masters)
     ]
 
@@ -1779,7 +1755,7 @@
                 )
     copies = moves.run()
 
-    io_grad = io_slices.reshape(2, padded, io_cols)[:, :values_count]
+    io_grad = io_slices.reshape(2, padded, io_cols)[:, :values_count].astype(f32)
     ada_res = adam_update(ada_master, ada_first, ada_second, clip * grad_ada, RATE_ADAM)
     io_res = adam_update(io_proj, io_first, io_second, clip * io_grad, RATE_ADAM)
     cond_res = adam_update(cond_table, cond_first, cond_second, clip * grad_table, RATE_TABLE)

time: 962 us -> 873 us (0.907)
  Pallas kernels: 659 us -> 627 us
  local copies, waits for them, and re-layouts: 83.1 us -> 53.7 us
  other arithmetic: 95.6 us -> 85.7 us
    pallas_call x6 -> x0, Pallas kernels: 116 us -> none  [the longest x1 69.5 us: newton_schulz(): pl.pallas_call(newton_kernel, out_shape=jax.ShapeDtypeStruct(block.shape,...]
    pallas_call x24 -> x20, Pallas kernels: 543 us -> 627 us  [run(): pl.pallas_call(self.kernel, out_shape=self.outputs, in_specs=self.operand...]
    unnamed x415 -> x410, local copies, waits for them, and re-layouts: 45.8 us -> 22.7 us
  transfers between devices with their start and end apart: 6 -> 2, of which waited for: 1 -> 0; matrix products, arithmetic and copies ran while one was open for 4% -> 4% of each run, Pallas kernels for 11% -> 7%
where the time goes in v4:
time: 873 us; the launch traced here: 868 us
  Pallas kernels  627 us (72%)
  matrix products  87.4 us (10%)
  other arithmetic  85.7 us (10%)
  local copies, waits for them, and re-layouts  53.7 us (6%)
  between operations  11.9 us (1%)
    pallas_call x20, Pallas kernels, run(): pl.pallas_call(self.kernel, out_shape=self.outputs, in_specs=self.operand...  627 us
    dot_general x13, matrix products, product(): return jnp.dot(left, right, preferred_element_type=jnp.float32)  35.3 us
    dot_general x11, matrix products, contract(): lax.dot_general(left, right, (((left_dim,), (right_dim,)), ((), ())), pre...  27.5 us
    unnamed x410, local copies, waits for them, and re-layouts  22.7 us
    dot_general x6, matrix products, rows_product(): lax.dot_general(flat_left, flat_right, (((0,), (0,)), ((), ())), preferre...  19.1 us
  transfers between devices with their start and end apart: 2, of which 0 were waited for; matrix products, arithmetic and copies ran while one was open for 4% of the time, Pallas kernels for 7%

profile of v4, /device:TPU:0, one launch (start us, length us, event | category | flops | bytes accessed | tf_op | source)
XLA Modules:
  0.0 867.7 jit_solution(16348508991053274086)
XLA Ops:
  4.9 5.3 tables.1
  18.4 55.5 %weights.1 = (f32[4,2,1536]{2,1,0:T(2,128)}, bf16[128,1024]{1,0:T(8,128)(2,1)}, bf16[768,1024]{1,0:T(8,128)(2,1)}, bf16[1024,1024]{1,0:T(8,128)(2,1)}, bf16[1024,3072]{1,0:T(8,128)(2,1)}) custom-call(f32[4,2,1536]{2,1,0:T(2,128)} %reshape.453.refs_0_, bf16[128,256]{1,0:T(8,128)(2,1)} %convert_element_type.343.refs_1_, bf16[768,256]{1,0:T(8,128)(2,1)} %bitcast.208, ...), custom_call_target="tpu_custom_call" | custom-call | tf_op jit(solution)/shard_map/weights/pallas_call | solution.py:662
  81.2 2.7 constant_dynamic-update-slice_fusion.13
  84.1 3.9 convolution_convert_fusion.1.refs_0_
  88.1 33.0 %attend0.1 = (bf16[3,1024,128]{2,1,0:T(8,128)(2,1)S(1)}, bf16[128,1024]{1,0:T(8,128)(2,1)S(1)}, bf16[4,128,1024]{2,1,0:T(8,128)(2,1)S(1)}, bf16[4,128,384]{2,1,0:T(8,128)(2,1)S(1)}) custom-call(bf16[128,3072]{1,0:T(8,128)(2,1)S(1)} %convolution_convert_fusion.1.refs_0_, bf16[128,1024]{1,0:T(8,128)(2,1)S(1)} %add_convert_fusion.3.refs_1_, ...), custom_call_target="tpu_custom_call" | custom-call | tf_op jit(solution)/shard_map/attend0/pallas_call | solution.py:662
  125.8 15.5 %tokens_moment.2 = (bf16[4,128,1024]{2,1,0:T(8,128)(2,1)}, bf16[8,64,512]{2,1,0:T(8,128)(2,1)}) custom-call(bf16[128,1024]{1,0:T(8,128)(2,1)} %add_convert_fusion.2.refs_0_, bf16[8,64,512]{2,1,0:T(8,128)(2,1)} %get-tuple-element.230.refs_1_), custom_call_target="tpu_custom_call" | custom-call | tf_op jit(solution)/shard_map/tokens_moment/pallas_call | solution.py:662
  141.4 4.9 multiply_convert_fusion.1
  146.3 2.3 convolution_convert_fusion.5
  148.6 12.5 %token_sums.4 = bf16[4,128,1024]{2,1,0:T(8,128)(2,1)} custom-call(bf16[4,128,1024]{2,1,0:T(8,128)(2,1)} %bitcast.219), custom_call_target="tpu_custom_call" | custom-call | tf_op jit(solution)/shard_map/token_sums/pallas_call | solution.py:662
  167.1 3.9 convolution_convert_fusion.refs_0_
  171.1 31.1 %attend1.1 = (bf16[3,1024,128]{2,1,0:T(8,128)(2,1)S(1)}, bf16[128,1024]{1,0:T(8,128)(2,1)S(1)}, bf16[4,128,1024]{2,1,0:T(8,128)(2,1)S(1)}, bf16[4,128,384]{2,1,0:T(8,128)(2,1)S(1)}, bf16[4,128,1024]{2,1,0:T(8,128)(2,1)S(1)}) custom-call(bf16[128,3072]{1,0:T(8,128)(2,1)S(1)} %convolution_convert_fusion.refs_0_, ...), custom_call_target="tpu_custom_call" | custom-call | tf_op jit(solution)/shard_map/attend1/pallas_call | solution.py:662
  205.6 14.6 %tokens_moment.3 = (bf16[4,128,1024]{2,1,0:T(8,128)(2,1)}, bf16[8,64,512]{2,1,0:T(8,128)(2,1)}) custom-call(bf16[128,1024]{1,0:T(8,128)(2,1)} %add_convert_fusion.refs_0_, bf16[8,64,512]{2,1,0:T(8,128)(2,1)} %get-tuple-element.229.refs_1_), custom_call_target="tpu_custom_call" | custom-call | tf_op jit(solution)/shard_map/tokens_moment/pallas_call | solution.py:662
  220.2 4.9 multiply_convert_fusion
  225.1 2.3 convolution_convert_fusion.4
  227.4 13.6 %token_sums.5 = bf16[4,128,1024]{2,1,0:T(8,128)(2,1)} custom-call(bf16[4,128,1024]{2,1,0:T(8,128)(2,1)} %bitcast.220), custom_call_target="tpu_custom_call" | custom-call | tf_op jit(solution)/shard_map/token_sums/pallas_call | solution.py:662
  251.4 2.8 multiply_reduce_fusion.26
  258.4 10.9 %tokens.2 = bf16[4,128,1024]{2,1,0:T(8,128)(2,1)} custom-call(bf16[128,1024]{1,0:T(8,128)(2,1)} %multiply_convert_fusion.5.refs_0_), custom_call_target="tpu_custom_call" | custom-call | tf_op jit(solution)/shard_map/tokens/pallas_call | solution.py:662
  269.3 5.2 fusion.13
  274.5 2.3 convolution_convert_fusion.3
  276.7 12.8 %token_sums.6 = bf16[4,128,1024]{2,1,0:T(8,128)(2,1)} custom-call(bf16[4,128,1024]{2,1,0:T(8,128)(2,1)} %bitcast.221), custom_call_target="tpu_custom_call" | custom-call | tf_op jit(solution)/shard_map/token_sums/pallas_call | solution.py:662
  289.6 2.4 convert_reduce_fusion.6
  292.0 2.0 multiply_reduce_fusion.3
  296.2 43.2 %attend_back1.1 = (bf16[128,3072]{1,0:T(8,128)(2,1)S(1)}, bf16[4,128,256]{2,1,0:T(8,128)(2,1)S(1)}, bf16[4,128,256]{2,1,0:T(8,128)(2,1)S(1)}, bf16[4,128,384]{2,1,0:T(8,128)(2,1)S(1)}, bf16[4,128,1024]{2,1,0:T(8,128)(2,1)S(1)}) custom-call(bf16[128,1024]{1,0:T(8,128)(2,1)S(1)} %convolution_convert_fusion.7.refs_0_, ...), custom_call_target="tpu_custom_call" | custom-call | tf_op jit(solution)/shard_map/attend_back1/pallas_call | solution.py:662
  339.5 6.5 multiply_reduce_fusion.5
  349.9 10.6 %tokens.3 = bf16[4,128,1024]{2,1,0:T(8,128)(2,1)} custom-call(bf16[128,1024]{1,0:T(8,128)(2,1)} %multiply_convert_fusion.3.refs_0_), custom_call_target="tpu_custom_call" | custom-call | tf_op jit(solution)/shard_map/tokens/pallas_call | solution.py:662
  360.5 5.0 fusion.6
  366.4 4.5 fusion.22
  370.9 2.8 dynamic-slice_convert_fusion.1
  374.5 4.1 fusion.29
  381.7 2.3 convolution_convert_fusion.2
  384.0 13.3 %token_sums.7 = bf16[4,128,1024]{2,1,0:T(8,128)(2,1)} custom-call(bf16[4,128,1024]{2,1,0:T(8,128)(2,1)} %bitcast.218), custom_call_target="tpu_custom_call" | custom-call | tf_op jit(solution)/shard_map/token_sums/pallas_call | solution.py:662
  399.2 2.0 multiply_reduce_fusion.7
  403.0 45.1 %attend_back0.1 = (bf16[128,3072]{1,0:T(8,128)(2,1)S(1)}, bf16[4,128,256]{2,1,0:T(8,128)(2,1)S(1)}, bf16[4,128,256]{2,1,0:T(8,128)(2,1)S(1)}, bf16[4,128,384]{2,...) custom-call(bf16[128,1024]{1,0:T(8,128)(2,1)S(1)} %convolution_convert_fusion.6.refs_0_, ...), custom_call_target="tpu_custom_call" | custom-call | tf_op jit(solution)/shard_map/attend_back0/pallas_call | solution.py:662
  448.2 6.1 multiply_reduce_fusion.9
  461.6 3.7 fusion.166
  466.0 2.7 fusion.47.refs_3_.refs_4_
  468.8 2.6 fusion.48.refs_4_.refs_5_
  471.3 24.8 %samples.1 = (bf16[4,128,768]{2,1,0:T(8,128)(2,1)}, bf16[4,128,256]{2,1,0:T(8,128)(2,1)}, f32[4,3,1536]{2,1,0:T(4,128)}, bf16[3,448,512]{2,1,0:T(8,128)(2,1)}, bf16[3,448,512]{2,1,0:T(8,128)(2,1)}) custom-call(bf16[128,3072]{1,0:T(8,128)(2,1)} %copy-done.1, bf16[128,1024]{1,0:T(8,128)(2,1)} %get-tuple-element.204.refs_1_, ...), custom_call_target="tpu_custom_call" | custom-call | tf_op jit(solution)/shard_map/samples/pallas_call | solution.py:662
  504.2 4.1 fusion.165
  508.3 40.7 %member_sums.1 = (bf16[1,1024,384]{2,1,0:T(8,128)(2,1)}, bf16[1,1024,128]{2,1,0:T(8,128)(2,1)}, bf16[8,112,128]{2,1,0:T(8,128)(2,1)}, bf16[8,96,256]{2,1,0:T(8,1...) custom-call(bf16[1024,768]{1,0:T(8,128)(2,1)} %get-tuple-element.270.refs_0_, ...), custom_call_target="tpu_custom_call" | custom-call | tf_op jit(solution)/shard_map/member_sums/pallas_call | solution.py:662
  550.1 2.5 fusion.169.refs_2_
  558.4 32.8 %group_sums.1 = (bf16[3,1024,128]{2,1,0:T(8,128)(2,1)S(1)}, f32[1024,384]{1,0:T(8,128)S(1)}, f32[4,8,1024]{2,1,0:T(8,128)S(1)}, f32[4,1,1792]{2,1,0:T(1,128)S(1)}) custom-call(bf16[1024,128]{1,0:T(8,128)(2,1)S(1)} %fusion.87.refs_0_, f32[1024,384]{1,0:T(8,128)S(1)} %convert_add_fusion.2.refs_1_, f32[8,1024]{1,0:T(8,128)S(1)} %fusion.169.refs_2_, ...), custom_call_target="tpu_custom_call" | custom-call | tf_op jit(solution)/shard_map/group_sums/pallas_call | solution.py:662
  597.4 4.0 fusion.145
  616.7 13.8 %total.1 = (f32[8,128]{1,0:T(8,128)}, bf16[8,96,256]{2,1,0:T(8,128)(2,1)}) custom-call(f32[8,128]{1,0:T(8,128)} %broadcast_in_dim.38.refs_0_, bf16[96,256]{1,0:T(8,128)(2,1)} %get-tuple-element.233.refs_1_), custom_call_target="tpu_custom_call" | custom-call | tf_op jit(solution)/shard_map/total/pallas_call | solution.py:662
  635.4 3.9 fusion.43.refs_0_
  639.2 120.1 %muon.1 = (bf16[8,128,512]{2,1,0:T(8,128)(2,1)}, bf16[8,128,512]{2,1,0:T(8,128)(2,1)}) custom-call(bf16[1024,512]{1,0:T(8,128)(2,1)} %fusion.43.refs_0_, bf16[8,128,512]{2,1,0:T(8,128)(2,1)} %bitcast.207), custom_call_target="tpu_custom_call" | custom-call | tf_op jit(solution)/shard_map/muon/pallas_call | solution.py:662
  766.7 77.9 %copies.1 = (bf16[1024,768]{1,0:T(8,128)(2,1)}, bf16[1024,1024]{1,0:T(8,128)(2,1)}, bf16[1024,1024]{1,0:T(8,128)(2,1)}, bf16[1024,256]{1,0:T(8,128)(2,1)}) custom-call(bf16[128,768]{1,0:T(8,128)(2,1)} %get-tuple-element.183.refs_0_, bf16[128,1024]{1,0:T(8,128)(2,1)} %get-tuple-element.181.refs_1_, bf16[128,1024]{1,0:T(8,128)(2,1)} %get-tuple-element.179.refs_2_, ...), custom_call_target="tpu_custom_call" | custom-call | tf_op jit(solution)/shard_map/copies/pallas_call | solution.py:662
  854.1 2.9 divide_subtract_fusion.1
  (587 shorter events, 129.6 us)
Async XLA Ops:
  0.7 12.1 %copy-start = (bf16[1024,1536]{1,0:T(8,128)(2,1)S(1)}, bf16[1024,1536]{1,0:T(8,128)(2,1)}, u32[]{:S(2)}) copy-start(bf16[1024,1536]{1,0:T(8,128)(2,1)} %param.49) | copy-start | bytes 9437188
  0.7 13.2 %copy-start.105 = (f32[128,256]{1,0:T(8,128)S(1)}, f32[128,256]{1,0:T(8,128)}, u32[]{:S(2)}) copy-start(f32[128,256]{1,0:T(8,128)} %param.59) | copy-start | bytes 393220
  12.6 64.1 %copy-start.132 = (f32[1024]{0:T(1024)}, f32[1024]{0:T(1024)S(1)}, u32[]{:S(2)}) copy-start(f32[1024]{0:T(1024)S(1)} %slice.250) | copy-start | bytes 12292
  74.8 46.3 %copy-start.124 = (f32[1,1024]{1,0:T(1,128)}, f32[1,1024]{1,0:T(1,128)S(1)}, u32[]{:S(2)}) copy-start(f32[1,1024]{1,0:T(1,128)S(1)} %get-tuple-element.250) | copy-start | bytes 12292
  74.8 50.1 %copy-start.120 = (f32[1,1024]{1,0:T(1,128)}, f32[1,1024]{1,0:T(1,128)S(1)}, u32[]{:S(2)}) copy-start(f32[1,1024]{1,0:T(1,128)S(1)} %get-tuple-element.247) | copy-start | bytes 12292
  74.8 87.8 %copy-start.126 = (f32[1,1024]{1,0:T(1,128)}, f32[1,1024]{1,0:T(1,128)S(1)}, u32[]{:S(2)}) copy-start(f32[1,1024]{1,0:T(1,128)S(1)} %get-tuple-element.245) | copy-start | bytes 12292
  84.1 37.0 %copy-start.33 = (bf16[1024,1024]{1,0:T(8,128)(2,1)S(1)}, bf16[1024,1024]{1,0:T(8,128)(2,1)}, u32[]{:S(2)}) copy-start(bf16[1024,1024]{1,0:T(8,128)(2,1)} %constant_dynamic-update-slice_fusion.12) | copy-start | bytes 6291460
  166.6 35.7 %copy-start.43 = (f32[128,1024]{1,0:T(8,128)}, f32[128,1024]{1,0:T(8,128)S(1)}, u32[]{:S(2)}) copy-start(f32[128,1024]{1,0:T(8,128)S(1)} %get-tuple-element.261) | copy-start | bytes 1572868
  166.6 35.6 %copy-start.128 = (f32[1,1024]{1,0:T(1,128)}, f32[1,1024]{1,0:T(1,128)S(1)}, u32[]{:S(2)}) copy-start(f32[1,1024]{1,0:T(1,128)S(1)} %get-tuple-element.242) | copy-start | bytes 12292
  166.7 37.5 %copy-start.122 = (f32[1,1024]{1,0:T(1,128)}, f32[1,1024]{1,0:T(1,128)S(1)}, u32[]{:S(2)}) copy-start(f32[1,1024]{1,0:T(1,128)S(1)} %get-tuple-element.241) | copy-start | bytes 12292
  166.7 75.8 %copy-start.130 = (f32[1,1024]{1,0:T(1,128)}, f32[1,1024]{1,0:T(1,128)S(1)}, u32[]{:S(2)}) copy-start(f32[1,1024]{1,0:T(1,128)S(1)} %get-tuple-element.239) | copy-start | bytes 12292
  167.1 35.2 %copy-start.34 = (bf16[1024,1024]{1,0:T(8,128)(2,1)S(1)}, bf16[1024,1024]{1,0:T(8,128)(2,1)}, u32[]{:S(2)}) copy-start(bf16[1024,1024]{1,0:T(8,128)(2,1)} %constant_dynamic-update-slice_fusion.12) | copy-start | bytes 6291460
  204.2 20.9 %copy-start.168 = (f32[128]{0:T(128)}, f32[128]{0:T(128)S(1)}, u32[]{:S(2)}) copy-start(f32[128]{0:T(128)S(1)} %add_rsqrt_fusion.1) | copy-start | bytes 1540
  241.0 7.8 copy-start.184
  244.8 11.1 %copy-start.170 = (f32[128]{0:T(128)}, f32[128]{0:T(128)S(1)}, u32[]{:S(2)}) copy-start(f32[128]{0:T(128)S(1)} %add_rsqrt_fusion) | copy-start | bytes 1540
  246.2 9.8 %copy-start.159 = (f32[1024]{0:T(1024)}, f32[1024]{0:T(1024)S(1)}, u32[]{:S(2)}) copy-start(f32[1024]{0:T(1024)S(1)} %fusion.117) | copy-start | bytes 12292
  276.7 15.2 %copy-start.123 = (f32[1,1024]{1,0:T(1,128)S(1)}, f32[1,1024]{1,0:T(1,128)}, u32[]{:S(2)}) copy-start(f32[1,1024]{1,0:T(1,128)} %copy-done.122) | copy-start | bytes 12292
  276.7 15.2 %copy-start.169 = (f32[128]{0:T(128)S(1)}, f32[128]{0:T(128)}, u32[]{:S(2)}) copy-start(f32[128]{0:T(128)} %copy-done.168) | copy-start | bytes 1540
  294.9 44.5 %copy-start.44 = (f32[128,1024]{1,0:T(8,128)S(1)}, f32[128,1024]{1,0:T(8,128)}, u32[]{:S(2)}) copy-start(f32[128,1024]{1,0:T(8,128)} %copy-done.43) | copy-start | bytes 1572868
  295.0 44.5 %copy-start.167 = (f32[128]{0:T(128)S(1)}, f32[128]{0:T(128)}, u32[]{:S(2)}) copy-start(f32[128]{0:T(128)} %copy-done.166) | copy-start | bytes 1540
  339.4 6.6 copy-start.2
  339.5 6.9 copy-start.52
  339.5 6.9 copy-start.176
  339.5 6.9 copy-start.185
  373.8 92.3 %collective-permute-start = (bf16[1024,512]{1,0:T(8,128)(2,1)}, bf16[1024,512]{1,0:T(8,128)(2,1)}, u32[]{:S(2)}, u32[]{:S(2)}) collective-permute-start(bf16[1024,512]{1,0:T(8,128)(2,1)} %dynamic-slice_convert_fusion.1), channel_id=1, source_target_pairs={{0,4},{4,0},{8,12},{12,8},{16,20},{20,16},{24,28},{28,24},{1,5},{5... | collective-permute-start | bytes 3145736 | tf_op jit(solution)/shard_map/ppermute | solution.py:1282
  374.5 6.6 copy-start.191
  379.7 89.0 %collective-permute-start.1 = (bf16[1024,512]{1,0:T(8,128)(2,1)}, bf16[1024,512]{1,0:T(8,128)(2,1)}, u32[]{:S(2)}, u32[]{:S(2)}) collective-permute-start(bf16[1024,512]{1,0:T(8,128)(2,1)} %dynamic-slice_convert_fusion), channel_id=1, source_target_pairs={{0,4},{4,0},{8,12},{12,8},{16,20},{20,16},{24,28},{28,24},{1,5},{5... | collective-permute-start | bytes 3145736 | tf_op jit(solution)/shard_map/ppermute | solution.py:1282
  384.0 15.2 %copy-start.121 = (f32[1,1024]{1,0:T(1,128)S(1)}, f32[1,1024]{1,0:T(1,128)}, u32[]{:S(2)}) copy-start(f32[1,1024]{1,0:T(1,128)} %copy-done.120) | copy-start | bytes 12292
  384.0 15.2 %copy-start.156 = (f32[128]{0:T(128)S(1)}, f32[128]{0:T(128)}, u32[]{:S(2)}) copy-start(f32[128]{0:T(128)} %copy-done.155) | copy-start | bytes 1540
  401.6 46.5 %copy-start.40 = (f32[128,1024]{1,0:T(8,128)S(1)}, f32[128,1024]{1,0:T(8,128)}, u32[]{:S(2)}) copy-start(f32[128,1024]{1,0:T(8,128)} %copy-done.38) | copy-start | bytes 1572868
  401.6 46.5 %copy-start.154 = (f32[128]{0:T(128)S(1)}, f32[128]{0:T(128)}, u32[]{:S(2)}) copy-start(f32[128]{0:T(128)} %copy-done.153) | copy-start | bytes 1540
  401.6 46.5 %copy-start.161 = (f32[128]{0:T(128)S(1)}, f32[128]{0:T(128)}, u32[]{:S(2)}) copy-start(f32[128]{0:T(128)} %copy-done.160) | copy-start | bytes 1540
  448.1 7.6 copy-start.173
  448.2 8.2 copy-start.144
  448.2 8.2 copy-start.142
  448.2 8.2 copy-start.143
  448.2 8.3 copy-start.28
  448.2 8.3 copy-start.31
  556.5 35.3 %copy-start.81 = (bf16[3,576,512]{2,1,0:T(8,128)(2,1)S(1)}, bf16[3,576,512]{2,1,0:T(8,128)(2,1)}, u32[]{:S(2)}) copy-start(bf16[3,576,512]{2,1,0:T(8,128)(2,1)} %get-tuple-element.124) | copy-start | bytes 5308420
  558.4 33.7 %copy-start.86 = (bf16[3,448,512]{2,1,0:T(8,128)(2,1)S(1)}, bf16[3,448,512]{2,1,0:T(8,128)(2,1)}, u32[]{:S(2)}) copy-start(bf16[3,448,512]{2,1,0:T(8,128)(2,1)} %get-tuple-element.123) | copy-start | bytes 4128772
  602.7 7.5 copy-start.108
  765.0 82.3 %copy-start.84 = (f32[128,768]{1,0:T(8,128)S(1)}, f32[128,768]{1,0:T(8,128)}, u32[]{:S(2)}) copy-start(f32[128,768]{1,0:T(8,128)} %param.39) | copy-start | bytes 1179652
  844.6 7.1 copy-start.75
  844.6 7.1 copy-start.100
  844.7 7.0 copy-start.101
  847.3 6.7 copy-start.71
  847.3 6.7 copy-start.96
  847.3 6.7 copy-start.97
  (146 other events, 476.4 us)

commit v5 on v4

--- a/solution.py
+++ b/solution.py
@@ -569,9 +569,23 @@
         self.scratches.append(pltpu.VMEM(shape, dtype))
         return (2, len(self.scratches) - 1)
 
-    def keep(self, source, source_at, target, target_at):
-        self.locals.append((source, source_at, target, target_at))
+    def keep(self, source, source_at, target, target_at, later=False):
+        self.locals.append((source, source_at, target, target_at, later))
         return len(self.locals) - 1
+
+    def load(self, array):
+        target = self.scratch(array.shape, array.dtype)
+        return target, self.keep(self.operand(array), None, target, None)
+
+    def save(self, source, shape, dtype):
+        number = self.keep(source, None, self.output(shape, dtype), None, True)
+        return number
+
+    def start_local(self, number):
+        self.steps.append((self.begin_local, number))
+
+    def begin_local(self, number):
+        self.local[number].start()
 
     def move(
         self, peer_key, peer, source, source_at, target, target_at, after=(), sends=None, takes=None, later=False
@@ -646,10 +660,11 @@
                 self.start_move(number)
         self.local = [
             pltpu.make_async_copy(self.view(source, source_at), self.view(target, target_at), local_sem.at[number])
-            for number, (source, source_at, target, target_at) in enumerate(self.locals)
+            for number, (source, source_at, target, target_at, _) in enumerate(self.locals)
         ]
-        for copy in self.local:
-            copy.start()
+        for copy, entry in zip(self.local, self.locals):
+            if not entry[4]:
+                copy.start()
         for action, number in self.steps:
             action(number)
         for number in range(len(self.locals)):
@@ -1019,6 +1034,318 @@
     moves.task(finish)
     for shift in (*range(1, MATRICES), 0):
         moves.head_rows(buffer, result, (1, 2), rows, width * count, members, shift)
+
+
+def mod_row(ref, table, row):
+    return ref(table)[pl.ds(row, 1), :]
+
+
+class Tokens:
+    def __init__(self, moves, rows, width):
+        self.moves = moves
+        self.shards = lax.axis_size(SHARDS)
+        self.rows = rows
+        self.tokens = moves.scratch((self.shards, rows, width), LOW)
+        self.own_part = moves.scratch((rows, width), jnp.float32)
+        self.leaving = moves.scratch((self.shards, rows, width), LOW)
+        self.arriving = moves.scratch((self.shards, rows, width), LOW)
+
+    def me(self):
+        return lax.axis_index(SHARDS)
+
+    def back(self, pair, sibling):
+        index = lax.rem(self.me() + self.shards - 2 * pair, self.shards)
+        return index + 1 - 2 * lax.rem(index, 2) if sibling else index
+
+    def part(self, pair, sibling, work):
+        moves = self.moves
+        slot = functools.partial(self.back, pair, sibling)
+
+        def action(ref):
+            value = work(ref, slot())
+            if pair or sibling:
+                ref(self.leaving)[slot()] = value.astype(LOW)
+            else:
+                ref(self.own_part)[...] = value
+
+        moves.task(action)
+        if pair or sibling:
+            number = moves.move(
+                (SHARDS, pair, sibling),
+                lambda: {SHARDS: slot()},
+                self.leaving,
+                lambda: (slot(),),
+                self.arriving,
+                lambda: (self.me(),),
+                later=True,
+            )
+            moves.start(number)
+            self.parts.append(number)
+
+    def run(self, work):
+        moves, halves = self.moves, 2
+        self.parts = []
+        size = self.rows // halves
+        pairs = self.shards // 2
+
+        def half(pair, sibling, number):
+            return (self.back(pair, sibling), pl.ds(number * size, size))
+
+        firsts = {}
+        for pair in range(1, pairs):
+            for number in range(halves):
+                place = functools.partial(half, 0, False, number)
+                firsts[pair, number] = moves.move(
+                    (SHARDS, pairs - pair, False),
+                    functools.partial(lambda pair: {SHARDS: self.back(pairs - pair, False)}, pair),
+                    self.tokens,
+                    place,
+                    self.tokens,
+                    place,
+                    later=True,
+                )
+                moves.start(firsts[pair, number])
+        own = functools.partial(self.back, 0, False)
+        near = moves.move(
+            (SHARDS, 0, True), sibling_peer, self.tokens, lambda: (own(),), self.tokens, lambda: (own(),), later=True
+        )
+        moves.start(near)
+        self.part(0, False, work)
+        moves.wait_for(near)
+        self.part(0, True, work)
+        for pair in range(1, pairs):
+            handed = []
+            for number in range(halves):
+                place = functools.partial(half, pair, False, number)
+                handed.append(
+                    moves.move(
+                        (SHARDS, 0, True),
+                        sibling_peer,
+                        self.tokens,
+                        place,
+                        self.tokens,
+                        place,
+                        (firsts[pair, number],),
+                    )
+                )
+            self.part(pair, False, work)
+            for number in handed:
+                moves.wait_for(number)
+            self.part(pair, True, work)
+
+    def wait(self):
+        for number in self.parts:
+            self.moves.wait_for(number)
+
+    def total(self, ref):
+        value = ref(self.own_part)[...]
+        for shift in range(1, self.shards):
+            value = value + ref(self.arriving)[lax.rem(self.me() + shift, self.shards)].astype(jnp.float32)
+        return value
+
+
+GELU_SCALE = math.sqrt(2.0 / math.pi)
+GELU_CUBE = 0.044715
+
+
+def gelu_inner(values):
+    return jnp.tanh(GELU_SCALE * (values + GELU_CUBE * values * values * values))
+
+
+def gelu_slope(values):
+    inner = gelu_inner(values)
+    rise = GELU_SCALE * (1.0 + 3.0 * GELU_CUBE * values * values)
+    return 0.5 * (1.0 + inner) + 0.5 * values * (1.0 - inner * inner) * rise
+
+
+def feed_forward(ids, step, mods, mods_next, mixed, embedded, state, pos, w_out, w_up, w_down, io_all, w_qkv, moment_part):
+    f32 = jnp.float32
+    last = mods_next is None
+    rows, width = mixed.shape
+    padded = state.shape[1]
+    hidden_count = w_up.shape[1]
+    shards = lax.axis_size(SHARDS)
+    moves = Moves(f"feed{step}", ids, 56 * 2**20)
+    vmem = functools.partial(moves.operand, space=pltpu.VMEM)
+    out_weights, out_load = moves.load(w_out)
+    mods, mixed, embedded, state = vmem(mods), vmem(mixed), vmem(embedded), vmem(state)
+    up_weights, up_load = moves.load(w_up)
+    down_weights, down_load = moves.load(w_down)
+    io_weights, io_load = moves.load(io_all)
+    attended, after_attn, downward, after_mlp = [moves.output((rows, width), f32, pltpu.VMEM) for _ in range(4)]
+    normed_c = moves.output((rows, width), LOW, pltpu.VMEM)
+    state_next = moves.output((rows, padded), f32, pltpu.VMEM)
+    upward = moves.scratch((shards, rows, hidden_count), f32)
+    hidden = moves.scratch((shards, rows, hidden_count), LOW)
+    feed = Tokens(moves, rows, width)
+    saves = [
+        moves.save(feed.tokens, (shards, rows, width), LOW),
+        moves.save(upward, (shards, rows, hidden_count), f32),
+        moves.save(hidden, (shards, rows, hidden_count), LOW),
+    ]
+    if not last:
+        mods_next, pos = vmem(mods_next), vmem(pos)
+        qkv_weights, qkv_load = moves.load(w_qkv)
+        embedded_next = moves.output((rows, width), f32, pltpu.VMEM)
+        normed_next = moves.output((rows, width), LOW, pltpu.VMEM)
+        state_low = moves.output((rows, padded), LOW, pltpu.VMEM)
+        qkv_next = moves.output((rows, w_qkv.shape[1]), LOW, pltpu.VMEM)
+    moves.exchange(PATCHES, moment_part)
+
+    def begin(ref):
+        value = contract(ref(mixed)[...], ref(out_weights)[...], 1, 0)
+        ref(attended)[...] = value
+        value = ref(embedded)[...] + mod_row(ref, mods, 2) * value
+        ref(after_attn)[...] = value
+        normed, _ = layer_norm(value)
+        normed = normed * (1.0 + mod_row(ref, mods, 4)) + mod_row(ref, mods, 3)
+        ref(feed.tokens)[feed.me()] = normed.astype(LOW)
+
+    def work(ref, slot):
+        value = contract(ref(feed.tokens)[slot], ref(up_weights)[...], 1, 0)
+        ref(upward)[slot] = value
+        value = (0.5 * value * (1.0 + gelu_inner(value))).astype(LOW)
+        ref(hidden)[slot] = value
+        return contract(value, ref(down_weights)[...], 1, 1)
+
+    def finish(ref):
+        value = feed.total(ref)
+        ref(downward)[...] = value
+        value = ref(after_attn)[...] + mod_row(ref, mods, 5) * value
+        ref(after_mlp)[...] = value
+        normed, _ = layer_norm(value)
+        normed = normed.astype(LOW)
+        ref(normed_c)[...] = normed
+        delta = contract(normed, ref(io_weights)[1], 1, 1)
+        value = ref(state)[...] + mod_row(ref, mods, 7)[:, :padded] * delta
+        ref(state_next)[...] = value
+        if not last:
+            value = value.astype(LOW)
+            ref(state_low)[...] = value
+            value = contract(value, ref(io_weights)[0], 1, 0) + mod_row(ref, mods, 6) + ref(pos)[...]
+            ref(embedded_next)[...] = value
+            normed, _ = layer_norm(value)
+            normed = (normed * (1.0 + mod_row(ref, mods_next, 1)) + mod_row(ref, mods_next, 0)).astype(LOW)
+            ref(normed_next)[...] = normed
+
+    def project(ref):
+        @pl.loop(0, w_qkv.shape[1] // width)
+        def _(part):
+            cols = pl.ds(pl.multiple_of(part * width, width), width)
+            value = contract(ref(normed_next)[...], ref(qkv_weights)[:, cols], 1, 0)
+            ref(qkv_next)[:, cols] = value.astype(LOW)
+
+    moves.wait_local(out_load)
+    moves.task(begin)
+    moves.wait_local(up_load)
+    moves.wait_local(down_load)
+    feed.run(work)
+    for number in saves:
+        moves.start_local(number)
+    moves.wait_local(io_load)
+    feed.wait()
+    moves.task(finish)
+    if not last:
+        moves.wait_local(qkv_load)
+        moves.task(project)
+    return moves.run()
+
+
+def feed_back(ids, step, mods, mods_later, later, grad_state, kept, w_out, w_up, w_down, io_all, w_qkv):
+    f32 = jnp.float32
+    attended, after_attn, downward, after_mlp, upward = kept
+    rows, width = attended.shape
+    padded = grad_state.shape[1]
+    hidden_count = w_up.shape[1]
+    shards = lax.axis_size(SHARDS)
+    moves = Moves(f"feed_back{step}", ids, 56 * 2**20)
+    vmem = functools.partial(moves.operand, space=pltpu.VMEM)
+    io_weights, io_load = moves.load(io_all)
+    if later is not None:
+        qkv_weights, qkv_load = moves.load(w_qkv)
+        later = [vmem(item) for item in later]
+        mods_later = vmem(mods_later)
+        embed_grad = moves.output((rows, width), LOW, pltpu.VMEM)
+    down_weights, down_load = moves.load(w_down)
+    up_weights, up_load = moves.load(w_up)
+    slopes, slopes_load = moves.load(upward)
+    out_weights, out_load = moves.load(w_out)
+    mods, grad_state = vmem(mods), vmem(grad_state)
+    attended, after_attn, downward, after_mlp = [vmem(item) for item in (attended, after_attn, downward, after_mlp)]
+    vectors = moves.output((8, width), f32, pltpu.VMEM)
+    state_out = moves.output((rows, padded), f32, pltpu.VMEM)
+    delta_grad = moves.output((rows, padded), LOW, pltpu.VMEM)
+    grad_attn = moves.output((rows, width), f32, pltpu.VMEM)
+    attn_grad, mixed_grad = [moves.output((rows, width), LOW, pltpu.VMEM) for _ in range(2)]
+    grad_mlp = moves.scratch((rows, width), f32)
+    up_grad = moves.scratch((shards, rows, hidden_count), LOW)
+    feed = Tokens(moves, rows, width)
+    saves = [
+        moves.save(feed.tokens, (shards, rows, width), LOW),
+        moves.save(up_grad, (shards, rows, hidden_count), LOW),
+    ]
+
+    def put(ref, row, value):
+        ref(vectors)[pl.ds(row, 1), :] = jnp.sum(value, 0, keepdims=True)
+
+    def before(ref):
+        qkv_grad, embedded, grad_later = later
+        grad = contract(ref(qkv_grad)[...], ref(qkv_weights)[...], 1, 1)
+        normed, inverse = layer_norm(ref(embedded)[...])
+        put(ref, 5, grad * normed)
+        put(ref, 4, grad)
+        grad = grad * (1.0 + mod_row(ref, mods_later, 1))
+        grad = ref(grad_later)[...] + norm_back(grad, normed, inverse)
+        put(ref, 6, grad)
+        grad = grad.astype(LOW)
+        ref(embed_grad)[...] = grad
+        ref(state_out)[...] = ref(grad_state)[...] + contract(grad, ref(io_weights)[0], 1, 1)
+
+    def begin(ref):
+        if later is None:
+            ref(state_out)[...] = ref(grad_state)[...]
+            ref(vectors)[...] = jnp.zeros((8, width), f32)
+        grad = (mod_row(ref, mods, 7)[:, :padded] * ref(state_out)[...]).astype(LOW)
+        ref(delta_grad)[...] = grad
+        normed, inverse = layer_norm(ref(after_mlp)[...])
+        grad = norm_back(contract(grad, ref(io_weights)[1], 1, 0), normed, inverse)
+        ref(grad_mlp)[...] = grad
+        put(ref, 3, grad * ref(downward)[...])
+        ref(feed.tokens)[feed.me()] = (mod_row(ref, mods, 5) * grad).astype(LOW)
+
+    def work(ref, slot):
+        value = contract(ref(feed.tokens)[slot], ref(down_weights)[...], 1, 0)
+        value = (value * gelu_slope(ref(slopes)[slot])).astype(LOW)
+        ref(up_grad)[slot] = value
+        return contract(value, ref(up_weights)[...], 1, 1)
+
+    def finish(ref):
+        grad = feed.total(ref)
+        normed, inverse = layer_norm(ref(after_attn)[...])
+        put(ref, 2, grad * normed)
+        put(ref, 1, grad)
+        grad = ref(grad_mlp)[...] + norm_back(grad * (1.0 + mod_row(ref, mods, 4)), normed, inverse)
+        ref(grad_attn)[...] = grad
+        put(ref, 0, grad * ref(attended)[...])
+        grad = (mod_row(ref, mods, 2) * grad).astype(LOW)
+        ref(attn_grad)[...] = grad
+        ref(mixed_grad)[...] = contract(grad, ref(out_weights)[...], 1, 1).astype(LOW)
+
+    moves.wait_local(io_load)
+    if later is not None:
+        moves.wait_local(qkv_load)
+        moves.task(before)
+    moves.task(begin)
+    for number in (down_load, up_load, slopes_load):
+        moves.wait_local(number)
+    feed.run(work)
+    for number in saves:
+        moves.start_local(number)
+    moves.wait_local(out_load)
+    feed.wait()
+    moves.task(finish)
+    results = moves.run()
+    return results if later is not None else [None, *results]
 
 
 def newton_schulz(source, gram, poly, once, gram_low, poly_low, once_low, block, block_next):
@@ -1199,13 +1526,21 @@
     gathered = {}
     moment_halves = []
 
+    extras = [
+        jnp.concatenate(
+            [
+                modul[step].reshape(6, width),
+                embed_bias[None],
+                jnp.broadcast_to((step < length).astype(f32), (1, width)),
+            ]
+        )
+        for step in range(ROLL)
+    ]
+    state_low = state.astype(LOW)
+    embedded = product(state_low, io_all[0]) + embed_bias + pos
+    normed_a = (layer_norm(embedded)[0] * (1.0 + extras[0][1]) + extras[0][0]).astype(LOW)
+    qkv_rows = product(normed_a, w_qkv).astype(LOW)
     for step in range(ROLL):
-        shift1, scale1, gate1, shift2, scale2, gate2 = jnp.split(modul[step][None], 6, -1)
-        state_low = state.astype(LOW)
-        embedded = product(state_low, io_all[0]) + embed_bias + pos
-        normed_one, inverse_one = layer_norm(embedded)
-        normed_a = (normed_one * (1.0 + scale1) + shift1).astype(LOW)
-        qkv_rows = product(normed_a, w_qkv).astype(LOW)
         moves = Moves(f"attend{step}", ids, 48 * 2**20)
         qkv_out = moves.output((3, local * seq_count, width // seq_count), LOW, pltpu.VMEM)
         mixed_out = moves.output((local, width), LOW, pltpu.VMEM)
@@ -1213,61 +1548,42 @@
         waiting = moves.gather_pairs(normed_a, hold=True)
         waiting += moves.gather_pairs(state_low, hold=True)
         if step:
-            waiting += moves.gather_pairs(kept[-1][5], hold=True)
+            waiting += moves.gather_pairs(kept[-1][2], hold=True)
         add_attention(moves, qkv_out, mixed_out, arrivals, local, members, waiting)
         qkv, mixed, gathered_a, gathered_state, *gathered_mixed = moves.run()
         gathered.setdefault("a", {})[step] = gathered_a
         gathered.setdefault("state", {})[step] = gathered_state
         if step:
             gathered["mixed"] = {step - 1: gathered_mixed[0]}
-        attended = product(mixed, w_out)
-        after_attn = embedded + gate1 * attended
-        normed_two, inverse_two = layer_norm(after_attn)
-        normed_b = (normed_two * (1.0 + scale2) + shift2).astype(LOW)
-        moves = Moves("tokens_moment", ids)
-        moves.gather_pairs(normed_b, 2)
-        moves.exchange(PATCHES, moment_parts[:, step * half_rows : (step + 1) * half_rows])
-        tokens_b, moment_half = moves.run()
+        *results, moment_half = feed_forward(
+            ids,
+            step,
+            extras[step],
+            extras[step + 1] if step + 1 < ROLL else None,
+            mixed,
+            embedded,
+            state,
+            pos,
+            w_out,
+            up_copy,
+            down_copy,
+            io_all,
+            w_qkv,
+            moment_parts[:, step * half_rows : (step + 1) * half_rows],
+        )
         moment_halves.append(moment_half)
-        tokens_b = tokens_b.reshape(shards * local, width)
-        upward = product(tokens_b, up_copy)
-        hidden = jax.nn.gelu(upward).astype(LOW)
-        down_part = contract(hidden, down_copy, 1, 1).astype(LOW).reshape(shards, local, width)
-        moves = Moves("token_sums", ids)
-        moves.exchange(SHARDS, down_part)
-        downward = jnp.sum(moves.run()[0].astype(f32), 0)
-        after_mlp = after_attn + gate2 * downward
-        normed_three, inverse_three = layer_norm(after_mlp)
-        normed_c = normed_three.astype(LOW)
-        delta = contract(normed_c, io_all[1], 1, 1)
+        attended, after_attn, downward, after_mlp, normed_c, state, tokens_b, upward, hidden, *following = results
         kept.append(
-            (
-                state_low,
-                normed_one,
-                inverse_one,
-                normed_a,
-                qkv,
-                mixed,
-                attended,
-                normed_two,
-                inverse_two,
-                tokens_b,
-                upward,
-                hidden,
-                downward,
-                normed_three,
-                inverse_three,
-                normed_c,
-            )
+            (embedded, qkv, mixed, (attended, after_attn, downward, after_mlp, upward), normed_c, tokens_b, hidden)
         )
-        state = state + (step < length).astype(f32) * delta
+        if following:
+            embedded, normed_a, state_low, qkv_rows = following
 
     lat = latitude_weights(local)
     diff = state - jnp.pad(targets[0].astype(f32), value_pad)
     loss_local = weight * jnp.sum(jnp.sum(diff * diff, -1) * lat)
     grad_state = 2.0 * weight * lat[:, None] * diff
 
-    back = [None] * ROLL
     mlp_back = []
 
     def patch_sum(item, cols):
@@ -1282,51 +1598,40 @@
             mine = mine + lax.ppermute(outgoing, PATCHES, pairs).astype(f32)
         return mine
 
+    later, mods_later = None, None
+    mod_grads = [[None] * 6 for _ in range(ROLL)]
+    bias_grads = []
+
+    def put_mods(step, names_and_rows):
+        for place, row in names_and_rows:
+            mod_grads[step][place] = row
+
     for step in reversed(range(ROLL)):
-        (
-            state_low,
-            normed_one,
-            inverse_one,
-            normed_a,
-            qkv,
-            mixed,
-            attended,
-            normed_two,
-            inverse_two,
-            tokens_b,
-            upward,
-            hidden,
-            downward,
-            normed_three,
-            inverse_three,
-            normed_c,
-        ) = kept[step]
-        shift1, scale1, gate1, shift2, scale2, gate2 = jnp.split(modul[step][None], 6, -1)
-        delta_grad = ((step < length).astype(f32) * grad_state).astype(LOW)
-        grad_mlp = norm_back(product(delta_grad, io_all[1]), normed_three, inverse_three)
-        grad_gate2 = jnp.sum(grad_mlp * downward, 0)
-        moves = Moves("tokens", ids)
-        moves.gather_pairs((gate2 * grad_mlp).astype(LOW), 2)
-        tokens_down = moves.run()[0].reshape(shards * local, width)
-        grad_hidden = product(tokens_down, down_copy)
-        up_grad = jax.vjp(jax.nn.gelu, upward)[1](grad_hidden)[0].astype(LOW)
+        embedded, qkv, mixed, for_feed, normed_c, tokens_b, hidden = kept[step]
+        embed_grad, vectors, grad_state, delta_grad, grad_attn, attn_grad, mixed_grad, tokens_down, up_grad = feed_back(
+            ids,
+            step,
+            extras[step],
+            mods_later,
+            later,
+            grad_state,
+            for_feed,
+            w_out,
+            up_copy,
+            down_copy,
+            io_all,
+            w_qkv,
+        )
+        put_mods(step, ((2, vectors[0]), (3, vectors[1]), (4, vectors[2]), (5, vectors[3])))
+        if later is not None:
+            put_mods(step + 1, ((0, vectors[4]), (1, vectors[5])))
+            bias_grads.append(vectors[6])
         mlp_back.append((tokens_b, up_grad, tokens_down, hidden))
         if step == 0:
-            all_b, all_up, all_down, all_hidden = [jnp.concatenate(items, 0) for items in zip(*mlp_back)]
-            mlp_sums = [
-                patch_sum(rows_product(left, right), cols)
-                for left, right, cols in ((all_b, all_up, group_cols[1]), (all_down, all_hidden, group_cols[2]))
-            ]
-        up_part = contract(up_grad, up_copy, 1, 1).astype(LOW).reshape(shards, local, width)
-        moves = Moves("token_sums", ids)
-        moves.exchange(SHARDS, up_part)
-        grad_normed_b = jnp.sum(moves.run()[0].astype(f32), 0)
-        grad_scale2 = jnp.sum(grad_normed_b * normed_two, 0)
-        grad_shift2 = jnp.sum(grad_normed_b, 0)
-        grad_attn = grad_mlp + norm_back(grad_normed_b * (1.0 + scale2), normed_two, inverse_two)
-        grad_gate1 = jnp.sum(grad_attn * attended, 0)
-        attn_grad = (gate1 * grad_attn).astype(LOW)
-        mixed_grad = contract(attn_grad, w_out, 1, 1).astype(LOW)
+            mlp_sums = []
+            for left, right, cols in ((0, 1, group_cols[1]), (2, 3, group_cols[2])):
+                total = sum(rows_product(items[left], items[right]) for items in mlp_back)
+                mlp_sums.append(patch_sum(total, cols))
         moves = Moves(f"attend_back{step}", ids, 48 * 2**20)
         grads_in = moves.scratch((1, local * seq_count, width // seq_count), LOW)
         result = moves.output((local, 3 * width), LOW, pltpu.VMEM)
@@ -1339,8 +1644,8 @@
             waiting += moves.gather_pairs(mixed, hold=True)
             names.append("mixed")
         else:
-            moves.exchange_columns(SHARDS, back[step + 1][0])
-            moves.exchange_columns(SHARDS, back[step + 1][1])
+            moves.exchange_columns(SHARDS, later[0])
+            moves.exchange_columns(SHARDS, embed_grad)
             names += ["qkv", "embed"]
         add_attention_back(
             moves, moves.operand(qkv, pltpu.VMEM), grads_in, result, arrivals, local, members, waiting
@@ -1348,19 +1653,17 @@
         qkv_grad, *others = moves.run()
         for name, item in zip(names, others):
             gathered.setdefault(name, {})[step + (name in ("qkv", "embed"))] = item
-        grad_normed_a = contract(qkv_grad, w_qkv, 1, 1)
-        grad_scale1 = jnp.sum(grad_normed_a * normed_one, 0)
-        grad_shift1 = jnp.sum(grad_normed_a, 0)
-        grad_embedded = grad_attn + norm_back(grad_normed_a * (1.0 + scale1), normed_one, inverse_one)
-        embed_grad = grad_embedded.astype(LOW)
-        grad_state = grad_state + contract(embed_grad, io_all[0], 1, 1)
-        grad_modul = jnp.concatenate([grad_shift1, grad_scale1, grad_gate1, grad_shift2, grad_scale2, grad_gate2])
-        back[step] = (qkv_grad, embed_grad, grad_modul, jnp.sum(grad_embedded, 0))
-
-    qkv_grad, embed_grad, _, _ = back[0]
+        later, mods_later = (qkv_grad, embedded, grad_attn), extras[step]
+    grad_normed_a = contract(qkv_grad, w_qkv, 1, 1)
+    normed_one, inverse_one = layer_norm(embedded)
+    put_mods(0, ((0, jnp.sum(grad_normed_a, 0)), (1, jnp.sum(grad_normed_a * normed_one, 0))))
+    grad_embedded = grad_attn + norm_back(grad_normed_a * (1.0 + extras[0][1:2]), normed_one, inverse_one)
+    embed_grad = grad_embedded.astype(LOW)
+    bias_grads.append(jnp.sum(grad_embedded, 0))
+
     mlp_low = [item.astype(LOW) for item in mlp_sums]
-    modul_parts = jnp.stack([item[2].reshape(shards, ada_cols) for item in back], 1)
-    embed_parts = sum(item[3] for item in back).reshape(shards, 1, -1)
+    modul_parts = jnp.stack([jnp.concatenate(item).reshape(shards, ada_cols) for item in mod_grads], 1)
+    embed_parts = sum(bias_grads).reshape(shards, 1, -1)
     vectors = jnp.concatenate(
         [modul_parts, jnp.pad(embed_parts, ((0, 0), (0, 0), (0, ada_cols - embed_parts.shape[-1])))], 1
     )

time: 873 us -> 861 us (0.986)
  matrix products: 87.4 us -> 35.2 us
  Pallas kernels: 627 us -> 666 us
    pallas_call x20 -> x16, Pallas kernels: 627 us -> 666 us  [run(): pl.pallas_call(self.kernel, out_shape=self.outputs, in_specs=self.operand...]
    dot_general x13 -> x3, matrix products: 35.3 us -> 6.45 us  [product(): return jnp.dot(left, right, preferred_element_type=jnp.float32)]
    dot_general x11 -> x1, matrix products: 27.5 us -> 2.53 us  [contract(): lax.dot_general(left, right, (((left_dim,), (right_dim,)), ((), ())), pre...]
    reduce_sum x14 -> x1, other arithmetic: 17.9 us -> 0.93 us  [fast_body(): bias_grads.append(jnp.sum(grad_embedded, 0))]
    unnamed x410 -> x286, local copies, waits for them, and re-layouts: 22.7 us -> 27.4 us
    dot_general x6 -> x8, matrix products: 19.1 us -> 20.7 us  [rows_product(): lax.dot_general(flat_left, flat_right, (((0,), (0,)), ((), ())), preferre...]
  transfers between devices with their start and end apart: 2 -> 2, of which waited for: 0 -> 0; matrix products, arithmetic and copies ran while one was open for 4% -> 2% of each run, Pallas kernels for 7% -> 8%
where the time goes in v5:
time: 861 us; the launch traced here: 856 us
  Pallas kernels  666 us (77%)
  other arithmetic  79.8 us (9%)
  local copies, waits for them, and re-layouts  61.4 us (7%)
  matrix products  35.2 us (4%)
  between operations  11 us (1%)
    pallas_call x16, Pallas kernels, run(): pl.pallas_call(self.kernel, out_shape=self.outputs, in_specs=self.operand...  666 us
    unnamed x286, local copies, waits for them, and re-layouts  27.4 us
    dot_general x8, matrix products, rows_product(): lax.dot_general(flat_left, flat_right, (((0,), (0,)), ((), ())), preferre...  20.7 us
  transfers between devices with their start and end apart: 2, of which 0 were waited for; matrix products, arithmetic and copies ran while one was open for 2% of the time, Pallas kernels for 8%

profile of v5, /device:TPU:0, one launch (start us, length us, event | category | flops | bytes accessed | tf_op | source)
XLA Modules:
  0.0 855.5 jit_solution(11038936703445471276)
XLA Ops:
  9.4 5.3 tables.1
  24.7 1.6 copy.81
  26.4 1.6 copy.82
  33.3 55.5 %weights.1 = (f32[4,2,1536]{2,1,0:T(2,128)}, bf16[128,1024]{1,0:T(8,128)(2,1)}, bf16[768,1024]{1,0:T(8,128)(2,1)}, bf16[1024,1024]{1,0:T(8,128)(2,1)}, bf16[1024,3072]{1,0:T(8,128)(2,1)}) custom-call(f32[4,2,1536]{2,1,0:T(2,128)} %reshape.338.refs_0_, bf16[128,256]{1,0:T(8,128)(2,1)} %convert_element_type.254.refs_1_, bf16[768,256]{1,0:T(8,128)(2,1)} %bitcast.189, ...), custom_call_target="tpu_custom_call" | custom-call | tf_op jit(solution)/shard_map/weights/pallas_call | solution.py:677
  88.8 1.6 slice_reduce_fusion
  92.4 1.8 convert_element_type.259.refs_9_
  94.2 1.9 constant_dynamic-update-slice_fusion.14.refs_0_.refs_4_.refs_9_
  96.1 1.8 constant_dynamic-update-slice_fusion.13
  100.5 1.9 fusion.82
  103.1 2.8 constant_dynamic-update-slice_fusion.12.refs_10_.refs_1_
  106.1 3.8 convolution_convert_fusion.refs_0_
  109.9 32.2 %attend0.1 = (bf16[3,1024,128]{2,1,0:T(8,128)(2,1)S(1)}, bf16[128,1024]{1,0:T(8,128)(2,1)S(1)}, bf16[4,128,1024]{2,1,0:T(8,128)(2,1)S(1)}, bf16[4,128,384]{2,1,0:T(8,128)(2,1)S(1)}) custom-call(bf16[128,3072]{1,0:T(8,128)(2,1)S(1)} %convolution_convert_fusion.refs_0_, bf16[128,1024]{1,0:T(8,128)(2,1)S(1)} %add_convert_fusion.refs_1_, ...), custom_call_target="tpu_custom_call" | custom-call | tf_op jit(solution)/shard_map/attend0/pallas_call | solution.py:677
  145.2 28.3 %feed0.1 = (f32[128,1024]{1,0:T(8,128)}, f32[128,1024]{1,0:T(8,128)}, f32[128,1024]{1,0:T(8,128)}, f32[128,1024]{1,0:T(8,128)}, bf16[128,1024]{1,0:T(8,128)(2,1)...) custom-call(bf16[1024,1024]{1,0:T(8,128)(2,1)} %constant_dynamic-upd, ...), custom_call_target="tpu_custom_call" | custom-call | tf_op jit(solution)/shard_map/feed0/pallas_call | solution.py:677
  176.5 34.2 %attend1.1 = (bf16[3,1024,128]{2,1,0:T(8,128)(2,1)S(1)}, bf16[128,1024]{1,0:T(8,128)(2,1)S(1)}, bf16[4,128,1024]{2,1,0:T(8,128)(2,1)S(1)}, bf16[4,128,384]{2,1,0:T(8,128)(2,1)S(1)}, bf16[4,128,1024]{2,1,0:T(8,128)(2,1)S(1)}) custom-call(bf16[128,3072]{1,0:T(8,128)(2,1)S(1)} %copy-done.11, bf16[128,1024]{1,0:T(8,128)(2,1)S(1)} %copy-done.12, ...), custom_call_target="tpu_custom_call" | custom-call | tf_op jit(solution)/shard_map/attend1/pallas_call | solution.py:677
  214.2 27.2 %feed1.1 = (f32[128,1024]{1,0:T(8,128)}, f32[128,1024]{1,0:T(8,128)}, f32[128,1024]{1,0:T(8,128)}, f32[128,1024]{1,0:T(8,128)}, bf16[128,1024]{1,0:T(8,128)(2,1)...) custom-call(bf16[1024,1024]{1,0:T(8,128)(2,1)} %constant_dynamic-upd, ...), custom_call_target="tpu_custom_call" | custom-call | tf_op jit(solution)/shard_map/feed1/pallas_call | solution.py:677
  241.4 1.7 multiply_reduce_fusion.6
  243.1 30.6 %feed_back1.1 = (f32[8,1024]{1,0:T(8,128)}, f32[128,384]{1,0:T(8,128)}, bf16[128,384]{1,0:T(8,128)(2,1)}, f32[128,1024]{1,0:T(8,128)}, bf16[128,1024]{1,0:T(8,12...) custom-call(bf16[2,384,1024]{2,1,0:T(8,128)(2,1)} %bitcast.186, ...), custom_call_target="tpu_custom_call" | custom-call | tf_op jit(solution)/shard_map/feed_back1/pallas_call | solution.py:677
  273.8 4.7 fusion.116
  278.5 42.3 %attend_back1.1 = (bf16[128,3072]{1,0:T(8,128)(2,1)S(1)}, bf16[4,128,256]{2,1,0:T(8,128)(2,1)S(1)}, bf16[4,128,256]{2,1,0:T(8,128)(2,1)S(1)}, bf16[4,128,384]{2,1,0:T(8,128)(2,1)S(1)}, bf16[4,128,1024]{2,1,0:T(8,128)(2,1)S(1)}) custom-call(bf16[128,1024]{1,0:T(8,128)(2,1)S(1)} %copy-done.19, bf16[128,1024]{1,0:T(8,128)(2,1)S(1)} %copy-done.18, ...), custom_call_target="tpu_custom_call" | custom-call | tf_op jit(solution)/shard_map/attend_back1/pallas_call | solution.py:677
  324.7 34.0 %feed_back0.1 = (bf16[128,1024]{1,0:T(8,128)(2,1)}, f32[8,1024]{1,0:T(8,128)}, f32[128,384]{1,0:T(8,128)}, bf16[128,384]{1,0:T(8,128)(2,1)}, f32[128,1024]{1,0:T...) custom-call(bf16[2,384,1024]{2,1,0:T(8,128)(2,1)} %bitcast.187, ...), custom_call_target="tpu_custom_call" | custom-call | tf_op jit(solution)/shard_map/feed_back0/pallas_call | solution.py:677
  358.7 2.9 bitcast_add_fusion.1
  372.1 66.9 %attend_back0.1 = (bf16[128,3072]{1,0:T(8,128)(2,1)S(1)}, bf16[4,128,256]{2,1,0:T(8,128)(2,1)S(1)}, bf16[4,128,256]{2,1,0:T(8,128)(2,1)S(1)}, bf16[4,128,384]{2,...) custom-call(bf16[128,1024]{1,0:T(8,128)(2,1)S(1)} %copy-done.16, ...), custom_call_target="tpu_custom_call" | custom-call | tf_op jit(solution)/shard_map/attend_back0/pallas_call | solution.py:677
  439.1 2.5 multiply_reduce_fusion.2
  446.4 3.7 fusion.113
  450.8 2.7 fusion.19.refs_3_.refs_4_
  453.5 2.6 fusion.20.refs_4_.refs_5_
  456.1 25.4 %samples.1 = (bf16[4,128,768]{2,1,0:T(8,128)(2,1)}, bf16[4,128,256]{2,1,0:T(8,128)(2,1)}, f32[4,3,1536]{2,1,0:T(4,128)}, bf16[3,448,512]{2,1,0:T(8,128)(2,1)}, bf16[3,448,512]{2,1,0:T(8,128)(2,1)}) custom-call(bf16[128,3072]{1,0:T(8,128)(2,1)} %copy-done.3, bf16[128,1024]{1,0:T(8,128)(2,1)} %get-tuple-element.250.refs_1_, ...), custom_call_target="tpu_custom_call" | custom-call | tf_op jit(solution)/shard_map/samples/pallas_call | solution.py:677
  483.3 1.8 convert_reduce_fusion.6
  488.1 4.1 fusion.112
  492.2 39.5 %member_sums.1 = (bf16[1,1024,384]{2,1,0:T(8,128)(2,1)}, bf16[1,1024,128]{2,1,0:T(8,128)(2,1)}, bf16[8,112,128]{2,1,0:T(8,128)(2,1)}, bf16[8,96,256]{2,1,0:T(8,1...) custom-call(bf16[1024,768]{1,0:T(8,128)(2,1)} %get-tuple-element.297.refs_0_, ...), custom_call_target="tpu_custom_call" | custom-call | tf_op jit(solution)/shard_map/member_sums/pallas_call | solution.py:677
  532.7 2.5 fusion.118.refs_2_
  535.3 1.8 convert_add_fusion.2.refs_1_
  537.3 32.5 %group_sums.1 = (bf16[3,1024,128]{2,1,0:T(8,128)(2,1)S(1)}, f32[1024,384]{1,0:T(8,128)S(1)}, f32[4,8,1024]{2,1,0:T(8,128)S(1)}, f32[4,1,1792]{2,1,0:T(1,128)S(1)}) custom-call(bf16[1024,128]{1,0:T(8,128)(2,1)S(1)} %fusion.43.refs_0_, f32[1024,384]{1,0:T(8,128)S(1)} %convert_add_fusion.2.refs_1_, f32[8,1024]{1,0:T(8,128)S(1)} %fusion.118.refs_2_, ...), custom_call_target="tpu_custom_call" | custom-call | tf_op jit(solution)/shard_map/group_sums/pallas_call | solution.py:677
  571.2 2.0 multiply_reduce_fusion.1
  583.0 2.0 convert_reduce_fusion.1
  585.0 2.0 convert_reduce_fusion
  587.1 4.5 fusion.100
  600.1 1.9 fusion.84
  602.6 13.1 %total.1 = (f32[8,128]{1,0:T(8,128)}, bf16[8,96,256]{2,1,0:T(8,128)(2,1)}) custom-call(f32[8,128]{1,0:T(8,128)} %broadcast_in_dim.79.refs_0_, bf16[96,256]{1,0:T(8,128)(2,1)} %get-tuple-element.271.refs_1_), custom_call_target="tpu_custom_call" | custom-call | tf_op jit(solution)/shard_map/total/pallas_call | solution.py:677
  617.8 1.7 slice.313
  621.1 3.9 fusion.15.refs_0_
  626.2 122.1 %muon.1 = (bf16[8,128,512]{2,1,0:T(8,128)(2,1)}, bf16[8,128,512]{2,1,0:T(8,128)(2,1)}) custom-call(bf16[1024,512]{1,0:T(8,128)(2,1)} %fusion.15.refs_0_, bf16[8,128,512]{2,1,0:T(8,128)(2,1)} %bitcast.188), custom_call_target="tpu_custom_call" | custom-call | tf_op jit(solution)/shard_map/muon/pallas_call | solution.py:677
  756.9 77.0 %copies.1 = (bf16[1024,768]{1,0:T(8,128)(2,1)}, bf16[1024,1024]{1,0:T(8,128)(2,1)}, bf16[1024,1024]{1,0:T(8,128)(2,1)}, bf16[1024,256]{1,0:T(8,128)(2,1)}) custom-call(bf16[128,768]{1,0:T(8,128)(2,1)} %get-tuple-element.239.refs_0_, bf16[128,1024]{1,0:T(8,128)(2,1)} %get-tuple-element.237.refs_1_, bf16[128,1024]{1,0:T(8,128)(2,1)} %get-tuple-element.235.refs_2_, ...), custom_call_target="tpu_custom_call" | custom-call | tf_op jit(solution)/shard_map/copies/pallas_call | solution.py:677
  835.4 1.6 multiply_add_fusion.7
  837.1 1.9 multiply_add_fusion.5
  839.0 2.0 multiply_add_fusion.2
  843.4 2.9 divide_subtract_fusion.1
  846.3 1.8 divide_subtract_fusion
  (403 shorter events, 100.4 us)
Async XLA Ops:
  0.7 18.4 %copy-start = (bf16[1024,1536]{1,0:T(8,128)(2,1)S(1)}, bf16[1024,1536]{1,0:T(8,128)(2,1)}, u32[]{:S(2)}) copy-start(bf16[1024,1536]{1,0:T(8,128)(2,1)} %param.49) | copy-start | bytes 9437188
  8.0 10.2 %copy-start.112 = (f32[4,2,5]{2,1,0:T(2,128)}, f32[4,2,5]{2,1,0:T(2,128)S(1)}, u32[]{:S(2)}) copy-start(f32[4,2,5]{2,1,0:T(2,128)S(1)} %broadcast_add_fusion) | copy-start | bytes 484
  18.2 9.8 %copy-start.65 = (f32[128,768]{1,0:T(8,128)S(1)}, f32[128,768]{1,0:T(8,128)}, u32[]{:S(2)}) copy-start(f32[128,768]{1,0:T(8,128)} %param.39) | copy-start | bytes 1179652
  88.8 9.2 %copy-start.72 = (bf16[128,1024]{1,0:T(8,128)(2,1)S(1)}, bf16[128,1024]{1,0:T(8,128)(2,1)}, u32[]{:S(2)}) copy-start(bf16[128,1024]{1,0:T(8,128)(2,1)} %get-tuple-element.125) | copy-start | bytes 786436
  99.4 6.4 copy-start.105
  99.5 6.4 copy-start.111
  99.5 6.5 copy-start.119
  100.4 9.4 %copy-start.121 = (f32[128]{0:T(128)}, f32[128]{0:T(128)S(1)}, u32[]{:S(2)}) copy-start(f32[128]{0:T(128)S(1)} %add_rsqrt_fusion) | copy-start | bytes 1540
  106.0 38.5 %copy-start.101 = (f32[6,1024]{1,0:T(8,128)S(1)}, f32[6,1024]{1,0:T(8,128)}, u32[]{:S(2)}) copy-start(f32[6,1024]{1,0:T(8,128)} %reshape_squeeze.7) | copy-start | bytes 73732
  106.0 38.5 %copy-start.107 = (f32[1024]{0:T(1024)S(1)}, f32[1024]{0:T(1024)}, u32[]{:S(2)}) copy-start(f32[1024]{0:T(1024)} %slice.285) | copy-start | bytes 12292
  106.0 38.5 %copy-start.123 = (f32[8]{0:T(128)S(1)}, f32[8]{0:T(128)}, u32[]{:S(2)}) copy-start(f32[8]{0:T(128)} %pad.113.clone) | copy-start | bytes 100
  106.1 38.4 %copy-start.124 = (f32[8]{0:T(128)S(1)}, f32[8]{0:T(128)}, u32[]{:S(2)}) copy-start(f32[8]{0:T(128)} %pad.110.clone) | copy-start | bytes 100
  143.7 29.8 %copy-start.31 = (bf16[4,128,384]{2,1,0:T(8,128)(2,1)}, bf16[4,128,384]{2,1,0:T(8,128)(2,1)S(1)}, u32[]{:S(2)}) copy-start(bf16[4,128,384]{2,1,0:T(8,128)(2,1)S(1)} %get-tuple-element.180) | copy-start | bytes 1179652
  145.2 28.3 %copy-start.7 = (bf16[128,1024]{1,0:T(8,128)(2,1)S(1)}, bf16[128,1024]{1,0:T(8,128)(2,1)}, u32[]{:S(2)}) copy-start(bf16[128,1024]{1,0:T(8,128)(2,1)} %copy-done.6) | copy-start | bytes 786436
  214.2 27.2 %copy-start.95 = (bf16[1,128,276]{2,1,0:T(8,128)(2,1)S(1)}, bf16[1,128,276]{2,1,0:T(8,128)(2,1)}, u32[]{:S(2)}) copy-start(bf16[1,128,276]{2,1,0:T(8,128)(2,1)} %copy.82) | copy-start | bytes 211972
  243.1 30.6 %copy-start.63 = (bf16[4,128,1024]{2,1,0:T(8,128)(2,1)S(1)}, bf16[4,128,1024]{2,1,0:T(8,128)(2,1)}, u32[]{:S(2)}) copy-start(bf16[4,128,1024]{2,1,0:T(8,128)(2,1)} %get-tuple-element.169) | copy-start | bytes 3145732
  324.7 34.0 %copy-start.44 = (f32[1024,1024,1]{1,0,2:T(8,128)S(1)}, f32[1024,1024,1]{1,0,2:T(8,128)}, u32[]{:S(2)}) copy-start(f32[1024,1024,1]{1,0,2:T(8,128)} %fusion.116) | copy-start | bytes 12582916
  362.8 88.0 %collective-permute-start = (bf16[1024,512]{1,0:T(8,128)(2,1)}, bf16[1024,512]{1,0:T(8,128)(2,1)}, u32[]{:S(2)}, u32[]{:S(2)}) collective-permute-start(bf16[1024,512]{1,0:T(8,128)(2,1)} %dynamic-slice_convert_fusion.1), channel_id=1, source_target_pairs={{0,4},{4,0},{8,12},{12,8},{16,20},{20,16},{24,28},{28,24},{1,5},{5... | collective-permute-start | bytes 3145736 | tf_op jit(solution)/shard_map/ppermute | solution.py:1598
  366.1 73.0 %slice-start = ((s8[6291456]{0:T(1024)(128)(4,1)}), s8[4194304]{0:T(1024)(128)(4,1)S(1)}, s32[]{:S(2)}) async-start(s8[6291456]{0:T(1024)(128)(4,1)} %bitcast.182), calls=%async_computation | async-start | bytes 8388608
  366.3 5.7 copy-start.110
  366.3 72.8 %slice-start.1 = ((s8[6291456]{0:T(1024)(128)(4,1)}), s8[2097152]{0:T(1024)(128)(4,1)S(1)}, s32[]{:S(2)}) async-start(s8[6291456]{0:T(1024)(128)(4,1)} %bitcast.182), calls=%async_computation.1 | async-start | bytes 4194304
  367.7 71.4 %copy-start.48 = (f32[128,1024]{1,0:T(8,128)S(1)}, f32[128,1024]{1,0:T(8,128)}, u32[]{:S(2)}) copy-start(f32[128,1024]{1,0:T(8,128)} %copy-done.46) | copy-start | bytes 1572868
  367.7 71.4 %copy-start.120 = (f32[128]{0:T(128)S(1)}, f32[128]{0:T(128)}, u32[]{:S(2)}) copy-start(f32[128]{0:T(128)} %copy-done.119) | copy-start | bytes 1540
  367.7 71.4 %copy-start.122 = (f32[128]{0:T(128)S(1)}, f32[128]{0:T(128)}, u32[]{:S(2)}) copy-start(f32[128]{0:T(128)} %copy-done.121) | copy-start | bytes 1540
  368.8 84.7 %collective-permute-start.1 = (bf16[1024,512]{1,0:T(8,128)(2,1)}, bf16[1024,512]{1,0:T(8,128)(2,1)}, u32[]{:S(2)}, u32[]{:S(2)}) collective-permute-start(bf16[1024,512]{1,0:T(8,128)(2,1)} %dynamic-slice_convert_fusion), channel_id=1, source_target_pairs={{0,4},{4,0},{8,12},{12,8},{16,20},{20,16},{24,28},{28,24},{1,5},{5... | collective-permute-start | bytes 3145736 | tf_op jit(solution)/shard_map/ppermute | solution.py:1598
  537.2 36.0 %copy-start.68 = (bf16[3,448,512]{2,1,0:T(8,128)(2,1)S(1)}, bf16[3,448,512]{2,1,0:T(8,128)(2,1)}, u32[]{:S(2)}) copy-start(bf16[3,448,512]{2,1,0:T(8,128)(2,1)} %get-tuple-element.193) | copy-start | bytes 4128772
  537.3 37.0 %copy-start.67 = (bf16[3,448,512]{2,1,0:T(8,128)(2,1)S(1)}, bf16[3,448,512]{2,1,0:T(8,128)(2,1)}, u32[]{:S(2)}) copy-start(bf16[3,448,512]{2,1,0:T(8,128)(2,1)} %get-tuple-element.195) | copy-start | bytes 4128772
  569.8 5.7 copy-start.4
  569.8 5.7 copy-start.10
  574.3 7.4 copy-start.75
  587.1 5.8 copy-start.50
  587.1 5.8 copy-start.52
  754.9 79.1 %copy-start.108 = (f32[5,256]{1,0:T(8,128)S(1)}, f32[5,256]{1,0:T(8,128)}, u32[]{:S(2)}) copy-start(f32[5,256]{1,0:T(8,128)} %refs_0_.1) | copy-start | bytes 15364
  754.9 82.1 %copy-start.66 = (f32[128,768]{1,0:T(8,128)S(1)}, f32[128,768]{1,0:T(8,128)}, u32[]{:S(2)}) copy-start(f32[128,768]{1,0:T(8,128)} %param.39) | copy-start | bytes 1179652
  833.9 7.0 copy-start.59
  833.9 7.0 copy-start.85
  833.9 7.0 copy-start.86
  833.9 7.9 copy-start.109
  833.9 7.9 copy-start.115
  834.0 7.9 copy-start.116
  834.0 8.5 copy-start.87
  834.0 8.5 copy-start.88
  834.0 8.5 copy-start.98
  834.0 8.5 copy-start.99
  837.0 6.3 copy-start.58
  837.0 6.3 copy-start.69
  837.1 6.3 copy-start.81
  837.1 6.3 copy-start.82
  (84 other events, 240.1 us)

commit v6 on v5

--- a/solution.py
+++ b/solution.py
@@ -573,6 +573,9 @@
         self.locals.append((source, source_at, target, target_at, later))
         return len(self.locals) - 1
 
+    def shape(self, scratch):
+        return self.scratches[scratch[1]].shape
+
     def load(self, array):
         target = self.scratch(array.shape, array.dtype)
         return target, self.keep(self.operand(array), None, target, None)
@@ -755,16 +758,16 @@
             return waiting
         self.to_sibling(waiting)
 
-    def gather_columns(self, axis, array):
+    def gather_columns(self, axis, array, target):
         width = array.shape[-1]
-        target = self.output(array.shape[:-1] + (lax.axis_size(axis) * width,), array.dtype)
         lead = (slice(None),) * (array.ndim - 1)
-        self.along(
+        numbers = self.along(
             axis,
             self.operand(array),
             target,
             [(None, lambda sender: lead + (pl.ds(pl.multiple_of(sender * width, LANES), width),))],
         )
+        return numbers, len(self.locals) - 1
 
     def gather_twice(self, arrays, members):
         shards = lax.axis_size(SHARDS)
@@ -772,7 +775,7 @@
         for array in arrays:
             source = self.operand(array)
             width = array.shape[1]
-            target = self.output((array.shape[0], shards * width), array.dtype)
+            target = self.scratch((array.shape[0], shards * width), array.dtype)
             rows = array.shape[0] // members
 
             def columns(back_pair, width=width):
@@ -786,6 +789,9 @@
             def mine(rows=rows):
                 index = lax.rem(lax.axis_index(PATCHES), members)
                 return (pl.ds(pl.multiple_of(index * rows, rows), rows),)
+
+            def whole(columns=columns):
+                return (slice(None), columns(0))
 
             firsts = [
                 self.move(
@@ -798,10 +804,11 @@
                 )
                 for pair in range(1, shards // 2)
             ]
-            entries.append((source, target, place, firsts))
-            self.move((SHARDS,), sibling_peer, source, None, target, lambda columns=columns: (slice(None), columns(0)))
+            near = self.move((SHARDS,), sibling_peer, source, None, target, whole)
+            local = self.keep(source, None, target, whole)
+            entries.append((target, place, firsts, [near, *firsts], local))
         last = []
-        for _, target, place, firsts in entries:
+        for target, place, firsts, numbers, _ in entries:
             for pair, first in enumerate(firsts, 1):
                 near = functools.partial(place, 0, pair)
                 for shift in range(1, members):
@@ -814,9 +821,11 @@
                         near,
                         (first,),
                     )
-                    last.append((target, functools.partial(place, shift, pair), number))
-                self.move((SHARDS,), sibling_peer, target, near, target, near, (first,))
-        self.to_sibling(last)
+                    last.append((target, functools.partial(place, shift, pair), number, numbers))
+                numbers.append(self.move((SHARDS,), sibling_peer, target, near, target, near, (first,)))
+        for target, at, number, numbers in last:
+            numbers += [number, self.move((SHARDS,), sibling_peer, target, at, target, at, (number,))]
+        return [(target, numbers, local) for target, _, _, numbers, local in entries]
 
     def to_sibling(self, waiting):
         for target, place, number in waiting:
@@ -1038,6 +1047,123 @@
 
 def mod_row(ref, table, row):
     return ref(table)[pl.ds(row, 1), :]
+
+
+def project(moves, source, weights, target, count):
+    def action(ref):
+        width = ref(source).shape[1]
+
+        @pl.loop(0, count // width)
+        def _(part):
+            cols = pl.ds(pl.multiple_of(part * width, width), width)
+            ref(target)[:, cols] = contract(ref(source)[...], ref(weights)[:, cols], 1, 0).astype(LOW)
+
+    moves.task(action)
+
+
+def embed(ref, state_low, io_weights, mods, pos, embedded, normed_low):
+    value = contract(ref(state_low)[...], io_weights, 1, 0) + mods(6) + ref(pos)[...].astype(jnp.float32)
+    ref(embedded)[...] = value
+    normed, _ = layer_norm(value)
+    ref(normed_low)[...] = (normed * (1.0 + mods(1)) + mods(0)).astype(LOW)
+
+
+def begin_step(ids, members, state, id_rows, active, cond_table, biases, pos, ada, io_low, w_out, w_qkv):
+    f32 = jnp.float32
+    shards = lax.axis_size(SHARDS)
+    (rows, padded), (table_rows, _) = state.shape, cond_table.shape
+    width = w_out.shape[0]
+    ada_cols = ada.shape[1]
+    moves = Moves("begin", ids, 56 * 2**20)
+    table = moves.scratch((table_rows, width), f32)
+    bias = moves.scratch((1, biases.shape[1] * shards), f32)
+    pos_all = moves.scratch((rows, width), LOW)
+    id_rows, active, state = [moves.operand(item, pltpu.VMEM) for item in (id_rows, active, state)]
+    small = [moves.gather_columns(SHARDS, cond_table, table), moves.gather_columns(SHARDS, biases, bias)]
+    pos_moves, pos_local = moves.gather_columns(SHARDS, pos, pos_all)
+    ada_weights, ada_load = moves.load(ada)
+    vmem = functools.partial(moves.output, space=pltpu.VMEM)
+    extras = vmem((ROLL, 8, width), f32)
+    cond_vec, silu_low = vmem((shards * ROLL, width), f32), vmem((shards * ROLL, width), LOW)
+    embedded, normed_low = vmem((rows, width), f32), vmem((rows, width), LOW)
+    state_low, qkv_rows = vmem((rows, padded), LOW), vmem((rows, 3 * width), LOW)
+    parts_leaving, parts = [moves.scratch((shards, ROLL, ada_cols), f32) for _ in range(2)]
+
+    def modulate(ref):
+        row = lax.broadcasted_iota(jnp.int32, (shards * ROLL, 1), 0)
+        ids_here = ref(id_rows)[:, :1]
+        value = jnp.zeros((shards * ROLL, width), f32)
+        for entry in range(table_rows):
+            of_entry = ref(table)[pl.ds(entry, 1), :].astype(LOW).astype(f32)
+            chosen = (ids_here == entry) if entry < NI else (lax.rem(row, ROLL) == entry - NI)
+            value = value + jnp.where(chosen, of_entry, 0.0)
+        ref(cond_vec)[...] = value
+        value = (value / (1.0 + jnp.exp(-value))).astype(LOW)
+        ref(silu_low)[...] = value
+        start = pl.multiple_of(lax.axis_index(SHARDS) * ada_cols, LANES)
+        value = contract(value, ref(ada_weights)[...], 1, 0)
+        value = value + ref(bias)[:, pl.ds(start, ada_cols)].astype(LOW).astype(f32)
+        for sample in range(shards):
+            ref(parts_leaving)[sample] = value[sample * ROLL : (sample + 1) * ROLL]
+        ref(parts)[lax.axis_index(SHARDS)] = ref(parts_leaving)[lax.axis_index(SHARDS)]
+
+    for numbers, local in small:
+        for number in numbers:
+            moves.wait_for(number)
+        moves.wait_local(local)
+    moves.wait_local(ada_load)
+    moves.task(modulate)
+    modul_moves = []
+    for shift in range(1, shards):
+
+        def other(shift=shift):
+            return lax.rem(lax.axis_index(SHARDS) + shift, shards)
+
+        number = moves.move(
+            (SHARDS, shift),
+            lambda other=other: {SHARDS: other()},
+            parts_leaving,
+            lambda other=other: (other(),),
+            parts,
+            lambda: (lax.axis_index(SHARDS),),
+            later=True,
+        )
+        modul_moves.append(number)
+        moves.start(number)
+    weights = moves.gather_twice((io_low.reshape(-1, io_low.shape[-1]), w_out, w_qkv), members)
+
+    def collect(ref):
+        bias_row = ref(bias)[:, pl.ds(6 * width, width)].astype(LOW).astype(f32)
+        for step in range(ROLL):
+            for piece in range(6 * 2):
+                start = piece * width // 2
+                value = ref(parts)[start // ada_cols, pl.ds(step, 1), pl.ds(start % ada_cols, width // 2)]
+                ref(extras)[step, pl.ds(piece // 2, 1), pl.ds(piece % 2 * width // 2, width // 2)] = value
+            ref(extras)[step, pl.ds(6, 1), :] = bias_row
+            ref(extras)[step, pl.ds(7, 1), :] = ref(active)[pl.ds(step, 1), :]
+
+    def start_step(ref):
+        ref(state_low)[...] = ref(state)[...].astype(LOW)
+        mods = lambda row: ref(extras)[0, pl.ds(row, 1), :]
+        embed(ref, state_low, ref(weights[0][0])[pl.ds(0, padded), :], mods, pos_all, embedded, normed_low)
+
+    for number in modul_moves:
+        moves.wait_for(number)
+    moves.task(collect)
+    for number in (*pos_moves, *weights[0][1]):
+        moves.wait_for(number)
+    moves.wait_local(pos_local)
+    moves.wait_local(weights[0][2])
+    moves.task(start_step)
+    for target, numbers, local in weights:
+        for number in numbers:
+            moves.wait_for(number)
+        moves.wait_local(local)
+        save = moves.save(target, moves.shape(target), LOW)
+        moves.start_local(save)
+    moves.start_local(moves.save(pos_all, (rows, width), LOW))
+    project(moves, normed_low, weights[2][0], qkv_rows, 3 * width)
+    return moves.run()
 
 
 class Tokens:
@@ -1220,20 +1346,9 @@
         value = ref(state)[...] + mod_row(ref, mods, 7)[:, :padded] * delta
         ref(state_next)[...] = value
         if not last:
-            value = value.astype(LOW)
-            ref(state_low)[...] = value
-            value = contract(value, ref(io_weights)[0], 1, 0) + mod_row(ref, mods, 6) + ref(pos)[...]
-            ref(embedded_next)[...] = value
-            normed, _ = layer_norm(value)
-            normed = (normed * (1.0 + mod_row(ref, mods_next, 1)) + mod_row(ref, mods_next, 0)).astype(LOW)
-            ref(normed_next)[...] = normed
-
-    def project(ref):
-        @pl.loop(0, w_qkv.shape[1] // width)
-        def _(part):
-            cols = pl.ds(pl.multiple_of(part * width, width), width)
-            value = contract(ref(normed_next)[...], ref(qkv_weights)[:, cols], 1, 0)
-            ref(qkv_next)[:, cols] = value.astype(LOW)
+            ref(state_low)[...] = value.astype(LOW)
+            mods_there = functools.partial(mod_row, ref, mods_next)
+            embed(ref, state_low, ref(io_weights)[0], mods_there, pos, embedded_next, normed_next)
 
     moves.wait_local(out_load)
     moves.task(begin)
@@ -1247,7 +1362,7 @@
     moves.task(finish)
     if not last:
         moves.wait_local(qkv_load)
-        moves.task(project)
+        project(moves, normed_next, qkv_weights, qkv_next, w_qkv.shape[1])
     return moves.run()
 
 
@@ -1346,6 +1461,370 @@
     moves.task(finish)
     results = moves.run()
     return results if later is not None else [None, *results]
+
+
+def reduce_step(
+    ids, members, group_cols, qkv_grad, embedded, grad_attn, mods, w_qkv, rows_late, rows_early, gathered, mlp, ada
+):
+    f32 = jnp.float32
+    shards, seq_count = lax.axis_size(SHARDS), lax.axis_size(PATCHES)
+    rows, width = embedded.shape
+    block_rows, most_cols = width, max(group_cols)
+    part, ada_cols = width // shards, ada.shape[1]
+    up_mine, down_mine, down_leaving = mlp
+    moves = Moves("reduce", ids, 60 * 2**20)
+    vmem = functools.partial(moves.operand, space=pltpu.VMEM)
+    qkv_grad, embedded, grad_attn, mods = vmem(qkv_grad), vmem(embedded), vmem(grad_attn), vmem(mods)
+    rows_late, rows_early = vmem(rows_late), vmem(rows_early)
+
+    def shard():
+        return lax.axis_index(SHARDS)
+
+    def patch():
+        return lax.axis_index(PATCHES)
+
+    def group():
+        return patch() // members
+
+    def member():
+        return lax.rem(patch(), members)
+
+    def columns(index, size):
+        return pl.ds(pl.multiple_of(index * size, LANES), size)
+
+    def await_all(numbers):
+        for number in numbers:
+            moves.wait_for(number)
+
+    def to_others(axis, source, source_at, target, leave_own=False):
+        count = lax.axis_size(axis)
+        numbers = []
+        for shift in range(1, count):
+
+            def other(shift=shift):
+                return lax.rem(lax.axis_index(axis) + shift, count)
+
+            number = moves.move(
+                (axis, shift),
+                lambda other=other: {axis: other()},
+                source,
+                lambda other=other: source_at(other()),
+                target,
+                lambda: (lax.axis_index(axis),),
+                later=True,
+            )
+            moves.start(number)
+            numbers.append(number)
+
+        def own(ref):
+            ref(target)[lax.axis_index(axis)] = ref(source)[source_at(lax.axis_index(axis))]
+
+        moves.task(own)
+        return numbers
+
+    def to_members(source, target, cols):
+        numbers = []
+        for shift in range(1, members):
+            number = moves.move(
+                (PATCHES, members, shift),
+                functools.partial(member_peer, members, shift),
+                source,
+                lambda shift=shift: (slice(None), columns(lax.rem(member() + shift, members), cols)),
+                target,
+                lambda shift=shift: (shift - 1,),
+                later=True,
+            )
+            moves.start(number)
+            numbers.append(number)
+        return numbers
+
+    def to_group(source, target, which):
+        numbers = []
+        for shift in range(1, MATRICES):
+            number = moves.move(
+                (PATCHES, seq_count, shift),
+                functools.partial(group_peer, members, shift),
+                source,
+                None,
+                target,
+                lambda shift=shift: (shift - 1,),
+                sends=lambda shift=shift: group() == (which - shift) % MATRICES,
+                takes=lambda: group() == which,
+                later=True,
+            )
+            moves.start(number)
+            numbers.append(number)
+        return numbers
+
+    def over_rows(action):
+        @pl.loop(0, block_rows // GRAM_COLS)
+        def _(tile):
+            action(pl.ds(pl.multiple_of(tile * GRAM_COLS, GRAM_COLS), GRAM_COLS))
+
+    def weight_grad(lefts, rights, full, low=None):
+        depth, cols = moves.shape(lefts[0])[2], moves.shape(rights[0])[2]
+        tile_rows = GRAM_COLS if depth % GRAM_COLS == 0 else LANES
+
+        def action(ref):
+            @pl.loop(0, depth // tile_rows)
+            def _(tile):
+                at = pl.ds(pl.multiple_of(tile * tile_rows, tile_rows), tile_rows)
+                value = jnp.zeros((tile_rows, cols), f32)
+                for left, right in zip(lefts, rights):
+                    left_rows = ref(left)[:, :, at].reshape(-1, tile_rows)
+                    value = value + contract(left_rows, ref(right)[...].reshape(-1, cols), 0, 0)
+                if full is not None:
+                    ref(full)[at, :] = value
+                if low is not None:
+                    ref(low)[at, :] = value.astype(LOW)
+
+        moves.task(action)
+
+    qkv_all = moves.scratch((shards, rows, 3 * part), LOW)
+    qkv_moves = moves.along(
+        SHARDS,
+        qkv_grad,
+        qkv_all,
+        [(lambda receiver: (slice(None), columns(receiver, 3 * part)), lambda sender: (sender,))],
+    )
+    qkv_local = len(moves.locals) - 1
+    down_arriving = moves.scratch((members - 1, block_rows, group_cols[2]), LOW)
+    down_moves = [
+        moves.move(
+            (PATCHES, members, shift),
+            functools.partial(member_peer, members, shift),
+            moves.operand(item),
+            None,
+            down_arriving,
+            lambda shift=shift: (shift - 1,),
+        )
+        for shift, item in enumerate(down_leaving, 1)
+    ]
+    up_full, up_load = moves.load(up_mine)
+    qkv_weights, qkv_load = moves.load(w_qkv)
+    loaded = {
+        name: [moves.load(steps[step]) for step in range(ROLL) if step in steps] for name, steps in gathered.items()
+    }
+    down_full, down_load = moves.load(down_mine)
+    ada_weights, ada_load = moves.load(ada)
+
+    def ready(*names):
+        for name in names:
+            for _, number in loaded[name]:
+                moves.wait_local(number)
+        return [[item for item, _ in loaded[name]] for name in names]
+
+    up_low, down_low = [moves.scratch((block_rows, cols), LOW) for cols in group_cols[1:3]]
+    group_target = moves.scratch((MATRICES - 1, block_rows, most_cols), LOW)
+
+    def round_up_grad(ref):
+        def action(at):
+            ref(up_low)[at, :] = ref(up_full)[at, :].astype(LOW)
+
+        over_rows(action)
+
+    moves.wait_local(up_load)
+    moves.task(round_up_grad)
+    up_moves = to_group(up_low, group_target, 1)
+
+    embed_low = moves.scratch((rows, width), LOW)
+    table = moves.scratch((8, 6 * width), f32)
+
+    def back(ref):
+        grad = contract(ref(qkv_grad)[...], ref(qkv_weights)[...], 1, 1)
+        normed, inverse = layer_norm(ref(embedded)[...])
+        ref(table)[...] = jnp.zeros((8, 6 * width), f32)
+        ref(table)[pl.ds(0, 1), pl.ds(0, width)] = jnp.sum(grad, 0, keepdims=True)
+        ref(table)[pl.ds(0, 1), pl.ds(width, width)] = jnp.sum(grad * normed, 0, keepdims=True)
+        grad = ref(grad_attn)[...] + norm_back(grad * (1.0 + mod_row(ref, mods, 1)), normed, inverse)
+        ref(embed_low)[...] = grad.astype(LOW)
+        bias_row = jnp.sum(grad, 0, keepdims=True) + mod_row(ref, rows_early, 6)
+        for entry in range(4):
+            cols = pl.ds((2 + entry) * width, width)
+            ref(table)[pl.ds(0, 1), cols] = mod_row(ref, rows_early, entry)
+            ref(table)[pl.ds(1, 1), cols] = mod_row(ref, rows_late, entry)
+        for entry in range(2):
+            ref(table)[pl.ds(1, 1), pl.ds(entry * width, width)] = mod_row(ref, rows_early, 4 + entry)
+        for entry in range(shards):
+            ref(table)[pl.ds(ROLL, 1), pl.ds(entry * ada_cols, part)] = bias_row[:, entry * part : (entry + 1) * part]
+
+    moves.wait_local(qkv_load)
+    moves.task(back)
+    embed_all = moves.scratch((shards, rows, part), LOW)
+    table_all = moves.scratch((shards, 8, ada_cols), f32)
+    embed_moves = to_others(SHARDS, embed_low, lambda there: (slice(None), columns(there, part)), embed_all)
+    table_moves = to_others(SHARDS, table, lambda there: (slice(None), columns(there, ada_cols)), table_all)
+
+    out_cols, qkv_cols = group_cols[3], group_cols[0]
+    out_full, out_low = moves.scratch((width, part), f32), moves.scratch((width, part), LOW)
+    qkv_full, qkv_low = moves.scratch((width, 3 * part), f32), moves.scratch((width, 3 * part), LOW)
+    out_arriving = moves.scratch((members - 1, block_rows, out_cols), LOW)
+    qkv_arriving = moves.scratch((members - 1, block_rows, qkv_cols), LOW)
+    padded = moves.shape(loaded["state"][0][0])[2]
+    io_low = moves.scratch((2 * padded, part), LOW)
+    io_grads = [moves.scratch((padded, part), f32) for _ in range(2)]
+    weight_grad(*ready("mixed", "attn"), out_full, out_low)
+    out_moves = to_members(out_low, out_arriving, out_cols)
+    weight_grad(*ready("delta", "c"), io_grads[1])
+    await_all(qkv_moves)
+    moves.wait_local(qkv_local)
+    (a_all, qkv_later) = ready("a", "qkv")
+    weight_grad(a_all, [qkv_all, *qkv_later], qkv_full, qkv_low)
+    qkv_member_moves = to_members(qkv_low, qkv_arriving, qkv_cols)
+    await_all(embed_moves)
+    (state_all, embed_later) = ready("state", "embed")
+    weight_grad(state_all, [embed_all, *embed_later], io_grads[0])
+    grad_pos = moves.output((rows, part), f32, pltpu.VMEM)
+    io_rows = 2 * padded // seq_count
+
+    def pos_and_io(ref):
+        value = jnp.zeros((rows, part), f32)
+        for item in (embed_all, *embed_later):
+            for sample in range(shards):
+                value = value + ref(item)[sample].astype(f32)
+        ref(grad_pos)[...] = value
+        for number, item in enumerate(io_grads):
+            ref(io_low)[pl.ds(number * padded, padded), :] = ref(item)[...].astype(LOW)
+
+    moves.task(pos_and_io)
+    io_all = moves.scratch((seq_count, io_rows, part), LOW)
+    io_moves = to_others(
+        PATCHES, io_low, lambda there: (pl.ds(pl.multiple_of(there * io_rows, io_rows), io_rows),), io_all
+    )
+
+    flat, flat_all = moves.scratch((16, ada_cols), LOW), moves.scratch((seq_count, 16, ada_cols), LOW)
+
+    def share(ref):
+        pieces = [ref(table_all)[sample, pl.ds(0, ROLL), :] for sample in range(shards)]
+        bias_row = sum(ref(table_all)[sample, pl.ds(ROLL, 1), :] for sample in range(shards))
+        rest = jnp.zeros((16 - shards * ROLL - 1, ada_cols), f32)
+        ref(flat)[...] = jnp.concatenate([*pieces, bias_row, rest], 0).astype(LOW)
+
+    await_all(table_moves)
+    moves.task(share)
+    flat_moves = to_others(PATCHES, flat, lambda there: (slice(None), slice(None)), flat_all)
+
+    def add_member(full, arriving, target, low, cols):
+        def action(ref):
+            def add(at):
+                value = ref(full)[at, columns(member(), cols)] if target is not full else ref(full)[at, :]
+                for shift in range(members - 1):
+                    value = value + ref(arriving)[shift, at, :].astype(f32)
+                ref(target)[at, :] = value
+                if low is not None:
+                    ref(low)[at, :] = value.astype(LOW)
+
+            over_rows(add)
+
+        moves.task(action)
+
+    moves.wait_local(down_load)
+    await_all(down_moves)
+    add_member(down_full, down_arriving, down_full, down_low, group_cols[2])
+    down_group_moves = to_group(down_low, group_target, 2)
+    out_mine, out_mine_low = moves.scratch((width, out_cols), f32), moves.scratch((width, out_cols), LOW)
+    out_target = moves.scratch((MATRICES - 1, block_rows, out_cols), LOW)
+    await_all(out_moves)
+    add_member(out_full, out_arriving, out_mine, out_mine_low, out_cols)
+    out_group_moves = to_group(out_mine_low, out_target, 3)
+
+    modul_all = moves.output((shards * ROLL, ada_cols), f32, pltpu.VMEM)
+    tail_all = moves.output((shards, 16, ada_cols), f32, pltpu.VMEM)
+    tail = moves.scratch((16, ada_cols), f32)
+
+    def close(ref):
+        value = jnp.zeros((16, ada_cols), f32)
+        for item in range(seq_count):
+            value = value + ref(flat_all)[item].astype(f32)
+        modul = value[: shards * ROLL]
+        ref(modul_all)[...] = modul
+        high = modul.astype(LOW)
+        rest = (modul - high.astype(f32)).astype(LOW)
+        weights = ref(ada_weights)[...]
+        ref(tail)[...] = jnp.zeros((16, ada_cols), f32)
+        ref(tail)[pl.ds(0, shards * ROLL), pl.ds(0, width)] = contract(high, weights, 1, 1) + contract(
+            rest, weights, 1, 1
+        )
+        ref(tail)[pl.ds(8, 1), :] = jnp.sum(modul, 0, keepdims=True)
+        ref(tail)[pl.ds(9, 1), :] = value[shards * ROLL : shards * ROLL + 1]
+
+    await_all(flat_moves)
+    moves.wait_local(ada_load)
+    moves.task(close)
+    to_others(SHARDS, tail, lambda there: (slice(None), slice(None)), tail_all)
+
+    def has_source():
+        return group() < MATRICES - 1
+
+    def is_source():
+        return group() > 0
+
+    chain = moves.scratch((width, qkv_cols), f32)
+    chain_in, chain_out = [moves.scratch((width, qkv_cols), LOW) for _ in range(2)]
+    await_all(qkv_member_moves)
+    add_member(qkv_full, qkv_arriving, chain, None, qkv_cols)
+    chunk = block_rows // CHAIN_CHUNKS
+    for number_of in range(CHAIN_CHUNKS):
+        place = (pl.ds(number_of * chunk, chunk),)
+        number = moves.move(
+            (PATCHES, seq_count, MATRICES - 1),
+            functools.partial(group_peer, members, MATRICES - 1),
+            chain_out,
+            lambda place=place: place,
+            chain_in,
+            lambda place=place: place,
+            sends=is_source,
+            takes=has_source,
+            later=True,
+        )
+
+        def add(ref, place=place):
+            def with_arriving():
+                ref(chain)[place] += ref(chain_in)[place].astype(f32)
+
+            pl.when(has_source())(with_arriving)
+            ref(chain_out)[place] = ref(chain)[place].astype(LOW)
+
+        moves.wait_for(number)
+        moves.task(add)
+        moves.start(number)
+
+    io_slice = moves.output((io_rows, part), f32, pltpu.VMEM)
+
+    def add_io(ref):
+        value = jnp.zeros((io_rows, part), f32)
+        for item in range(seq_count):
+            value = value + ref(io_all)[item].astype(f32)
+        ref(io_slice)[...] = value
+
+    await_all(io_moves)
+    moves.task(add_io)
+
+    grad_group = moves.output((block_rows, most_cols), f32, pltpu.VMEM)
+
+    def put(full, target, cols):
+        def action(ref):
+            def add(at):
+                value = ref(full)[at, :]
+                if target is not None:
+                    for shift in range(MATRICES - 1):
+                        value = value + ref(target)[shift, at, pl.ds(0, cols)].astype(f32)
+                ref(grad_group)[at, pl.ds(0, cols)] = value
+                if cols < most_cols:
+                    ref(grad_group)[at, pl.ds(cols, most_cols - cols)] = jnp.zeros((GRAM_COLS, most_cols - cols), f32)
+
+            over_rows(add)
+
+        return action
+
+    def settle(ref):
+        entries = ((chain, None), (up_full, group_target), (down_full, group_target), (out_mine, out_target))
+        for which, (full, target) in enumerate(entries):
+            pl.when(group() == which)(functools.partial(put(full, target, group_cols[which]), ref))
+
+    await_all((*up_moves, *down_group_moves, *out_group_moves))
+    moves.task(settle)
+    return moves.run()
 
 
 def newton_schulz(source, gram, poly, once, gram_low, poly_low, once_low, block, block_next):
@@ -1469,33 +1948,40 @@
     ada_cols = ada_copy.shape[1]
     padded = round_up(values_count, LANES)
 
-    moves = Moves("tables", ids)
-    moves.gather(SHARDS, cond_table)
-    moves.gather(SHARDS, biases[None])
-    table_parts, bias_parts = moves.run()
-    table = jnp.moveaxis(table_parts, 0, 1).reshape(table_rows, width).astype(LOW).astype(f32)
-    bias = bias_parts.reshape(-1).astype(LOW).astype(f32)
+    value_pad = ((0, 0), (0, padded - values_count))
+    state = jnp.pad(states[0].astype(f32), value_pad)
+    length = lengths[0]
+    (
+        extras,
+        cond_vec,
+        silu_low,
+        embedded,
+        normed_a,
+        state_low,
+        qkv_rows,
+        io_all,
+        w_out,
+        w_qkv,
+        pos,
+    ) = begin_step(
+        ids,
+        members,
+        state,
+        jnp.broadcast_to(intervals[:, None, None], (shards, ROLL, LANES)).reshape(-1, LANES),
+        jnp.broadcast_to((jnp.arange(ROLL, dtype=jnp.int32)[:, None] < length).astype(f32), (ROLL, width)),
+        cond_table,
+        biases[None],
+        pos_table.astype(LOW),
+        ada_copy,
+        jnp.pad(io_proj.astype(LOW), ((0, 0), (0, padded - values_count), (0, 0))),
+        out_copy,
+        qkv_copy,
+    )
+    io_all = io_all.reshape(2, padded, width)
     rows_iota = jnp.arange(table_rows, dtype=jnp.int32)
     id_rows = (intervals[:, None] == rows_iota[None]).astype(f32)
     step_rows = (rows_iota[None] == NI + jnp.arange(ROLL, dtype=jnp.int32)[:, None]).astype(f32)
     select = (id_rows[:, None] + step_rows[None]).reshape(-1, table_rows)
-    cond_vec = jnp.sum(select[:, :, None] * table[None], 1)
-    silu_low = jax.nn.silu(cond_vec).astype(LOW)
-    modul_shard = product(silu_low, ada_copy) + lax.dynamic_slice_in_dim(bias, shard * ada_cols, ada_cols)[None]
-
-    moves = Moves("weights", ids)
-    moves.exchange(SHARDS, modul_shard.reshape(shards, ROLL, ada_cols))
-    moves.gather_columns(SHARDS, pos_table.astype(LOW))
-    io_low = jnp.pad(io_proj.astype(LOW), ((0, 0), (0, padded - values_count), (0, 0)))
-    own_parts = (io_low.reshape(2 * padded, -1), out_copy, qkv_copy)
-    moves.gather_twice(own_parts, members)
-    modul, pos, *parts = moves.run()
-    io_all, w_out, w_qkv = [
-        lax.dynamic_update_slice_in_dim(part, own, shard * own.shape[1], 1) for part, own in zip(parts, own_parts)
-    ]
-    io_all = io_all.reshape(2, padded, width)
-    modul = jnp.moveaxis(modul, 0, 1).reshape(ROLL, 6 * width)
-    pos = pos.astype(f32)
 
     masters = (qkv_master, up_master, down_master, out_master)
     momenta = (qkv_moment, up_moment, down_moment, out_moment)
@@ -1518,28 +2004,10 @@
     my_id = lax.dynamic_slice_in_dim(intervals, shard, 1)
     id_count = jnp.sum((my_id == jnp.arange(NI, dtype=jnp.int32)).astype(f32) * counts)
     weight = 1.0 / (NI * local * seq_count * values_count * id_count)
-    length = lengths[0]
-    value_pad = ((0, 0), (0, padded - values_count))
-    state = jnp.pad(states[0].astype(f32), value_pad)
-    embed_bias = bias[6 * width :]
     kept = []
     gathered = {}
     moment_halves = []
 
-    extras = [
-        jnp.concatenate(
-            [
-                modul[step].reshape(6, width),
-                embed_bias[None],
-                jnp.broadcast_to((step < length).astype(f32), (1, width)),
-            ]
-        )
-        for step in range(ROLL)
-    ]
-    state_low = state.astype(LOW)
-    embedded = product(state_low, io_all[0]) + embed_bias + pos
-    normed_a = (layer_norm(embedded)[0] * (1.0 + extras[0][1]) + extras[0][0]).astype(LOW)
-    qkv_rows = product(normed_a, w_qkv).astype(LOW)
     for step in range(ROLL):
         moves = Moves(f"attend{step}", ids, 48 * 2**20)
         qkv_out = moves.output((3, local * seq_count, width // seq_count), LOW, pltpu.VMEM)
@@ -1599,12 +2067,7 @@
         return mine
 
     later, mods_later = None, None
-    mod_grads = [[None] * 6 for _ in range(ROLL)]
-    bias_grads = []
-
-    def put_mods(step, names_and_rows):
-        for place, row in names_and_rows:
-            mod_grads[step][place] = row
+    vector_rows = [None] * ROLL
 
     for step in reversed(range(ROLL)):
         embedded, qkv, mixed, for_feed, normed_c, tokens_b, hidden = kept[step]
@@ -1622,16 +2085,20 @@
             io_all,
             w_qkv,
         )
-        put_mods(step, ((2, vectors[0]), (3, vectors[1]), (4, vectors[2]), (5, vectors[3])))
-        if later is not None:
-            put_mods(step + 1, ((0, vectors[4]), (1, vectors[5])))
-            bias_grads.append(vectors[6])
+        vector_rows[step] = vectors
         mlp_back.append((tokens_b, up_grad, tokens_down, hidden))
         if step == 0:
-            mlp_sums = []
-            for left, right, cols in ((0, 1, group_cols[1]), (2, 3, group_cols[2])):
-                total = sum(rows_product(items[left], items[right]) for items in mlp_back)
-                mlp_sums.append(patch_sum(total, cols))
+            up_total, down_total = [
+                sum(rows_product(items[left], items[right]) for items in mlp_back) for left, right in ((0, 1), (2, 3))
+            ]
+            up_mine = patch_sum(up_total, group_cols[1])
+            down_mine = lax.dynamic_slice_in_dim(down_total, member * group_cols[2], group_cols[2], 1)
+            down_leaving = [
+                lax.dynamic_slice_in_dim(
+                    down_total, lax.rem(member + shift, members) * group_cols[2], group_cols[2], 1
+                ).astype(LOW)
+                for shift in range(1, members)
+            ]
         moves = Moves(f"attend_back{step}", ids, 48 * 2**20)
         grads_in = moves.scratch((1, local * seq_count, width // seq_count), LOW)
         result = moves.output((local, 3 * width), LOW, pltpu.VMEM)
@@ -1654,155 +2121,26 @@
         for name, item in zip(names, others):
             gathered.setdefault(name, {})[step + (name in ("qkv", "embed"))] = item
         later, mods_later = (qkv_grad, embedded, grad_attn), extras[step]
-    grad_normed_a = contract(qkv_grad, w_qkv, 1, 1)
-    normed_one, inverse_one = layer_norm(embedded)
-    put_mods(0, ((0, jnp.sum(grad_normed_a, 0)), (1, jnp.sum(grad_normed_a * normed_one, 0))))
-    grad_embedded = grad_attn + norm_back(grad_normed_a * (1.0 + extras[0][1:2]), normed_one, inverse_one)
-    embed_grad = grad_embedded.astype(LOW)
-    bias_grads.append(jnp.sum(grad_embedded, 0))
-
-    mlp_low = [item.astype(LOW) for item in mlp_sums]
-    modul_parts = jnp.stack([jnp.concatenate(item).reshape(shards, ada_cols) for item in mod_grads], 1)
-    embed_parts = sum(bias_grads).reshape(shards, 1, -1)
-    vectors = jnp.concatenate(
-        [modul_parts, jnp.pad(embed_parts, ((0, 0), (0, 0), (0, ada_cols - embed_parts.shape[-1])))], 1
-    )
-
-    def to_group(moves, item, which, start, size):
-        source = moves.operand(item)
-        target = moves.output((MATRICES - 1, size, item.shape[1]), LOW)
-        for shift in range(1, MATRICES):
-            moves.move(
-                (PATCHES, seq_count, shift),
-                functools.partial(group_peer, members, shift),
-                source,
-                lambda: (pl.ds(start, size),),
-                target,
-                lambda shift=shift: (shift - 1,),
-                sends=lambda shift=shift: lax.axis_index(PATCHES) // members == (which - shift) % MATRICES,
-                takes=lambda: lax.axis_index(PATCHES) // members == which,
-            )
 
     block_rows = qkv_copy.shape[0]
-    early = (1, 2)
-    first_rows = block_rows * 7 // 16
-    moves = Moves("samples", ids)
-    moves.exchange_columns(SHARDS, qkv_grad)
-    moves.exchange_columns(SHARDS, embed_grad)
-    moves.exchange(SHARDS, vectors)
-    for item, which in zip(mlp_low, early):
-        to_group(moves, item, which, 0, first_rows)
-    gathered["qkv"][0], gathered["embed"][0], vectors, *mlp_first = moves.run()
-    grad_pos = sum(jnp.sum(item.astype(f32), 0) for item in gathered["embed"].values())
-
-    def from_all(left, right):
-        both = [
-            jnp.concatenate([gathered[name][step].reshape(shards * local, -1) for step in range(ROLL)], 0)
-            for name in (left, right)
-        ]
-        return rows_product(*both)
-
-    io_here = jnp.stack([from_all("state", "embed"), from_all("delta", "c")])
-    io_cols = io_here.shape[-1]
-    grads_here = [from_all("a", "qkv"), from_all("mixed", "attn")]
-    late = (0, MATRICES - 1)
-
-    moves = Moves("member_sums", ids)
-    for item, which in zip(grads_here, late):
-        cols = group_cols[which]
-        source = moves.operand(item.astype(LOW))
-        target = moves.output((members - 1, item.shape[0], cols), LOW)
-        for shift in range(1, members):
-
-            def source_at(shift=shift, cols=cols):
-                to_member = lax.rem(lax.rem(lax.axis_index(PATCHES), members) + shift, members)
-                return (slice(None), pl.ds(pl.multiple_of(to_member * cols, LANES), cols))
-
-            moves.move(
-                (PATCHES, members, shift),
-                functools.partial(member_peer, members, shift),
-                source,
-                source_at,
-                target,
-                lambda shift=shift: (shift - 1,),
-            )
-    modul_here, embed_here = vectors[:, :ROLL].reshape(-1), jnp.sum(vectors[:, ROLL, : width // shards], 0)
-    flat = jnp.concatenate([modul_here, embed_here]).astype(LOW)
-    flat_rows = round_up(flat.size, 16 * LANES) // LANES
-    moves.gather(PATCHES, jnp.pad(flat, (0, flat_rows * LANES - flat.size)).reshape(flat_rows, LANES))
-    moves.exchange(PATCHES, io_here.reshape(seq_count, -1, io_cols).astype(LOW))
-    for item, which in zip(mlp_low, early):
-        to_group(moves, item, which, first_rows, block_rows - first_rows)
-    *halves, vectors, io_parts, up_rest, down_rest = moves.run()
-    mlp_sums = [
-        mine + jnp.concatenate([jnp.sum(part.astype(f32), 0) for part in parts], 0)
-        for mine, *parts in zip(mlp_sums, mlp_first, (up_rest, down_rest))
-    ]
-    vectors = jnp.sum(vectors.astype(f32), 0).reshape(-1)
-    io_slice = jnp.sum(io_parts.astype(f32), 0)
-    late_sums = [
-        lax.dynamic_slice_in_dim(item, member * group_cols[which], group_cols[which], 1)
-        + jnp.sum(half.astype(f32), 0)
-        for item, half, which in zip(grads_here, halves, late)
-    ]
-    modul_all = vectors[: modul_here.size].reshape(-1, ada_cols)
-    bias_part = jnp.concatenate([jnp.sum(modul_all, 0), vectors[modul_here.size : flat.size]])
-    silu_part = lax.dot_general(
-        modul_all, ada_copy.astype(f32), (((1,), (1,)), ((), ())), precision=HIGHEST_PRECISION
-    )
-
-    moves = Moves("group_sums", ids)
-    moves.vmem = 32 * 2**20
-    to_group(moves, late_sums[1].astype(LOW), late[1], 0, block_rows)
-
-    def has_source():
-        return lax.axis_index(PATCHES) // members < MATRICES - 1
-
-    def is_source():
-        return lax.axis_index(PATCHES) // members > 0
-
-    chain = late_sums[0]
-    mine = moves.operand(chain, pltpu.VMEM)
-    chain_total = moves.output(chain.shape, f32, pltpu.VMEM)
-    arriving, leaving = moves.scratch(chain.shape, LOW), moves.scratch(chain.shape, LOW)
-    chunk = block_rows // CHAIN_CHUNKS
-    for part in range(CHAIN_CHUNKS):
-        place = (pl.ds(part * chunk, chunk),)
-        number = moves.move(
-            (PATCHES, seq_count, MATRICES - 1),
-            functools.partial(group_peer, members, MATRICES - 1),
-            leaving,
-            lambda place=place: place,
-            arriving,
-            lambda place=place: place,
-            sends=is_source,
-            takes=has_source,
-            later=True,
-        )
-
-        def add(ref, place=place):
-            def with_arriving():
-                ref(chain_total)[place] = ref(mine)[place] + ref(arriving)[place].astype(f32)
-
-            def alone():
-                ref(chain_total)[place] = ref(mine)[place]
-
-            pl.when(has_source())(with_arriving)
-            pl.when(jnp.logical_not(has_source()))(alone)
-            ref(leaving)[place] = ref(chain_total)[place].astype(LOW)
-
-        moves.wait_for(number)
-        moves.task(add)
-        moves.start(number)
-    moves.gather(SHARDS, silu_part)
-    moves.gather(SHARDS, bias_part[None])
-    out_parts, chain, silu_parts, bias_parts = moves.run()
-    late_sums = [widen(chain), widen(late_sums[1] + jnp.sum(out_parts.astype(f32), 0))]
-    grad_group = jnp.where(
-        group == late[0],
-        late_sums[0],
-        jnp.where(group == late[1], late_sums[1], widen(jnp.where(group == early[0], *mlp_sums))),
-    )
+    grad_pos, modul_all, tail_all, io_slice, grad_group = reduce_step(
+        ids,
+        members,
+        group_cols,
+        qkv_grad,
+        embedded,
+        grad_attn,
+        extras[0],
+        w_qkv,
+        vector_rows[1],
+        vector_rows[0],
+        gathered,
+        (up_mine, down_mine, down_leaving),
+        ada_copy,
+    )
+    io_cols = io_slice.shape[1]
+    silu_parts = tail_all[:, : shards * ROLL, :width]
+    bias_parts = jnp.concatenate([tail_all[:, 8], tail_all[:, 9, : width // shards]], -1)[:, None]
     grad_silu = jnp.sum(silu_parts, 0)
     grad_cond = jax.vjp(jax.nn.silu, cond_vec)[1](grad_silu)[0]
     grad_table_all = lax.dot_general(select, grad_cond, (((0,), (0,)), ((), ())), precision=HIGHEST_PRECISION)

time: 861 us -> 752 us (0.87)
  other arithmetic: 79.8 us -> 36.6 us
  matrix products: 35.2 us -> 12.8 us
  Pallas kernels: 666 us -> 645 us
  local copies, waits for them, and re-layouts: 61.4 us -> 42.1 us
    pallas_call x16 -> x13, Pallas kernels: 666 us -> 645 us  [run(): pl.pallas_call(self.kernel, out_shape=self.outputs, in_specs=self.operand...]
    reduce_sum x14 -> x0, other arithmetic: 13.1 us -> none  [the longest x4 6.32 us: fast_body(): jnp.sum(part.astype(f32), 0)]
    convert_element_type x10 -> x2, other arithmetic: 14.2 us -> 1.54 us  [the longest x1 1.54 us: fast_body(): pos_table.astype(LOW)]
    dot_general x5 -> x0, matrix products: 11.5 us -> none  [the longest x3 6.45 us: product(): return jnp.dot(left, right, preferred_element_type=jnp.float32)]
    dot_general x8 -> x4, matrix products: 20.7 us -> 9.88 us  [rows_product(): lax.dot_general(flat_left, flat_right, (((0,), (0,)), ((), ())), preferre...]
    unnamed x286 -> x193, local copies, waits for them, and re-layouts: 27.4 us -> 22.6 us
  transfers between devices with their start and end apart: 2 -> 1, of which waited for: 0 -> 0; matrix products, arithmetic and copies ran while one was open for 2% -> 1% of each run, Pallas kernels for 8% -> 6%
where the time goes in v6:
time: 752 us; the launch traced here: 748 us
  Pallas kernels  645 us (86%)
  local copies, waits for them, and re-layouts  42.1 us (6%)
  other arithmetic  36.6 us (5%)
  matrix products  12.8 us (2%)
  between operations  10.8 us (1%)
    pallas_call x13, Pallas kernels, run(): pl.pallas_call(self.kernel, out_shape=self.outputs, in_specs=self.operand...  645 us
    unnamed x193, local copies, waits for them, and re-layouts  22.6 us
  transfers between devices with their start and end apart: 1, of which 0 were waited for; matrix products, arithmetic and copies ran while one was open for 1% of the time, Pallas kernels for 6%

profile of v6, /device:TPU:0, one launch (start us, length us, event | category | flops | bytes accessed | tf_op | source)
XLA Modules:
  0.0 748.0 jit_solution(15552602841202617971)
XLA Ops:
  3.5 1.0 copy.79
  5.2 1.3 broadcast_in_dim.65.refs_4_
  6.5 1.5 convert_element_type.134.refs_5_
  8.1 1.2 convert_element_type.135
  11.5 60.7 %begin.1 = (f32[2,8,1024]{2,1,0:T(8,128)}, f32[8,1024]{1,0:T(8,128)}, bf16[8,1024]{1,0:T(8,128)(2,1)}, f32[128,1024]{1,0:T(8,128)}, bf16[128,1024]{1,0:T(8,128)(...) custom-call(s32[8,128]{1,0:T(8,128)} %broadcast_in_dim.63.refs_0_, ...), custom_call_target="tpu_custom_call" | custom-call | tf_op jit(solution)/shard_map/begin/pallas_call | solution.py:680
  72.2 1.5 slice_bitcast_fusion.20
  74.1 1.1 fusion.61
  76.6 1.2 fusion.45
  78.5 32.4 %attend0.1 = (bf16[3,1024,128]{2,1,0:T(8,128)(2,1)S(1)}, bf16[128,1024]{1,0:T(8,128)(2,1)S(1)}, bf16[4,128,1024]{2,1,0:T(8,128)(2,1)S(1)}, bf16[4,128,384]{2,1,0:T(8,128)(2,1)S(1)}) custom-call(bf16[128,3072]{1,0:T(8,128)(2,1)S(1)} %copy-done.12, bf16[128,1024]{1,0:T(8,128)(2,1)S(1)} %copy-done.23, bf16[128,384]{1,0:T(8,128)(2,1)S(1)} %copy-done.32), custom_call_target="tpu_custom_call" | custom-call | tf_op jit(solution)/shard_map/attend0/pallas_call | solution.py:680
  113.4 28.5 %feed0.1 = (f32[128,1024]{1,0:T(8,128)}, f32[128,1024]{1,0:T(8,128)}, f32[128,1024]{1,0:T(8,128)}, f32[128,1024]{1,0:T(8,128)}, bf16[128,1024]{1,0:T(8,128)(2,1)...) custom-call(bf16[1024,1024]{1,0:T(8,128)(2,1)} %get-tuple-element.11, ...), custom_call_target="tpu_custom_call" | custom-call | tf_op jit(solution)/shard_map/feed0/pallas_call | solution.py:680
  141.9 1.1 copy-done.13
  144.8 34.3 %attend1.1 = (bf16[3,1024,128]{2,1,0:T(8,128)(2,1)S(1)}, bf16[128,1024]{1,0:T(8,128)(2,1)S(1)}, bf16[4,128,1024]{2,1,0:T(8,128)(2,1)S(1)}, bf16[4,128,384]{2,1,0:T(8,128)(2,1)S(1)}, bf16[4,128,1024]{2,1,0:T(8,128)(2,1)S(1)}) custom-call(bf16[128,3072]{1,0:T(8,128)(2,1)S(1)} %copy-done.13, bf16[128,1024]{1,0:T(8,128)(2,1)S(1)} %copy-done.24, ...), custom_call_target="tpu_custom_call" | custom-call | tf_op jit(solution)/shard_map/attend1/pallas_call | solution.py:680
  180.2 1.0 copy-done.6
  182.7 26.2 %feed1.1 = (f32[128,1024]{1,0:T(8,128)}, f32[128,1024]{1,0:T(8,128)}, f32[128,1024]{1,0:T(8,128)}, f32[128,1024]{1,0:T(8,128)}, bf16[128,1024]{1,0:T(8,128)(2,1)...) custom-call(bf16[1024,1024]{1,0:T(8,128)(2,1)} %get-tuple-element.11, ...), custom_call_target="tpu_custom_call" | custom-call | tf_op jit(solution)/shard_map/feed1/pallas_call | solution.py:680
  208.9 1.7 multiply_reduce_fusion.2
  210.7 30.7 %feed_back1.1 = (f32[8,1024]{1,0:T(8,128)}, f32[128,384]{1,0:T(8,128)}, bf16[128,384]{1,0:T(8,128)(2,1)}, f32[128,1024]{1,0:T(8,128)}, bf16[128,1024]{1,0:T(8,12...) custom-call(bf16[2,384,1024]{2,1,0:T(8,128)(2,1)} %bitcast.108, ...), custom_call_target="tpu_custom_call" | custom-call | tf_op jit(solution)/shard_map/feed_back1/pallas_call | solution.py:680
  241.4 2.6 fusion.67
  244.0 42.6 %attend_back1.1 = (bf16[128,3072]{1,0:T(8,128)(2,1)S(1)}, bf16[4,128,256]{2,1,0:T(8,128)(2,1)S(1)}, bf16[4,128,256]{2,1,0:T(8,128)(2,1)S(1)}, bf16[4,128,384]{2,1,0:T(8,128)(2,1)S(1)}, bf16[4,128,1024]{2,1,0:T(8,128)(2,1)S(1)}) custom-call(bf16[128,1024]{1,0:T(8,128)(2,1)S(1)} %copy-done.31, bf16[128,1024]{1,0:T(8,128)(2,1)S(1)} %copy-done.30, ...), custom_call_target="tpu_custom_call" | custom-call | tf_op jit(solution)/shard_map/attend_back1/pallas_call | solution.py:680
  290.6 34.6 %feed_back0.1 = (bf16[128,1024]{1,0:T(8,128)(2,1)}, f32[8,1024]{1,0:T(8,128)}, f32[128,384]{1,0:T(8,128)}, bf16[128,384]{1,0:T(8,128)(2,1)}, f32[128,1024]{1,0:T...) custom-call(bf16[2,384,1024]{2,1,0:T(8,128)(2,1)} %bitcast.109, ...), custom_call_target="tpu_custom_call" | custom-call | tf_op jit(solution)/shard_map/feed_back0/pallas_call | solution.py:680
  325.2 2.6 bitcast_add_fusion
  327.8 1.1 dynamic-slice_convert_fusion
  331.0 1.3 fusion.66
  332.5 3.4 bitcast_add_fusion.1
  336.7 45.7 %attend_back0.1 = (bf16[128,3072]{1,0:T(8,128)(2,1)S(1)}, bf16[4,128,256]{2,1,0:T(8,128)(2,1)S(1)}, bf16[4,128,256]{2,1,0:T(8,128)(2,1)S(1)}, bf16[4,128,384]{2,...) custom-call(bf16[128,1024]{1,0:T(8,128)(2,1)S(1)} %copy-done.28, ...), custom_call_target="tpu_custom_call" | custom-call | tf_op jit(solution)/shard_map/attend_back0/pallas_call | solution.py:680
  382.5 1.3 fusion
  383.8 2.7 dynamic-slice_convert_fusion.1.refs_6_
  386.5 1.6 constant_dynamic-slice_fusion.1.refs_23_
  389.5 2.9 convert_add_fusion.refs_7_
  392.4 95.6 %reduce.8 = (f32[128,256]{1,0:T(8,128)}, f32[8,1536]{1,0:T(8,128)}, f32[4,16,1536]{2,1,0:T(8,128)}, f32[96,256]{1,0:T(8,128)}, f32[1024,512]{1,0:T(8,128)}) custom-call(bf16[128,3072]{1,0:T(8,128)(2,1)} %copy-done.10, f32[128,1024]{1,0:T(8,128)} %get-tuple-element.122.refs_3_.refs_1_, f32[128,1024]{1,0:T(8,128)} %get-tuple-element.156.refs_2_, ...), custom_call_target="tpu_custom_call" | custom-call | tf_op jit(solution)/shard_map/reduce/pallas_call | solution.py:680
  490.7 2.9 fusion.1
  493.6 1.2 fusion.62
  495.5 2.7 multiply_reduce_fusion.1
  503.6 1.9 fusion.47
  506.2 16.8 %total.1 = (f32[8,128]{1,0:T(8,128)}, bf16[8,96,256]{2,1,0:T(8,128)(2,1)}) custom-call(f32[8,128]{1,0:T(8,128)} %broadcast_in_dim.72.refs_0_, bf16[96,256]{1,0:T(8,128)(2,1)} %get-tuple-element.249.refs_1_), custom_call_target="tpu_custom_call" | custom-call | tf_op jit(solution)/shard_map/total/pallas_call | solution.py:680
  523.0 1.3 fusion.64
  527.8 2.4 fusion.60
  530.2 120.2 %muon.1 = (bf16[8,128,512]{2,1,0:T(8,128)(2,1)}, bf16[8,128,512]{2,1,0:T(8,128)(2,1)}) custom-call(bf16[1024,512]{1,0:T(8,128)(2,1)} %get-tuple-element.228.refs_0_, bf16[8,128,512]{2,1,0:T(8,128)(2,1)} %bitcast.110), custom_call_target="tpu_custom_call" | custom-call | tf_op jit(solution)/shard_map/muon/pallas_call | solution.py:680
  650.5 1.4 slice_bitcast_fusion.11
  653.1 1.0 fusion.57
  654.1 1.2 fusion.55
  655.4 76.9 %copies.1 = (bf16[1024,768]{1,0:T(8,128)(2,1)}, bf16[1024,1024]{1,0:T(8,128)(2,1)}, bf16[1024,1024]{1,0:T(8,128)(2,1)}, bf16[1024,256]{1,0:T(8,128)(2,1)}) custom-call(bf16[128,768]{1,0:T(8,128)(2,1)} %get-tuple-element.221.refs_0_, bf16[128,1024]{1,0:T(8,128)(2,1)} %get-tuple-element.262.refs_1_, bf16[128,1024]{1,0:T(8,128)(2,1)} %get-tuple-element.217.refs_2_, ...), custom_call_target="tpu_custom_call" | custom-call | tf_op jit(solution)/shard_map/copies/pallas_call | solution.py:680
  733.1 2.9 divide_subtract_fusion.1
  737.5 1.1 multiply_add_fusion.2
  738.7 1.8 divide_subtract_fusion
  740.6 1.1 copy.109
  742.9 1.3 copy.111
  744.3 1.0 copy-done.47
  745.3 1.3 copy.112
  (242 shorter events, 33.1 us)
Async XLA Ops:
  11.5 62.2 %copy-start.56 = (f32[128,768]{1,0:T(8,128)S(1)}, f32[128,768]{1,0:T(8,128)}, u32[]{:S(2)}) copy-start(f32[128,768]{1,0:T(8,128)} %param.39) | copy-start | bytes 1179652
  11.5 62.2 %copy-start.87 = (pred[512]{0:T(512)(128)(4,1)S(1)}, pred[512]{0:T(512)(128)(4,1)}, u32[]{:S(2)}) copy-start(pred[512]{0:T(512)(128)(4,1)} %constant.54.clone.1) | copy-start | bytes 1540
  11.5 62.3 %copy-start.49 = (f32[128,1024]{1,0:T(8,128)S(1)}, f32[128,1024]{1,0:T(8,128)}, u32[]{:S(2)}) copy-start(f32[128,1024]{1,0:T(8,128)} %param.45) | copy-start | bytes 1572868
  73.9 4.6 copy-start.12
  73.9 4.6 copy-start.23
  73.9 4.6 copy-start.32
  113.4 28.5 %copy-start.3 = (bf16[128,1024]{1,0:T(8,128)(2,1)S(1)}, bf16[128,1024]{1,0:T(8,128)(2,1)}, u32[]{:S(2)}) copy-start(bf16[128,1024]{1,0:T(8,128)(2,1)} %copy-done.2) | copy-start | bytes 786436
  210.7 30.7 %copy-start.54 = (bf16[4,128,1024]{2,1,0:T(8,128)(2,1)S(1)}, bf16[4,128,1024]{2,1,0:T(8,128)(2,1)}, u32[]{:S(2)}) copy-start(bf16[4,128,1024]{2,1,0:T(8,128)(2,1)} %get-tuple-element.163) | copy-start | bytes 3145732
  290.6 34.6 %copy-start.43 = (bf16[4,128,1024]{2,1,0:T(8,128)(2,1)S(1)}, bf16[4,128,1024]{2,1,0:T(8,128)(2,1)}, u32[]{:S(2)}) copy-start(bf16[4,128,1024]{2,1,0:T(8,128)(2,1)} %get-tuple-element.165) | copy-start | bytes 3145732
  327.8 3.1 copy-start.60
  329.0 59.5 %collective-permute-start = (bf16[1024,512]{1,0:T(8,128)(2,1)}, bf16[1024,512]{1,0:T(8,128)(2,1)}, u32[]{:S(2)}, u32[]{:S(2)}) collective-permute-start(bf16[1024,512]{1,0:T(8,128)(2,1)} %dynamic-slice_convert_fusion), channel_id=1, source_target_pairs={{0,4},{4,0},{8,12},{12,8},{16,20},{20,16},{24,28},{28,24},{1,5},{5... | collective-permute-start | bytes 3145736 | tf_op jit(solution)/shard_map/ppermute | solution.py:2066
  332.5 4.2 copy-start.1
  332.5 4.2 copy-start.25
  332.5 4.2 copy-start.26
  332.5 4.2 copy-start.27
  332.5 4.2 copy-start.28
  332.5 4.2 copy-start.33
  335.9 46.5 %copy-start.40 = (bf16[8,64,512]{2,1,0:T(8,128)(2,1)S(1)}, bf16[8,64,512]{2,1,0:T(8,128)(2,1)}, u32[]{:S(2)}) copy-start(bf16[8,64,512]{2,1,0:T(8,128)(2,1)} %get-tuple-element.188) | copy-start | bytes 1572868
  336.6 45.8 %copy-start.41 = (bf16[8,64,512]{2,1,0:T(8,128)(2,1)S(1)}, bf16[8,64,512]{2,1,0:T(8,128)(2,1)}, u32[]{:S(2)}) copy-start(bf16[8,64,512]{2,1,0:T(8,128)(2,1)} %get-tuple-element.189) | copy-start | bytes 1572868
  336.7 49.8 %copy-start.36 = (f32[1024,1024]{1,0:T(8,128)S(1)}, f32[1024,1024]{1,0:T(8,128)}, u32[]{:S(2)}) copy-start(f32[1024,1024]{1,0:T(8,128)} %bitcast_add_fusion.1) | copy-start | bytes 12582916
  382.4 5.7 copy-start.10
  382.4 5.7 copy-start.11
  382.4 5.7 copy-start.17
  382.4 5.7 copy-start.20
  382.4 5.9 copy-start.21
  382.5 5.9 copy-start.22
  386.5 2.9 copy-start.38
  488.0 5.6 copy-start.77
  488.0 6.8 copy-start.68
  488.0 7.5 copy-start.79
  490.7 10.0 %copy-start.89 = (f32[8,1024]{1,0:T(8,128)S(1)}, f32[8,1024]{1,0:T(8,128)}, u32[]{:S(2)}) copy-start(f32[8,1024]{1,0:T(8,128)} %get-tuple-element.187) | copy-start | bytes 98308
  490.7 37.1 %copy-start.39 = (f32[1024,512]{1,0:T(8,128)S(1)}, f32[1024,512]{1,0:T(8,128)}, u32[]{:S(2)}) copy-start(f32[1024,512]{1,0:T(8,128)} %get-tuple-element.181) | copy-start | bytes 6291460
  490.7 37.1 %copy-start.42 = (bf16[8,64,512]{2,1,0:T(8,128)(2,1)S(1)}, bf16[8,64,512]{2,1,0:T(8,128)(2,1)}, u32[]{:S(2)}) copy-start(bf16[8,64,512]{2,1,0:T(8,128)(2,1)} %get-tuple-element.189) | copy-start | bytes 1572868
  654.1 78.2 %copy-start.73 = (bf16[8,96,256]{2,1,0:T(8,128)(2,1)S(1)}, bf16[8,96,256]{2,1,0:T(8,128)(2,1)}, u32[]{:S(2)}) copy-start(bf16[8,96,256]{2,1,0:T(8,128)(2,1)} %get-tuple-element.197) | copy-start | bytes 1179652
  654.1 78.3 %copy-start.80 = (f32[5,256]{1,0:T(8,128)S(1)}, f32[5,256]{1,0:T(8,128)}, u32[]{:S(2)}) copy-start(f32[5,256]{1,0:T(8,128)} %refs_3_.1) | copy-start | bytes 15364
  654.1 78.3 %copy-start.82 = (f32[5,256]{1,0:T(8,128)S(1)}, f32[5,256]{1,0:T(8,128)}, u32[]{:S(2)}) copy-start(f32[5,256]{1,0:T(8,128)} %param.57) | copy-start | bytes 15364
  654.1 78.3 %copy-start.83 = (f32[5,256]{1,0:T(8,128)S(1)}, f32[5,256]{1,0:T(8,128)}, u32[]{:S(2)}) copy-start(f32[5,256]{1,0:T(8,128)} %param.58) | copy-start | bytes 15364
  654.1 79.0 %copy-start.46 = (f32[2,276,256]{2,0,1:T(2,128)S(1)}, f32[2,276,256]{2,0,1:T(2,128)}, u32[]{:S(2)}) copy-start(f32[2,276,256]{2,0,1:T(2,128)} %param.53) | copy-start | bytes 1695748
  654.1 79.0 %copy-start.64 = (f32[2,276,256]{2,0,1:T(2,128)S(1)}, f32[2,276,256]{2,0,1:T(2,128)}, u32[]{:S(2)}) copy-start(f32[2,276,256]{2,0,1:T(2,128)} %param.54) | copy-start | bytes 1695748
  654.1 79.0 %copy-start.65 = (f32[2,276,256]{2,0,1:T(2,128)S(1)}, f32[2,276,256]{2,0,1:T(2,128)}, u32[]{:S(2)}) copy-start(f32[2,276,256]{2,0,1:T(2,128)} %param.55) | copy-start | bytes 1695748
  732.3 3.7 copy-start.81
  732.3 3.7 copy-start.84
  732.3 3.7 copy-start.85
  732.3 4.3 copy-start.66
  732.4 4.3 copy-start.75
  732.4 4.3 copy-start.76
  733.1 4.4 copy-start.50
  733.1 4.4 copy-start.52
  (43 other events, 70.9 us)

commit v7 on v6

--- a/solution.py
+++ b/solution.py
@@ -910,46 +910,6 @@
                     self.task(own)
 
 
-def total_of(ids, values, shared):
-    moves = Moves("total", ids)
-    source, result = moves.operand(values, pltpu.VMEM), moves.output(values.shape, values.dtype, pltpu.VMEM)
-    moves.gather(PATCHES, shared)
-    for axis in (SHARDS, PATCHES):
-        count = lax.axis_size(axis)
-        buffer = moves.scratch((count,) + values.shape, values.dtype)
-
-        def own(axis=axis):
-            return (lax.axis_index(axis),)
-
-        def put(ref, source=source, buffer=buffer, own=own):
-            ref(buffer)[own()] = ref(source)[...]
-
-        moves.task(put)
-        numbers = []
-        for shift in range(1, count):
-            numbers.append(
-                moves.move(
-                    (axis, shift),
-                    lambda axis=axis, shift=shift, count=count: {axis: lax.rem(lax.axis_index(axis) + shift, count)},
-                    buffer,
-                    own,
-                    buffer,
-                    own,
-                    later=True,
-                )
-            )
-            moves.start(numbers[-1])
-        for number in numbers:
-            moves.wait_for(number)
-
-        def add(ref, buffer=buffer):
-            ref(result)[...] = jnp.sum(ref(buffer)[...], 0)
-
-        moves.task(add)
-        source = result
-    return moves.run()
-
-
 def contract(left, right, left_dim, right_dim):
     return lax.dot_general(
         left, right, (((left_dim,), (right_dim,)), ((), ())), preferred_element_type=jnp.float32
@@ -1834,71 +1794,85 @@
         lax.broadcasted_iota(jnp.int32, (GRAM_COLS, GRAM_COLS), 1),
     ).astype(jnp.float32)
 
-    def over_tiles(action, width=size):
-        def step(tile, total):
-            return total + action(pl.ds(pl.multiple_of(tile * GRAM_COLS, GRAM_COLS), GRAM_COLS))
-
-        return lax.fori_loop(0, width // GRAM_COLS, step, jnp.float32(0.0))
-
-    def store(full, low, cols, value, mean, excess):
-        full[:, cols] = value
-        low[:, cols] = value.astype(LOW)
-        corner = full[cols, cols] - excess * eye
+    tiles = size // GRAM_COLS
+
+    def tile_at(tile):
+        return pl.ds(tile * GRAM_COLS, GRAM_COLS)
+
+    def store(full, low, tile, value, mean, excess):
+        cols = tile_at(tile)
+        if tile:
+            above = pl.ds(0, tile * GRAM_COLS)
+            full[above, cols] = value[: tile * GRAM_COLS]
+            low[above, cols] = value[: tile * GRAM_COLS].astype(LOW)
+            for row in range(tile):
+                low[cols, tile_at(row)] = value[row * GRAM_COLS : (row + 1) * GRAM_COLS].T.astype(LOW)
+        corner = value[tile * GRAM_COLS :] - excess * eye
         full[cols, cols] = corner
         low[cols, cols] = (corner - mean * eye).astype(LOW)
 
+    def inner(tile, left, right):
+        both = left * right
+        return 2.0 * jnp.sum(both) - jnp.sum(both[tile * GRAM_COLS :])
+
+    def product_cols(left, right, tile):
+        return contract(left[pl.ds(0, (tile + 1) * GRAM_COLS), :], right[:, tile_at(tile)], 1, 0)
+
+    def upper(full, tile):
+        return full[pl.ds(0, (tile + 1) * GRAM_COLS), tile_at(tile)]
+
     def advance(gram_mean, gram_squares, last):
         poly_mean = NS_B * gram_mean + NS_C * gram_squares / size
-
-        def poly_cols(cols):
-            own = gram[:, cols]
-            value = contract(gram_low[...], gram_low[:, cols], 1, 0)
+        total = jnp.float32(0.0)
+        for tile in range(tiles):
+            own = upper(gram, tile)
+            value = product_cols(gram_low, gram_low, tile)
             value = NS_C * value + (NS_B + 2.0 * NS_C * gram_mean) * own
-            store(poly, poly_low, cols, value, poly_mean, NS_C * gram_mean * gram_mean)
-            return jnp.sum(value * own)
-
-        once_mean = over_tiles(poly_cols) / size - NS_C * gram_mean * gram_mean * gram_mean
-
-        def block_cols(cols):
+            store(poly, poly_low, tile, value, poly_mean, NS_C * gram_mean * gram_mean)
+            total = total + inner(tile, value, own)
+        once_mean = total / size - NS_C * gram_mean * gram_mean * gram_mean
+
+        for tile in range(block.shape[1] // GRAM_COLS):
+            cols = tile_at(tile)
             value = contract(poly_low[...], block[:, cols], 1, 0)
             block_next[:, cols] = (value + (NS_A + poly_mean) * block[:, cols].astype(jnp.float32)).astype(LOW)
-            return jnp.float32(0.0)
-
-        over_tiles(block_cols, block.shape[1])
         block[...] = block_next[...]
         if last:
             return None
 
-        def once_cols(cols):
-            own = poly[:, cols]
-            value = contract(poly_low[...], gram_low[:, cols], 1, 0)
-            value = value + poly_mean * gram[:, cols] + gram_mean * own
-            store(once, once_low, cols, value, once_mean, poly_mean * gram_mean)
-            return jnp.sum(value * own)
-
-        poly_once = over_tiles(once_cols) / size - poly_mean * gram_mean * poly_mean
+        total = jnp.float32(0.0)
+        for tile in range(tiles):
+            own = upper(poly, tile)
+            value = product_cols(poly_low, gram_low, tile)
+            value = value + poly_mean * upper(gram, tile) + gram_mean * own
+            store(once, once_low, tile, value, once_mean, poly_mean * gram_mean)
+            total = total + inner(tile, value, own)
+        poly_once = total / size - poly_mean * gram_mean * poly_mean
         mean_next = NS_A * NS_A * gram_mean + 2.0 * NS_A * once_mean + poly_once
         excess = poly_mean * once_mean
 
-        def gram_cols(cols):
-            value = contract(poly_low[...], once_low[:, cols], 1, 0)
-            value = value + (2.0 * NS_A + poly_mean) * once[:, cols] + once_mean * poly[:, cols]
-            value = value + NS_A * NS_A * gram[:, cols]
-            store(gram, gram_low, cols, value, mean_next, excess)
-            return jnp.sum(value * value)
-
-        return mean_next, over_tiles(gram_cols) - excess * (2.0 * mean_next + excess) * size
+        total = jnp.float32(0.0)
+        for tile in range(tiles):
+            value = product_cols(poly_low, once_low, tile)
+            value = value + (2.0 * NS_A + poly_mean) * upper(once, tile) + once_mean * upper(poly, tile)
+            value = value + NS_A * NS_A * upper(gram, tile)
+            store(gram, gram_low, tile, value, mean_next, excess)
+            total = total + inner(tile, value, value)
+        return mean_next, total - excess * (2.0 * mean_next + excess) * size
 
     block[...] = source[...]
-    mean = over_tiles(lambda cols: jnp.sum(gram[cols, cols] * eye)) / size
-
-    def start(cols):
+    mean = jnp.float32(0.0)
+    for tile in range(tiles):
+        mean = mean + jnp.sum(gram[tile_at(tile), tile_at(tile)] * eye)
+    mean = mean / size
+    squares = jnp.float32(0.0)
+    for tile in range(tiles):
+        cols = tile_at(tile)
         value = gram[:, cols]
         gram_low[:, cols] = value.astype(LOW)
         gram_low[cols, cols] = (gram[cols, cols] - mean * eye).astype(LOW)
-        return jnp.sum(value * value)
-
-    state = lax.fori_loop(0, NS_ITERS - 1, lambda turn, state: advance(*state, False), (mean, over_tiles(start)))
+        squares = squares + jnp.sum(value * value)
+    state = lax.fori_loop(0, NS_ITERS - 1, lambda turn, state: advance(*state, False), (mean, squares))
     advance(*state, True)
 
 
@@ -1951,6 +1925,7 @@
     value_pad = ((0, 0), (0, padded - values_count))
     state = jnp.pad(states[0].astype(f32), value_pad)
     length = lengths[0]
+    id_rows = jnp.broadcast_to(intervals[:, None, None], (shards, ROLL, LANES)).reshape(-1, LANES)
     (
         extras,
         cond_vec,
@@ -1967,7 +1942,7 @@
         ids,
         members,
         state,
-        jnp.broadcast_to(intervals[:, None, None], (shards, ROLL, LANES)).reshape(-1, LANES),
+        id_rows,
         jnp.broadcast_to((jnp.arange(ROLL, dtype=jnp.int32)[:, None] < length).astype(f32), (ROLL, width)),
         cond_table,
         biases[None],
@@ -1978,11 +1953,6 @@
         qkv_copy,
     )
     io_all = io_all.reshape(2, padded, width)
-    rows_iota = jnp.arange(table_rows, dtype=jnp.int32)
-    id_rows = (intervals[:, None] == rows_iota[None]).astype(f32)
-    step_rows = (rows_iota[None] == NI + jnp.arange(ROLL, dtype=jnp.int32)[:, None]).astype(f32)
-    select = (id_rows[:, None] + step_rows[None]).reshape(-1, table_rows)
-
     masters = (qkv_master, up_master, down_master, out_master)
     momenta = (qkv_moment, up_moment, down_moment, out_moment)
     group_cols = [item.shape[1] // members for item in momenta]
@@ -2139,51 +2109,138 @@
         ada_copy,
     )
     io_cols = io_slice.shape[1]
-    silu_parts = tail_all[:, : shards * ROLL, :width]
-    bias_parts = jnp.concatenate([tail_all[:, 8], tail_all[:, 9, : width // shards]], -1)[:, None]
-    grad_silu = jnp.sum(silu_parts, 0)
-    grad_cond = jax.vjp(jax.nn.silu, cond_vec)[1](grad_silu)[0]
-    grad_table_all = lax.dot_general(select, grad_cond, (((0,), (0,)), ((), ())), precision=HIGHEST_PRECISION)
-    grad_table = lax.dynamic_slice_in_dim(grad_table_all, shard * table_cols, table_cols, 1)
-    bias_parts = bias_parts[:, 0]
-    grad_bias_all = jnp.concatenate([bias_parts[:, :ada_cols].reshape(-1), bias_parts[:, ada_cols:].reshape(-1)])
-    grad_bias = lax.dynamic_slice_in_dim(grad_bias_all, shard * biases.shape[0], biases.shape[0])
-    silu_rows = lax.dynamic_slice_in_dim(silu_low, seq_index * ada_master.shape[0], ada_master.shape[0], 1)
-    grad_ada = lax.dot_general(
-        silu_rows.astype(f32), modul_all, (((0,), (0,)), ((), ())), precision=HIGHEST_PRECISION
-    )
-
-    moment_group = jnp.concatenate(moment_halves, 1).reshape(-1, most_cols).astype(f32)
-    grad_squares = jnp.sum(grad_group * grad_group)
-    squares = (
-        grad_squares
-        + jnp.sum(grad_ada * grad_ada)
-        + jnp.sum(io_slice * io_slice)
-        + jnp.sum(grad_pos * grad_pos)
-        + (seq_index == 0).astype(f32) * (jnp.sum(grad_table * grad_table) + jnp.sum(grad_bias * grad_bias))
-    )
-    lane = jnp.arange(LANES, dtype=jnp.int32)
-    place = 2 + 3 * group
-    entries = jnp.where(lane == 0, squares, 0.0) + jnp.where(lane == 1, loss_local, 0.0)
-    entries = entries + jnp.where(lane == place, jnp.sum(moment_group * moment_group), 0.0)
-    entries = entries + jnp.where(lane == place + 1, jnp.sum(moment_group * grad_group), 0.0)
-    entries = entries + jnp.where(lane == place + 2, grad_squares, 0.0)
-    sums, io_slices = total_of(ids, jnp.broadcast_to(entries[None], (8, LANES)), io_slice.astype(LOW))
-    sums = sums[0]
-    grad_norm = jnp.sqrt(sums[0])
-    loss_total = sums[1]
-    clip = jnp.minimum(1.0, CLIP_LIMIT / (grad_norm + 1e-06))
-    terms = sums[2 : 2 + 3 * MATRICES].reshape(MATRICES, 3)
-    size_squares = MOMENTUM * MOMENTUM * terms[:, 0] + 2.0 * MOMENTUM * clip * terms[:, 1] + clip * clip * terms[:, 2]
-    sizes = jnp.sqrt(jnp.maximum(size_squares, 0.0))
-    moment_sizes = sizes[jnp.array([0, 3, 1, 2])] / CLIP_LIMIT
-    my_size = lax.dynamic_slice_in_dim(sizes, group, 1)[0]
-    block = ((MOMENTUM * moment_group + clip * grad_group) / (my_size + 1e-07)).astype(LOW)
-
-    moves = Moves("muon", ids, 56 * 2**20)
-    source = moves.operand(block, pltpu.VMEM)
+    moves = Moves("finish", ids, 60 * 2**20)
+    vmem = functools.partial(moves.operand, space=pltpu.VMEM)
+    vmem_out = functools.partial(moves.output, space=pltpu.VMEM)
     full, low = (block_rows, block_rows), (block_rows, most_cols)
-    update = moves.output((seq_count, block_rows // seq_count, most_cols), LOW, pltpu.VMEM)
+    block_part = block_rows // seq_count
+    grad_in, io_in, pos_in, modul_in, tail_in = [
+        vmem(item) for item in (grad_group, io_slice, grad_pos, modul_all, tail_all)
+    ]
+    silu_in, cond_in, ids_in = vmem(silu_low), vmem(cond_vec), vmem(id_rows)
+    loss_in = vmem(jnp.broadcast_to(loss_local, (1, LANES)))
+    moment = moves.scratch((seq_count, block_part, most_cols), LOW)
+    moment_loads = [
+        moves.keep(
+            moves.operand(item),
+            None,
+            moment,
+            lambda half=half: (slice(None), pl.ds(half * half_rows, half_rows)),
+        )
+        for half, item in enumerate(moment_halves)
+    ]
+    master_loads = [moves.load(item) for item in masters]
+    sums = vmem_out((8, LANES), f32)
+    grad_ada = vmem_out((block_part, ada_cols), f32)
+    grad_table_all = vmem_out((8, width), f32)
+    io_all_parts = vmem_out((seq_count,) + io_slice.shape, LOW)
+    fresh = [vmem_out(item.shape, f32) for item in masters]
+    fresh_low = [moves.scratch(item.shape, LOW) for item in masters]
+    near, far = [moves.scratch((count, 8, LANES), f32) for count in (shards, seq_count)]
+    grad_low, source = moves.scratch(low, LOW), moves.scratch(low, LOW)
+    io_low = moves.scratch(io_slice.shape, LOW)
+
+    def measure(ref):
+        def add(item, totals):
+            rows = pl.ds(pl.multiple_of(item * block_part, block_part), block_part)
+            old, grad = ref(moment)[item].astype(f32), ref(grad_in)[rows, :]
+            ref(grad_low)[rows, :] = grad.astype(LOW)
+            return totals[0] + jnp.sum(old * old), totals[1] + jnp.sum(old * grad), totals[2] + jnp.sum(grad * grad)
+
+        zero = jnp.float32(0.0)
+        terms = lax.fori_loop(0, seq_count, add, (zero, zero, zero))
+        patch = lax.axis_index(PATCHES)
+        count = shards * ROLL
+        silu_rows = ref(silu_in)[:, pl.ds(pl.multiple_of(patch * block_part, LANES), block_part)]
+        silu_rows = jnp.concatenate([silu_rows, jnp.zeros((16 - count, block_part), LOW)], 0)
+        modul = jnp.concatenate([ref(modul_in)[...], jnp.zeros((16 - count, ada_cols), f32)], 0)
+        modul_high = modul.astype(LOW)
+        modul_rest = (modul - modul_high.astype(f32)).astype(LOW)
+        value = contract(silu_rows, modul_high, 0, 0) + contract(silu_rows, modul_rest, 0, 0)
+        ref(grad_ada)[...] = value
+        squares = terms[2] + jnp.sum(value * value)
+        squares = squares + jnp.sum(ref(io_in)[...] * ref(io_in)[...]) + jnp.sum(ref(pos_in)[...] * ref(pos_in)[...])
+        ref(io_low)[...] = ref(io_in)[...].astype(LOW)
+        cond = ref(cond_in)[...]
+        gate = 1.0 / (1.0 + jnp.exp(-cond))
+        grad_silu = sum(ref(tail_in)[item, pl.ds(0, count), pl.ds(0, width)] for item in range(shards))
+        grad_cond = grad_silu * gate * (1.0 + cond * (1.0 - gate))
+        row = lax.broadcasted_iota(jnp.int32, (count, 1), 0)
+        ref(grad_table_all)[...] = jnp.zeros((8, width), f32)
+        for entry in range(table_rows):
+            chosen = (ref(ids_in)[:, :1] == entry) if entry < NI else (lax.rem(row, ROLL) == entry - NI)
+            value = jnp.sum(jnp.where(chosen, grad_cond, 0.0), 0, keepdims=True)
+            ref(grad_table_all)[pl.ds(entry, 1), :] = value
+        me = lax.axis_index(SHARDS)
+        value = ref(grad_table_all)[:, pl.ds(pl.multiple_of(me * table_cols, LANES), table_cols)]
+        once = jnp.sum(value * value)
+        for entry, cols in ((8, ada_cols), (9, table_cols)):
+            value = ref(tail_in)[me, pl.ds(entry, 1), pl.ds(0, cols)]
+            once = once + jnp.sum(value * value)
+        squares = squares + jnp.where(patch == 0, once, 0.0)
+        lane = lax.broadcasted_iota(jnp.int32, (8, LANES), 1)
+        entries = jnp.where(lane == 0, squares, 0.0) + jnp.where(lane == 1, ref(loss_in)[...], 0.0)
+        for number, term in enumerate(terms):
+            entries = entries + jnp.where(lane == 2 + 3 * (patch // members) + number, term, 0.0)
+        ref(near)[me] = entries
+
+    for number in moment_loads:
+        moves.wait_local(number)
+    moves.task(measure)
+
+    def spread(axis, buffer, at):
+        count = lax.axis_size(axis)
+        numbers = []
+        for shift in range(1, count):
+            numbers.append(
+                moves.move(
+                    (axis, shift),
+                    lambda shift=shift: {axis: lax.rem(lax.axis_index(axis) + shift, count)},
+                    buffer,
+                    at,
+                    io_all_parts if buffer is io_low else buffer,
+                    lambda: (lax.axis_index(axis),),
+                    later=True,
+                )
+            )
+            moves.start(numbers[-1])
+        return numbers
+
+    def add_near(ref):
+        ref(far)[lax.axis_index(PATCHES)] = jnp.sum(ref(near)[...], 0)
+
+    def scale(ref):
+        ref(sums)[...] = jnp.sum(ref(far)[...], 0)
+        row = ref(sums)[pl.ds(0, 1), :]
+        lane = lax.broadcasted_iota(jnp.int32, (1, LANES), 1)
+
+        def entry(place):
+            return jnp.sum(jnp.where(lane == place, row, 0.0), 1, keepdims=True)
+
+        clip = jnp.minimum(1.0, CLIP_LIMIT / (jnp.sqrt(entry(0)) + 1e-06))
+        place = 2 + 3 * (lax.axis_index(PATCHES) // members)
+        size = MOMENTUM * MOMENTUM * entry(place) + 2.0 * MOMENTUM * clip * entry(place + 1)
+        size = jnp.sqrt(jnp.maximum(size + clip * clip * entry(place + 2), 0.0))
+        per_size = 1.0 / (size + 1e-07)
+
+        @pl.loop(0, seq_count)
+        def _(item):
+            rows = pl.ds(pl.multiple_of(item * block_part, block_part), block_part)
+            value = MOMENTUM * ref(moment)[item].astype(f32) + clip * ref(grad_in)[rows, :]
+            ref(source)[rows, :] = (value * per_size).astype(LOW)
+
+        ref(io_all_parts)[lax.axis_index(PATCHES)] = ref(io_low)[...]
+
+    for number in spread(SHARDS, near, lambda: (lax.axis_index(SHARDS),)):
+        moves.wait_for(number)
+    moves.task(add_near)
+    far_moves = spread(PATCHES, far, lambda: (lax.axis_index(PATCHES),))
+    spread(PATCHES, io_low, None)
+    for number in far_moves:
+        moves.wait_for(number)
+    moves.task(scale)
+
+    update = moves.scratch((seq_count, block_part, most_cols), LOW)
     target = moves.scratch((members * shards,) + low, LOW)
     gram, poly, once = [moves.scratch(full, f32) for _ in range(3)]
     gram_low, poly_low, once_low = [moves.scratch(full, LOW) for _ in range(3)]
@@ -2216,18 +2273,33 @@
     def pair_peer(shift):
         return {SHARDS: lax.rem(lax.axis_index(SHARDS) + 2 * shift, shards)}
 
+    def row_part(shift):
+        there = lax.rem(lax.axis_index(PATCHES) + shift, seq_count)
+        size = block_rows // seq_count
+        return (pl.ds(pl.multiple_of(there * size, size), size),)
+
     slot_own = functools.partial(slot, 0, 0)
     by_member = {
         shift: moves.move(
-            (PATCHES, members, shift), functools.partial(member_peer, members, shift), source, None, target, slot_own
+            (PATCHES, members, shift),
+            functools.partial(member_peer, members, shift),
+            source,
+            None,
+            target,
+            slot_own,
+            later=True,
         )
         for shift in range(1, members)
     }
     by_pair = {
-        shift: moves.move((SHARDS, 2 * shift), functools.partial(pair_peer, shift), source, None, target, slot_own)
+        shift: moves.move(
+            (SHARDS, 2 * shift), functools.partial(pair_peer, shift), source, None, target, slot_own, later=True
+        )
         for shift in range(1, pairs)
     }
-    from_sibling = [(moves.move((SHARDS,), sibling_peer, source, None, target, slot_own), slot_own)]
+    from_sibling = [(moves.move((SHARDS,), sibling_peer, source, None, target, slot_own, later=True), slot_own)]
+    for number in (*by_member.values(), *by_pair.values(), from_sibling[0][0]):
+        moves.start(number)
     moves.task(start_gram)
 
     def sibling_place(place):
@@ -2287,21 +2359,31 @@
             moves.wait_for(number)
         moves.task(add_gram(sibling_place(place)))
 
-    for number in moves.exchange(PATCHES, grad_group.astype(LOW).reshape(seq_count, -1, most_cols), later=True):
-        moves.start(number)
+    grad_rows = moves.output((seq_count, block_rows // seq_count, most_cols), LOW)
+    for shift in range(1, seq_count):
+        moves.start(
+            moves.move(
+                (PATCHES, shift),
+                lambda shift=shift: {PATCHES: lax.rem(lax.axis_index(PATCHES) + shift, seq_count)},
+                grad_low,
+                lambda shift=shift: row_part(shift),
+                grad_rows,
+                lambda: (lax.axis_index(PATCHES),),
+                later=True,
+            )
+        )
+    moves.start_local(
+        moves.keep(grad_low, lambda: row_part(0), grad_rows, lambda: (lax.axis_index(PATCHES),), True)
+    )
     moves.task(
         lambda ref: newton_schulz(
             *[ref(item) for item in (source, gram, poly, once, gram_low, poly_low, once_low, state, state_next)]
         )
     )
 
-    def row_part(shift):
-        there = lax.rem(lax.axis_index(PATCHES) + shift, seq_count)
-        size = block_rows // seq_count
-        return (pl.ds(pl.multiple_of(there * size, size), size),)
-
+    update_moves = []
     for shift in range(1, seq_count):
-        moves.start(
+        update_moves.append(
             moves.move(
                 (PATCHES, shift),
                 lambda shift=shift: {PATCHES: lax.rem(lax.axis_index(PATCHES) + shift, seq_count)},
@@ -2312,27 +2394,31 @@
                 later=True,
             )
         )
+        moves.start(update_moves[-1])
 
     def keep_rows(ref):
         ref(update)[lax.axis_index(PATCHES)] = ref(state)[row_part(0)]
 
     moves.task(keep_rows)
-    update, grad_rows = moves.run()
-
-    def rows_of(which, parts):
-        return jnp.concatenate(
-            [parts[which * members + part][:, : group_cols[which]] for part in range(members)], -1
-        ).astype(f32)
-
-    moments = [MOMENTUM * old + clip * rows_of(which, grad_rows) for which, old in enumerate(momenta)]
-    fresh = [
-        master * (1.0 - RATE_MUON * DECAY_MUON)
-        - RATE_MUON * 0.2 * math.sqrt(master.shape[1] * shards) * rows_of(which, update)
-        for which, master in enumerate(masters)
-    ]
-
-    moves = Moves("copies", ids)
-    rows = qkv_master.shape[0]
+
+    def renew(ref):
+        for which, (master, _) in enumerate(master_loads):
+            cols = group_cols[which]
+            rate = RATE_MUON * 0.2 * math.sqrt(masters[which].shape[1] * shards)
+            for part in range(members):
+                at = (slice(None), pl.ds(part * cols, cols))
+                value = ref(update)[which * members + part, :, pl.ds(0, cols)].astype(f32)
+                value = ref(master)[at] * (1.0 - RATE_MUON * DECAY_MUON) - rate * value
+                ref(fresh[which])[at] = value
+                ref(fresh_low[which])[at] = value.astype(LOW)
+
+    for number in update_moves:
+        moves.wait_for(number)
+    for _, number in master_loads:
+        moves.wait_local(number)
+    moves.task(renew)
+
+    rows = block_rows // seq_count
 
     def row_place(back_group):
         who = lax.axis_index(PATCHES) - back_group * members
@@ -2354,15 +2440,17 @@
                 after,
                 there,
                 there,
+                later=True,
             )
+            if not after:
+                moves.start(len(moves.moves) - 1)
 
     places = []
-    for item in fresh:
-        source = moves.operand(item.astype(LOW))
-        target = moves.output((rows * seq_count, item.shape[1]), LOW)
+    for item_from in fresh_low:
+        item_to = moves.output((rows * seq_count, moves.shape(item_from)[1]), LOW)
         own = functools.partial(row_place, 0)
-        moves.keep(source, None, target, own)
-        places.append((source, target, {}))
+        moves.start_local(moves.keep(item_from, None, item_to, own, True))
+        places.append((item_from, item_to, {}))
 
     def along_line(distance, way, source, target, numbers):
         both = lambda: jnp.logical_and(has_group(way), has_group(-distance * way))
@@ -2377,25 +2465,47 @@
             (numbers[way],) if distance else (),
             both,
             functools.partial(has_group, -(distance + 1) * way),
+            later=True,
         )
-
-    for source, target, numbers in places:
+        if not distance:
+            moves.start(numbers[way])
+
+    for item_from, item_to, numbers in places:
         for way in (1, -1):
-            along_line(0, way, source, target, numbers)
-    for source, target, numbers in places:
-        member_copies(source, None, target, own, (), None)
+            along_line(0, way, item_from, item_to, numbers)
+    for item_from, item_to, numbers in places:
+        member_copies(item_from, None, item_to, own, (), None)
     for distance in range(1, MATRICES):
-        for source, target, numbers in places:
+        for item_from, item_to, numbers in places:
             for way in (1, -1):
                 number = numbers[way]
                 if distance < MATRICES - 1:
-                    along_line(distance, way, source, target, numbers)
+                    along_line(distance, way, item_from, item_to, numbers)
                 place = functools.partial(row_place, distance * way)
                 member_copies(
-                    target, place, target, place, (number,), functools.partial(has_group, -distance * way)
+                    item_to, place, item_to, place, (number,), functools.partial(has_group, -distance * way)
                 )
-    copies = moves.run()
-
+    sums, grad_ada, grad_table_all, io_slices, *rest = moves.run()
+    fresh, grad_rows, copies = rest[:MATRICES], rest[MATRICES], rest[MATRICES + 1 :]
+    sums = sums[0]
+    grad_norm = jnp.sqrt(sums[0])
+    loss_total = sums[1]
+    clip = jnp.minimum(1.0, CLIP_LIMIT / (grad_norm + 1e-06))
+    terms = sums[2 : 2 + 3 * MATRICES].reshape(MATRICES, 3)
+    size_squares = MOMENTUM * MOMENTUM * terms[:, 0] + 2.0 * MOMENTUM * clip * terms[:, 1] + clip * clip * terms[:, 2]
+    sizes = jnp.sqrt(jnp.maximum(size_squares, 0.0))
+    moment_sizes = jnp.stack([sizes[which] for which in (0, 3, 1, 2)]) / CLIP_LIMIT
+    moments = [
+        MOMENTUM * old
+        + clip
+        * jnp.concatenate(
+            [grad_rows[which * members + part, :, : group_cols[which]] for part in range(members)], -1
+        ).astype(f32)
+        for which, old in enumerate(momenta)
+    ]
+    grad_table = lax.dynamic_slice_in_dim(grad_table_all[:table_rows], shard * table_cols, table_cols, 1)
+    grad_bias_all = jnp.concatenate([tail_all[:, 8].reshape(-1), tail_all[:, 9, :table_cols].reshape(-1)])
+    grad_bias = lax.dynamic_slice_in_dim(grad_bias_all, shard * biases.shape[0], biases.shape[0])
     io_grad = io_slices.reshape(2, padded, io_cols)[:, :values_count].astype(f32)
     ada_res = adam_update(ada_master, ada_first, ada_second, clip * grad_ada, RATE_ADAM)
     io_res = adam_update(io_proj, io_first, io_second, clip * io_grad, RATE_ADAM)

time: 752 us -> 724 us (0.963)
  Pallas kernels: 645 us -> 626 us
  other arithmetic: 36.6 us -> 24.1 us
  local copies, waits for them, and re-layouts: 42.1 us -> 51.4 us
    pallas_call x13 -> x11, Pallas kernels: 645 us -> 626 us  [run(): pl.pallas_call(self.kernel, out_shape=self.outputs, in_specs=self.operand...]
    unnamed x193 -> x169, local copies, waits for them, and re-layouts: 22.6 us -> 30.7 us
  transfers between devices with their start and end apart: 1 -> 1, of which waited for: 0 -> 0; matrix products, arithmetic and copies ran while one was open for 1% -> 1% of each run, Pallas kernels for 6% -> 7%
where the time goes in v7:
time: 724 us; the launch traced here: 716 us
  Pallas kernels  626 us (86%)
  local copies, waits for them, and re-layouts  51.4 us (7%)
  other arithmetic  24.1 us (3%)
  matrix products  8.03 us (1%)
    pallas_call x11, Pallas kernels, run(): pl.pallas_call(self.kernel, out_shape=self.outputs, in_specs=self.operand...  626 us
    unnamed x169, local copies, waits for them, and re-layouts  30.7 us
  transfers between devices with their start and end apart: 1, of which 0 were waited for; matrix products, arithmetic and copies ran while one was open for 1% of the time, Pallas kernels for 7%

profile of v7, /device:TPU:0, one launch (start us, length us, event | category | flops | bytes accessed | tf_op | source)
XLA Modules:
  0.0 716.3 jit_solution(5587141542334708833)
XLA Ops:
  2.7 1.2 dynamic_slice.24
  5.5 1.3 broadcast_in_dim.29.refs_4_
  7.7 1.5 convert_element_type.76.refs_5_
  9.3 1.0 copy.78
  11.0 1.0 copy.80
  12.0 1.0 convert.22
  13.5 1.1 fusion.30
  16.7 60.6 %begin.1 = (f32[2,8,1024]{2,1,0:T(8,128)}, f32[8,1024]{1,0:T(8,128)}, bf16[8,1024]{1,0:T(8,128)(2,1)}, f32[128,1024]{1,0:T(8,128)}, bf16[128,1024]{1,0:T(8,128)(...) custom-call(s32[8,128]{1,0:T(8,128)} %broadcast_in_dim.27.refs_0_.re, ...), custom_call_target="tpu_custom_call" | custom-call | tf_op jit(solution)/shard_map/begin/pallas_call | solution.py:680
  77.3 1.4 slice_bitcast_fusion.12
  78.7 1.2 fusion.24
  80.7 1.1 copy-done.12
  83.7 32.3 %attend0.1 = (bf16[3,1024,128]{2,1,0:T(8,128)(2,1)S(1)}, bf16[128,1024]{1,0:T(8,128)(2,1)S(1)}, bf16[4,128,1024]{2,1,0:T(8,128)(2,1)S(1)}, bf16[4,128,384]{2,1,0:T(8,128)(2,1)S(1)}) custom-call(bf16[128,3072]{1,0:T(8,128)(2,1)S(1)} %copy-done.12, bf16[128,1024]{1,0:T(8,128)(2,1)S(1)} %copy-done.23, bf16[128,384]{1,0:T(8,128)(2,1)S(1)} %copy-done.32), custom_call_target="tpu_custom_call" | custom-call | tf_op jit(solution)/shard_map/attend0/pallas_call | solution.py:680
  116.7 1.0 copy-done.4
  118.4 28.6 %feed0.1 = (f32[128,1024]{1,0:T(8,128)}, f32[128,1024]{1,0:T(8,128)}, f32[128,1024]{1,0:T(8,128)}, f32[128,1024]{1,0:T(8,128)}, bf16[128,1024]{1,0:T(8,128)(2,1)...) custom-call(bf16[1024,1024]{1,0:T(8,128)(2,1)} %get-tuple-element.12, ...), custom_call_target="tpu_custom_call" | custom-call | tf_op jit(solution)/shard_map/feed0/pallas_call | solution.py:680
  147.0 1.1 copy-done.13
  150.0 34.3 %attend1.1 = (bf16[3,1024,128]{2,1,0:T(8,128)(2,1)S(1)}, bf16[128,1024]{1,0:T(8,128)(2,1)S(1)}, bf16[4,128,1024]{2,1,0:T(8,128)(2,1)S(1)}, bf16[4,128,384]{2,1,0:T(8,128)(2,1)S(1)}, bf16[4,128,1024]{2,1,0:T(8,128)(2,1)S(1)}) custom-call(bf16[128,3072]{1,0:T(8,128)(2,1)S(1)} %copy-done.13, bf16[128,1024]{1,0:T(8,128)(2,1)S(1)} %copy-done.24, ...), custom_call_target="tpu_custom_call" | custom-call | tf_op jit(solution)/shard_map/attend1/pallas_call | solution.py:680
  184.3 1.0 copy-done.5
  185.3 1.0 copy-done.6
  187.7 26.5 %feed1.1 = (f32[128,1024]{1,0:T(8,128)}, f32[128,1024]{1,0:T(8,128)}, f32[128,1024]{1,0:T(8,128)}, f32[128,1024]{1,0:T(8,128)}, bf16[128,1024]{1,0:T(8,128)(2,1)...) custom-call(bf16[1024,1024]{1,0:T(8,128)(2,1)} %get-tuple-element.12, ...), custom_call_target="tpu_custom_call" | custom-call | tf_op jit(solution)/shard_map/feed1/pallas_call | solution.py:680
  214.2 1.7 multiply_reduce_fusion
  215.9 30.6 %feed_back1.1 = (f32[8,1024]{1,0:T(8,128)}, f32[128,384]{1,0:T(8,128)}, bf16[128,384]{1,0:T(8,128)(2,1)}, f32[128,1024]{1,0:T(8,128)}, bf16[128,1024]{1,0:T(8,12...) custom-call(bf16[2,384,1024]{2,1,0:T(8,128)(2,1)} %bitcast.79, ...), custom_call_target="tpu_custom_call" | custom-call | tf_op jit(solution)/shard_map/feed_back1/pallas_call | solution.py:680
  246.6 2.6 fusion.35
  249.3 42.4 %attend_back1.1 = (bf16[128,3072]{1,0:T(8,128)(2,1)S(1)}, bf16[4,128,256]{2,1,0:T(8,128)(2,1)S(1)}, bf16[4,128,256]{2,1,0:T(8,128)(2,1)S(1)}, bf16[4,128,384]{2,1,0:T(8,128)(2,1)S(1)}, bf16[4,128,1024]{2,1,0:T(8,128)(2,1)S(1)}) custom-call(bf16[128,1024]{1,0:T(8,128)(2,1)S(1)} %copy-done.31, bf16[128,1024]{1,0:T(8,128)(2,1)S(1)} %copy-done.30, ...), custom_call_target="tpu_custom_call" | custom-call | tf_op jit(solution)/shard_map/attend_back1/pallas_call | solution.py:680
  292.5 1.0 copy-done.7
  295.7 34.5 %feed_back0.1 = (bf16[128,1024]{1,0:T(8,128)(2,1)}, f32[8,1024]{1,0:T(8,128)}, f32[128,384]{1,0:T(8,128)}, bf16[128,384]{1,0:T(8,128)(2,1)}, f32[128,1024]{1,0:T...) custom-call(bf16[2,384,1024]{2,1,0:T(8,128)(2,1)} %bitcast.80, ...), custom_call_target="tpu_custom_call" | custom-call | tf_op jit(solution)/shard_map/feed_back0/pallas_call | solution.py:680
  330.2 2.6 bitcast_add_fusion
  332.8 2.1 copy-done.36
  334.9 1.1 dynamic-slice_convert_fusion
  338.2 51.3 %attend_back0.1 = (bf16[128,3072]{1,0:T(8,128)(2,1)S(1)}, bf16[4,128,256]{2,1,0:T(8,128)(2,1)S(1)}, bf16[4,128,256]{2,1,0:T(8,128)(2,1)S(1)}, bf16[4,128,384]{2,...) custom-call(bf16[128,1024]{1,0:T(8,128)(2,1)S(1)} %copy-done.28, ...), custom_call_target="tpu_custom_call" | custom-call | tf_op jit(solution)/shard_map/attend_back0/pallas_call | solution.py:680
  389.6 1.5 fusion.34
  392.0 1.3 bitcast_add_fusion.1
  393.3 1.1 dynamic-slice_convert_fusion.1.refs_6_
  394.5 1.5 constant_dynamic-slice_fusion.refs_23_
  396.0 1.4 copy-done.37
  397.4 2.9 convert_add_fusion.refs_7_
  400.3 95.6 %reduce.7 = (f32[128,256]{1,0:T(8,128)}, f32[8,1536]{1,0:T(8,128)}, f32[4,16,1536]{2,1,0:T(8,128)}, f32[96,256]{1,0:T(8,128)}, f32[1024,512]{1,0:T(8,128)}) custom-call(bf16[128,3072]{1,0:T(8,128)(2,1)} %copy-done.10, f32[128,1024]{1,0:T(8,128)} %get-tuple-element.127.refs_3_.refs_1_, f32[128,1024]{1,0:T(8,128)} %get-tuple-element.161.refs_2_, ...), custom_call_target="tpu_custom_call" | custom-call | tf_op jit(solution)/shard_map/reduce/pallas_call | solution.py:680
  498.1 189.2 %finish.1 = (f32[8,128]{1,0:T(8,128)}, f32[128,1536]{1,0:T(8,128)}, f32[8,1024]{1,0:T(8,128)}, bf16[8,96,256]{2,1,0:T(8,128)(2,1)}, f32[128,768]{1,0:T(8,128)}, ...) custom-call(f32[1024,512]{1,0:T(8,128)} %get-tuple-element.186.refs_, ...), custom_call_target="tpu_custom_call" | custom-call | tf_op jit(solution)/shard_map/finish/pallas_call | solution.py:680
  688.2 1.3 fusion.32
  692.9 1.1 slice_bitcast_fusion.5
  694.0 1.0 slice.168
  695.9 1.9 maximum_multiply_fusion
  697.8 2.9 divide_subtract_fusion.1
  700.7 1.5 divide_subtract_fusion.4
  703.1 1.1 multiply_add_fusion.2
  704.3 1.8 divide_subtract_fusion
  707.6 1.1 copy.113
  711.0 1.3 copy.117
  713.7 1.3 copy.119
  (191 shorter events, 30.9 us)
Async XLA Ops:
  0.7 12.3 %copy-start.43 = (f32[128,1024]{1,0:T(8,128)S(1)}, f32[128,1024]{1,0:T(8,128)}, u32[]{:S(2)}) copy-start(f32[128,1024]{1,0:T(8,128)} %param.44) | copy-start | bytes 1572868
  0.7 12.4 %copy-start.45 = (f32[128,1024]{1,0:T(8,128)S(1)}, f32[128,1024]{1,0:T(8,128)}, u32[]{:S(2)}) copy-start(f32[128,1024]{1,0:T(8,128)} %param.47) | copy-start | bytes 1572868
  0.7 12.4 %copy-start.40 = (f32[2,276,256]{2,0,1:T(2,128)S(1)}, f32[2,276,256]{2,0,1:T(2,128)}, u32[]{:S(2)}) copy-start(f32[2,276,256]{2,0,1:T(2,128)} %param.52) | copy-start | bytes 1695748
  10.3 3.1 copy-start.75
  118.4 28.6 %copy-start.3 = (bf16[128,1024]{1,0:T(8,128)(2,1)S(1)}, bf16[128,1024]{1,0:T(8,128)(2,1)}, u32[]{:S(2)}) copy-start(bf16[128,1024]{1,0:T(8,128)(2,1)} %copy-done.2) | copy-start | bytes 786436
  215.9 30.6 %copy-start.48 = (bf16[4,128,1024]{2,1,0:T(8,128)(2,1)S(1)}, bf16[4,128,1024]{2,1,0:T(8,128)(2,1)}, u32[]{:S(2)}) copy-start(bf16[4,128,1024]{2,1,0:T(8,128)(2,1)} %get-tuple-element.168) | copy-start | bytes 3145732
  246.6 2.7 copy-start.9
  246.6 2.7 copy-start.29
  246.6 2.7 copy-start.30
  246.6 2.7 copy-start.31
  246.6 2.7 copy-start.34
  295.7 34.5 %copy-start.38 = (bf16[4,128,1024]{2,1,0:T(8,128)(2,1)S(1)}, bf16[4,128,1024]{2,1,0:T(8,128)(2,1)}, u32[]{:S(2)}) copy-start(bf16[4,128,1024]{2,1,0:T(8,128)(2,1)} %get-tuple-element.170) | copy-start | bytes 3145732
  332.8 2.1 copy-start.36
  334.9 3.2 copy-start.1
  334.9 3.2 copy-start.25
  334.9 3.2 copy-start.26
  334.9 3.3 copy-start.27
  334.9 3.3 copy-start.28
  334.9 3.3 copy-start.33
  336.1 59.9 %collective-permute-start = (bf16[1024,512]{1,0:T(8,128)(2,1)}, bf16[1024,512]{1,0:T(8,128)(2,1)}, u32[]{:S(2)}, u32[]{:S(2)}) collective-permute-start(bf16[1024,512]{1,0:T(8,128)(2,1)} %dynamic-slice_convert_fusion), channel_id=1, source_target_pairs={{0,4},{4,0},{8,12},{12,8},{16,20},{20,16},{24,28},{28,24},{1,5},{5... | collective-permute-start | bytes 3145736 | tf_op jit(solution)/shard_map/ppermute | solution.py:2036
  338.1 51.4 %copy-start.47 = (bf16[4,128,1024]{2,1,0:T(8,128)(2,1)S(1)}, bf16[4,128,1024]{2,1,0:T(8,128)(2,1)}, u32[]{:S(2)}) copy-start(bf16[4,128,1024]{2,1,0:T(8,128)(2,1)} %get-tuple-element.164) | copy-start | bytes 3145732
  338.1 51.4 %copy-start.52 = (bf16[4,128,1024]{2,1,0:T(8,128)(2,1)S(1)}, bf16[4,128,1024]{2,1,0:T(8,128)(2,1)}, u32[]{:S(2)}) copy-start(bf16[4,128,1024]{2,1,0:T(8,128)(2,1)} %get-tuple-element.165) | copy-start | bytes 3145732
  389.5 2.4 copy-start.51
  394.5 2.9 copy-start.37
  687.3 7.7 %copy-start.50 = (f32[128,768]{1,0:T(8,128)S(1)}, f32[128,768]{1,0:T(8,128)}, u32[]{:S(2)}) copy-start(f32[128,768]{1,0:T(8,128)} %param.38) | copy-start | bytes 1179652
  687.3 10.5 %copy-start.57 = (f32[2,276,256]{2,0,1:T(2,128)S(1)}, f32[2,276,256]{2,0,1:T(2,128)}, u32[]{:S(2)}) copy-start(f32[2,276,256]{2,0,1:T(2,128)} %param.53) | copy-start | bytes 1695748
  687.3 10.5 %copy-start.58 = (f32[2,276,256]{2,0,1:T(2,128)S(1)}, f32[2,276,256]{2,0,1:T(2,128)}, u32[]{:S(2)}) copy-start(f32[2,276,256]{2,0,1:T(2,128)} %param.54) | copy-start | bytes 1695748
  695.0 5.7 copy-start.69
  695.0 5.7 copy-start.71
  695.0 5.7 copy-start.72
  695.8 6.4 copy-start.59
  695.8 6.4 copy-start.60
  695.8 6.4 copy-start.61
  695.8 6.4 copy-start.66
  695.8 6.4 copy-start.67
  697.8 5.3 copy-start.44
  697.8 5.3 copy-start.46
  700.7 3.5 copy-start.53
  700.7 3.5 copy-start.54
  700.7 3.5 copy-start.55
  700.7 3.5 copy-start.56
  704.3 2.5 copy-start.65
  704.3 3.3 copy-start.49
  706.1 2.6 copy-start.68
  706.8 2.6 copy-start.64
  707.6 2.6 copy-start.63
  707.6 3.4 copy-start.42
  711.0 2.7 copy-start.41
  (29 other events, 34.6 us)

commit v8 on v7

--- a/solution.py
+++ b/solution.py
@@ -717,12 +717,18 @@
                     )
                 )
         for source_at, target_at in pairs:
-            self.keep(
+            local = self.keep(
                 source,
                 None if source_at is None else (lambda at=source_at: at(lax.axis_index(axis))),
                 target,
                 lambda at=target_at: at(lax.axis_index(axis)),
+                later,
             )
+            if later:
+                self.start_local(local)
+        if later:
+            for number in numbers:
+                self.start(number)
         return numbers
 
     def gather(self, axis, array):
@@ -769,48 +775,55 @@
         )
         return numbers, len(self.locals) - 1
 
-    def gather_twice(self, arrays, members):
+    def gather_twice(self, arrays, members, chunks):
         shards = lax.axis_size(SHARDS)
         entries = []
-        for array in arrays:
+        for array, pieces in zip(arrays, chunks):
             source = self.operand(array)
             width = array.shape[1]
             target = self.scratch((array.shape[0], shards * width), array.dtype)
-            rows = array.shape[0] // members
+            rows = array.shape[0] // members // pieces
 
             def columns(back_pair, width=width):
                 who = lax.rem(lax.axis_index(SHARDS) + shards - 2 * back_pair, shards)
                 return pl.ds(pl.multiple_of(who * width, LANES), width)
 
-            def place(back_member, back_pair, rows=rows, columns=columns):
+            def piece_rows(back_member, piece, rows=rows, pieces=pieces):
                 index = lax.rem(lax.rem(lax.axis_index(PATCHES), members) + members - back_member, members)
-                return (pl.ds(pl.multiple_of(index * rows, rows), rows), columns(back_pair))
-
-            def mine(rows=rows):
-                index = lax.rem(lax.axis_index(PATCHES), members)
-                return (pl.ds(pl.multiple_of(index * rows, rows), rows),)
+                return pl.ds(pl.multiple_of((index * pieces + piece) * rows, rows), rows)
+
+            def place(back_member, back_pair, piece, columns=columns, piece_rows=piece_rows):
+                return (piece_rows(back_member, piece), columns(back_pair))
+
+            def mine(piece, piece_rows=piece_rows):
+                return (piece_rows(0, piece),)
 
             def whole(columns=columns):
                 return (slice(None), columns(0))
 
             firsts = [
-                self.move(
-                    (SHARDS, 2 * pair),
-                    lambda pair=pair: {SHARDS: lax.rem(lax.axis_index(SHARDS) + 2 * pair, shards)},
-                    source,
-                    mine,
-                    target,
-                    functools.partial(place, 0, 0),
+                (
+                    pair,
+                    piece,
+                    self.move(
+                        (SHARDS, 2 * pair),
+                        lambda pair=pair: {SHARDS: lax.rem(lax.axis_index(SHARDS) + 2 * pair, shards)},
+                        source,
+                        functools.partial(mine, piece),
+                        target,
+                        functools.partial(place, 0, 0, piece),
+                    ),
                 )
+                for piece in range(pieces)
                 for pair in range(1, shards // 2)
             ]
             near = self.move((SHARDS,), sibling_peer, source, None, target, whole)
             local = self.keep(source, None, target, whole)
-            entries.append((target, place, firsts, [near, *firsts], local))
+            entries.append((target, place, firsts, [near, *[number for _, _, number in firsts]], local))
         last = []
         for target, place, firsts, numbers, _ in entries:
-            for pair, first in enumerate(firsts, 1):
-                near = functools.partial(place, 0, pair)
+            for pair, piece, first in firsts:
+                near = functools.partial(place, 0, pair, piece)
                 for shift in range(1, members):
                     number = self.move(
                         (PATCHES, members, shift),
@@ -821,7 +834,7 @@
                         near,
                         (first,),
                     )
-                    last.append((target, functools.partial(place, shift, pair), number, numbers))
+                    last.append((target, functools.partial(place, shift, pair, piece), number, numbers))
                 numbers.append(self.move((SHARDS,), sibling_peer, target, near, target, near, (first,)))
         for target, at, number, numbers in last:
             numbers += [number, self.move((SHARDS,), sibling_peer, target, at, target, at, (number,))]
@@ -917,6 +930,7 @@
 
 
 CHAIN_CHUNKS = 8
+KERNEL_VMEM = 62 * 2**20
 GRAM_COLS = 256
 
 
@@ -1034,7 +1048,7 @@
     (rows, padded), (table_rows, _) = state.shape, cond_table.shape
     width = w_out.shape[0]
     ada_cols = ada.shape[1]
-    moves = Moves("begin", ids, 56 * 2**20)
+    moves = Moves("begin", ids, KERNEL_VMEM)
     table = moves.scratch((table_rows, width), f32)
     bias = moves.scratch((1, biases.shape[1] * shards), f32)
     pos_all = moves.scratch((rows, width), LOW)
@@ -1090,7 +1104,7 @@
         )
         modul_moves.append(number)
         moves.start(number)
-    weights = moves.gather_twice((io_low.reshape(-1, io_low.shape[-1]), w_out, w_qkv), members)
+    weights = moves.gather_twice((io_low.reshape(-1, io_low.shape[-1]), w_out, w_qkv), members, (1, 1, 4))
 
     def collect(ref):
         bias_row = ref(bias)[:, pl.ds(6 * width, width)].astype(LOW).astype(f32)
@@ -1230,6 +1244,7 @@
         return value
 
 
+TOKENS, UP_GRAD = 1, 2
 GELU_SCALE = math.sqrt(2.0 / math.pi)
 GELU_CUBE = 0.044715
 
@@ -1244,14 +1259,14 @@
     return 0.5 * (1.0 + inner) + 0.5 * values * (1.0 - inner * inner) * rise
 
 
-def feed_forward(ids, step, mods, mods_next, mixed, embedded, state, pos, w_out, w_up, w_down, io_all, w_qkv, moment_part):
+def feed_forward(ids, step, mods, mods_next, mixed, embedded, state, pos, w_out, w_up, w_down, io_all, w_qkv, momenta, members):
     f32 = jnp.float32
     last = mods_next is None
     rows, width = mixed.shape
     padded = state.shape[1]
     hidden_count = w_up.shape[1]
     shards = lax.axis_size(SHARDS)
-    moves = Moves(f"feed{step}", ids, 56 * 2**20)
+    moves = Moves(f"feed{step}", ids, KERNEL_VMEM)
     vmem = functools.partial(moves.operand, space=pltpu.VMEM)
     out_weights, out_load = moves.load(w_out)
     mods, mixed, embedded, state = vmem(mods), vmem(mixed), vmem(embedded), vmem(state)
@@ -1276,7 +1291,25 @@
         normed_next = moves.output((rows, width), LOW, pltpu.VMEM)
         state_low = moves.output((rows, padded), LOW, pltpu.VMEM)
         qkv_next = moves.output((rows, w_qkv.shape[1]), LOW, pltpu.VMEM)
-    moves.exchange(PATCHES, moment_part)
+    half = rows // ROLL
+    seq_count = lax.axis_size(PATCHES)
+    most_cols = max(item.shape[1] for item in momenta) // members
+    moment_loads = []
+    for item in momenta:
+        scratch = moves.scratch((half, item.shape[1]), f32)
+        number = moves.keep(moves.operand(item), lambda: (pl.ds(step * half, half),), scratch, None)
+        moment_loads.append((scratch, number))
+    moment_leaving = moves.scratch((seq_count, half, most_cols), LOW)
+    moment_arriving = moves.output((seq_count, half, most_cols), LOW)
+
+    def pack(ref):
+        for which, (scratch, _) in enumerate(moment_loads):
+            cols = momenta[which].shape[1] // members
+            for part in range(members):
+                value = ref(scratch)[:, part * cols : (part + 1) * cols].astype(LOW)
+                if cols < most_cols:
+                    value = jnp.concatenate([value, jnp.zeros((half, most_cols - cols), LOW)], 1)
+                ref(moment_leaving)[which * members + part] = value
 
     def begin(ref):
         value = contract(ref(mixed)[...], ref(out_weights)[...], 1, 0)
@@ -1317,6 +1350,12 @@
     feed.run(work)
     for number in saves:
         moves.start_local(number)
+    for _, number in moment_loads:
+        moves.wait_local(number)
+    moves.task(pack)
+    moves.along(
+        PATCHES, moment_leaving, moment_arriving, [(lambda there: (there,), lambda sender: (sender,))], later=True
+    )
     moves.wait_local(io_load)
     feed.wait()
     moves.task(finish)
@@ -1326,14 +1365,14 @@
     return moves.run()
 
 
-def feed_back(ids, step, mods, mods_later, later, grad_state, kept, w_out, w_up, w_down, io_all, w_qkv):
+def feed_back(ids, step, mods, mods_later, later, grad_state, kept, w_out, w_up, w_down, io_all, w_qkv, members, pairs):
     f32 = jnp.float32
     attended, after_attn, downward, after_mlp, upward = kept
     rows, width = attended.shape
     padded = grad_state.shape[1]
     hidden_count = w_up.shape[1]
     shards = lax.axis_size(SHARDS)
-    moves = Moves(f"feed_back{step}", ids, 56 * 2**20)
+    moves = Moves(f"feed_back{step}", ids, KERNEL_VMEM)
     vmem = functools.partial(moves.operand, space=pltpu.VMEM)
     io_weights, io_load = moves.load(io_all)
     if later is not None:
@@ -1360,6 +1399,41 @@
         moves.save(up_grad, (shards, rows, hidden_count), LOW),
     ]
 
+    weight_outputs, weight_tasks = [], []
+    if pairs is not None:
+        half_cols = hidden_count // members
+        whole = moves.scratch((GRAM_COLS, hidden_count), f32)
+        for made, operands in pairs:
+            mine = moves.output((width, half_cols), f32)
+            leaving = [moves.output((width, half_cols), LOW) for _ in range(members - 1)]
+            held = moves.scratch((width, half_cols), f32)
+            held_low = [moves.scratch((width, half_cols), LOW) for _ in range(members - 1)]
+            loads = [[None if item is None else moves.load(item) for item in entry] for entry in operands]
+            weight_outputs += [(held, mine)] + list(zip(held_low, leaving))
+            weight_tasks.append((made, loads, held, held_low))
+
+    def weight_grad(made, loads, held, held_low):
+        def action(ref):
+            @pl.loop(0, width // GRAM_COLS)
+            def _(tile):
+                at = pl.ds(pl.multiple_of(tile * GRAM_COLS, GRAM_COLS), GRAM_COLS)
+                value = jnp.zeros((GRAM_COLS, hidden_count), f32)
+                for entry in loads:
+                    left, right = [made_here if item is None else item[0] for item, made_here in zip(entry, made)]
+                    left_rows = ref(left)[:, :, at].reshape(-1, GRAM_COLS)
+                    value = value + contract(left_rows, ref(right)[...].reshape(-1, hidden_count), 0, 0)
+                ref(whole)[...] = value
+                member = lax.rem(lax.axis_index(PATCHES), members)
+                for shift in range(members):
+                    there = lax.rem(member + shift, members)
+                    part = ref(whole)[:, pl.ds(pl.multiple_of(there * half_cols, LANES), half_cols)]
+                    if shift:
+                        ref(held_low[shift - 1])[at, :] = part.astype(LOW)
+                    else:
+                        ref(held)[at, :] = part
+
+        return action
+
     def put(ref, row, value):
         ref(vectors)[pl.ds(row, 1), :] = jnp.sum(value, 0, keepdims=True)
 
@@ -1416,6 +1490,15 @@
     feed.run(work)
     for number in saves:
         moves.start_local(number)
+    for made, loads, held, held_low in weight_tasks:
+        for entry in loads:
+            for item in entry:
+                if item is not None:
+                    moves.wait_local(item[1])
+        made = [feed.tokens if item is TOKENS else up_grad if item is UP_GRAD else None for item in made]
+        moves.task(weight_grad(made, loads, held, held_low))
+    for held, target in weight_outputs:
+        moves.start_local(moves.keep(held, None, target, None, True))
     moves.wait_local(out_load)
     feed.wait()
     moves.task(finish)
@@ -1431,8 +1514,8 @@
     rows, width = embedded.shape
     block_rows, most_cols = width, max(group_cols)
     part, ada_cols = width // shards, ada.shape[1]
-    up_mine, down_mine, down_leaving = mlp
-    moves = Moves("reduce", ids, 60 * 2**20)
+    up_mine, up_arrived, down_mine, down_leaving = mlp
+    moves = Moves("reduce", ids, KERNEL_VMEM)
     vmem = functools.partial(moves.operand, space=pltpu.VMEM)
     qkv_grad, embedded, grad_attn, mods = vmem(qkv_grad), vmem(embedded), vmem(grad_attn), vmem(mods)
     rows_late, rows_early = vmem(rows_late), vmem(rows_early)
@@ -1561,6 +1644,7 @@
         for shift, item in enumerate(down_leaving, 1)
     ]
     up_full, up_load = moves.load(up_mine)
+    up_others = [moves.load(item) for item in up_arrived]
     qkv_weights, qkv_load = moves.load(w_qkv)
     loaded = {
         name: [moves.load(steps[step]) for step in range(ROLL) if step in steps] for name, steps in gathered.items()
@@ -1579,11 +1663,16 @@
 
     def round_up_grad(ref):
         def action(at):
-            ref(up_low)[at, :] = ref(up_full)[at, :].astype(LOW)
+            value = ref(up_full)[at, :]
+            for item, _ in up_others:
+                value = value + ref(item)[at, :].astype(f32)
+            ref(up_full)[at, :] = value
+            ref(up_low)[at, :] = value.astype(LOW)
 
         over_rows(action)
 
-    moves.wait_local(up_load)
+    for number in (up_load, *[number for _, number in up_others]):
+        moves.wait_local(number)
     moves.task(round_up_grad)
     up_moves = to_group(up_low, group_target, 1)
 
@@ -1958,17 +2047,7 @@
     group_cols = [item.shape[1] // members for item in momenta]
     most_cols = max(group_cols)
 
-    def widen(item):
-        return jnp.pad(item, ((0, 0), (0, most_cols - item.shape[1])))
-
-    moment_parts = jnp.stack(
-        [
-            widen(item[:, part * cols : (part + 1) * cols].astype(LOW))
-            for item, cols in zip(momenta, group_cols)
-            for part in range(members)
-        ]
-    )
-    half_rows = moment_parts.shape[1] // 2
+    half_rows = local // ROLL
 
     counts = jnp.sum((intervals[:, None] == jnp.arange(NI, dtype=jnp.int32)[None]).astype(f32), 0)
     my_id = lax.dynamic_slice_in_dim(intervals, shard, 1)
@@ -1979,7 +2058,7 @@
     moment_halves = []
 
     for step in range(ROLL):
-        moves = Moves(f"attend{step}", ids, 48 * 2**20)
+        moves = Moves(f"attend{step}", ids, KERNEL_VMEM)
         qkv_out = moves.output((3, local * seq_count, width // seq_count), LOW, pltpu.VMEM)
         mixed_out = moves.output((local, width), LOW, pltpu.VMEM)
         arrivals = moves.rows_to_heads(PATCHES, qkv_rows, 3, qkv_out)
@@ -2007,7 +2086,8 @@
             down_copy,
             io_all,
             w_qkv,
-            moment_parts[:, step * half_rows : (step + 1) * half_rows],
+            momenta,
+            members,
         )
         moment_halves.append(moment_half)
         attended, after_attn, downward, after_mlp, normed_c, state, tokens_b, upward, hidden, *following = results
@@ -2024,24 +2104,18 @@
 
     mlp_back = []
 
-    def patch_sum(item, cols):
-        mine = lax.dynamic_slice_in_dim(item, member * cols, cols, 1)
-        low = item.astype(LOW)
-        for shift in range(1, members):
-            pairs = [
-                (index, index // members * members + (index + shift) % members) for index in range(seq_count)
-            ]
-            to_member = lax.rem(member + shift, members)
-            outgoing = lax.dynamic_slice_in_dim(low, to_member * cols, cols, 1)
-            mine = mine + lax.ppermute(outgoing, PATCHES, pairs).astype(f32)
-        return mine
-
     later, mods_later = None, None
     vector_rows = [None] * ROLL
 
     for step in reversed(range(ROLL)):
         embedded, qkv, mixed, for_feed, normed_c, tokens_b, hidden = kept[step]
-        embed_grad, vectors, grad_state, delta_grad, grad_attn, attn_grad, mixed_grad, tokens_down, up_grad = feed_back(
+        pairs = None
+        if step == 0:
+            pairs = (
+                ((None, UP_GRAD), [(tokens_b, None), *[(item[0], item[1]) for item in mlp_back]]),
+                ((TOKENS, None), [(None, hidden), *[(item[2], item[3]) for item in mlp_back]]),
+            )
+        results = feed_back(
             ids,
             step,
             extras[step],
@@ -2054,22 +2128,23 @@
             down_copy,
             io_all,
             w_qkv,
+            members,
+            pairs,
         )
+        embed_grad, vectors, grad_state, delta_grad, grad_attn, attn_grad, mixed_grad, *results = results
+        tokens_down, up_grad, *weight_grads = results
         vector_rows[step] = vectors
         mlp_back.append((tokens_b, up_grad, tokens_down, hidden))
         if step == 0:
-            up_total, down_total = [
-                sum(rows_product(items[left], items[right]) for items in mlp_back) for left, right in ((0, 1), (2, 3))
-            ]
-            up_mine = patch_sum(up_total, group_cols[1])
-            down_mine = lax.dynamic_slice_in_dim(down_total, member * group_cols[2], group_cols[2], 1)
-            down_leaving = [
-                lax.dynamic_slice_in_dim(
-                    down_total, lax.rem(member + shift, members) * group_cols[2], group_cols[2], 1
-                ).astype(LOW)
-                for shift in range(1, members)
-            ]
-        moves = Moves(f"attend_back{step}", ids, 48 * 2**20)
+            up_mine, *up_leaving = weight_grads[:members]
+            down_mine, *down_leaving = weight_grads[members:]
+            up_arrived = []
+            for shift, item in enumerate(up_leaving, 1):
+                routes = [
+                    (index, index // members * members + (index + shift) % members) for index in range(seq_count)
+                ]
+                up_arrived.append(lax.ppermute(item, PATCHES, routes))
+        moves = Moves(f"attend_back{step}", ids, KERNEL_VMEM)
         grads_in = moves.scratch((1, local * seq_count, width // seq_count), LOW)
         result = moves.output((local, 3 * width), LOW, pltpu.VMEM)
         arrivals = moves.rows_to_heads(PATCHES, mixed_grad, 1, grads_in)
@@ -2105,11 +2180,11 @@
         vector_rows[1],
         vector_rows[0],
         gathered,
-        (up_mine, down_mine, down_leaving),
+        (up_mine, up_arrived, down_mine, down_leaving),
         ada_copy,
     )
     io_cols = io_slice.shape[1]
-    moves = Moves("finish", ids, 60 * 2**20)
+    moves = Moves("finish", ids, KERNEL_VMEM)
     vmem = functools.partial(moves.operand, space=pltpu.VMEM)
     vmem_out = functools.partial(moves.output, space=pltpu.VMEM)
     full, low = (block_rows, block_rows), (block_rows, most_cols)

time: 724 us -> 690 us (0.953)
  local copies, waits for them, and re-layouts: 51.4 us -> 27.2 us
  matrix products: 8.03 us -> 0 us
    unnamed x169 -> x71, local copies, waits for them, and re-layouts: 30.7 us -> 11.3 us
    dot_general x4 -> x0, matrix products: 8.03 us -> none  [rows_product(): lax.dot_general(flat_left, flat_right, (((0,), (0,)), ((), ())), preferre...]
  transfers between devices with their start and end apart: 1 -> 1, of which waited for: 0 -> 0; matrix products, arithmetic and copies ran while one was open for 1% -> 0% of each run, Pallas kernels for 7% -> 8%
where the time goes in v8:
time: 690 us; the launch traced here: 676 us
  Pallas kernels  621 us (90%)
  local copies, waits for them, and re-layouts  27.2 us (4%)
  other arithmetic  20.3 us (3%)
    pallas_call x11, Pallas kernels, run(): pl.pallas_call(self.kernel, out_shape=self.outputs, in_specs=self.operand...  621 us
  transfers between devices with their start and end apart: 1, of which 0 were waited for; matrix products, arithmetic and copies ran while one was open for 0% of the time, Pallas kernels for 8%

profile of v8, /device:TPU:0, one launch (start us, length us, event | category | flops | bytes accessed | tf_op | source)
XLA Modules:
  0.0 676.2 jit_solution(4234133860055040483)
XLA Ops:
  2.0 0.7 convert_reduce_fusion
  2.7 1.2 dynamic_slice.12
  4.0 0.7 broadcast_in_dim.12
  5.5 1.3 broadcast_in_dim.29.refs_4_
  6.8 1.5 convert_element_type.53.refs_5_
  8.3 1.0 copy.70
  10.0 1.0 copy.72
  11.0 1.3 convert_element_type.54
  12.3 0.8 pad.18.clone
  14.4 49.4 %begin.1 = (f32[2,8,1024]{2,1,0:T(8,128)}, f32[8,1024]{1,0:T(8,128)}, bf16[8,1024]{1,0:T(8,128)(2,1)}, f32[128,1024]{1,0:T(8,128)}, bf16[128,1024]{1,0:T(8,128)(...) custom-call(s32[8,128]{1,0:T(8,128)} %broadcast_in_dim.27.refs_0_.re, ...), custom_call_target="tpu_custom_call" | custom-call | tf_op jit(solution)/shard_map/begin/pallas_call | solution.py:680
  63.8 1.4 slice_bitcast_fusion.8
  65.2 1.2 fusion.18
  67.2 32.9 %attend0.1 = (bf16[3,1024,128]{2,1,0:T(8,128)(2,1)}, bf16[128,1024]{1,0:T(8,128)(2,1)}, bf16[4,128,1024]{2,1,0:T(8,128)(2,1)}, bf16[4,128,384]{2,1,0:T(8,128)(2,1)}) custom-call(bf16[128,3072]{1,0:T(8,128)(2,1)} %get-tuple-element.125.refs_0_, bf16[128,1024]{1,0:T(8,128)(2,1)} %get-tuple-element.126.refs_1_, bf16[128,384]{1,0:T(8,128)(2,1)} %get-tuple-element.127.refs_2_), custom_call_target="tpu_custom_call" | custom-call | tf_op jit(solution)/shard_map/attend0/pallas_call | solution.py:680
  100.1 28.6 %feed0.1 = (f32[128,1024]{1,0:T(8,128)}, f32[128,1024]{1,0:T(8,128)}, f32[128,1024]{1,0:T(8,128)}, f32[128,1024]{1,0:T(8,128)}, bf16[128,1024]{1,0:T(8,128)(2,1)...) custom-call(bf16[1024,1024]{1,0:T(8,128)(2,1)} %get-tuple-element.12, ...), custom_call_target="tpu_custom_call" | custom-call | tf_op jit(solution)/shard_map/feed0/pallas_call | solution.py:680
  128.7 36.0 %attend1.1 = (bf16[3,1024,128]{2,1,0:T(8,128)(2,1)}, bf16[128,1024]{1,0:T(8,128)(2,1)}, bf16[4,128,1024]{2,1,0:T(8,128)(2,1)}, bf16[4,128,384]{2,1,0:T(8,128)(2,1)}, bf16[4,128,1024]{2,1,0:T(8,128)(2,1)}) custom-call(bf16[128,3072]{1,0:T(8,128)(2,1)} %get-tuple-element.131.refs_0_, bf16[128,1024]{1,0:T(8,128)(2,1)} %get-tuple-element.132.refs_1_, ...), custom_call_target="tpu_custom_call" | custom-call | tf_op jit(solution)/shard_map/attend1/pallas_call | solution.py:680
  164.7 27.6 %feed1.1 = (f32[128,1024]{1,0:T(8,128)}, f32[128,1024]{1,0:T(8,128)}, f32[128,1024]{1,0:T(8,128)}, f32[128,1024]{1,0:T(8,128)}, bf16[128,1024]{1,0:T(8,128)(2,1)...) custom-call(bf16[1024,1024]{1,0:T(8,128)(2,1)} %get-tuple-element.12, ...), custom_call_target="tpu_custom_call" | custom-call | tf_op jit(solution)/shard_map/feed1/pallas_call | solution.py:680
  192.3 1.7 multiply_reduce_fusion
  194.0 29.3 %feed_back1.1 = (f32[8,1024]{1,0:T(8,128)}, f32[128,384]{1,0:T(8,128)}, bf16[128,384]{1,0:T(8,128)(2,1)}, f32[128,1024]{1,0:T(8,128)}, bf16[128,1024]{1,0:T(8,12...) custom-call(bf16[2,384,1024]{2,1,0:T(8,128)(2,1)} %bitcast.37, ...), custom_call_target="tpu_custom_call" | custom-call | tf_op jit(solution)/shard_map/feed_back1/pallas_call | solution.py:680
  223.3 47.5 %attend_back1.1 = (bf16[128,3072]{1,0:T(8,128)(2,1)}, bf16[4,128,256]{2,1,0:T(8,128)(2,1)}, bf16[4,128,256]{2,1,0:T(8,128)(2,1)}, bf16[4,128,384]{2,1,0:T(8,128)(2,1)}, bf16[4,128,1024]{2,1,0:T(8,128)(2,1)}) custom-call(bf16[128,1024]{1,0:T(8,128)(2,1)} %get-tuple-element.143.refs_0_, bf16[128,1024]{1,0:T(8,128)(2,1)} %get-tuple-element.144.refs_1_, ...), custom_call_target="tpu_custom_call" | custom-call | tf_op jit(solution)/shard_map/attend_back1/pallas_call | solution.py:680
  270.9 33.0 %feed_back0.1 = (bf16[128,1024]{1,0:T(8,128)(2,1)}, f32[8,1024]{1,0:T(8,128)}, f32[128,384]{1,0:T(8,128)}, bf16[128,384]{1,0:T(8,128)(2,1)}, f32[128,1024]{1,0:T...) custom-call(bf16[2,384,1024]{2,1,0:T(8,128)(2,1)} %bitcast.38, ...), custom_call_target="tpu_custom_call" | custom-call | tf_op jit(solution)/shard_map/feed_back0/pallas_call | solution.py:680
  303.9 1.5 collective-permute-start
  306.7 51.4 %attend_back0.1 = (bf16[128,3072]{1,0:T(8,128)(2,1)}, bf16[4,128,256]{2,1,0:T(8,128)(2,1)}, bf16[4,128,256]{2,1,0:T(8,128)(2,1)}, bf16[4,128,384]{2,1,0:T(8,128)...) custom-call(bf16[128,1024]{1,0:T(8,128)(2,1)} %get-tuple-element.162.refs_0_, ...), custom_call_target="tpu_custom_call" | custom-call | tf_op jit(solution)/shard_map/attend_back0/pallas_call | solution.py:680
  358.1 1.0 copy-done.8
  359.1 97.5 %reduce.7 = (f32[128,256]{1,0:T(8,128)}, f32[8,1536]{1,0:T(8,128)}, f32[4,16,1536]{2,1,0:T(8,128)}, f32[96,256]{1,0:T(8,128)}, f32[1024,512]{1,0:T(8,128)}) custom-call(bf16[128,3072]{1,0:T(8,128)(2,1)} %get-tuple-element.168.refs_0_, f32[128,1024]{1,0:T(8,128)} %get-tuple-element.129.refs_3_.refs_1_, f32[128,1024]{1,0:T(8,128)} %get-tuple-element.169.refs_2_, ...), custom_call_target="tpu_custom_call" | custom-call | tf_op jit(solution)/shard_map/reduce/pallas_call | solution.py:680
  456.6 0.8 slice.105
  457.3 0.9 slice.104
  458.8 188.2 %finish.1 = (f32[8,128]{1,0:T(8,128)}, f32[128,1536]{1,0:T(8,128)}, f32[8,1024]{1,0:T(8,128)}, bf16[8,96,256]{2,1,0:T(8,128)(2,1)}, f32[128,768]{1,0:T(8,128)}, ...) custom-call(f32[1024,512]{1,0:T(8,128)} %get-tuple-element.190.refs_, ...), custom_call_target="tpu_custom_call" | custom-call | tf_op jit(solution)/shard_map/finish/pallas_call | solution.py:680
  647.0 0.9 slice_reduce_fusion.1
  648.0 1.3 fusion.24
  650.8 0.8 slice_bitcast_fusion.7
  651.6 1.0 slice_bitcast_fusion.5
  652.6 1.1 slice_bitcast_fusion.1
  653.7 1.0 slice.109
  654.7 0.8 multiply_add_fusion.4
  655.6 1.9 maximum_multiply_fusion
  657.6 2.9 divide_subtract_fusion.1
  660.5 1.5 divide_subtract_fusion.4
  662.0 0.9 divide_subtract_fusion.2
  662.8 1.1 multiply_add_fusion.2
  664.1 1.8 divide_subtract_fusion
  665.8 0.7 divide_subtract_fusion.3
  666.6 0.7 copy.89
  667.3 1.1 copy.90
  669.1 0.8 copy.92
  669.9 0.8 copy.93
  670.7 1.3 copy.94
  672.1 0.8 copy.95
  673.4 1.3 copy.96
  (76 shorter events, 6.3 us)
Async XLA Ops:
  303.9 54.2 %collective-permute-start = (bf16[1024,512]{1,0:T(8,128)(2,1)}, bf16[1024,512]{1,0:T(8,128)(2,1)S(1)}, u32[]{:S(2)}, u32[]{:S(2)}) collective-permute-start(bf16[1024,512]{1,0:T(8,128)(2,1)} %get-tuple-element.174), channel_id=1, source_target_pairs={{0,4},{4,0},{8,12},{12,8},{16,20},{20,16},{24,28},{28,24},{1,5},{5... | collective-permute-start | bytes 3145736 | tf_op jit(solution)/shard_map/ppermute | solution.py:2146
  358.1 1.0 copy-start.8
  647.0 7.7 %copy-start.2 = (f32[128,768]{1,0:T(8,128)S(1)}, f32[128,768]{1,0:T(8,128)}, u32[]{:S(2)}) copy-start(f32[128,768]{1,0:T(8,128)} %refs_8_.3) | copy-start | bytes 1179652
  647.0 10.5 %copy-start.3 = (f32[2,276,256]{2,0,1:T(2,128)S(1)}, f32[2,276,256]{2,0,1:T(2,128)}, u32[]{:S(2)}) copy-start(f32[2,276,256]{2,0,1:T(2,128)} %param.52) | copy-start | bytes 1695748
  647.0 10.5 %copy-start.13 = (f32[2,276,256]{2,0,1:T(2,128)S(1)}, f32[2,276,256]{2,0,1:T(2,128)}, u32[]{:S(2)}) copy-start(f32[2,276,256]{2,0,1:T(2,128)} %param.53) | copy-start | bytes 1695748
  647.0 10.5 %copy-start.14 = (f32[2,276,256]{2,0,1:T(2,128)S(1)}, f32[2,276,256]{2,0,1:T(2,128)}, u32[]{:S(2)}) copy-start(f32[2,276,256]{2,0,1:T(2,128)} %param.54) | copy-start | bytes 1695748
  654.7 5.7 copy-start.24
  654.7 5.7 copy-start.26
  654.7 5.7 copy-start.27
  655.6 6.4 copy-start.7
  655.6 6.4 copy-start.15
  655.6 6.4 copy-start.16
  655.6 6.4 copy-start.21
  655.6 6.4 copy-start.22
  657.5 5.3 copy-start
  657.5 5.3 copy-start.1
  660.4 3.6 copy-start.9
  660.4 3.6 copy-start.10
  660.4 3.6 copy-start.11
  660.4 3.6 copy-start.12
  664.0 1.8 copy-start.25
  664.0 1.8 copy-start.28
  664.0 1.8 copy-start.29
  664.0 2.5 copy-start.20
  664.0 3.3 copy-start.6
  665.8 2.6 copy-start.23
  666.6 2.6 copy-start.19
  667.3 2.6 copy-start.18
  667.3 3.4 copy-start.5
  670.7 1.4 copy-start.17
  670.7 2.7 copy-start.4

commit v9 on v8

--- a/solution.py
+++ b/solution.py
@@ -930,7 +930,9 @@
 
 
 CHAIN_CHUNKS = 8
+DOWN_CHUNKS = 4
 KERNEL_VMEM = 62 * 2**20
+UPDATE_BLOCKS = 4
 GRAM_COLS = 256
 
 
@@ -1659,7 +1661,7 @@
         return [[item for item, _ in loaded[name]] for name in names]
 
     up_low, down_low = [moves.scratch((block_rows, cols), LOW) for cols in group_cols[1:3]]
-    group_target = moves.scratch((MATRICES - 1, block_rows, most_cols), LOW)
+    group_target, up_target = [moves.scratch((MATRICES - 1, block_rows, most_cols), LOW) for _ in range(2)]
 
     def round_up_grad(ref):
         def action(at):
@@ -1674,7 +1676,7 @@
     for number in (up_load, *[number for _, number in up_others]):
         moves.wait_local(number)
     moves.task(round_up_grad)
-    up_moves = to_group(up_low, group_target, 1)
+    up_moves = to_group(up_low, up_target, 1)
 
     embed_low = moves.scratch((rows, width), LOW)
     table = moves.scratch((8, 6 * width), f32)
@@ -1770,7 +1772,31 @@
     moves.wait_local(down_load)
     await_all(down_moves)
     add_member(down_full, down_arriving, down_full, down_low, group_cols[2])
-    down_group_moves = to_group(down_low, group_target, 2)
+
+    hops = [(0, 1, down_low, 0), (1, 2, down_low, 1), (3, 2, down_low, 2)]
+    down_chunk = block_rows // DOWN_CHUNKS
+    down_hops = []
+    for sender, receiver, source, place in hops:
+        numbers = []
+        for piece in range(DOWN_CHUNKS if place < 2 else 1):
+            at = pl.ds(piece * down_chunk, down_chunk) if place < 2 else slice(None)
+            shift = (receiver - sender) % MATRICES
+            numbers.append(
+                moves.move(
+                    (PATCHES, seq_count, shift),
+                    functools.partial(group_peer, members, shift),
+                    source,
+                    lambda at=at: (at,),
+                    group_target,
+                    lambda at=at, place=place: (place, at),
+                    sends=lambda sender=sender: group() == sender,
+                    takes=lambda receiver=receiver: group() == receiver,
+                    later=True,
+                )
+            )
+        down_hops.append(numbers)
+    for number in (*down_hops[0], *down_hops[2]):
+        moves.start(number)
     out_mine, out_mine_low = moves.scratch((width, out_cols), f32), moves.scratch((width, out_cols), LOW)
     out_target = moves.scratch((MATRICES - 1, block_rows, out_cols), LOW)
     await_all(out_moves)
@@ -1801,6 +1827,20 @@
     moves.wait_local(ada_load)
     moves.task(close)
     to_others(SHARDS, tail, lambda there: (slice(None), slice(None)), tail_all)
+
+    for piece, (number, following) in enumerate(zip(*down_hops[:2])):
+        at = pl.ds(piece * down_chunk, down_chunk)
+
+        def add_down(ref, at=at):
+            def sum_up():
+                value = ref(down_full)[at, :] + ref(group_target)[0, at, :].astype(f32)
+                ref(down_low)[at, :] = value.astype(LOW)
+
+            pl.when(group() == 1)(sum_up)
+
+        moves.wait_for(number)
+        moves.task(add_down)
+        moves.start(following)
 
     def has_source():
         return group() < MATRICES - 1
@@ -1851,13 +1891,12 @@
 
     grad_group = moves.output((block_rows, most_cols), f32, pltpu.VMEM)
 
-    def put(full, target, cols):
+    def put(full, target, places, cols):
         def action(ref):
             def add(at):
                 value = ref(full)[at, :]
-                if target is not None:
-                    for shift in range(MATRICES - 1):
-                        value = value + ref(target)[shift, at, pl.ds(0, cols)].astype(f32)
+                for place in places:
+                    value = value + ref(target)[place, at, pl.ds(0, cols)].astype(f32)
                 ref(grad_group)[at, pl.ds(0, cols)] = value
                 if cols < most_cols:
                     ref(grad_group)[at, pl.ds(cols, most_cols - cols)] = jnp.zeros((GRAM_COLS, most_cols - cols), f32)
@@ -1867,13 +1906,57 @@
         return action
 
     def settle(ref):
-        entries = ((chain, None), (up_full, group_target), (down_full, group_target), (out_mine, out_target))
-        for which, (full, target) in enumerate(entries):
-            pl.when(group() == which)(functools.partial(put(full, target, group_cols[which]), ref))
-
-    await_all((*up_moves, *down_group_moves, *out_group_moves))
+        every = range(MATRICES - 1)
+        entries = ((chain, None, ()), (up_full, up_target, every), (down_full, group_target, (1, 2)), (out_mine, out_target, every))
+        for which, (full, target, places) in enumerate(entries):
+            pl.when(group() == which)(functools.partial(put(full, target, places, group_cols[which]), ref))
+
+    await_all((*up_moves, *down_hops[1], *down_hops[2], *out_group_moves))
     moves.task(settle)
     return moves.run()
+
+
+def update_kernel(members, sums_ref, *refs):
+    row = sums_ref[pl.ds(0, 1), :]
+    lane = lax.broadcasted_iota(jnp.int32, (1, LANES), 1)
+    squares = jnp.sum(jnp.where(lane == 0, row, 0.0), 1, keepdims=True)
+    clip = jnp.minimum(1.0, CLIP_LIMIT / (jnp.sqrt(squares) + 1e-06))
+    adam_in, (rows_ref, *momenta), out = refs[:8], refs[8 : 9 + MATRICES], refs[9 + MATRICES :]
+    for number, rate in enumerate((RATE_ADAM, RATE_TABLE)):
+        weight, first, second, grad = [item[...] for item in adam_in[4 * number : 4 * number + 4]]
+        for place, value in enumerate(adam_update(weight, first, second, clip * grad, rate)):
+            out[3 * number + place][...] = value
+    for which, old in enumerate(momenta):
+        cols = old.shape[1] // members
+        for part in range(members):
+            at = (slice(None), pl.ds(part * cols, cols))
+            grad = rows_ref[which * members + part, :, pl.ds(0, cols)].astype(jnp.float32)
+            out[6 + which][at] = MOMENTUM * old[at] + clip * grad
+
+
+def update_all(members, sums, ada, pos, grad_rows, momenta):
+    rows = ada[0].shape[0]
+    block = rows // UPDATE_BLOCKS
+
+    def spec(item):
+        return pl.BlockSpec((block, item.shape[1]), lambda step: (step, 0))
+
+    arrays = [*ada, *pos]
+    results = [*ada[:3], *pos[:3], *momenta]
+    return pl.pallas_call(
+        functools.partial(update_kernel, members),
+        out_shape=[jax.ShapeDtypeStruct(item.shape, jnp.float32) for item in results],
+        grid=(UPDATE_BLOCKS,),
+        in_specs=[
+            pl.BlockSpec(sums.shape, lambda step: (0, 0)),
+            *[spec(item) for item in arrays],
+            pl.BlockSpec((grad_rows.shape[0], block, grad_rows.shape[2]), lambda step: (0, step, 0)),
+            *[spec(item) for item in momenta],
+        ],
+        out_specs=[spec(item) for item in results],
+        compiler_params=pltpu.CompilerParams(vmem_limit_bytes=KERNEL_VMEM),
+        name="update",
+    )(sums, *arrays, grad_rows, *momenta)
 
 
 def newton_schulz(source, gram, poly, once, gram_low, poly_low, once_low, block, block_next):
@@ -2495,73 +2578,107 @@
 
     rows = block_rows // seq_count
 
-    def row_place(back_group):
-        who = lax.axis_index(PATCHES) - back_group * members
-        return (pl.ds(pl.multiple_of(who * rows, rows), rows),)
+    def row_place(back_group, back_member, start, size):
+        seq_me = lax.axis_index(PATCHES)
+        who = (seq_me // members - back_group) * members
+        who = who + lax.rem(lax.rem(seq_me, members) + members - back_member, members)
+        return (pl.ds(pl.multiple_of(who * rows + start, 16), size),)
 
     def has_group(offset):
         place = lax.axis_index(PATCHES) // members + offset
         return jnp.logical_and(place >= 0, place < MATRICES)
 
-    def member_copies(source, source_at, target, target_at, after, there):
+    def to_members(item_from, from_at, item_to, place, after, there):
+        numbers = []
         for shift in range(1, members):
-            moves.move(
-                (PATCHES, members, shift),
-                functools.partial(member_peer, members, shift),
-                source,
-                source_at,
-                target,
-                target_at,
-                after,
-                there,
-                there,
-                later=True,
+            numbers.append(
+                moves.move(
+                    (PATCHES, members, shift),
+                    functools.partial(member_peer, members, shift),
+                    item_from,
+                    from_at,
+                    item_to,
+                    place,
+                    after,
+                    there,
+                    there,
+                    later=True,
+                )
             )
             if not after:
-                moves.start(len(moves.moves) - 1)
-
-    places = []
-    for item_from in fresh_low:
-        item_to = moves.output((rows * seq_count, moves.shape(item_from)[1]), LOW)
-        own = functools.partial(row_place, 0)
-        moves.start_local(moves.keep(item_from, None, item_to, own, True))
-        places.append((item_from, item_to, {}))
-
-    def along_line(distance, way, source, target, numbers):
+                moves.start(numbers[-1])
+        return numbers
+
+    def along_line(distance, way, item_from, from_at, item_to, back_member, start, size, after):
         both = lambda: jnp.logical_and(has_group(way), has_group(-distance * way))
-        place = functools.partial(row_place, distance * way)
-        numbers[way] = moves.move(
+        number = moves.move(
             (PATCHES, seq_count, way),
             functools.partial(group_peer, members, (MATRICES + way) % MATRICES),
-            target if distance else source,
-            place if distance else None,
-            target,
-            place,
-            (numbers[way],) if distance else (),
+            item_from,
+            from_at,
+            item_to,
+            functools.partial(row_place, distance * way, back_member, start, size),
+            after,
             both,
             functools.partial(has_group, -(distance + 1) * way),
             later=True,
         )
-        if not distance:
-            moves.start(numbers[way])
-
-    for item_from, item_to, numbers in places:
+        if not after:
+            moves.start(number)
+        return number
+
+    items = []
+    for which, item_from in enumerate(fresh_low):
+        item_to = moves.output((rows * seq_count, moves.shape(item_from)[1]), LOW)
+        place = functools.partial(row_place, 0, 0, 0, rows)
+        moves.start_local(moves.keep(item_from, None, item_to, place, True))
+        if which:
+            items.append((item_from, item_to, 0, rows, False))
+        else:
+            items.append((item_from, item_to, rows // 2, rows // 2, True))
+            items.append((item_from, item_to, 0, rows // 2, False))
+    lines = []
+    for item_from, item_to, start, size, members_first in items:
+        from_at = lambda start=start, size=size: (pl.ds(start, size),)
+        place = functools.partial(row_place, 0, 0, start, size)
+        if members_first:
+            crossing = to_members(item_from, from_at, item_to, place, (), None)
         for way in (1, -1):
-            along_line(0, way, item_from, item_to, numbers)
-    for item_from, item_to, numbers in places:
-        member_copies(item_from, None, item_to, own, (), None)
+            number = along_line(0, way, item_from, from_at, item_to, 0, start, size, ())
+            lines.append([number, way, item_to, 0, start, size, members_first])
+    for item_from, item_to, start, size, members_first in items:
+        if not members_first:
+            from_at = lambda start=start, size=size: (pl.ds(start, size),)
+            to_members(item_from, from_at, item_to, functools.partial(row_place, 0, 0, start, size), (), None)
+    for item_from, item_to, start, size, members_first in items:
+        if members_first:
+            for back_member, number in enumerate(crossing, 1):
+                place = functools.partial(row_place, 0, back_member, start, size)
+                for way in (1, -1):
+                    following = along_line(0, way, item_to, place, item_to, back_member, start, size, (number,))
+                    lines.append([following, way, item_to, back_member, start, size, True])
     for distance in range(1, MATRICES):
-        for item_from, item_to, numbers in places:
-            for way in (1, -1):
-                number = numbers[way]
-                if distance < MATRICES - 1:
-                    along_line(distance, way, item_from, item_to, numbers)
-                place = functools.partial(row_place, distance * way)
-                member_copies(
-                    item_to, place, item_to, place, (number,), functools.partial(has_group, -distance * way)
+        for line in lines:
+            number, way, item_to, back_member, start, size, members_first = line
+            place = functools.partial(row_place, distance * way, back_member, start, size)
+            if distance < MATRICES - 1:
+                line[0] = along_line(
+                    distance, way, item_to, place, item_to, back_member, start, size, (number,)
                 )
+            if not members_first:
+                there = functools.partial(has_group, -distance * way)
+                to_members(item_to, place, item_to, place, (number,), there)
     sums, grad_ada, grad_table_all, io_slices, *rest = moves.run()
     fresh, grad_rows, copies = rest[:MATRICES], rest[MATRICES], rest[MATRICES + 1 :]
+    updated = update_all(
+        members,
+        sums,
+        (ada_master, ada_first, ada_second, grad_ada),
+        (pos_table, pos_first, pos_second, grad_pos),
+        grad_rows,
+        momenta,
+    )
+    ada_res, pos_res, moments = updated[:3], updated[3:6], updated[6:]
     sums = sums[0]
     grad_norm = jnp.sqrt(sums[0])
     loss_total = sums[1]
@@ -2570,22 +2687,12 @@
     size_squares = MOMENTUM * MOMENTUM * terms[:, 0] + 2.0 * MOMENTUM * clip * terms[:, 1] + clip * clip * terms[:, 2]
     sizes = jnp.sqrt(jnp.maximum(size_squares, 0.0))
     moment_sizes = jnp.stack([sizes[which] for which in (0, 3, 1, 2)]) / CLIP_LIMIT
-    moments = [
-        MOMENTUM * old
-        + clip
-        * jnp.concatenate(
-            [grad_rows[which * members + part, :, : group_cols[which]] for part in range(members)], -1
-        ).astype(f32)
-        for which, old in enumerate(momenta)
-    ]
     grad_table = lax.dynamic_slice_in_dim(grad_table_all[:table_rows], shard * table_cols, table_cols, 1)
     grad_bias_all = jnp.concatenate([tail_all[:, 8].reshape(-1), tail_all[:, 9, :table_cols].reshape(-1)])
     grad_bias = lax.dynamic_slice_in_dim(grad_bias_all, shard * biases.shape[0], biases.shape[0])
     io_grad = io_slices.reshape(2, padded, io_cols)[:, :values_count].astype(f32)
-    ada_res = adam_update(ada_master, ada_first, ada_second, clip * grad_ada, RATE_ADAM)
     io_res = adam_update(io_proj, io_first, io_second, clip * io_grad, RATE_ADAM)
     cond_res = adam_update(cond_table, cond_first, cond_second, clip * grad_table, RATE_TABLE)
-    pos_res = adam_update(pos_table, pos_first, pos_second, clip * grad_pos, RATE_TABLE)
     bias_res = adam_update(biases, bias_first, bias_second, clip * grad_bias, RATE_ADAM)
     matrices = []
     for which in (0, 3, 1, 2):

time: 690 us -> 684 us (level)
  no operation moved by 1% of the time
where the time goes in v9:
time: 684 us; the launch traced here: 674 us
  Pallas kernels  627 us (92%)
  local copies, waits for them, and re-layouts  24.2 us (4%)
  other arithmetic  15.6 us (2%)
    pallas_call x11, Pallas kernels, run(): pl.pallas_call(self.kernel, out_shape=self.outputs, in_specs=self.operand...  621 us
  transfers between devices with their start and end apart: 1, of which 0 were waited for; matrix products, arithmetic and copies ran while one was open for 0% of the time, Pallas kernels for 8%

profile of v9, /device:TPU:0, one launch (start us, length us, event | category | flops | bytes accessed | tf_op | source)
XLA Modules:
  0.0 674.0 jit_solution(13322892343798845414)
XLA Ops:
  0.7 0.6 fusion.15
  2.0 0.7 convert_reduce_fusion
  2.7 1.2 dynamic_slice.12
  4.0 0.7 broadcast_in_dim.12
  5.5 1.3 broadcast_in_dim.29.refs_4_
  6.8 1.5 convert_element_type.41.refs_5_
  8.3 1.0 copy.70
  9.3 0.7 pad_convert_fusion.refs_2_.refs_4_
  10.0 1.0 copy.72
  11.0 1.3 convert_element_type.42
  12.3 0.8 pad.18.clone
  13.1 0.7 broadcast_in_dim.27.refs_0_.refs_7_
  13.7 0.7 broadcast_in_dim.28.refs_1_
  14.4 49.4 %begin.1 = (f32[2,8,1024]{2,1,0:T(8,128)}, f32[8,1024]{1,0:T(8,128)}, bf16[8,1024]{1,0:T(8,128)(2,1)}, f32[128,1024]{1,0:T(8,128)}, bf16[128,1024]{1,0:T(8,128)(...) custom-call(s32[8,128]{1,0:T(8,128)} %broadcast_in_dim.27.refs_0_.re, ...), custom_call_target="tpu_custom_call" | custom-call | tf_op jit(solution)/shard_map/begin/pallas_call | solution.py:680
  63.8 1.4 slice_bitcast_fusion
  65.2 1.2 fusion.16
  67.2 32.9 %attend0.1 = (bf16[3,1024,128]{2,1,0:T(8,128)(2,1)}, bf16[128,1024]{1,0:T(8,128)(2,1)}, bf16[4,128,1024]{2,1,0:T(8,128)(2,1)}, bf16[4,128,384]{2,1,0:T(8,128)(2,1)}) custom-call(bf16[128,3072]{1,0:T(8,128)(2,1)} %get-tuple-element.135.refs_0_, bf16[128,1024]{1,0:T(8,128)(2,1)} %get-tuple-element.136.refs_1_, bf16[128,384]{1,0:T(8,128)(2,1)} %get-tuple-element.137.refs_2_), custom_call_target="tpu_custom_call" | custom-call | tf_op jit(solution)/shard_map/attend0/pallas_call | solution.py:680
  100.1 28.7 %feed0.1 = (f32[128,1024]{1,0:T(8,128)}, f32[128,1024]{1,0:T(8,128)}, f32[128,1024]{1,0:T(8,128)}, f32[128,1024]{1,0:T(8,128)}, bf16[128,1024]{1,0:T(8,128)(2,1)...) custom-call(bf16[1024,1024]{1,0:T(8,128)(2,1)} %get-tuple-element.13, ...), custom_call_target="tpu_custom_call" | custom-call | tf_op jit(solution)/shard_map/feed0/pallas_call | solution.py:680
  128.8 35.9 %attend1.1 = (bf16[3,1024,128]{2,1,0:T(8,128)(2,1)}, bf16[128,1024]{1,0:T(8,128)(2,1)}, bf16[4,128,1024]{2,1,0:T(8,128)(2,1)}, bf16[4,128,384]{2,1,0:T(8,128)(2,1)}, bf16[4,128,1024]{2,1,0:T(8,128)(2,1)}) custom-call(bf16[128,3072]{1,0:T(8,128)(2,1)} %get-tuple-element.141.refs_0_, bf16[128,1024]{1,0:T(8,128)(2,1)} %get-tuple-element.142.refs_1_, ...), custom_call_target="tpu_custom_call" | custom-call | tf_op jit(solution)/shard_map/attend1/pallas_call | solution.py:680
  164.7 27.7 %feed1.1 = (f32[128,1024]{1,0:T(8,128)}, f32[128,1024]{1,0:T(8,128)}, f32[128,1024]{1,0:T(8,128)}, f32[128,1024]{1,0:T(8,128)}, bf16[128,1024]{1,0:T(8,128)(2,1)...) custom-call(bf16[1024,1024]{1,0:T(8,128)(2,1)} %get-tuple-element.13, ...), custom_call_target="tpu_custom_call" | custom-call | tf_op jit(solution)/shard_map/feed1/pallas_call | solution.py:680
  192.4 1.7 multiply_reduce_fusion
  194.1 29.2 %feed_back1.1 = (f32[8,1024]{1,0:T(8,128)}, f32[128,384]{1,0:T(8,128)}, bf16[128,384]{1,0:T(8,128)(2,1)}, f32[128,1024]{1,0:T(8,128)}, bf16[128,1024]{1,0:T(8,12...) custom-call(bf16[2,384,1024]{2,1,0:T(8,128)(2,1)} %bitcast.21, ...), custom_call_target="tpu_custom_call" | custom-call | tf_op jit(solution)/shard_map/feed_back1/pallas_call | solution.py:680
  223.4 47.5 %attend_back1.1 = (bf16[128,3072]{1,0:T(8,128)(2,1)}, bf16[4,128,256]{2,1,0:T(8,128)(2,1)}, bf16[4,128,256]{2,1,0:T(8,128)(2,1)}, bf16[4,128,384]{2,1,0:T(8,128)(2,1)}, bf16[4,128,1024]{2,1,0:T(8,128)(2,1)}) custom-call(bf16[128,1024]{1,0:T(8,128)(2,1)} %get-tuple-element.153.refs_0_, bf16[128,1024]{1,0:T(8,128)(2,1)} %get-tuple-element.154.refs_1_, ...), custom_call_target="tpu_custom_call" | custom-call | tf_op jit(solution)/shard_map/attend_back1/pallas_call | solution.py:680
  270.9 33.1 %feed_back0.1 = (bf16[128,1024]{1,0:T(8,128)(2,1)}, f32[8,1024]{1,0:T(8,128)}, f32[128,384]{1,0:T(8,128)}, bf16[128,384]{1,0:T(8,128)(2,1)}, f32[128,1024]{1,0:T...) custom-call(bf16[2,384,1024]{2,1,0:T(8,128)(2,1)} %bitcast.22, ...), custom_call_target="tpu_custom_call" | custom-call | tf_op jit(solution)/shard_map/feed_back0/pallas_call | solution.py:680
  304.1 1.5 collective-permute-start
  305.5 0.7 multiply_reduce_fusion.1
  306.9 51.3 %attend_back0.1 = (bf16[128,3072]{1,0:T(8,128)(2,1)}, bf16[4,128,256]{2,1,0:T(8,128)(2,1)}, bf16[4,128,256]{2,1,0:T(8,128)(2,1)}, bf16[4,128,384]{2,1,0:T(8,128)...) custom-call(bf16[128,1024]{1,0:T(8,128)(2,1)} %get-tuple-element.172.refs_0_, ...), custom_call_target="tpu_custom_call" | custom-call | tf_op jit(solution)/shard_map/attend_back0/pallas_call | solution.py:680
  358.2 1.0 copy-done.4
  359.2 97.6 %reduce.7 = (f32[128,256]{1,0:T(8,128)}, f32[8,1536]{1,0:T(8,128)}, f32[4,16,1536]{2,1,0:T(8,128)}, f32[96,256]{1,0:T(8,128)}, f32[1024,512]{1,0:T(8,128)}) custom-call(bf16[128,3072]{1,0:T(8,128)(2,1)} %get-tuple-element.178.refs_0_, f32[128,1024]{1,0:T(8,128)} %get-tuple-element.139.refs_3_.refs_1_, f32[128,1024]{1,0:T(8,128)} %get-tuple-element.179.refs_2_, ...), custom_call_target="tpu_custom_call" | custom-call | tf_op jit(solution)/shard_map/reduce/pallas_call | solution.py:680
  456.8 0.8 slice.73
  457.6 0.9 slice.72
  459.0 187.8 %finish.1 = (f32[8,128]{1,0:T(8,128)}, f32[128,1536]{1,0:T(8,128)}, f32[8,1024]{1,0:T(8,128)}, bf16[8,96,256]{2,1,0:T(8,128)(2,1)}, f32[128,768]{1,0:T(8,128)}, ...) custom-call(f32[1024,512]{1,0:T(8,128)} %get-tuple-element.200.refs_, ...), custom_call_target="tpu_custom_call" | custom-call | tf_op jit(solution)/shard_map/finish/pallas_call | solution.py:680
  646.9 0.8 slice_reduce_fusion.1
  647.7 1.3 fusion.20
  650.6 1.0 slice.77
  651.6 1.9 maximum_multiply_fusion
  653.5 2.9 divide_subtract_fusion
  656.4 1.3 divide_subtract_fusion.2
  657.8 0.7 divide_subtract_fusion.1
  658.5 5.7 update.1
  664.3 0.7 copy.89
  665.0 1.1 copy.90
  666.2 0.7 copy.91
  666.8 0.8 copy.92
  667.6 0.8 copy.93
  668.4 1.3 copy.94
  669.8 0.8 copy.95
  671.1 1.3 copy.96
  (46 shorter events, 2.2 us)
Async XLA Ops:
  304.1 54.2 %collective-permute-start = (bf16[1024,512]{1,0:T(8,128)(2,1)}, bf16[1024,512]{1,0:T(8,128)(2,1)S(1)}, u32[]{:S(2)}, u32[]{:S(2)}) collective-permute-start(bf16[1024,512]{1,0:T(8,128)(2,1)} %get-tuple-element.184), channel_id=1, source_target_pairs={{0,4},{4,0},{8,12},{12,8},{16,20},{20,16},{24,28},{28,24},{1,5},{5... | collective-permute-start | bytes 3145736 | tf_op jit(solution)/shard_map/ppermute | solution.py:2229
  358.2 1.0 copy-start.4
  459.0 194.5 %copy-start = (f32[2,276,256]{2,0,1:T(2,128)S(1)}, f32[2,276,256]{2,0,1:T(2,128)}, u32[]{:S(2)}) copy-start(f32[2,276,256]{2,0,1:T(2,128)} %param.52) | copy-start | bytes 1695748
  459.0 194.5 %copy-start.5 = (f32[2,276,256]{2,0,1:T(2,128)S(1)}, f32[2,276,256]{2,0,1:T(2,128)}, u32[]{:S(2)}) copy-start(f32[2,276,256]{2,0,1:T(2,128)} %param.53) | copy-start | bytes 1695748
  459.0 194.5 %copy-start.6 = (f32[2,276,256]{2,0,1:T(2,128)S(1)}, f32[2,276,256]{2,0,1:T(2,128)}, u32[]{:S(2)}) copy-start(f32[2,276,256]{2,0,1:T(2,128)} %param.54) | copy-start | bytes 1695748
  650.5 5.9 copy-start.12
  650.5 5.9 copy-start.14
  650.5 5.9 copy-start.15
  650.5 7.2 %copy-start.13 = (f32[1792]{0:T(1024)S(1)}, f32[1792]{0:T(1024)}, u32[]{:S(2)}) copy-start(f32[1792]{0:T(1024)} %param.61) | copy-start | bytes 21508
  650.6 7.2 %copy-start.16 = (f32[1792]{0:T(1024)S(1)}, f32[1792]{0:T(1024)}, u32[]{:S(2)}) copy-start(f32[1792]{0:T(1024)} %param.62) | copy-start | bytes 21508
  650.6 7.2 %copy-start.17 = (f32[1792]{0:T(1024)S(1)}, f32[1792]{0:T(1024)}, u32[]{:S(2)}) copy-start(f32[1792]{0:T(1024)} %param.63) | copy-start | bytes 21508
  658.5 5.8 copy-start.10
  658.5 6.5 copy-start.3
  664.2 1.9 copy-start.11
  664.3 2.6 copy-start.9
  665.0 2.6 copy-start.8
  665.0 3.4 copy-start.2
  668.4 1.4 copy-start.7
  668.4 2.7 copy-start.1

commit v10 on v9

--- a/solution.py
+++ b/solution.py
@@ -580,6 +580,11 @@
         target = self.scratch(array.shape, array.dtype)
         return target, self.keep(self.operand(array), None, target, None)
 
+    def prefetch(self, array):
+        target, number = self.load(array)
+        self.steps.insert(0, (self.await_local, number))
+        return target
+
     def save(self, source, shape, dtype):
         number = self.keep(source, None, self.output(shape, dtype), None, True)
         return number
@@ -642,6 +647,13 @@
         self.refs = (refs[: sizes[0]], refs[sizes[0] : sizes[0] + sizes[1]], refs[sizes[0] + sizes[1] : sum(sizes)])
         local_sem, send_sem, recv_sem = refs[sum(sizes) :]
         self.arrived, self.kept = set(), set()
+        self.local = [
+            pltpu.make_async_copy(self.view(source, source_at), self.view(target, target_at), local_sem.at[number])
+            for number, (source, source_at, target, target_at, _) in enumerate(self.locals)
+        ]
+        for copy, entry in zip(self.local, self.locals):
+            if not entry[4]:
+                copy.start()
         devices = {key: peer() for key, peer in self.peers.items()}
         barrier = pltpu.get_barrier_semaphore()
         for device in devices.values():
@@ -661,13 +673,6 @@
             )
             if not later:
                 self.start_move(number)
-        self.local = [
-            pltpu.make_async_copy(self.view(source, source_at), self.view(target, target_at), local_sem.at[number])
-            for number, (source, source_at, target, target_at, _) in enumerate(self.locals)
-        ]
-        for copy, entry in zip(self.local, self.locals):
-            if not entry[4]:
-                copy.start()
         for action, number in self.steps:
             action(number)
         for number in range(len(self.locals)):
@@ -1054,7 +1059,7 @@
     table = moves.scratch((table_rows, width), f32)
     bias = moves.scratch((1, biases.shape[1] * shards), f32)
     pos_all = moves.scratch((rows, width), LOW)
-    id_rows, active, state = [moves.operand(item, pltpu.VMEM) for item in (id_rows, active, state)]
+    id_rows, active, state = [moves.prefetch(item) for item in (id_rows, active, state)]
     small = [moves.gather_columns(SHARDS, cond_table, table), moves.gather_columns(SHARDS, biases, bias)]
     pos_moves, pos_local = moves.gather_columns(SHARDS, pos, pos_all)
     ada_weights, ada_load = moves.load(ada)
@@ -1269,7 +1274,7 @@
     hidden_count = w_up.shape[1]
     shards = lax.axis_size(SHARDS)
     moves = Moves(f"feed{step}", ids, KERNEL_VMEM)
-    vmem = functools.partial(moves.operand, space=pltpu.VMEM)
+    vmem = moves.prefetch
     out_weights, out_load = moves.load(w_out)
     mods, mixed, embedded, state = vmem(mods), vmem(mixed), vmem(embedded), vmem(state)
     up_weights, up_load = moves.load(w_up)
@@ -1375,7 +1380,7 @@
     hidden_count = w_up.shape[1]
     shards = lax.axis_size(SHARDS)
     moves = Moves(f"feed_back{step}", ids, KERNEL_VMEM)
-    vmem = functools.partial(moves.operand, space=pltpu.VMEM)
+    vmem = moves.prefetch
     io_weights, io_load = moves.load(io_all)
     if later is not None:
         qkv_weights, qkv_load = moves.load(w_qkv)
@@ -1518,7 +1523,8 @@
     part, ada_cols = width // shards, ada.shape[1]
     up_mine, up_arrived, down_mine, down_leaving = mlp
     moves = Moves("reduce", ids, KERNEL_VMEM)
-    vmem = functools.partial(moves.operand, space=pltpu.VMEM)
+    vmem = moves.prefetch
+    qkv_source = moves.operand(qkv_grad)
     qkv_grad, embedded, grad_attn, mods = vmem(qkv_grad), vmem(embedded), vmem(grad_attn), vmem(mods)
     rows_late, rows_early = vmem(rows_late), vmem(rows_early)
 
@@ -1628,7 +1634,7 @@
     qkv_all = moves.scratch((shards, rows, 3 * part), LOW)
     qkv_moves = moves.along(
         SHARDS,
-        qkv_grad,
+        qkv_source,
         qkv_all,
         [(lambda receiver: (slice(None), columns(receiver, 3 * part)), lambda sender: (sender,))],
     )
@@ -1828,7 +1834,8 @@
     moves.task(close)
     to_others(SHARDS, tail, lambda there: (slice(None), slice(None)), tail_all)
 
-    for piece, (number, following) in enumerate(zip(*down_hops[:2])):
+    def hand_down(piece):
+        number, following = down_hops[0][piece], down_hops[1][piece]
         at = pl.ds(piece * down_chunk, down_chunk)
 
         def add_down(ref, at=at):
@@ -1877,6 +1884,9 @@
         moves.wait_for(number)
         moves.task(add)
         moves.start(number)
+        turns = CHAIN_CHUNKS // DOWN_CHUNKS
+        if number_of % turns == turns - 1:
+            hand_down(number_of // turns)
 
     io_slice = moves.output((io_rows, part), f32, pltpu.VMEM)
 
@@ -2132,9 +2142,7 @@
 
     half_rows = local // ROLL
 
-    counts = jnp.sum((intervals[:, None] == jnp.arange(NI, dtype=jnp.int32)[None]).astype(f32), 0)
-    my_id = lax.dynamic_slice_in_dim(intervals, shard, 1)
-    id_count = jnp.sum((my_id == jnp.arange(NI, dtype=jnp.int32)).astype(f32) * counts)
+    id_count = jnp.sum((intervals == lax.dynamic_slice_in_dim(intervals, shard, 1)).astype(f32))
     weight = 1.0 / (NI * local * seq_count * values_count * id_count)
     kept = []
     gathered = {}
@@ -2243,7 +2251,7 @@
             moves.exchange_columns(SHARDS, embed_grad)
             names += ["qkv", "embed"]
         add_attention_back(
-            moves, moves.operand(qkv, pltpu.VMEM), grads_in, result, arrivals, local, members, waiting
+            moves, moves.prefetch(qkv), grads_in, result, arrivals, local, members, waiting
         )
         qkv_grad, *others = moves.run()
         for name, item in zip(names, others):
@@ -2268,7 +2276,7 @@
     )
     io_cols = io_slice.shape[1]
     moves = Moves("finish", ids, KERNEL_VMEM)
-    vmem = functools.partial(moves.operand, space=pltpu.VMEM)
+    vmem = moves.prefetch
     vmem_out = functools.partial(moves.output, space=pltpu.VMEM)
     full, low = (block_rows, block_rows), (block_rows, most_cols)
     block_part = block_rows // seq_count

time: 684 us -> 673 us (0.984)
  Pallas kernels: 627 us -> 614 us
    pallas_call x11, Pallas kernels: 621 us -> 608 us  [run(): pl.pallas_call(self.kernel, out_shape=self.outputs, in_specs=self.operand...]
where the time goes in v10:
time: 673 us; the launch traced here: 663 us
  Pallas kernels  614 us (91%)
  local copies, waits for them, and re-layouts  24.2 us (4%)
  other arithmetic  15.5 us (2%)
    pallas_call x11, Pallas kernels, run(): pl.pallas_call(self.kernel, out_shape=self.outputs, in_specs=self.operand...  608 us
  transfers between devices with their start and end apart: 1, of which 0 were waited for; matrix products, arithmetic and copies ran while one was open for 0% of the time, Pallas kernels for 8%

profile of v10, /device:TPU:0, one launch (start us, length us, event | category | flops | bytes accessed | tf_op | source)
XLA Modules:
  0.0 662.6 jit_solution(2432979962510253437)
XLA Ops:
  0.7 0.6 fusion.15
  2.0 1.2 dynamic_slice.12
  3.2 1.9 fusion.16
  5.1 0.7 broadcast_in_dim.23
  6.6 1.3 broadcast_in_dim.27.refs_4_
  7.9 1.5 convert_element_type.40.refs_5_
  9.5 1.0 copy.66
  10.5 0.7 pad_convert_fusion.refs_2_.refs_4_
  11.2 1.0 copy.68
  12.2 1.3 convert_element_type.41
  13.5 0.8 pad.18.clone
  14.2 0.7 broadcast_in_dim.25.refs_0_.refs_7_
  14.9 0.7 broadcast_in_dim.26.refs_1_
  15.6 48.5 %begin.1 = (f32[2,8,1024]{2,1,0:T(8,128)}, f32[8,1024]{1,0:T(8,128)}, bf16[8,1024]{1,0:T(8,128)(2,1)}, f32[128,1024]{1,0:T(8,128)}, bf16[128,1024]{1,0:T(8,128)(...) custom-call(s32[8,128]{1,0:T(8,128)} %broadcast_in_dim.25.refs_0_.re, ...), custom_call_target="tpu_custom_call" | custom-call | tf_op jit(solution)/shard_map/begin/pallas_call | solution.py:685
  64.0 1.4 slice_bitcast_fusion
  66.2 32.9 %attend0.1 = (bf16[3,1024,128]{2,1,0:T(8,128)(2,1)}, bf16[128,1024]{1,0:T(8,128)(2,1)}, bf16[4,128,1024]{2,1,0:T(8,128)(2,1)}, bf16[4,128,384]{2,1,0:T(8,128)(2,1)}) custom-call(bf16[128,3072]{1,0:T(8,128)(2,1)} %get-tuple-element.135.refs_0_, bf16[128,1024]{1,0:T(8,128)(2,1)} %get-tuple-element.136.refs_1_, bf16[128,384]{1,0:T(8,128)(2,1)} %get-tuple-element.137.refs_2_), custom_call_target="tpu_custom_call" | custom-call | tf_op jit(solution)/shard_map/attend0/pallas_call | solution.py:685
  99.1 26.6 %feed0.1 = (f32[128,1024]{1,0:T(8,128)}, f32[128,1024]{1,0:T(8,128)}, f32[128,1024]{1,0:T(8,128)}, f32[128,1024]{1,0:T(8,128)}, bf16[128,1024]{1,0:T(8,128)(2,1)...) custom-call(bf16[1024,1024]{1,0:T(8,128)(2,1)} %get-tuple-element.13, ...), custom_call_target="tpu_custom_call" | custom-call | tf_op jit(solution)/shard_map/feed0/pallas_call | solution.py:685
  125.7 36.1 %attend1.1 = (bf16[3,1024,128]{2,1,0:T(8,128)(2,1)}, bf16[128,1024]{1,0:T(8,128)(2,1)}, bf16[4,128,1024]{2,1,0:T(8,128)(2,1)}, bf16[4,128,384]{2,1,0:T(8,128)(2,1)}, bf16[4,128,1024]{2,1,0:T(8,128)(2,1)}) custom-call(bf16[128,3072]{1,0:T(8,128)(2,1)} %get-tuple-element.141.refs_0_, bf16[128,1024]{1,0:T(8,128)(2,1)} %get-tuple-element.142.refs_1_, ...), custom_call_target="tpu_custom_call" | custom-call | tf_op jit(solution)/shard_map/attend1/pallas_call | solution.py:685
  161.9 24.0 %feed1.1 = (f32[128,1024]{1,0:T(8,128)}, f32[128,1024]{1,0:T(8,128)}, f32[128,1024]{1,0:T(8,128)}, f32[128,1024]{1,0:T(8,128)}, bf16[128,1024]{1,0:T(8,128)(2,1)...) custom-call(bf16[1024,1024]{1,0:T(8,128)(2,1)} %get-tuple-element.13, ...), custom_call_target="tpu_custom_call" | custom-call | tf_op jit(solution)/shard_map/feed1/pallas_call | solution.py:685
  185.8 1.7 multiply_reduce_fusion
  187.5 29.7 %feed_back1.1 = (f32[8,1024]{1,0:T(8,128)}, f32[128,384]{1,0:T(8,128)}, bf16[128,384]{1,0:T(8,128)(2,1)}, f32[128,1024]{1,0:T(8,128)}, bf16[128,1024]{1,0:T(8,12...) custom-call(bf16[2,384,1024]{2,1,0:T(8,128)(2,1)} %bitcast.21, ...), custom_call_target="tpu_custom_call" | custom-call | tf_op jit(solution)/shard_map/feed_back1/pallas_call | solution.py:685
  217.3 44.5 %attend_back1.1 = (bf16[128,3072]{1,0:T(8,128)(2,1)}, bf16[4,128,256]{2,1,0:T(8,128)(2,1)}, bf16[4,128,256]{2,1,0:T(8,128)(2,1)}, bf16[4,128,384]{2,1,0:T(8,128)(2,1)}, bf16[4,128,1024]{2,1,0:T(8,128)(2,1)}) custom-call(bf16[128,1024]{1,0:T(8,128)(2,1)} %get-tuple-element.153.refs_0_, bf16[128,1024]{1,0:T(8,128)(2,1)} %get-tuple-element.154.refs_1_, ...), custom_call_target="tpu_custom_call" | custom-call | tf_op jit(solution)/shard_map/attend_back1/pallas_call | solution.py:685
  261.8 31.0 %feed_back0.1 = (bf16[128,1024]{1,0:T(8,128)(2,1)}, f32[8,1024]{1,0:T(8,128)}, f32[128,384]{1,0:T(8,128)}, bf16[128,384]{1,0:T(8,128)(2,1)}, f32[128,1024]{1,0:T...) custom-call(bf16[2,384,1024]{2,1,0:T(8,128)(2,1)} %bitcast.22, ...), custom_call_target="tpu_custom_call" | custom-call | tf_op jit(solution)/shard_map/feed_back0/pallas_call | solution.py:685
  292.8 3.4 collective-permute-start
  296.2 0.7 multiply_reduce_fusion.1
  297.6 51.7 %attend_back0.1 = (bf16[128,3072]{1,0:T(8,128)(2,1)}, bf16[4,128,256]{2,1,0:T(8,128)(2,1)}, bf16[4,128,256]{2,1,0:T(8,128)(2,1)}, bf16[4,128,384]{2,1,0:T(8,128)...) custom-call(bf16[128,1024]{1,0:T(8,128)(2,1)} %get-tuple-element.172.refs_0_, ...), custom_call_target="tpu_custom_call" | custom-call | tf_op jit(solution)/shard_map/attend_back0/pallas_call | solution.py:685
  349.2 1.0 copy-done.4
  350.2 95.2 %reduce.7 = (f32[128,256]{1,0:T(8,128)}, f32[8,1536]{1,0:T(8,128)}, f32[4,16,1536]{2,1,0:T(8,128)}, f32[96,256]{1,0:T(8,128)}, f32[1024,512]{1,0:T(8,128)}) custom-call(bf16[128,3072]{1,0:T(8,128)(2,1)} %get-tuple-element.178.refs_0_.refs_1_, bf16[128,3072]{1,0:T(8,128)(2,1)} %get-tuple-element.178.refs_0_.refs_1_, ...), custom_call_target="tpu_custom_call" | custom-call | tf_op jit(solution)/shard_map/reduce/pallas_call | solution.py:685
  445.4 0.8 slice.73
  446.2 0.9 slice.72
  447.6 187.8 %finish.1 = (f32[8,128]{1,0:T(8,128)}, f32[128,1536]{1,0:T(8,128)}, f32[8,1024]{1,0:T(8,128)}, bf16[8,96,256]{2,1,0:T(8,128)(2,1)}, f32[128,768]{1,0:T(8,128)}, ...) custom-call(f32[1024,512]{1,0:T(8,128)} %get-tuple-element.200.refs_, ...), custom_call_target="tpu_custom_call" | custom-call | tf_op jit(solution)/shard_map/finish/pallas_call | solution.py:685
  635.5 0.8 slice_reduce_fusion.1
  636.2 1.3 fusion.20
  639.2 1.0 slice.77
  640.2 1.9 maximum_multiply_fusion
  642.1 2.9 divide_subtract_fusion
  645.0 1.3 divide_subtract_fusion.2
  646.4 0.7 divide_subtract_fusion.1
  647.1 5.7 update.1
  652.9 0.7 copy.85
  653.6 1.1 copy.86
  654.8 0.7 copy.87
  655.4 0.8 copy.88
  656.2 0.8 copy.89
  657.0 1.3 copy.90
  658.4 0.8 copy.91
  659.2 0.5 copy-done.1
  659.7 1.3 copy.92
  (45 shorter events, 1.7 us)
Async XLA Ops:
  292.8 56.4 %collective-permute-start = (bf16[1024,512]{1,0:T(8,128)(2,1)}, bf16[1024,512]{1,0:T(8,128)(2,1)S(1)}, u32[]{:S(2)}, u32[]{:S(2)}) collective-permute-start(bf16[1024,512]{1,0:T(8,128)(2,1)} %get-tuple-element.184), channel_id=1, source_target_pairs={{0,4},{4,0},{8,12},{12,8},{16,20},{20,16},{24,28},{28,24},{1,5},{5... | collective-permute-start | bytes 3145736 | tf_op jit(solution)/shard_map/ppermute | solution.py:2237
  349.2 1.0 copy-start.4
  447.6 194.4 %copy-start = (f32[2,276,256]{2,0,1:T(2,128)S(1)}, f32[2,276,256]{2,0,1:T(2,128)}, u32[]{:S(2)}) copy-start(f32[2,276,256]{2,0,1:T(2,128)} %param.52) | copy-start | bytes 1695748
  447.6 194.4 %copy-start.5 = (f32[2,276,256]{2,0,1:T(2,128)S(1)}, f32[2,276,256]{2,0,1:T(2,128)}, u32[]{:S(2)}) copy-start(f32[2,276,256]{2,0,1:T(2,128)} %param.53) | copy-start | bytes 1695748
  447.6 194.4 %copy-start.6 = (f32[2,276,256]{2,0,1:T(2,128)S(1)}, f32[2,276,256]{2,0,1:T(2,128)}, u32[]{:S(2)}) copy-start(f32[2,276,256]{2,0,1:T(2,128)} %param.54) | copy-start | bytes 1695748
  639.1 5.9 copy-start.12
  639.1 5.9 copy-start.14
  639.1 5.9 copy-start.15
  639.1 7.2 %copy-start.13 = (f32[1792]{0:T(1024)S(1)}, f32[1792]{0:T(1024)}, u32[]{:S(2)}) copy-start(f32[1792]{0:T(1024)} %param.61) | copy-start | bytes 21508
  639.1 7.2 %copy-start.16 = (f32[1792]{0:T(1024)S(1)}, f32[1792]{0:T(1024)}, u32[]{:S(2)}) copy-start(f32[1792]{0:T(1024)} %param.62) | copy-start | bytes 21508
  639.1 7.2 %copy-start.17 = (f32[1792]{0:T(1024)S(1)}, f32[1792]{0:T(1024)}, u32[]{:S(2)}) copy-start(f32[1792]{0:T(1024)} %param.63) | copy-start | bytes 21508
  647.1 5.8 copy-start.10
  647.1 6.5 copy-start.3
  652.8 1.9 copy-start.11
  652.8 2.6 copy-start.9
  653.6 2.6 copy-start.8
  653.6 3.4 copy-start.2
  657.0 1.4 copy-start.7
  657.0 2.7 copy-start.1

commit v11 on v10

--- a/solution.py
+++ b/solution.py
@@ -3,6 +3,7 @@
 
 import jax
 import jax.numpy as jnp
+import numpy as np
 from jax import lax
 from jax.experimental import pallas as pl
 from jax.experimental.pallas import tpu as pltpu
@@ -554,6 +555,7 @@
         self.locals = []
         self.steps = []
         self.peers = {}
+        self.delivered = {}
 
     def operand(self, array, space=pl.ANY):
         self.operands.append(array)
@@ -588,6 +590,15 @@
     def save(self, source, shape, dtype):
         number = self.keep(source, None, self.output(shape, dtype), None, True)
         return number
+
+    def deliver(self, shape, dtype):
+        source = self.scratch(shape, dtype)
+        self.delivered[source] = self.save(source, shape, dtype)
+        return source
+
+    def hand_over(self, *sources):
+        for source in sources:
+            self.start_local(self.delivered.pop(source))
 
     def start_local(self, number):
         self.steps.append((self.begin_local, number))
@@ -682,6 +693,7 @@
             where(self.moves[number][5], copy.wait_send)
 
     def run(self):
+        self.hand_over(*list(self.delivered))
         return pl.pallas_call(
             self.kernel,
             out_shape=self.outputs,
@@ -849,12 +861,6 @@
         for target, place, number in waiting:
             self.move((SHARDS,), sibling_peer, target, place, target, place, (number,))
 
-    def exchange(self, axis, array, later=False):
-        target = self.output(array.shape, array.dtype)
-        return self.along(
-            axis, self.operand(array), target, [(lambda receiver: (receiver,), lambda sender: (sender,))], later
-        )
-
     def exchange_columns(self, axis, array):
         width = array.shape[-1] // lax.axis_size(axis)
         target = self.output((lax.axis_size(axis), array.shape[0], width), array.dtype)
@@ -954,11 +960,12 @@
     return pl.ds(pl.multiple_of(there * size, size), size)
 
 
-def add_attention(moves, qkv, mixed, arrivals, rows, members, waiting):
+def add_attention(moves, qkv, mixed, arrivals, planes, rows, members, waiting):
     for number in arrivals:
         moves.wait_for(number)
-    for number in range(3):
+    for number in planes:
         moves.wait_local(number)
+    moves.hand_over(qkv)
     moves.to_sibling(waiting)
     count = lax.axis_size(PATCHES)
     width = HEADS // count * HEAD
@@ -1063,7 +1070,7 @@
     small = [moves.gather_columns(SHARDS, cond_table, table), moves.gather_columns(SHARDS, biases, bias)]
     pos_moves, pos_local = moves.gather_columns(SHARDS, pos, pos_all)
     ada_weights, ada_load = moves.load(ada)
-    vmem = functools.partial(moves.output, space=pltpu.VMEM)
+    vmem = moves.deliver
     extras = vmem((ROLL, 8, width), f32)
     cond_vec, silu_low = vmem((shards * ROLL, width), f32), vmem((shards * ROLL, width), LOW)
     embedded, normed_low = vmem((rows, width), f32), vmem((rows, width), LOW)
@@ -1143,6 +1150,7 @@
         save = moves.save(target, moves.shape(target), LOW)
         moves.start_local(save)
     moves.start_local(moves.save(pos_all, (rows, width), LOW))
+    moves.hand_over(extras, cond_vec, silu_low, embedded, normed_low, state_low)
     project(moves, normed_low, weights[2][0], qkv_rows, 3 * width)
     return moves.run()
 
@@ -1280,9 +1288,9 @@
     up_weights, up_load = moves.load(w_up)
     down_weights, down_load = moves.load(w_down)
     io_weights, io_load = moves.load(io_all)
-    attended, after_attn, downward, after_mlp = [moves.output((rows, width), f32, pltpu.VMEM) for _ in range(4)]
-    normed_c = moves.output((rows, width), LOW, pltpu.VMEM)
-    state_next = moves.output((rows, padded), f32, pltpu.VMEM)
+    attended, after_attn, downward, after_mlp = [moves.deliver((rows, width), f32) for _ in range(4)]
+    normed_c = moves.deliver((rows, width), LOW)
+    state_next = moves.deliver((rows, padded), f32)
     upward = moves.scratch((shards, rows, hidden_count), f32)
     hidden = moves.scratch((shards, rows, hidden_count), LOW)
     feed = Tokens(moves, rows, width)
@@ -1294,10 +1302,10 @@
     if not last:
         mods_next, pos = vmem(mods_next), vmem(pos)
         qkv_weights, qkv_load = moves.load(w_qkv)
-        embedded_next = moves.output((rows, width), f32, pltpu.VMEM)
-        normed_next = moves.output((rows, width), LOW, pltpu.VMEM)
-        state_low = moves.output((rows, padded), LOW, pltpu.VMEM)
-        qkv_next = moves.output((rows, w_qkv.shape[1]), LOW, pltpu.VMEM)
+        embedded_next = moves.deliver((rows, width), f32)
+        normed_next = moves.deliver((rows, width), LOW)
+        state_low = moves.deliver((rows, padded), LOW)
+        qkv_next = moves.deliver((rows, w_qkv.shape[1]), LOW)
     half = rows // ROLL
     seq_count = lax.axis_size(PATCHES)
     most_cols = max(item.shape[1] for item in momenta) // members
@@ -1352,6 +1360,7 @@
 
     moves.wait_local(out_load)
     moves.task(begin)
+    moves.hand_over(attended, after_attn)
     moves.wait_local(up_load)
     moves.wait_local(down_load)
     feed.run(work)
@@ -1366,7 +1375,9 @@
     moves.wait_local(io_load)
     feed.wait()
     moves.task(finish)
+    moves.hand_over(downward, after_mlp, normed_c, state_next)
     if not last:
+        moves.hand_over(embedded_next, normed_next, state_low)
         moves.wait_local(qkv_load)
         project(moves, normed_next, qkv_weights, qkv_next, w_qkv.shape[1])
     return moves.run()
@@ -1386,18 +1397,18 @@
         qkv_weights, qkv_load = moves.load(w_qkv)
         later = [vmem(item) for item in later]
         mods_later = vmem(mods_later)
-        embed_grad = moves.output((rows, width), LOW, pltpu.VMEM)
+        embed_grad = moves.deliver((rows, width), LOW)
     down_weights, down_load = moves.load(w_down)
     up_weights, up_load = moves.load(w_up)
     slopes, slopes_load = moves.load(upward)
     out_weights, out_load = moves.load(w_out)
     mods, grad_state = vmem(mods), vmem(grad_state)
     attended, after_attn, downward, after_mlp = [vmem(item) for item in (attended, after_attn, downward, after_mlp)]
-    vectors = moves.output((8, width), f32, pltpu.VMEM)
-    state_out = moves.output((rows, padded), f32, pltpu.VMEM)
-    delta_grad = moves.output((rows, padded), LOW, pltpu.VMEM)
-    grad_attn = moves.output((rows, width), f32, pltpu.VMEM)
-    attn_grad, mixed_grad = [moves.output((rows, width), LOW, pltpu.VMEM) for _ in range(2)]
+    vectors = moves.deliver((8, width), f32)
+    state_out = moves.deliver((rows, padded), f32)
+    delta_grad = moves.deliver((rows, padded), LOW)
+    grad_attn = moves.deliver((rows, width), f32)
+    attn_grad, mixed_grad = [moves.deliver((rows, width), LOW) for _ in range(2)]
     grad_mlp = moves.scratch((rows, width), f32)
     up_grad = moves.scratch((shards, rows, hidden_count), LOW)
     feed = Tokens(moves, rows, width)
@@ -1492,6 +1503,9 @@
         moves.wait_local(qkv_load)
         moves.task(before)
     moves.task(begin)
+    moves.hand_over(state_out, delta_grad)
+    if later is not None:
+        moves.hand_over(embed_grad)
     for number in (down_load, up_load, slopes_load):
         moves.wait_local(number)
     feed.run(work)
@@ -1731,7 +1745,7 @@
     await_all(embed_moves)
     (state_all, embed_later) = ready("state", "embed")
     weight_grad(state_all, [embed_all, *embed_later], io_grads[0])
-    grad_pos = moves.output((rows, part), f32, pltpu.VMEM)
+    grad_pos = moves.deliver((rows, part), f32)
     io_rows = 2 * padded // seq_count
 
     def pos_and_io(ref):
@@ -1809,7 +1823,7 @@
     add_member(out_full, out_arriving, out_mine, out_mine_low, out_cols)
     out_group_moves = to_group(out_mine_low, out_target, 3)
 
-    modul_all = moves.output((shards * ROLL, ada_cols), f32, pltpu.VMEM)
+    modul_all = moves.deliver((shards * ROLL, ada_cols), f32)
     tail_all = moves.output((shards, 16, ada_cols), f32, pltpu.VMEM)
     tail = moves.scratch((16, ada_cols), f32)
 
@@ -1833,6 +1847,7 @@
     moves.wait_local(ada_load)
     moves.task(close)
     to_others(SHARDS, tail, lambda there: (slice(None), slice(None)), tail_all)
+    moves.hand_over(grad_pos, modul_all)
 
     def hand_down(piece):
         number, following = down_hops[0][piece], down_hops[1][piece]
@@ -1888,7 +1903,7 @@
         if number_of % turns == turns - 1:
             hand_down(number_of // turns)
 
-    io_slice = moves.output((io_rows, part), f32, pltpu.VMEM)
+    io_slice = moves.deliver((io_rows, part), f32)
 
     def add_io(ref):
         value = jnp.zeros((io_rows, part), f32)
@@ -1899,7 +1914,7 @@
     await_all(io_moves)
     moves.task(add_io)
 
-    grad_group = moves.output((block_rows, most_cols), f32, pltpu.VMEM)
+    grad_group = moves.deliver((block_rows, most_cols), f32)
 
     def put(full, target, places, cols):
         def action(ref):
@@ -2150,14 +2165,15 @@
 
     for step in range(ROLL):
         moves = Moves(f"attend{step}", ids, KERNEL_VMEM)
-        qkv_out = moves.output((3, local * seq_count, width // seq_count), LOW, pltpu.VMEM)
+        qkv_out = moves.deliver((3, local * seq_count, width // seq_count), LOW)
         mixed_out = moves.output((local, width), LOW, pltpu.VMEM)
         arrivals = moves.rows_to_heads(PATCHES, qkv_rows, 3, qkv_out)
+        planes = range(len(moves.locals) - 3, len(moves.locals))
         waiting = moves.gather_pairs(normed_a, hold=True)
         waiting += moves.gather_pairs(state_low, hold=True)
         if step:
             waiting += moves.gather_pairs(kept[-1][2], hold=True)
-        add_attention(moves, qkv_out, mixed_out, arrivals, local, members, waiting)
+        add_attention(moves, qkv_out, mixed_out, arrivals, planes, local, members, waiting)
         qkv, mixed, gathered_a, gathered_state, *gathered_mixed = moves.run()
         gathered.setdefault("a", {})[step] = gathered_a
         gathered.setdefault("state", {})[step] = gathered_state
@@ -2188,7 +2204,9 @@
         if following:
             embedded, normed_a, state_low, qkv_rows = following
 
-    lat = latitude_weights(local)
+    bands = (np.arange(local * seq_count) // LON + 0.5) * (math.pi / (local * seq_count // LON)) - math.pi / 2
+    cosines = np.cos(bands) / np.mean(np.cos(bands))
+    lat = lax.dynamic_slice_in_dim(jnp.asarray(cosines, f32), seq_index * local, local)
     diff = state - jnp.pad(targets[0].astype(f32), value_pad)
     loss_local = weight * jnp.sum(jnp.sum(diff * diff, -1) * lat)
     grad_state = 2.0 * weight * lat[:, None] * diff
@@ -2296,11 +2314,11 @@
         for half, item in enumerate(moment_halves)
     ]
     master_loads = [moves.load(item) for item in masters]
-    sums = vmem_out((8, LANES), f32)
-    grad_ada = vmem_out((block_part, ada_cols), f32)
-    grad_table_all = vmem_out((8, width), f32)
+    sums = moves.deliver((8, LANES), f32)
+    grad_ada = moves.deliver((block_part, ada_cols), f32)
+    grad_table_all = moves.deliver((8, width), f32)
     io_all_parts = vmem_out((seq_count,) + io_slice.shape, LOW)
-    fresh = [vmem_out(item.shape, f32) for item in masters]
+    fresh = [moves.deliver(item.shape, f32) for item in masters]
     fresh_low = [moves.scratch(item.shape, LOW) for item in masters]
     near, far = [moves.scratch((count, 8, LANES), f32) for count in (shards, seq_count)]
     grad_low, source = moves.scratch(low, LOW), moves.scratch(low, LOW)
@@ -2583,6 +2601,7 @@
     for _, number in master_loads:
         moves.wait_local(number)
     moves.task(renew)
+    moves.hand_over(sums, grad_ada, grad_table_all, *fresh)
 
     rows = block_rows // seq_count
 

time: 673 us -> 665 us (0.988)
  Pallas kernels: 614 us -> 607 us
where the time goes in v11:
time: 665 us; the launch traced here: 655 us
  Pallas kernels  607 us (91%)
  local copies, waits for them, and re-layouts  24.2 us (4%)
  other arithmetic  16.2 us (2%)
    pallas_call x11, Pallas kernels, run(): pl.pallas_call(self.kernel, out_shape=self.outputs, in_specs=self.operand...  602 us
  transfers between devices with their start and end apart: 1, of which 0 were waited for; matrix products, arithmetic and copies ran while one was open for 0% of the time, Pallas kernels for 8%

profile of v11, /device:TPU:0, one launch (start us, length us, event | category | flops | bytes accessed | tf_op | source)
XLA Modules:
  0.0 655.4 jit_solution(4921183871790373080)
XLA Ops:
  1.3 1.2 dynamic_slice.12
  2.6 1.9 fusion.6
  4.5 0.7 broadcast_in_dim.23
  5.3 1.3 broadcast_in_dim.27.refs_4_
  6.6 1.5 convert_element_type.35.refs_5_
  8.1 1.0 copy.67
  9.1 0.7 pad_convert_fusion.refs_2_.refs_4_
  9.8 1.0 copy.69
  10.8 1.3 convert_element_type.36
  12.1 0.8 pad.18.clone
  12.9 0.7 broadcast_in_dim.25.refs_0_.refs_7_
  13.6 0.7 broadcast_in_dim.26.refs_1_
  14.2 47.9 %begin.1 = (f32[2,8,1024]{2,1,0:T(8,128)}, f32[8,1024]{1,0:T(8,128)}, bf16[8,1024]{1,0:T(8,128)(2,1)}, f32[128,1024]{1,0:T(8,128)}, bf16[128,1024]{1,0:T(8,128)(...) custom-call(s32[8,128]{1,0:T(8,128)} %broadcast_in_dim.25.refs_0_.re, ...), custom_call_target="tpu_custom_call" | custom-call | tf_op jit(solution)/shard_map/begin/pallas_call | solution.py:697
  62.1 1.4 slice_bitcast_fusion
  64.2 0.8 dynamic-slice_multiply_fusion.1
  65.0 32.5 %attend0.1 = (bf16[3,1024,128]{2,1,0:T(8,128)(2,1)}, bf16[128,1024]{1,0:T(8,128)(2,1)}, bf16[4,128,1024]{2,1,0:T(8,128)(2,1)}, bf16[4,128,384]{2,1,0:T(8,128)(2,1)}) custom-call(bf16[128,3072]{1,0:T(8,128)(2,1)} %get-tuple-element.135.refs_0_, bf16[128,1024]{1,0:T(8,128)(2,1)} %get-tuple-element.136.refs_1_, bf16[128,384]{1,0:T(8,128)(2,1)} %get-tuple-element.137.refs_2_), custom_call_target="tpu_custom_call" | custom-call | tf_op jit(solution)/shard_map/attend0/pallas_call | solution.py:697
  97.5 24.9 %feed0.1 = (f32[128,1024]{1,0:T(8,128)}, f32[128,1024]{1,0:T(8,128)}, f32[128,1024]{1,0:T(8,128)}, f32[128,1024]{1,0:T(8,128)}, bf16[128,1024]{1,0:T(8,128)(2,1)...) custom-call(bf16[1024,1024]{1,0:T(8,128)(2,1)} %get-tuple-element.13, ...), custom_call_target="tpu_custom_call" | custom-call | tf_op jit(solution)/shard_map/feed0/pallas_call | solution.py:697
  122.4 35.1 %attend1.1 = (bf16[3,1024,128]{2,1,0:T(8,128)(2,1)}, bf16[128,1024]{1,0:T(8,128)(2,1)}, bf16[4,128,1024]{2,1,0:T(8,128)(2,1)}, bf16[4,128,384]{2,1,0:T(8,128)(2,1)}, bf16[4,128,1024]{2,1,0:T(8,128)(2,1)}) custom-call(bf16[128,3072]{1,0:T(8,128)(2,1)} %get-tuple-element.141.refs_0_, bf16[128,1024]{1,0:T(8,128)(2,1)} %get-tuple-element.142.refs_1_, ...), custom_call_target="tpu_custom_call" | custom-call | tf_op jit(solution)/shard_map/attend1/pallas_call | solution.py:697
  157.5 23.1 %feed1.1 = (f32[128,1024]{1,0:T(8,128)}, f32[128,1024]{1,0:T(8,128)}, f32[128,1024]{1,0:T(8,128)}, f32[128,1024]{1,0:T(8,128)}, bf16[128,1024]{1,0:T(8,128)(2,1)...) custom-call(bf16[1024,1024]{1,0:T(8,128)(2,1)} %get-tuple-element.13, ...), custom_call_target="tpu_custom_call" | custom-call | tf_op jit(solution)/shard_map/feed1/pallas_call | solution.py:697
  180.6 1.7 multiply_reduce_fusion
  182.4 29.5 %feed_back1.1 = (f32[8,1024]{1,0:T(8,128)}, f32[128,384]{1,0:T(8,128)}, bf16[128,384]{1,0:T(8,128)(2,1)}, f32[128,1024]{1,0:T(8,128)}, bf16[128,1024]{1,0:T(8,12...) custom-call(bf16[2,384,1024]{2,1,0:T(8,128)(2,1)} %bitcast.21, ...), custom_call_target="tpu_custom_call" | custom-call | tf_op jit(solution)/shard_map/feed_back1/pallas_call | solution.py:697
  211.8 44.3 %attend_back1.1 = (bf16[128,3072]{1,0:T(8,128)(2,1)}, bf16[4,128,256]{2,1,0:T(8,128)(2,1)}, bf16[4,128,256]{2,1,0:T(8,128)(2,1)}, bf16[4,128,384]{2,1,0:T(8,128)(2,1)}, bf16[4,128,1024]{2,1,0:T(8,128)(2,1)}) custom-call(bf16[128,1024]{1,0:T(8,128)(2,1)} %get-tuple-element.153.refs_0_, bf16[128,1024]{1,0:T(8,128)(2,1)} %get-tuple-element.154.refs_1_, ...), custom_call_target="tpu_custom_call" | custom-call | tf_op jit(solution)/shard_map/attend_back1/pallas_call | solution.py:697
  256.1 30.1 %feed_back0.1 = (bf16[128,1024]{1,0:T(8,128)(2,1)}, f32[8,1024]{1,0:T(8,128)}, f32[128,384]{1,0:T(8,128)}, bf16[128,384]{1,0:T(8,128)(2,1)}, f32[128,1024]{1,0:T...) custom-call(bf16[2,384,1024]{2,1,0:T(8,128)(2,1)} %bitcast.22, ...), custom_call_target="tpu_custom_call" | custom-call | tf_op jit(solution)/shard_map/feed_back0/pallas_call | solution.py:697
  286.2 2.5 collective-permute-start
  288.6 1.4 multiply_reduce_fusion.1
  290.6 51.3 %attend_back0.1 = (bf16[128,3072]{1,0:T(8,128)(2,1)}, bf16[4,128,256]{2,1,0:T(8,128)(2,1)}, bf16[4,128,256]{2,1,0:T(8,128)(2,1)}, bf16[4,128,384]{2,1,0:T(8,128)...) custom-call(bf16[128,1024]{1,0:T(8,128)(2,1)} %get-tuple-element.172.refs_0_, ...), custom_call_target="tpu_custom_call" | custom-call | tf_op jit(solution)/shard_map/attend_back0/pallas_call | solution.py:697
  341.9 1.0 copy-done.4
  342.9 96.1 %reduce.7 = (f32[128,256]{1,0:T(8,128)}, f32[8,1536]{1,0:T(8,128)}, f32[4,16,1536]{2,1,0:T(8,128)}, f32[96,256]{1,0:T(8,128)}, f32[1024,512]{1,0:T(8,128)}) custom-call(bf16[128,3072]{1,0:T(8,128)(2,1)} %get-tuple-element.178.refs_0_.refs_1_, bf16[128,3072]{1,0:T(8,128)(2,1)} %get-tuple-element.178.refs_0_.refs_1_, ...), custom_call_target="tpu_custom_call" | custom-call | tf_op jit(solution)/shard_map/reduce/pallas_call | solution.py:697
  439.0 0.8 slice.73
  439.8 0.9 slice.72
  441.2 187.1 %finish.1 = (f32[8,128]{1,0:T(8,128)}, f32[128,1536]{1,0:T(8,128)}, f32[8,1024]{1,0:T(8,128)}, bf16[8,96,256]{2,1,0:T(8,128)(2,1)}, f32[128,768]{1,0:T(8,128)}, ...) custom-call(f32[1024,512]{1,0:T(8,128)} %get-tuple-element.200.refs_, ...), custom_call_target="tpu_custom_call" | custom-call | tf_op jit(solution)/shard_map/finish/pallas_call | solution.py:697
  628.3 0.8 slice_reduce_fusion.1
  629.1 1.3 fusion.10
  632.0 1.0 slice.77
  633.0 1.9 maximum_multiply_fusion
  634.9 2.9 divide_subtract_fusion
  637.9 1.3 divide_subtract_fusion.2
  639.2 0.7 divide_subtract_fusion.1
  639.9 5.7 update.1
  645.7 0.7 copy.86
  646.4 1.1 copy.87
  647.6 0.7 copy.88
  648.2 0.8 copy.89
  649.0 0.8 copy.90
  649.8 1.3 copy.91
  651.2 0.8 copy.92
  652.0 0.5 copy-done.1
  652.6 1.3 copy.93
  (43 shorter events, 1.6 us)
Async XLA Ops:
  286.2 55.8 %collective-permute-start = (bf16[1024,512]{1,0:T(8,128)(2,1)}, bf16[1024,512]{1,0:T(8,128)(2,1)S(1)}, u32[]{:S(2)}, u32[]{:S(2)}) collective-permute-start(bf16[1024,512]{1,0:T(8,128)(2,1)} %get-tuple-element.184), channel_id=1, source_target_pairs={{0,4},{4,0},{8,12},{12,8},{16,20},{20,16},{24,28},{28,24},{1,5},{5... | collective-permute-start | bytes 3145736 | tf_op jit(solution)/shard_map/ppermute | solution.py:2255
  341.9 1.0 copy-start.4
  441.2 193.7 %copy-start = (f32[2,276,256]{2,0,1:T(2,128)S(1)}, f32[2,276,256]{2,0,1:T(2,128)}, u32[]{:S(2)}) copy-start(f32[2,276,256]{2,0,1:T(2,128)} %param.53) | copy-start | bytes 1695748
  441.2 193.7 %copy-start.5 = (f32[2,276,256]{2,0,1:T(2,128)S(1)}, f32[2,276,256]{2,0,1:T(2,128)}, u32[]{:S(2)}) copy-start(f32[2,276,256]{2,0,1:T(2,128)} %param.54) | copy-start | bytes 1695748
  441.2 193.7 %copy-start.6 = (f32[2,276,256]{2,0,1:T(2,128)S(1)}, f32[2,276,256]{2,0,1:T(2,128)}, u32[]{:S(2)}) copy-start(f32[2,276,256]{2,0,1:T(2,128)} %param.55) | copy-start | bytes 1695748
  632.0 5.9 copy-start.12
  632.0 5.9 copy-start.14
  632.0 5.9 copy-start.15
  632.0 7.2 %copy-start.13 = (f32[1792]{0:T(1024)S(1)}, f32[1792]{0:T(1024)}, u32[]{:S(2)}) copy-start(f32[1792]{0:T(1024)} %param.62) | copy-start | bytes 21508
  632.0 7.2 %copy-start.16 = (f32[1792]{0:T(1024)S(1)}, f32[1792]{0:T(1024)}, u32[]{:S(2)}) copy-start(f32[1792]{0:T(1024)} %param.63) | copy-start | bytes 21508
  632.0 7.2 %copy-start.17 = (f32[1792]{0:T(1024)S(1)}, f32[1792]{0:T(1024)}, u32[]{:S(2)}) copy-start(f32[1792]{0:T(1024)} %param.64) | copy-start | bytes 21508
  639.9 5.8 copy-start.10
  639.9 6.5 copy-start.3
  645.7 1.9 copy-start.11
  645.7 2.6 copy-start.9
  646.4 2.6 copy-start.8
  646.4 3.4 copy-start.2
  649.8 1.4 copy-start.7
  649.8 2.7 copy-start.1
